TPU v7x, 32 devices: a whole 2x2x4 slice. The times are simulated.
32 devices in a mesh: row: 8 (over z, core), col: 4 (over y, x).
Axes of the slice: x: 2, y: 2, z: 4, core: 2. Of those that a mesh axis runs over, the one named last changes fastest.
Arguments:
- pre_silu: bfloat16 [2, 24, 24, 256], P(None, 'row', 'col'), may hold values from -6 to 6
- out_grad: bfloat16 [2, 24, 24, 256], P(None, 'row', 'col'), may hold values from -6 to 6
- query_heads: bfloat16 [8, 576, 64], P('col', 'row'), may hold values from -10 to 10
- key_heads: bfloat16 [8, 576, 64], P('col', 'row'), may hold values from -10 to 10
- value_heads: bfloat16 [8, 576, 64], P('col', 'row'), may hold values from -6 to 6
- conv_weight: bfloat16 [3, 3, 256, 256], replicated, may hold values from -0.125 to 0.125
- out_weight: bfloat16 [256, 256], replicated, may hold values from -0.375 to 0.375
- input_weight: bfloat16 [256, 768], replicated, may hold values from -0.375 to 0.375
Outputs:
- grad_input: bfloat16 [2, 24, 24, 256], P(None, 'row', 'col')
All inputs are finite; a program needn't handle non-finite values.
Results may differ from a plain program's by a relative error of at most 0.0095.
Values may be sent and summed in bfloat16 or wider, within the bound.
No kernel may reach another device: no remote copies, remote signals or barrier semaphores. Data moves between devices by JAX's collectives and lax.ppermute only.
A program may use at most 64 MiB of HBM per device.

v0:
```python
import jax
import jax.numpy as jnp
from jax import lax
from jax.sharding import PartitionSpec as P

HEADS = 4


def with_halo(cells, sides, width):
    for axis, dim in sides:
        count = lax.axis_size(axis)
        ends = count - 1
        head = lax.slice_in_dim(cells, 0, width, axis=dim)
        tail = lax.slice_in_dim(cells, cells.shape[dim] - width, cells.shape[dim], axis=dim)
        cells = jnp.concatenate(
            [
                lax.ppermute(tail, axis, [(i, (i + 1) % count) for i in range(ends)]),
                cells,
                lax.ppermute(head, axis, [((i + 1) % count, i) for i in range(ends)]),
            ],
            axis=dim,
        )
    return cells


def run_blocks(update, running, arrays, block_rows):
    amount = arrays[0].shape[1]
    grouped = tuple(
        (
            jnp.moveaxis(
                member.reshape(
                    (member.shape[0], amount // block_rows, block_rows) + member.shape[2:]
                ),
                1,
                0,
            )
            for member in arrays
        )
    )

    def advance(current, sliced):
        return (update(current, *sliced), None)

    running, unused = lax.scan(advance, running, grouped)
    return running


def contract(left, right):
    return jnp.einsum("ptd,pud->ptu", left, right, preferred_element_type=jnp.float32)


def shards(
    pre_silu, out_grad, query_heads, key_heads, value_heads, conv_weight, out_weight, input_weight
):
    samples, rows_dev, cols_dev, channels = pre_silu.shape
    head_count = HEADS
    pairs = query_heads.shape[0]
    head_dim = query_heads.shape[2]
    factor = head_dim ** (-0.5)
    padded = with_halo(out_grad, (("row", 1), ("col", 2)), 1)
    conv_sum = jnp.zeros((samples, rows_dev, cols_dev, channels), jnp.float32)
    for shift_r in (-1, 0, 1):
        for shift_c in (-1, 0, 1):
            window = padded[
                :, 1 - shift_r : 1 - shift_r + rows_dev, 1 - shift_c : 1 - shift_c + cols_dev, :
            ]
            conv_sum = conv_sum + jnp.einsum(
                "srcd,ed->srce",
                window,
                conv_weight[shift_r + 1, shift_c + 1],
                preferred_element_type=jnp.float32,
            )
    z_float = pre_silu.astype(jnp.float32)
    sigmoid_z = jax.nn.sigmoid(z_float)
    grad_z = (conv_sum * sigmoid_z * (1.0 + z_float * (1.0 - sigmoid_z))).astype(jnp.bfloat16)
    grad_attn = jnp.einsum(
        "srcd,hed->shrce",
        grad_z,
        out_weight.reshape(head_count, head_dim, channels),
        preferred_element_type=jnp.float32,
    ).astype(jnp.bfloat16)
    grad_attn = grad_attn.reshape(samples * head_count, rows_dev, cols_dev, head_dim)
    strip_heads = lax.all_to_all(grad_attn, "col", split_axis=0, concat_axis=2, tiled=True)
    width_all = strip_heads.shape[2]
    strip_rows = rows_dev * width_all
    grad_out = strip_heads.reshape(pairs, strip_rows, head_dim)
    block_rows = 4 * strip_rows

    def stats_update(running, key_block, value_block):
        running_max, norm_sum, weighted = running
        scores = contract(query_heads, key_block) * factor
        grad_probs = contract(grad_out, value_block)
        new_max = jnp.maximum(running_max, jnp.max(scores, axis=2))
        exp_scores = jnp.exp(scores - new_max[:, :, None])
        rescale = jnp.exp(running_max - new_max)
        return (
            new_max,
            norm_sum * rescale + jnp.sum(exp_scores, axis=2),
            weighted * rescale + jnp.sum(exp_scores * grad_probs, axis=2),
        )

    zero_vec = jnp.zeros((pairs, strip_rows), jnp.float32)
    init_stats = (jnp.full((pairs, strip_rows), -jnp.inf, jnp.float32), zero_vec, zero_vec)
    keys_all, values_all = (
        lax.all_gather(key_heads, "row", axis=1, tiled=True),
        lax.all_gather(value_heads, "row", axis=1, tiled=True),
    )
    stats = run_blocks(stats_update, init_stats, (keys_all, values_all), block_rows)
    log_norm = stats[0] + jnp.log(stats[1])
    row_dot = stats[2] / stats[1]

    def query_update(grad_query, key_block, value_block):
        scores = contract(query_heads, key_block) * factor
        prob_block = jnp.exp(scores - log_norm[:, :, None])
        grad_probs = contract(grad_out, value_block)
        grad_scores = (prob_block * (grad_probs - row_dot[:, :, None])).astype(jnp.bfloat16)
        return (
            grad_query
            + jnp.einsum("ptu,pud->ptd", grad_scores, key_block, preferred_element_type=jnp.float32)
            * factor
        )

    zero_rows = jnp.zeros((pairs, strip_rows, head_dim), jnp.float32)
    grad_query = run_blocks(query_update, zero_rows, (keys_all, values_all), block_rows)
    log_all, dot_all = (
        lax.all_gather(log_norm, "row", axis=1, tiled=True),
        lax.all_gather(row_dot, "row", axis=1, tiled=True),
    )

    def pair_update(running, query_block, grad_block, log_block, dot_block):
        grad_key, grad_value = running
        scores = contract(key_heads, query_block) * factor
        prob_block = jnp.exp(scores - log_block[:, None, :])
        grad_probs = contract(value_heads, grad_block)
        grad_scores = (prob_block * (grad_probs - dot_block[:, None, :])).astype(jnp.bfloat16)
        grad_key = (
            grad_key
            + jnp.einsum(
                "ptu,pud->ptd", grad_scores, query_block, preferred_element_type=jnp.float32
            )
            * factor
        )
        grad_value = grad_value + jnp.einsum(
            "ptu,pud->ptd",
            prob_block.astype(jnp.bfloat16),
            grad_block,
            preferred_element_type=jnp.float32,
        )
        return (grad_key, grad_value)

    query_block = lax.all_gather(query_heads, "row", axis=1, tiled=True)
    grad_block = lax.all_gather(grad_out, "row", axis=1, tiled=True)
    log_block = log_all
    dot_block = dot_all
    grad_key, grad_value = run_blocks(
        pair_update,
        (zero_rows, zero_rows),
        (query_block, grad_block, log_block, dot_block),
        block_rows,
    )
    returned = lax.all_to_all(
        jnp.stack([grad_query, grad_key, grad_value])
        .astype(jnp.bfloat16)
        .reshape(3, pairs, rows_dev, width_all, head_dim),
        "col",
        split_axis=3,
        concat_axis=1,
        tiled=True,
    )
    returned = returned.reshape(3, samples, head_count, rows_dev, cols_dev, head_dim)
    projected = jnp.einsum(
        "kshrce,dkhe->srcd",
        returned,
        input_weight.reshape(channels, 3, head_count, head_dim),
        preferred_element_type=jnp.float32,
    )
    return (grad_z.astype(jnp.float32) + projected).astype(jnp.bfloat16)


def solution(mesh):
    in_specs = (
        P(None, "row", "col", None),
        P(None, "row", "col", None),
        P("col", "row", None),
        P("col", "row", None),
        P("col", "row", None),
        P(),
        P(),
        P(),
    )
    out_specs = P(None, "row", "col", None)
    return jax.shard_map(shards, mesh=mesh, in_specs=in_specs, out_specs=out_specs, check_vma=False)
```

profile of v0, /device:TPU:0, one launch (start us, length us, event | category | flops | bytes accessed | tf_op | source)
XLA Modules:
  0.0 122.2 jit_solution(16813186111870210571)
XLA Ops:
  0.0 0.8 copy.91
  0.8 2.4 %collective-permute-start = (bf16[2,1,6,256]{3,2,1,0:T(8,128)(2,1)S(1)}, bf16[2,1,6,256]{3,2,1,0:T(8,128)(2,1)S(1)}, u32[]{:S(2)}, u32[]{:S(2)}) collective-permute-start(bf16[2,1,6,256]{3,2,1,0:T(8,128)(2,1)S(1)} %get-tuple-element.371), channel_id=1, source_target_pairs={{0,4},{4,8},{8,12},{12,16},{16,20},{20,24},{24,28},{1,5},{5,9},{9,... | collective-permute-start | bytes 18440 | tf_op jit(solution)/shard_map/ppermute | solution.py:17
  3.2 1.3 %collective-permute-start.1 = (bf16[2,1,6,256]{3,2,1,0:T(8,128)(2,1)S(1)}, bf16[2,1,6,256]{3,2,1,0:T(8,128)(2,1)S(1)}, u32[]{:S(2)}, u32[]{:S(2)}) collective-permute-start(bf16[2,1,6,256]{3,2,1,0:T(8,128)(2,1)S(1)} %get-tuple-element.370), channel_id=1, source_target_pairs={{4,0},{8,4},{12,8},{16,12},{20,16},{24,20},{28,24},{5,1},{9,5},{13... | collective-permute-start | bytes 18440 | tf_op jit(solution)/shard_map/ppermute | solution.py:19
  4.5 1.1 fusion.76
  5.6 0.9 copy.100
  6.5 17.8 %all_gather.19 = bf16[2,576,64]{2,0,1:T(2,128)(2,1)S(1)} all-gather(bf16[2,72,64]{2,0,1:T(2,128)(2,1)S(1)} %copy.100), channel_id=1, replica_groups=mesh['row'=8,'col'=4] {'row'}, dimensions={1}, use_global_device_ids=true | all-gather | bytes 165888 | tf_op jit(solution)/shard_map/all_gather | solution.py:106
  24.3 0.9 copy.98
  25.2 14.2 %all_gather.18 = bf16[2,576,64]{2,0,1:T(2,128)(2,1)S(1)} all-gather(bf16[2,72,64]{2,0,1:T(2,128)(2,1)S(1)} %copy.98), channel_id=1, replica_groups=mesh['row'=8,'col'=4] {'row'}, dimensions={1}, use_global_device_ids=true | all-gather | bytes 165888 | tf_op jit(solution)/shard_map/all_gather | solution.py:105
  39.4 0.8 copy.113
  40.4 1.3 %collective-permute-start.2 = (bf16[2,5,1,256]{3,2,1,0:T(2,128)(2,1)S(1)}, bf16[2,5,1,256]{3,2,1,0:T(2,128)(2,1)S(1)}, u32[]{:S(2)}, u32[]{:S(2)}) collective-permute-start(bf16[2,5,1,256]{3,2,1,0:T(2,128)(2,1)S(1)} %get-tuple-element.368), channel_id=1, source_target_pairs={{1,0},{2,1},{3,2},{5,4},{6,5},{7,6},{9,8},{10,9},{11,10},{13,12},{... | collective-permute-start | bytes 15368 | tf_op jit(solution)/shard_map/ppermute | solution.py:19
  41.7 4.5 %collective-permute-start.3 = (bf16[2,5,1,256]{3,2,1,0:T(2,128)(2,1)S(1)}, bf16[2,5,1,256]{3,2,1,0:T(2,128)(2,1)S(1)}, u32[]{:S(2)}, u32[]{:S(2)}) collective-permute-start(bf16[2,5,1,256]{3,2,1,0:T(2,128)(2,1)S(1)} %get-tuple-element.369), channel_id=1, source_target_pairs={{0,1},{1,2},{2,3},{4,5},{5,6},{6,7},{8,9},{9,10},{10,11},{12,13},{... | collective-permute-start | bytes 15368 | tf_op jit(solution)/shard_map/ppermute | solution.py:17
  46.4 0.2 fusion.71
  46.6 1.0 collective-permute-done.3
  47.8 0.2 fusion.69
  48.2 0.2 fusion.73
  48.4 0.2 fusion.61
  48.6 0.2 fusion.66
  49.1 0.7 reshape.82
  49.8 5.4 %all-to-all-start = ((bf16[4,2,1152]{2,1,0:T(2,128)(2,1)}), bf16[4,2,1152]{2,1,0:T(2,128)(2,1)S(1)}, u32[]{:S(2)}, u32[]{:S(2)}) async-start(bf16[4,2,1152]{2,1,0:T(2,128)(2,1)} %reshape.82), calls=%async_computation | async-start | bytes 36864 | tf_op jit(solution)/shard_map/all_to_all | solution.py:83
  55.2 14.6 %all_gather.20 = bf16[2,576,64]{2,0,1:T(2,128)(2,1)S(1)} all-gather(bf16[2,72,64]{2,0,1:T(2,128)(2,1)S(1)} %copy.113), channel_id=1, replica_groups=mesh['row'=8,'col'=4] {'row'}, dimensions={1}, use_global_device_ids=true | all-gather | bytes 165888 | tf_op jit(solution)/shard_map/all_gather | solution.py:151
  70.6 14.2 %all_gather.22 = bf16[2,576,64]{2,0,1:T(2,128)(2,1)S(1)} all-gather(bf16[2,72,64]{2,0,1:T(2,128)(2,1)S(1)} %bitcast.226), channel_id=1, replica_groups=mesh['row'=8,'col'=4] {'row'}, dimensions={1}, use_global_device_ids=true | all-gather | bytes 165888 | tf_op jit(solution)/shard_map/all_gather | solution.py:152
  84.9 1.8 %while.39 = (s32[]{:T(128)}, f32[2,72]{1,0:T(2,128)S(1)}, f32[2,72]{1,0:T(2,128)S(1)}, f32[2,72]{1,0:T(2,128)S(1)}, bf16[2,2,288,64]{2,3,1,0:T(8,128)(2,1)S(1)},...) while((s32[]{:T(128)}, f32[2,72]{1,0:T(2,128)S(1)}, ...), condition=%wide.region_4.5_spmd.clone, body=%wide.region_0.4_spmd.clone.sunk | while | flops 10908147 | bytes 826040 | solution.py:44
  84.9 0.3 fusion.161
  85.2 0.3 fusion.163
  85.5 0.2 fusion.164
  85.8 0.3 fusion.161
  86.1 0.3 fusion.163
  86.5 0.2 fusion.164
  86.7 1.3 %while.40 = (s32[]{:T(128)}, f32[2,72,64]{1,2,0:T(8,128)S(1)}, bf16[2,2,288,64]{2,3,1,0:T(8,128)(2,1)S(1)}, bf16[2,72,64]{1,2,0:T(8,128)(2,1)S(1)}, f32[2,72]{1,...) while((s32[]{:T(128)}, f32[2,72,64]{1,2,0:T(8,128)S(1)}, ...), condition=%wide.region_6.7_spmd.clone, body=%wide.region_5.6_spmd.clone.sunk | while | flops 16160259 | bytes 705203 | solution.py:44
  86.8 0.2 convolution_subtract_fusion.3
  87.0 0.4 fusion.171
  87.4 0.2 convolution_subtract_fusion.3
  87.7 0.4 fusion.171
  88.2 0.2 copy.120
  88.4 11.8 %all-gather = f32[8,72,2]{1,2,0:T(2,128)S(1)} all-gather(f32[1,72,2]{1,2,0:T(2,128)S(1)} %bitcast.238), channel_id=1, replica_groups=mesh['row'=8,'col'=4] {'row'}, dimensions={0}, use_global_device_ids=true | all-gather | bytes 5184 | tf_op jit(solution)/shard_map/all_gather | solution.py:126
  100.3 8.7 %all-gather.1 = f32[8,72,2]{1,2,0:T(2,128)S(1)} all-gather(f32[1,72,2]{1,2,0:T(2,128)S(1)} %bitcast.237), channel_id=1, replica_groups=mesh['row'=8,'col'=4] {'row'}, dimensions={0}, use_global_device_ids=true | all-gather | bytes 5184 | tf_op jit(solution)/shard_map/all_gather | solution.py:127
  109.2 1.8 %while.41 = (s32[]{:T(128)}, f32[2,72,64]{1,2,0:T(8,128)S(1)}, f32[2,72,64]{1,2,0:T(8,128)S(1)}, bf16[2,2,288,64]{2,3,1,0:T(8,128)(2,1)S(1)}, bf16[2,72,64]{1,2,...) while((s32[]{:T(128)}, f32[2,72,64]{1,2,0:T(8,128)S(1)}, ...), condition=%wide.region_8.9_spmd.clone, body=%wide.region_7.8_spmd.clone.sunk | while | flops 21528580 | bytes 1297540 | solution.py:44
  109.2 0.2 fusion.179
  109.5 0.4 fusion.180
  109.9 0.2 convolution_add_fusion.4
  110.1 0.2 fusion.179
  110.4 0.4 fusion.180
  110.8 0.2 convolution_add_fusion.4
  111.3 0.8 reshape.84
  112.1 4.2 %all-to-all-start.1 = ((bf16[4,2,3456]{2,1,0:T(2,128)(2,1)}), bf16[4,2,3456]{2,1,0:T(2,128)(2,1)S(1)}, u32[]{:S(2)}, u32[]{:S(2)}) async-start(bf16[4,2,3456]{2,1,0:T(2,128)(2,1)} %reshape.84), calls=%async_computation.1 | async-start | bytes 110592 | tf_op jit(solution)/shard_map/all_to_all | solution.py:161
  116.5 4.6 %all-to-all-done.1 = bf16[4,2,3456]{2,1,0:T(2,128)(2,1)S(1)} async-done(((bf16[4,2,3456]{2,1,0:T(2,128)(2,1)}), bf16[4,2,3456]{2,1,0:T(2,128)(2,1)S(1)}, u32[]{:S(2)}, u32[]{:S(2)}) %all-to-all-start.1) | async-done | bytes 55328 | tf_op jit(solution)/shard_map/all_to_all | solution.py:161
  121.3 0.2 fusion.65
  121.6 0.6 copy.130
  (71 shorter events, 2.8 us)
Async XLA Ops:
  0.0 48.8 %copy-start = (bf16[256,256]{1,0:T(8,128)(2,1)S(1)}, bf16[256,256]{1,0:T(8,128)(2,1)}, u32[]{:S(2)}) copy-start(bf16[256,256]{1,0:T(8,128)(2,1)} %param.20) | copy-start | bytes 393220
  0.0 40.3 %copy-start.6 = (bf16[2,3,6,256]{3,0,2,1:T(2,128)(2,1)S(1)}, bf16[2,3,6,256]{3,0,2,1:T(2,128)(2,1)}, u32[]{:S(2)}) copy-start(bf16[2,3,6,256]{3,0,2,1:T(2,128)(2,1)} %param.15) | copy-start | bytes 55300
  0.0 46.2 %copy-start.4 = (bf16[3,3,256,256]{3,2,1,0:T(8,128)(2,1)S(1)}, bf16[3,3,256,256]{3,2,1,0:T(8,128)(2,1)}, u32[]{:S(2)}) copy-start(bf16[3,3,256,256]{3,2,1,0:T(8,128)(2,1)} %param.19) | copy-start | bytes 3538948
  0.8 39.5 %collective-permute-start = (bf16[2,1,6,256]{3,2,1,0:T(8,128)(2,1)S(1)}, bf16[2,1,6,256]{3,2,1,0:T(8,128)(2,1)S(1)}, u32[]{:S(2)}, u32[]{:S(2)}) collective-permute-start(bf16[2,1,6,256]{3,2,1,0:T(8,128)(2,1)S(1)} %get-tuple-element.371), channel_id=1, source_target_pairs={{0,4},{4,8},{8,12},{12,16},{16,20},{20,24},{24,28},{1,5},{5,9},{9,... | collective-permute-start | bytes 18440 | tf_op jit(solution)/shard_map/ppermute | solution.py:17
  3.2 37.1 %collective-permute-start.1 = (bf16[2,1,6,256]{3,2,1,0:T(8,128)(2,1)S(1)}, bf16[2,1,6,256]{3,2,1,0:T(8,128)(2,1)S(1)}, u32[]{:S(2)}, u32[]{:S(2)}) collective-permute-start(bf16[2,1,6,256]{3,2,1,0:T(8,128)(2,1)S(1)} %get-tuple-element.370), channel_id=1, source_target_pairs={{4,0},{8,4},{12,8},{16,12},{20,16},{24,20},{28,24},{5,1},{9,5},{13... | collective-permute-start | bytes 18440 | tf_op jit(solution)/shard_map/ppermute | solution.py:19
  24.3 24.3 %copy-start.7 = (bf16[2,3,6,256]{3,0,2,1:T(2,128)(2,1)S(1)}, bf16[2,3,6,256]{3,0,2,1:T(2,128)(2,1)}, u32[]{:S(2)}) copy-start(bf16[2,3,6,256]{3,0,2,1:T(2,128)(2,1)} %param.14) | copy-start | bytes 55300
  40.4 7.6 %collective-permute-start.2 = (bf16[2,5,1,256]{3,2,1,0:T(2,128)(2,1)S(1)}, bf16[2,5,1,256]{3,2,1,0:T(2,128)(2,1)S(1)}, u32[]{:S(2)}, u32[]{:S(2)}) collective-permute-start(bf16[2,5,1,256]{3,2,1,0:T(2,128)(2,1)S(1)} %get-tuple-element.368), channel_id=1, source_target_pairs={{1,0},{2,1},{3,2},{5,4},{6,5},{7,6},{9,8},{10,9},{11,10},{13,12},{... | collective-permute-start | bytes 15368 | tf_op jit(solution)/shard_map/ppermute | solution.py:19
  41.7 5.9 %collective-permute-start.3 = (bf16[2,5,1,256]{3,2,1,0:T(2,128)(2,1)S(1)}, bf16[2,5,1,256]{3,2,1,0:T(2,128)(2,1)S(1)}, u32[]{:S(2)}, u32[]{:S(2)}) collective-permute-start(bf16[2,5,1,256]{3,2,1,0:T(2,128)(2,1)S(1)} %get-tuple-element.369), channel_id=1, source_target_pairs={{0,1},{1,2},{2,3},{4,5},{5,6},{6,7},{8,9},{9,10},{10,11},{12,13},{... | collective-permute-start | bytes 15368 | tf_op jit(solution)/shard_map/ppermute | solution.py:17
  49.8 20.6 %all-to-all-start = ((bf16[4,2,1152]{2,1,0:T(2,128)(2,1)}), bf16[4,2,1152]{2,1,0:T(2,128)(2,1)S(1)}, u32[]{:S(2)}, u32[]{:S(2)}) async-start(bf16[4,2,1152]{2,1,0:T(2,128)(2,1)} %reshape.82), calls=%async_computation | async-start | bytes 36864 | tf_op jit(solution)/shard_map/all_to_all | solution.py:83
  55.2 29.7 %copy-start.1 = (bf16[2,72,64]{1,2,0:T(8,128)(2,1)S(1)}, bf16[2,72,64]{1,2,0:T(8,128)(2,1)}, u32[]{:S(2)}) copy-start(bf16[2,72,64]{1,2,0:T(8,128)(2,1)} %param.16) | copy-start | bytes 55300
  86.7 22.5 %copy-start.2 = (bf16[2,72,64]{1,2,0:T(8,128)(2,1)S(1)}, bf16[2,72,64]{1,2,0:T(8,128)(2,1)}, u32[]{:S(2)}) copy-start(bf16[2,72,64]{1,2,0:T(8,128)(2,1)} %param.17) | copy-start | bytes 55300
  86.7 22.5 %copy-start.3 = (bf16[2,72,64]{1,2,0:T(8,128)(2,1)S(1)}, bf16[2,72,64]{1,2,0:T(8,128)(2,1)}, u32[]{:S(2)}) copy-start(bf16[2,72,64]{1,2,0:T(8,128)(2,1)} %param.18) | copy-start | bytes 55300
  111.0 5.3 %copy-start.5 = (bf16[256,768]{1,0:T(8,128)(2,1)S(1)}, bf16[256,768]{1,0:T(8,128)(2,1)}, u32[]{:S(2)}) copy-start(bf16[256,768]{1,0:T(8,128)(2,1)} %param.21) | copy-start | bytes 1179652
  112.1 9.0 %all-to-all-start.1 = ((bf16[4,2,3456]{2,1,0:T(2,128)(2,1)}), bf16[4,2,3456]{2,1,0:T(2,128)(2,1)S(1)}, u32[]{:S(2)}, u32[]{:S(2)}) async-start(bf16[4,2,3456]{2,1,0:T(2,128)(2,1)} %reshape.84), calls=%async_computation.1 | async-start | bytes 110592 | tf_op jit(solution)/shard_map/all_to_all | solution.py:161
where the time goes:
time: 123 us; the launch traced here: 122 us
  blocking collectives  81.4 us (66%)
  starting transfers between devices  19.1 us (16%)
  local copies, waits for them, and re-layouts  7.72 us (6%)
  matrix products  7.21 us (6%)
  waiting for transfers between devices  5.68 us (5%)
    all_gather x1, blocking collectives, shards(): lax.all_gather(value_heads, 'row', axis=1, tiled=True)  17.8 us
    all_gather x1, blocking collectives, shards(): query_block = lax.all_gather(query_heads, 'row', axis=1, tiled=True)  14.6 us
    all_gather x1, blocking collectives, shards(): grad_block = lax.all_gather(grad_out, 'row', axis=1, tiled=True)  14.2 us
    all_gather x1, blocking collectives, shards(): lax.all_gather(key_heads, 'row', axis=1, tiled=True)  14.2 us
    all_gather x1, blocking collectives, shards(): lax.all_gather(log_norm, 'row', axis=1, tiled=True)  11.8 us
    all_gather x1, blocking collectives, shards(): lax.all_gather(row_dot, 'row', axis=1, tiled=True)  8.7 us
    ppermute x2, starting transfers between devices, with_halo(): lax.ppermute(tail, axis, [(i, (i + 1) % count) for i in range(ends)])  6.9 us
    unnamed x34, local copies, waits for them, and re-layouts  6.35 us
  transfers between devices with their start and end apart: 6, of which 2 were waited for; matrix products, arithmetic and copies ran while one was open for 4% of the time, Pallas kernels for 0%

commit v1 on v0

v1 whole, which is shorter than its diff:
```python
import functools

import jax
import jax.numpy as jnp
import numpy as np
from jax import lax
from jax.experimental import pallas as pl
from jax.experimental.pallas import tpu as pltpu
from jax.sharding import PartitionSpec as P

HEADS = 4
VMEM_BYTES = 60 * 1024 * 1024
UNROLLED_CHUNKS = 16
F32 = jnp.float32
BF16 = jnp.bfloat16


def dot(left, right, left_dim=1, right_dim=0):
    return lax.dot_general(
        left, right, (((left_dim,), (right_dim,)), ((), ())), preferred_element_type=F32
    )


def call(kernel, out_shape, scratch=(), scalars=1):
    whole = pl.BlockSpec(memory_space=pltpu.VMEM)
    scalar = pl.BlockSpec(memory_space=pltpu.SMEM)

    def run(*operands):
        return pl.pallas_call(
            kernel,
            out_shape=out_shape,
            in_specs=[scalar] * scalars + [whole] * (len(operands) - scalars),
            out_specs=jax.tree.map(lambda _: whole, out_shape),
            scratch_shapes=list(scratch),
            compiler_params=pltpu.CompilerParams(vmem_limit_bytes=VMEM_BYTES),
        )(*operands)

    return run


def pad8(amount):
    return -(-amount // 8) * 8


def shift_selector(rows, cols, tiles):
    width, padded = tiles * cols, pad8(cols)
    select = np.zeros((3, rows, width, tiles, rows, padded), np.float32)
    for shift in (-1, 0, 1):
        for j in range(max(0, shift), min(width, width + shift)):
            tile, inner = divmod(j - shift, cols)
            for i in range(rows):
                select[shift + 1, i, j, tile, i, inner] = 1
    return select.reshape(3, rows * width, tiles * rows * padded)


def tile_selector(rows, cols, tiles):
    width, padded = tiles * cols, pad8(cols)
    select = np.zeros((tiles, rows, padded, rows, width), np.float32)
    for tile in range(tiles):
        for i in range(rows):
            for inner in range(cols):
                select[tile, i, inner, i, tile * cols + inner] = 1
    return select.reshape(tiles, rows * padded, rows * width)


def strip_kernel(n_col, per_sample, *refs):
    (place, own_grad, own_silu, *rest) = refs
    received, rest = rest[: n_col - 1], rest[n_col - 1 :]
    (
        halo_core,
        halo_chip,
        kv_own,
        kv_other,
        queries,
        conv_weight,
        out_weight,
        shifts,
        middle,
        dkv_own,
        dkv_other,
        dq_ref,
        gz_ref,
        grads,
        silus,
    ) = rest
    col, core = place[0], place[1]
    sample = col // per_sample
    rows, cols, channels = own_grad.shape[1:]
    width = n_col * cols
    strip = rows * width

    grads[...] = jnp.zeros_like(grads)
    silus[...] = jnp.zeros_like(silus)
    lower = jnp.where(core == 0, rows + 1, 0)
    upper = jnp.where(core == 0, 0, rows + 1)
    for k in range(n_col):
        tile = col ^ k
        for i in range(rows):
            grad = own_grad[sample, i] if k == 0 else received[k - 1][0, i]
            silu = own_silu[sample, i] if k == 0 else received[k - 1][1, i]
            grads[tile, i + 1, :cols] = grad.astype(F32)
            silus[tile, i, :cols] = silu.astype(F32)
        grads[tile, lower, :cols] = halo_core[k].astype(F32)
        grads[tile, upper, :cols] = halo_chip[k].astype(F32)
    flat = grads[...].reshape(-1, channels).astype(BF16)
    conv = jnp.zeros((strip, channels), F32)
    for b in (-1, 0, 1):
        shifted = dot(shifts[b + 1], flat)
        for a in (-1, 0, 1):
            window = shifted[(1 - a) * width : (1 - a) * width + strip].astype(BF16)
            conv = conv + dot(window, conv_weight[a + 1, b + 1], 1, 1)
    z = dot(middle[...], silus[...].reshape(-1, channels).astype(BF16))
    sigma = 1.0 / (1.0 + jnp.exp(-z))
    grad_z = (conv * sigma * (1.0 + z * (1.0 - sigma))).astype(BF16)
    gz_ref[...] = grad_z

    lanes = queries.shape[1]
    half = lanes // 2
    first = col % per_sample * lanes
    grad_out = dot(grad_z, out_weight[pl.ds(pl.multiple_of(first, lanes), lanes), :], 1, 1)
    grad_out = grad_out.astype(BF16)
    low = lax.broadcasted_iota(jnp.int32, (strip, lanes), 1) < half
    factor = half**-0.5
    query = queries[...] * jnp.asarray(factor, BF16)
    none = jnp.zeros_like(query)
    padded_query = (jnp.where(low, none, query), jnp.where(low, query, none))
    padded_grad = (jnp.where(low, grad_out, none), jnp.where(low, none, grad_out))

    blocks = kv_own.shape[0]
    sources = ((kv_own, dkv_own), (kv_other, dkv_other))
    small = 2 * blocks <= UNROLLED_CHUNKS
    grad_query = []
    for head in (0, 1):
        ask, cot = padded_query[head], padded_grad[head]

        def products(kv):
            return dot(kv, ask, 1, 1), dot(kv, cot, 1, 1)

        def finish(kv, scores, probs_grad, top, scale, row_dot):
            probs = jnp.exp(scores - top) * scale
            grad_scores = (probs * (probs_grad - row_dot)).astype(BF16)
            dkv = dot(grad_scores, ask) + dot(probs.astype(BF16), cot)
            return dkv, dot(grad_scores, kv, 0, 0)

        if small:
            chunks = [(src[j, head], dst, j) for src, dst in sources for j in range(blocks)]
            both = [products(kv) for kv, _, _ in chunks]
            top = functools.reduce(jnp.maximum, [s for s, _ in both])
            top = jnp.max(top, axis=0, keepdims=True)
            exps = [jnp.exp(s - top) for s, _ in both]
            norm = jnp.sum(sum(exps), axis=0, keepdims=True)
            weighted = sum(e * p for e, (_, p) in zip(exps, both))
            scale = 1.0 / norm
            row_dot = jnp.sum(weighted, axis=0, keepdims=True) * scale
            total = jnp.zeros((strip, lanes), F32)
            for (kv, dst, j), e, (_, probs_grad) in zip(chunks, exps, both):
                probs = e * scale
                grad_scores = (probs * (probs_grad - row_dot)).astype(BF16)
                dkv = dot(grad_scores, ask) + dot(probs.astype(BF16), cot)
                dst[j, head] = dkv.astype(BF16)
                total = total + dot(grad_scores, kv, 0, 0)
        else:
            stats = (
                jnp.full((1, strip), -jnp.inf, F32),
                jnp.zeros((1, strip), F32),
                jnp.zeros((1, strip), F32),
            )
            for src, _ in sources:

                def gather(j, carry, src=src):
                    top, norm, weighted = carry
                    scores, probs_grad = products(src[j, head])
                    new = jnp.maximum(top, jnp.max(scores, axis=0, keepdims=True))
                    exps = jnp.exp(scores - new)
                    rescale = jnp.exp(top - new)
                    return (
                        new,
                        norm * rescale + jnp.sum(exps, axis=0, keepdims=True),
                        weighted * rescale + jnp.sum(exps * probs_grad, axis=0, keepdims=True),
                    )

                stats = lax.fori_loop(0, blocks, gather, stats)
            top, norm, weighted = stats
            scale = 1.0 / norm
            row_dot = weighted * scale
            total = jnp.zeros((strip, lanes), F32)
            for src, dst in sources:

                def spread(j, total, src=src, dst=dst):
                    kv = src[j, head]
                    scores, probs_grad = products(kv)
                    dkv, dq = finish(kv, scores, probs_grad, top, scale, row_dot)
                    dst[j, head] = dkv.astype(BF16)
                    return total + dq

                total = lax.fori_loop(0, blocks, spread, total)
        grad_query.append(total)
    dq_ref[...] = jnp.where(low, grad_query[1], grad_query[0]) * factor


def core_sum_kernel(own, received, *outs):
    for j, out in enumerate(outs):
        out[...] = (own[j].astype(F32) + received[j].astype(F32)).astype(BF16)


def project_kernel(n_col, per_sample, place, *refs):
    n_in = len(refs) - n_col
    *parts, dq_ref, gz_ref, input_weight, tiles = refs[:n_in]
    outs = refs[n_in:]
    col = place[0]
    part = col % per_sample
    total = sum(ref[...].astype(F32) for ref in parts)
    strip, lanes = dq_ref.shape
    half = lanes // 2
    channels = gz_ref.shape[1]
    low = lax.broadcasted_iota(jnp.int32, (strip, lanes), 1) < half
    dv = jnp.where(low, total[0], total[1])
    dk = pltpu.roll(jnp.where(low, total[1], total[0]), half, 1)
    dq = pltpu.roll(dq_ref[...], half, 1)
    grad = jnp.where(part == 0, gz_ref[...].astype(F32), 0.0)
    for kind, value in enumerate((dq, dk, dv)):
        first = pl.multiple_of(kind * channels + part * lanes, lanes)
        weight = input_weight[:, pl.ds(first, lanes)]
        grad = grad + dot(value.astype(BF16), weight, 1, 1)
    grad = grad.astype(BF16)
    for k, out in enumerate(outs):
        out[...] = dot(tiles[col ^ k], grad).astype(BF16)


def output_kernel(per_sample, place, *refs):
    *parts, out = refs
    samples, rows, cols, _ = out.shape
    padded = pad8(cols)
    sample = place[0] // per_sample
    for group in range(samples):
        total = sum(
            ref[...].astype(F32) for ref in parts[group * per_sample : (group + 1) * per_sample]
        )
        for i in range(rows):
            out[sample ^ group, i] = total[i * padded : i * padded + cols].astype(BF16)


def shards(
    pre_silu, out_grad, query_heads, key_heads, value_heads, conv_weight, out_weight, input_weight
):
    samples, rows, cols, channels = pre_silu.shape
    pairs, strip, head_dim = query_heads.shape
    n_row, n_col = lax.axis_size("row"), lax.axis_size("col")
    chips = n_row // 2
    per_sample = HEADS // pairs
    lanes = pairs * head_dim
    row, col = lax.axis_index("row"), lax.axis_index("col")
    core = row % 2
    sample = col // per_sample
    place = jnp.stack([col, core]).astype(jnp.int32)

    def to_col(array, k):
        return lax.ppermute(array, "col", [(i, i ^ k) for i in range(n_col)])

    def to_chip(array, k):
        return lax.ppermute(array, "row", [(i, i ^ (2 * k)) for i in range(n_row)])

    def to_core(array):
        return lax.ppermute(array, "row", [(i, i ^ 1) for i in range(n_row)])

    def to_next_chip(array):
        edge = [(i, i + 1) for i in range(1, n_row - 1, 2)]
        return lax.ppermute(array, "row", edge + [(j, i) for i, j in edge])

    both = jnp.stack([out_grad, pre_silu])
    payload = [
        lax.dynamic_index_in_dim(both, sample ^ group, 1, keepdims=False)
        for group in range(samples)
    ]
    received = [to_col(payload[k // per_sample], k) for k in range(1, n_col)]

    kv = jnp.stack(
        [
            jnp.concatenate([value_heads[0], key_heads[0]], -1),
            jnp.concatenate([key_heads[1], value_heads[1]], -1),
        ]
    )
    kv_own = jnp.stack([kv] + [to_chip(kv, k) for k in range(1, chips)])
    kv_other = to_core(kv_own)
    queries = jnp.concatenate([query_heads[1], query_heads[0]], -1)

    strip_grads = [payload[0][0]] + [piece[0] for piece in received]
    first_row = jnp.stack([piece[0] for piece in strip_grads])
    last_row = jnp.stack([piece[rows - 1] for piece in strip_grads])
    halo_core = to_core(jnp.where(core == 0, last_row, first_row))
    halo_chip = to_next_chip(jnp.where(core == 0, first_row, last_row))

    select = shift_selector(rows + 2, cols, n_col)
    middle = shift_selector(rows, cols, n_col)[1]
    padded = pad8(cols)
    block = jax.ShapeDtypeStruct((chips, pairs, strip, lanes), BF16)
    dkv_own, dkv_other, dq, grad_z = call(
        functools.partial(strip_kernel, n_col, per_sample),
        (
            block,
            block,
            jax.ShapeDtypeStruct((strip, lanes), F32),
            jax.ShapeDtypeStruct((strip, channels), BF16),
        ),
        (
            pltpu.VMEM((n_col, rows + 2, padded, channels), F32),
            pltpu.VMEM((n_col, rows, padded, channels), F32),
        ),
    )(
        place,
        out_grad,
        pre_silu,
        *received,
        halo_core,
        halo_chip,
        kv_own,
        kv_other,
        queries,
        conv_weight,
        out_weight,
        jnp.asarray(select, BF16),
        jnp.asarray(middle, BF16),
    )

    sums = call(
        core_sum_kernel,
        [jax.ShapeDtypeStruct((pairs, strip, lanes), BF16) for _ in range(chips)],
        scalars=0,
    )(dkv_own, to_core(dkv_other))
    parts = [sums[0]] + [to_chip(sums[k], k) for k in range(1, chips)]

    tile = jax.ShapeDtypeStruct((rows * padded, channels), BF16)
    cut = call(functools.partial(project_kernel, n_col, per_sample), [tile] * n_col)(
        place,
        *parts,
        dq,
        grad_z,
        input_weight,
        jnp.asarray(tile_selector(rows, cols, n_col), BF16),
    )
    returned = [cut[0]] + [to_col(cut[k], k) for k in range(1, n_col)]
    return call(
        functools.partial(output_kernel, per_sample),
        jax.ShapeDtypeStruct((samples, rows, cols, channels), BF16),
    )(place, *returned)


def solution(mesh):
    tile = P(None, "row", "col", None)
    heads = P("col", "row", None)
    return jax.shard_map(
        shards,
        mesh=mesh,
        in_specs=(tile, tile, heads, heads, heads, P(), P(), P()),
        out_specs=tile,
        check_vma=False,
    )
```

time: 123 us -> 56.5 us (0.46)
  blocking collectives: 81.4 us -> 0 us
  Pallas kernels: 0 us -> 10 us
  waiting for transfers between devices: 5.68 us -> 13.6 us
  matrix products: 7.21 us -> 0 us
  starting transfers between devices: 19.1 us -> 22.3 us
    all_gather x6 -> x0, blocking collectives: 81.4 us -> none  [the longest x1 17.8 us: shards(): lax.all_gather(value_heads, 'row', axis=1, tiled=True)]
    ppermute x4 -> x16, starting transfers between devices: 9.49 us -> 22.3 us  [the longest x6 10.1 us: to_chip(): return lax.ppermute(array, 'row', [(i, i ^ 2 * k) for i in range(n_row)])]
    ppermute x4 -> x16, waiting for transfers between devices: 1.04 us -> 13.6 us  [the longest x6 6.63 us: to_col(): return lax.ppermute(array, 'col', [(i, i ^ k) for i in range(n_col)])]
    pallas_call x0 -> x4, Pallas kernels: none -> 10 us  [run(): pl.pallas_call(kernel, out_shape=out_shape, in_specs=[scalar] * scalars +...]
    all_to_all x2 -> x0, starting transfers between devices: 9.57 us -> none  [the longest x1 5.38 us: shards(): lax.all_to_all(grad_attn, 'col', split_axis=0, concat_axis=2, tiled=True)]
    dot_general x25 -> x0, matrix products: 7.21 us -> none  [the longest x9 2.59 us: shards(): jnp.einsum('srcd,ed->srce', window, conv_weight[shift_r + 1, shift_c + 1]...]
    all_to_all x2 -> x0, waiting for transfers between devices: 4.64 us -> none  [the longest x1 4.64 us: shards(): lax.all_to_all(jnp.stack([grad_query, grad_key, grad_value]).astype(jnp.b...]
    unnamed x34, local copies, waits for them, and re-layouts: 6.35 us -> 3.06 us
  transfers between devices with their start and end apart: 6 -> 16, of which waited for: 2 -> 9; matrix products, arithmetic and copies ran while one was open for 4% -> 7% of each run, Pallas kernels for 0% -> 0%
where the time goes in v1:
time: 56.5 us; the launch traced here: 55.7 us
  starting transfers between devices  22.3 us (39%)
  waiting for transfers between devices  13.6 us (24%)
  Pallas kernels  10 us (18%)
  local copies, waits for them, and re-layouts  8 us (14%)
  other arithmetic  1.5 us (3%)
    ppermute x6, starting transfers between devices, to_chip(): return lax.ppermute(array, 'row', [(i, i ^ 2 * k) for i in range(n_row)])  10.1 us
    pallas_call x4, Pallas kernels, run(): pl.pallas_call(kernel, out_shape=out_shape, in_specs=[scalar] * scalars +...  10 us
    ppermute x6, starting transfers between devices, to_col(): return lax.ppermute(array, 'col', [(i, i ^ k) for i in range(n_col)])  7.47 us
    ppermute x6, waiting for transfers between devices, to_col(): return lax.ppermute(array, 'col', [(i, i ^ k) for i in range(n_col)])  6.63 us
    ppermute x6, waiting for transfers between devices, to_chip(): return lax.ppermute(array, 'row', [(i, i ^ 2 * k) for i in range(n_row)])  5.61 us
    ppermute x3, starting transfers between devices, to_core(): return lax.ppermute(array, 'row', [(i, i ^ 1) for i in range(n_row)])  4.13 us
    unnamed x34, local copies, waits for them, and re-layouts  3.06 us
    ppermute x3, waiting for transfers between devices, to_core(): return lax.ppermute(array, 'row', [(i, i ^ 1) for i in range(n_row)])  1.41 us
  transfers between devices with their start and end apart: 16, of which 9 were waited for; matrix products, arithmetic and copies ran while one was open for 7% of the time, Pallas kernels for 0%

profile of v1, /device:TPU:0, one launch (start us, length us, event | category | flops | bytes accessed | tf_op | source)
XLA Modules:
  0.0 55.7 jit_solution(6865049648236468503)
XLA Ops:
  0.0 0.7 %fusion.6 = (bf16[1,72,64]{1,2,0:T(8,128)(2,1)S(1)}, bf16[1,72,64]{1,2,0:T(8,128)(2,1)S(1)}) fusion(bf16[2,72,64]{1,2,0:T(8,128)(2,1)} %param.14), kind=kLoop, calls=%fused_computation.30 | loop fusion | bytes 36864 | tf_op jit(solution)/shard_map/slice | solution.py:279
  0.7 0.1 copy.24
  0.8 0.1 copy.25
  0.9 0.7 %fusion.5 = (bf16[1,72,64]{1,2,0:T(8,128)(2,1)S(1)}, bf16[1,72,64]{1,2,0:T(8,128)(2,1)S(1)}) fusion(bf16[2,72,64]{1,2,0:T(8,128)(2,1)} %param.15), kind=kLoop, calls=%fused_computation.29 | loop fusion | bytes 36864 | tf_op jit(solution)/shard_map/slice | solution.py:279
  1.7 0.1 copy.23
  1.8 0.1 copy.26
  1.9 0.1 maximum_bitcast_fusion
  2.0 4.1 %collective-permute-start.6 = (bf16[2,72,128]{2,1,0:T(8,128)(2,1)S(1)}, bf16[2,72,128]{2,1,0:T(8,128)(2,1)S(1)}, u32[]{:S(2)}, u32[]{:S(2)}) collective-permute-start(bf16[2,72,128]{2,1,0:T(8,128)(2,1)S(1)} %get-tuple-element.32), channel_id=1, source_target_pairs={{0,16},{4,20},{8,24},{12,28},{16,0},{20,4},{24,8},{28,12},{1,17},{... | collective-permute-start | bytes 110600 | tf_op jit(solution)/shard_map/ppermute | solution.py:261
  6.1 1.6 %collective-permute-start.5 = (bf16[2,72,128]{2,1,0:T(8,128)(2,1)S(1)}, bf16[2,72,128]{2,1,0:T(8,128)(2,1)S(1)}, u32[]{:S(2)}, u32[]{:S(2)}) collective-permute-start(bf16[2,72,128]{2,1,0:T(8,128)(2,1)S(1)} %get-tuple-element.32), channel_id=1, source_target_pairs={{0,8},{4,12},{8,0},{12,4},{16,24},{20,28},{24,16},{28,20},{1,9},{5... | collective-permute-start | bytes 110600 | tf_op jit(solution)/shard_map/ppermute | solution.py:261
  7.7 1.4 %copy_bitcast_fusion = (bf16[1,2,3,6,256]{4,3,2,1,0:T(8,128)(2,1)S(1)}, bf16[2,3,6,256]{3,2,1,0:T(8,128)(2,1)}, bf16[2,3,6,256]{3,2,1,0:T(8,128)(2,1)}, bf16[1,2,3,6,256]{4,3,2,1,0:T(8,128)(2,1)S(1)}) fusion(bf16[2,3,6,256]{3,0,2,1:T(2,128)(2,1)} %param.11, bf16[2,3,6,256]{3,0,2,1:T(2,128)(2,1)} %param.12), kind=kLoop, calls=%fused_computation.25 | loop fusion | bytes 110592 | tf_op jit(solution)/shard_map/stack | solution.py:270
  9.1 1.8 %collective-permute-start = (bf16[2,3,6,256]{3,2,1,0:T(8,128)(2,1)S(1)}, bf16[2,3,6,256]{3,2,1,0:T(8,128)(2,1)S(1)}, u32[]{:S(2)}, u32[]{:S(2)}) collective-permute-start(bf16[2,3,6,256]{3,2,1,0:T(8,128)(2,1)S(1)} %bitcast.46), channel_id=1, source_target_pairs={{0,1},{1,0},{2,3},{3,2},{4,5},{5,4},{6,7},{7,6},{8,9},{9,8},{10,11... | collective-permute-start | bytes 55304 | tf_op jit(solution)/shard_map/ppermute | solution.py:258
  10.8 1.5 %collective-permute-start.2 = (bf16[2,3,6,256]{3,2,1,0:T(8,128)(2,1)S(1)}, bf16[2,3,6,256]{3,2,1,0:T(8,128)(2,1)S(1)}, u32[]{:S(2)}, u32[]{:S(2)}) collective-permute-start(bf16[2,3,6,256]{3,2,1,0:T(8,128)(2,1)S(1)} %get-tuple-element.29), channel_id=1, source_target_pairs={{0,3},{1,2},{2,1},{3,0},{4,7},{5,6},{6,5},{7,4},{8,11},{9,10},{10,... | collective-permute-start | bytes 55304 | tf_op jit(solution)/shard_map/ppermute | solution.py:258
  12.3 0.7 %fusion.4 = (bf16[1,72,64]{1,2,0:T(8,128)(2,1)S(1)}, bf16[1,72,64]{1,2,0:T(8,128)(2,1)S(1)}) fusion(bf16[2,72,64]{1,2,0:T(8,128)(2,1)} %param.13), kind=kLoop, calls=%fused_computation.28 | loop fusion | bytes 36864 | tf_op jit(solution)/shard_map/slice | solution.py:285
  13.1 0.1 copy.27
  13.2 0.1 copy.28
  13.3 0.7 %pad_maximum_fusion.2.refs_10_ = bf16[72,128]{1,0:T(8,128)(2,1)} fusion(bf16[72,64]{1,0:T(8,128)(2,1)S(1)} %bitcast.45, bf16[72,64]{1,0:T(8,128)(2,1)S(1)} %bitcast.44), kind=kLoop, calls=%fused_computation.11 | loop fusion | flops 36864 | bytes 36864 | tf_op jit(solution)/shard_map/concatenate | solution.py:285
  14.0 0.7 %collective-permute-start.1 = (bf16[2,3,6,256]{3,2,1,0:T(8,128)(2,1)S(1)}, bf16[2,3,6,256]{3,2,1,0:T(8,128)(2,1)S(1)}, u32[]{:S(2)}, u32[]{:S(2)}) collective-permute-start(bf16[2,3,6,256]{3,2,1,0:T(8,128)(2,1)S(1)} %get-tuple-element.29), channel_id=1, source_target_pairs={{0,2},{1,3},{2,0},{3,1},{4,6},{5,7},{6,4},{7,5},{8,10},{9,11},{10,... | collective-permute-start | bytes 55304 | tf_op jit(solution)/shard_map/ppermute | solution.py:258
  14.7 0.9 %collective-permute-done.2.refs_5_ = bf16[2,3,6,256]{3,2,1,0:T(8,128)(2,1)S(1)} collective-permute-done((bf16[2,3,6,256]{3,2,1,0:T(8,128)(2,1)S(1)}, bf16[2,3,6,256]{3,2,1,0:T(8,128)(2,1)S(1)}, u32[]{:S(2)}, u32[]{:S(2)}) %collective-permute-start.2) | collective-permute-done | bytes 18464 | tf_op jit(solution)/shard_map/ppermute | solution.py:258
  15.6 2.2 %collective-permute-done.1.refs_4_ = bf16[2,3,6,256]{3,2,1,0:T(8,128)(2,1)S(1)} collective-permute-done((bf16[2,3,6,256]{3,2,1,0:T(8,128)(2,1)S(1)}, bf16[2,3,6,256]{3,2,1,0:T(8,128)(2,1)S(1)}, u32[]{:S(2)}, u32[]{:S(2)}) %collective-permute-start.1) | collective-permute-done | bytes 18464 | tf_op jit(solution)/shard_map/ppermute | solution.py:258
  17.9 0.1 collective-permute-start.8
  18.0 0.7 %collective-permute-start.4 = (bf16[4,6,256]{2,1,0:T(8,128)(2,1)S(1)}, bf16[4,6,256]{2,1,0:T(8,128)(2,1)S(1)}, u32[]{:S(2)}, u32[]{:S(2)}) collective-permute-start(bf16[4,6,256]{2,1,0:T(8,128)(2,1)S(1)} %get-tuple-element.39), channel_id=1, source_target_pairs={{4,8},{12,16},{20,24},{8,4},{16,12},{24,20},{5,9},{13,17},{21,25},... | collective-permute-start | bytes 36872 | tf_op jit(solution)/shard_map/ppermute | solution.py:268
  18.6 2.1 %collective-permute-start.3 = (bf16[4,6,256]{2,1,0:T(8,128)(2,1)S(1)}, bf16[4,6,256]{2,1,0:T(8,128)(2,1)S(1)}, u32[]{:S(2)}, u32[]{:S(2)}) collective-permute-start(bf16[4,6,256]{2,1,0:T(8,128)(2,1)S(1)} %get-tuple-element.40), channel_id=1, source_target_pairs={{0,4},{4,0},{8,12},{12,8},{16,20},{20,16},{24,28},{28,24},{1,5},{5... | collective-permute-start | bytes 36872 | tf_op jit(solution)/shard_map/ppermute | solution.py:264
  20.7 0.6 %pad_add_fusion.refs_0_.place = s32[2]{0:T(128)} fusion(s32[1]{0:T(128)} %bitcast.1, s32[1]{0:T(128)} %bitcast), kind=kLoop, calls=%fused_computation.24 | loop fusion | flops 2 | bytes 16 | tf_op jit(solution)/shard_map/stack | solution.py:255
  21.4 0.2 collective-permute-done.3.refs_6_
  21.6 0.4 copy-done.9
  22.0 0.2 copy-done.10
  22.2 0.1 copy-done.1
  22.2 4.8 %shard_map.109 = (bf16[4,2,72,128]{3,2,1,0:T(8,128)(2,1)}, bf16[4,2,72,128]{3,2,1,0:T(8,128)(2,1)}, f32[72,128]{1,0:T(8,128)}, bf16[72,256]{1,0:T(8,128)(2,1)}) custom-call(s32[2]{0:T(128)} %pad_add_fusion.refs_0_.place, bf16[2,3,6,256]{3,2,1,0:T(8,128)(2,1)} %get-tuple-element.53.refs_1_, bf16[2,3,6,256]{3,2,1,0:T(8,128)(2,1)} %get-tuple-element.50.refs_2_, ...), custom_call_target="tpu_custom_call" | custom-call | tf_op jit(solution)/shard_map/pallas_call | solution.py:29
  27.1 1.9 %collective-permute-start.9 = (bf16[4,2,72,128]{3,2,1,0:T(8,128)(2,1)}, bf16[4,2,72,128]{3,2,1,0:T(8,128)(2,1)S(1)}, u32[]{:S(2)}, u32[]{:S(2)}) collective-permute-start(bf16[4,2,72,128]{3,2,1,0:T(8,128)(2,1)} %get-tuple-element.18), channel_id=1, source_target_pairs={{0,4},{4,0},{8,12},{12,8},{16,20},{20,16},{24,28},{28,24},{1,5},{5... | collective-permute-start | bytes 442376 | tf_op jit(solution)/shard_map/ppermute | solution.py:264
  29.0 1.2 %collective-permute-done.9.received = bf16[4,2,72,128]{3,2,1,0:T(8,128)(2,1)S(1)} collective-permute-done((bf16[4,2,72,128]{3,2,1,0:T(8,128)(2,1)}, bf16[4,2,72,128]{3,2,1,0:T(8,128)(2,1)S(1)}, u32[]{:S(2)}, u32[]{:S(2)}) %collective-permute-start.9) | collective-permute-done | bytes 147488 | tf_op jit(solution)/shard_map/ppermute | solution.py:264
  30.2 0.7 %copy-done.2 = bf16[4,2,72,128]{3,2,1,0:T(8,128)(2,1)} copy-done((bf16[4,2,72,128]{3,2,1,0:T(8,128)(2,1)}, bf16[4,2,72,128]{3,2,1,0:T(8,128)(2,1)S(1)}, u32[]{:S(2)}) %copy-start.2) | copy-done | bytes 147480
  30.9 1.6 %shard_map.110 = (bf16[2,72,128]{2,1,0:T(8,128)(2,1)}, bf16[2,72,128]{2,1,0:T(8,128)(2,1)}, bf16[2,72,128]{2,1,0:T(8,128)(2,1)}, bf16[2,72,128]{2,1,0:T(8,128)(2,1)}) custom-call(bf16[4,2,72,128]{3,2,1,0:T(8,128)(2,1)} %get-tuple-element.17.own, bf16[4,2,72,128]{3,2,1,0:T(8,128)(2,1)} %copy-done.2), custom_call_target="tpu_custom_call" | custom-call | tf_op jit(solution)/shard_map/pallas_call | solution.py:29
  32.5 0.7 %collective-permute-start.10 = (bf16[2,72,128]{2,1,0:T(8,128)(2,1)}, bf16[2,72,128]{2,1,0:T(8,128)(2,1)S(1)}, u32[]{:S(2)}, u32[]{:S(2)}) collective-permute-start(bf16[2,72,128]{2,1,0:T(8,128)(2,1)} %get-tuple-element.20), channel_id=1, source_target_pairs={{0,8},{4,12},{8,0},{12,4},{16,24},{20,28},{24,16},{28,20},{1,9},{5... | collective-permute-start | bytes 110600 | tf_op jit(solution)/shard_map/ppermute | solution.py:261
  33.2 3.3 %collective-permute-start.11 = (bf16[2,72,128]{2,1,0:T(8,128)(2,1)}, bf16[2,72,128]{2,1,0:T(8,128)(2,1)S(1)}, u32[]{:S(2)}, u32[]{:S(2)}) collective-permute-start(bf16[2,72,128]{2,1,0:T(8,128)(2,1)} %get-tuple-element.21), channel_id=1, source_target_pairs={{0,16},{4,20},{8,24},{12,28},{16,0},{20,4},{24,8},{28,12},{1,17},{... | collective-permute-start | bytes 110600 | tf_op jit(solution)/shard_map/ppermute | solution.py:261
  36.6 0.4 collective-permute-start.12
  36.9 2.4 %collective-permute-done.11.refs_2_ = bf16[2,72,128]{2,1,0:T(8,128)(2,1)S(1)} collective-permute-done((bf16[2,72,128]{2,1,0:T(8,128)(2,1)}, bf16[2,72,128]{2,1,0:T(8,128)(2,1)S(1)}, u32[]{:S(2)}, u32[]{:S(2)}) %collective-permute-start.11) | collective-permute-done | bytes 36896 | tf_op jit(solution)/shard_map/ppermute | solution.py:261
  39.4 3.2 %collective-permute-done.12.refs_3_ = bf16[2,72,128]{2,1,0:T(8,128)(2,1)S(1)} collective-permute-done((bf16[2,72,128]{2,1,0:T(8,128)(2,1)}, bf16[2,72,128]{2,1,0:T(8,128)(2,1)S(1)}, u32[]{:S(2)}, u32[]{:S(2)}) %collective-permute-start.12) | collective-permute-done | bytes 36896 | tf_op jit(solution)/shard_map/ppermute | solution.py:261
  42.5 0.6 %copy-done.8 = bf16[2,72,128]{2,1,0:T(8,128)(2,1)} copy-done((bf16[2,72,128]{2,1,0:T(8,128)(2,1)}, bf16[2,72,128]{2,1,0:T(8,128)(2,1)S(1)}, u32[]{:S(2)}) %copy-start.8) | copy-done | bytes 36888
  43.1 2.1 %shard_map.111 = (bf16[24,256]{1,0:T(8,128)(2,1)}, bf16[24,256]{1,0:T(8,128)(2,1)}, bf16[24,256]{1,0:T(8,128)(2,1)}, bf16[24,256]{1,0:T(8,128)(2,1)}) custom-call(s32[2]{0:T(128)} %pad_add_fusion.refs_0_.place, bf16[2,72,128]{2,1,0:T(8,128)(2,1)} %get-tuple-element.19.refs_0_, bf16[2,72,128]{2,1,0:T(8,128)(2,1)} %copy-done.6, bf16[2,72,128]{2,1,0:T(8,128)(2,1)} %copy-done.7, ...), custom_call_target="tpu_custom_call" | custom-call | tf_op jit(solution)/shard_map/pallas_call | solution.py:29
  45.3 1.5 %collective-permute-start.13 = (bf16[24,256]{1,0:T(8,128)(2,1)}, bf16[24,256]{1,0:T(8,128)(2,1)S(1)}, u32[]{:S(2)}, u32[]{:S(2)}) collective-permute-start(bf16[24,256]{1,0:T(8,128)(2,1)} %get-tuple-element.26), channel_id=1, source_target_pairs={{0,1},{1,0},{2,3},{3,2},{4,5},{5,4},{6,7},{7,6},{8,9},{9,8},{10,11... | collective-permute-start | bytes 36872 | tf_op jit(solution)/shard_map/ppermute | solution.py:258
  46.8 0.7 %collective-permute-start.14 = (bf16[24,256]{1,0:T(8,128)(2,1)}, bf16[24,256]{1,0:T(8,128)(2,1)S(1)}, u32[]{:S(2)}, u32[]{:S(2)}) collective-permute-start(bf16[24,256]{1,0:T(8,128)(2,1)} %get-tuple-element.27), channel_id=1, source_target_pairs={{0,2},{1,3},{2,0},{3,1},{4,6},{5,7},{6,4},{7,5},{8,10},{9,11},{10,... | collective-permute-start | bytes 36872 | tf_op jit(solution)/shard_map/ppermute | solution.py:258
  47.5 1.3 %collective-permute-start.15 = (bf16[24,256]{1,0:T(8,128)(2,1)}, bf16[24,256]{1,0:T(8,128)(2,1)S(1)}, u32[]{:S(2)}, u32[]{:S(2)}) collective-permute-start(bf16[24,256]{1,0:T(8,128)(2,1)} %get-tuple-element.28), channel_id=1, source_target_pairs={{0,3},{1,2},{2,1},{3,0},{4,7},{5,6},{6,5},{7,4},{8,11},{9,10},{10,... | collective-permute-start | bytes 36872 | tf_op jit(solution)/shard_map/ppermute | solution.py:258
  48.8 0.4 collective-permute-done.13.refs_1_
  49.2 1.5 %collective-permute-done.14.refs_2_ = bf16[24,256]{1,0:T(8,128)(2,1)S(1)} collective-permute-done((bf16[24,256]{1,0:T(8,128)(2,1)}, bf16[24,256]{1,0:T(8,128)(2,1)S(1)}, u32[]{:S(2)}, u32[]{:S(2)}) %collective-permute-start.14) | collective-permute-done | bytes 12320 | tf_op jit(solution)/shard_map/ppermute | solution.py:258
  50.7 1.6 %collective-permute-done.15.refs_3_ = bf16[24,256]{1,0:T(8,128)(2,1)S(1)} collective-permute-done((bf16[24,256]{1,0:T(8,128)(2,1)}, bf16[24,256]{1,0:T(8,128)(2,1)S(1)}, u32[]{:S(2)}, u32[]{:S(2)}) %collective-permute-start.15) | collective-permute-done | bytes 12320 | tf_op jit(solution)/shard_map/ppermute | solution.py:258
  52.3 0.6 %copy-done.13 = bf16[24,256]{1,0:T(8,128)(2,1)} copy-done((bf16[24,256]{1,0:T(8,128)(2,1)}, bf16[24,256]{1,0:T(8,128)(2,1)S(1)}, u32[]{:S(2)}) %copy-start.13) | copy-done | bytes 12312
  52.9 1.4 %shard_map.112 = bf16[2,3,6,256]{3,2,1,0:T(8,128)(2,1)} custom-call(s32[2]{0:T(128)} %pad_add_fusion.refs_0_.place, bf16[24,256]{1,0:T(8,128)(2,1)} %get-tuple-element.25.refs_0_, bf16[24,256]{1,0:T(8,128)(2,1)} %copy-done.11, bf16[24,256]{1,0:T(8,128)(2,1)} %copy-done.12, bf16[24,256]{1,0:T(8,128)(2,1)} %copy-done.13), custom_call_target="tpu_custom_call" | custom-call | tf_op jit(solution)/shard_map/pallas_call | solution.py:29
  54.3 1.4 %copy.22 = bf16[2,3,6,256]{3,0,2,1:T(2,128)(2,1)} copy(bf16[2,3,6,256]{3,2,1,0:T(8,128)(2,1)} %shard_map.112) | data formatting | bytes 36864 | tf_op jit(solution)/shard_map/pallas_call | solution.py:29
  (38 shorter events, 0.1 us)
Async XLA Ops:
  2.0 15.8 %collective-permute-start.6 = (bf16[2,72,128]{2,1,0:T(8,128)(2,1)S(1)}, bf16[2,72,128]{2,1,0:T(8,128)(2,1)S(1)}, u32[]{:S(2)}, u32[]{:S(2)}) collective-permute-start(bf16[2,72,128]{2,1,0:T(8,128)(2,1)S(1)} %get-tuple-element.32), channel_id=1, source_target_pairs={{0,16},{4,20},{8,24},{12,28},{16,0},{20,4},{24,8},{28,12},{1,17},{... | collective-permute-start | bytes 110600 | tf_op jit(solution)/shard_map/ppermute | solution.py:261
  6.1 11.7 %collective-permute-start.5 = (bf16[2,72,128]{2,1,0:T(8,128)(2,1)S(1)}, bf16[2,72,128]{2,1,0:T(8,128)(2,1)S(1)}, u32[]{:S(2)}, u32[]{:S(2)}) collective-permute-start(bf16[2,72,128]{2,1,0:T(8,128)(2,1)S(1)} %get-tuple-element.32), channel_id=1, source_target_pairs={{0,8},{4,12},{8,0},{12,4},{16,24},{20,28},{24,16},{28,20},{1,9},{5... | collective-permute-start | bytes 110600 | tf_op jit(solution)/shard_map/ppermute | solution.py:261
  7.7 10.1 %collective-permute-start.7 = (bf16[2,72,128]{2,1,0:T(8,128)(2,1)S(1)}, bf16[2,72,128]{2,1,0:T(8,128)(2,1)S(1)}, u32[]{:S(2)}, u32[]{:S(2)}) collective-permute-start(bf16[2,72,128]{2,1,0:T(8,128)(2,1)S(1)} %get-tuple-element.32), channel_id=1, source_target_pairs={{0,24},{4,28},{8,16},{12,20},{16,8},{20,12},{24,0},{28,4},{1,25},{... | collective-permute-start | bytes 110600 | tf_op jit(solution)/shard_map/ppermute | solution.py:261
  9.1 4.9 %collective-permute-start = (bf16[2,3,6,256]{3,2,1,0:T(8,128)(2,1)S(1)}, bf16[2,3,6,256]{3,2,1,0:T(8,128)(2,1)S(1)}, u32[]{:S(2)}, u32[]{:S(2)}) collective-permute-start(bf16[2,3,6,256]{3,2,1,0:T(8,128)(2,1)S(1)} %bitcast.46), channel_id=1, source_target_pairs={{0,1},{1,0},{2,3},{3,2},{4,5},{5,4},{6,7},{7,6},{8,9},{9,8},{10,11... | collective-permute-start | bytes 55304 | tf_op jit(solution)/shard_map/ppermute | solution.py:258
  10.8 4.8 %collective-permute-start.2 = (bf16[2,3,6,256]{3,2,1,0:T(8,128)(2,1)S(1)}, bf16[2,3,6,256]{3,2,1,0:T(8,128)(2,1)S(1)}, u32[]{:S(2)}, u32[]{:S(2)}) collective-permute-start(bf16[2,3,6,256]{3,2,1,0:T(8,128)(2,1)S(1)} %get-tuple-element.29), channel_id=1, source_target_pairs={{0,3},{1,2},{2,1},{3,0},{4,7},{5,6},{6,5},{7,4},{8,11},{9,10},{10,... | collective-permute-start | bytes 55304 | tf_op jit(solution)/shard_map/ppermute | solution.py:258
  14.0 7.6 %copy-start.3 = (bf16[2,3,6,256]{3,2,1,0:T(8,128)(2,1)}, bf16[2,3,6,256]{3,2,1,0:T(8,128)(2,1)S(1)}, u32[]{:S(2)}) copy-start(bf16[2,3,6,256]{3,2,1,0:T(8,128)(2,1)S(1)} %collective-permute-done.refs_3_) | copy-start | bytes 55300
  14.0 3.8 %collective-permute-start.1 = (bf16[2,3,6,256]{3,2,1,0:T(8,128)(2,1)S(1)}, bf16[2,3,6,256]{3,2,1,0:T(8,128)(2,1)S(1)}, u32[]{:S(2)}, u32[]{:S(2)}) collective-permute-start(bf16[2,3,6,256]{3,2,1,0:T(8,128)(2,1)S(1)} %get-tuple-element.29), channel_id=1, source_target_pairs={{0,2},{1,3},{2,0},{3,1},{4,6},{5,7},{6,4},{7,5},{8,10},{9,11},{10,... | collective-permute-start | bytes 55304 | tf_op jit(solution)/shard_map/ppermute | solution.py:258
  15.6 6.0 %copy-start.4 = (bf16[2,3,6,256]{3,2,1,0:T(8,128)(2,1)}, bf16[2,3,6,256]{3,2,1,0:T(8,128)(2,1)S(1)}, u32[]{:S(2)}) copy-start(bf16[2,3,6,256]{3,2,1,0:T(8,128)(2,1)S(1)} %collective-permute-done.2.refs_5_) | copy-start | bytes 55300
  17.8 3.8 %copy-start.5 = (bf16[2,3,6,256]{3,2,1,0:T(8,128)(2,1)}, bf16[2,3,6,256]{3,2,1,0:T(8,128)(2,1)S(1)}, u32[]{:S(2)}) copy-start(bf16[2,3,6,256]{3,2,1,0:T(8,128)(2,1)S(1)} %collective-permute-done.1.refs_4_) | copy-start | bytes 55300
  17.9 3.8 %copy-start = (bf16[4,2,72,128]{3,2,1,0:T(8,128)(2,1)}, bf16[4,2,72,128]{3,2,1,0:T(8,128)(2,1)S(1)}, u32[]{:S(2)}) copy-start(bf16[4,2,72,128]{3,2,1,0:T(8,128)(2,1)S(1)} %pad_maximum_fusion.refs_8_) | copy-start | bytes 442372
  17.9 3.7 %collective-permute-start.8 = (bf16[4,2,72,128]{3,2,1,0:T(8,128)(2,1)S(1)}, bf16[4,2,72,128]{3,2,1,0:T(8,128)(2,1)S(1)}, u32[]{:S(2)}, u32[]{:S(2)}) collective-permute-start(bf16[4,2,72,128]{3,2,1,0:T(8,128)(2,1)S(1)} %pad_maximum_fusion.refs_8_), channel_id=1, source_target_pairs={{0,4},{4,0},{8,12},{12,8},{16,20},{20,16},{24,28},{28,24},{1,5},{5... | collective-permute-start | bytes 442376 | tf_op jit(solution)/shard_map/ppermute | solution.py:264
  18.0 3.4 %collective-permute-start.4 = (bf16[4,6,256]{2,1,0:T(8,128)(2,1)S(1)}, bf16[4,6,256]{2,1,0:T(8,128)(2,1)S(1)}, u32[]{:S(2)}, u32[]{:S(2)}) collective-permute-start(bf16[4,6,256]{2,1,0:T(8,128)(2,1)S(1)} %get-tuple-element.39), channel_id=1, source_target_pairs={{4,8},{12,16},{20,24},{8,4},{16,12},{24,20},{5,9},{13,17},{21,25},... | collective-permute-start | bytes 36872 | tf_op jit(solution)/shard_map/ppermute | solution.py:268
  18.6 2.9 %collective-permute-start.3 = (bf16[4,6,256]{2,1,0:T(8,128)(2,1)S(1)}, bf16[4,6,256]{2,1,0:T(8,128)(2,1)S(1)}, u32[]{:S(2)}, u32[]{:S(2)}) collective-permute-start(bf16[4,6,256]{2,1,0:T(8,128)(2,1)S(1)} %get-tuple-element.40), channel_id=1, source_target_pairs={{0,4},{4,0},{8,12},{12,8},{16,20},{20,16},{24,28},{28,24},{1,5},{5... | collective-permute-start | bytes 36872 | tf_op jit(solution)/shard_map/ppermute | solution.py:264
  21.4 0.6 %copy-start.9 = (bf16[4,6,256]{2,1,0:T(8,128)(2,1)}, bf16[4,6,256]{2,1,0:T(8,128)(2,1)S(1)}, u32[]{:S(2)}) copy-start(bf16[4,6,256]{2,1,0:T(8,128)(2,1)S(1)} %collective-permute-done.4.refs_7_) | copy-start | bytes 36868
  21.6 0.6 %copy-start.10 = (bf16[4,6,256]{2,1,0:T(8,128)(2,1)}, bf16[4,6,256]{2,1,0:T(8,128)(2,1)S(1)}, u32[]{:S(2)}) copy-start(bf16[4,6,256]{2,1,0:T(8,128)(2,1)S(1)} %collective-permute-done.3.refs_6_) | copy-start | bytes 36868
  21.6 0.6 %copy-start.1 = (bf16[4,2,72,128]{3,2,1,0:T(8,128)(2,1)}, bf16[4,2,72,128]{3,2,1,0:T(8,128)(2,1)S(1)}, u32[]{:S(2)}) copy-start(bf16[4,2,72,128]{3,2,1,0:T(8,128)(2,1)S(1)} %collective-permute-done.8.refs_9_) | copy-start | bytes 442372
  27.1 3.2 %collective-permute-start.9 = (bf16[4,2,72,128]{3,2,1,0:T(8,128)(2,1)}, bf16[4,2,72,128]{3,2,1,0:T(8,128)(2,1)S(1)}, u32[]{:S(2)}, u32[]{:S(2)}) collective-permute-start(bf16[4,2,72,128]{3,2,1,0:T(8,128)(2,1)} %get-tuple-element.18), channel_id=1, source_target_pairs={{0,4},{4,0},{8,12},{12,8},{16,20},{20,16},{24,28},{28,24},{1,5},{5... | collective-permute-start | bytes 442376 | tf_op jit(solution)/shard_map/ppermute | solution.py:264
  30.2 0.7 %copy-start.2 = (bf16[4,2,72,128]{3,2,1,0:T(8,128)(2,1)}, bf16[4,2,72,128]{3,2,1,0:T(8,128)(2,1)S(1)}, u32[]{:S(2)}) copy-start(bf16[4,2,72,128]{3,2,1,0:T(8,128)(2,1)S(1)} %collective-permute-done.9.received) | copy-start | bytes 442372
  32.5 4.4 %collective-permute-start.10 = (bf16[2,72,128]{2,1,0:T(8,128)(2,1)}, bf16[2,72,128]{2,1,0:T(8,128)(2,1)S(1)}, u32[]{:S(2)}, u32[]{:S(2)}) collective-permute-start(bf16[2,72,128]{2,1,0:T(8,128)(2,1)} %get-tuple-element.20), channel_id=1, source_target_pairs={{0,8},{4,12},{8,0},{12,4},{16,24},{20,28},{24,16},{28,20},{1,9},{5... | collective-permute-start | bytes 110600 | tf_op jit(solution)/shard_map/ppermute | solution.py:261
  33.2 6.1 %collective-permute-start.11 = (bf16[2,72,128]{2,1,0:T(8,128)(2,1)}, bf16[2,72,128]{2,1,0:T(8,128)(2,1)S(1)}, u32[]{:S(2)}, u32[]{:S(2)}) collective-permute-start(bf16[2,72,128]{2,1,0:T(8,128)(2,1)} %get-tuple-element.21), channel_id=1, source_target_pairs={{0,16},{4,20},{8,24},{12,28},{16,0},{20,4},{24,8},{28,12},{1,17},{... | collective-permute-start | bytes 110600 | tf_op jit(solution)/shard_map/ppermute | solution.py:261
  36.6 6.0 %collective-permute-start.12 = (bf16[2,72,128]{2,1,0:T(8,128)(2,1)}, bf16[2,72,128]{2,1,0:T(8,128)(2,1)S(1)}, u32[]{:S(2)}, u32[]{:S(2)}) collective-permute-start(bf16[2,72,128]{2,1,0:T(8,128)(2,1)} %get-tuple-element.22), channel_id=1, source_target_pairs={{0,24},{4,28},{8,16},{12,20},{16,8},{20,12},{24,0},{28,4},{1,25},{... | collective-permute-start | bytes 110600 | tf_op jit(solution)/shard_map/ppermute | solution.py:261
  36.9 5.6 %copy-start.6 = (bf16[2,72,128]{2,1,0:T(8,128)(2,1)}, bf16[2,72,128]{2,1,0:T(8,128)(2,1)S(1)}, u32[]{:S(2)}) copy-start(bf16[2,72,128]{2,1,0:T(8,128)(2,1)S(1)} %collective-permute-done.10.refs_1_) | copy-start | bytes 110596
  39.4 3.2 %copy-start.7 = (bf16[2,72,128]{2,1,0:T(8,128)(2,1)}, bf16[2,72,128]{2,1,0:T(8,128)(2,1)S(1)}, u32[]{:S(2)}) copy-start(bf16[2,72,128]{2,1,0:T(8,128)(2,1)S(1)} %collective-permute-done.11.refs_2_) | copy-start | bytes 110596
  42.5 0.6 %copy-start.8 = (bf16[2,72,128]{2,1,0:T(8,128)(2,1)}, bf16[2,72,128]{2,1,0:T(8,128)(2,1)S(1)}, u32[]{:S(2)}) copy-start(bf16[2,72,128]{2,1,0:T(8,128)(2,1)S(1)} %collective-permute-done.12.refs_3_) | copy-start | bytes 110596
  45.3 3.9 %collective-permute-start.13 = (bf16[24,256]{1,0:T(8,128)(2,1)}, bf16[24,256]{1,0:T(8,128)(2,1)S(1)}, u32[]{:S(2)}, u32[]{:S(2)}) collective-permute-start(bf16[24,256]{1,0:T(8,128)(2,1)} %get-tuple-element.26), channel_id=1, source_target_pairs={{0,1},{1,0},{2,3},{3,2},{4,5},{5,4},{6,7},{7,6},{8,9},{9,8},{10,11... | collective-permute-start | bytes 36872 | tf_op jit(solution)/shard_map/ppermute | solution.py:258
  46.8 3.9 %collective-permute-start.14 = (bf16[24,256]{1,0:T(8,128)(2,1)}, bf16[24,256]{1,0:T(8,128)(2,1)S(1)}, u32[]{:S(2)}, u32[]{:S(2)}) collective-permute-start(bf16[24,256]{1,0:T(8,128)(2,1)} %get-tuple-element.27), channel_id=1, source_target_pairs={{0,2},{1,3},{2,0},{3,1},{4,6},{5,7},{6,4},{7,5},{8,10},{9,11},{10,... | collective-permute-start | bytes 36872 | tf_op jit(solution)/shard_map/ppermute | solution.py:258
  47.5 4.8 %collective-permute-start.15 = (bf16[24,256]{1,0:T(8,128)(2,1)}, bf16[24,256]{1,0:T(8,128)(2,1)S(1)}, u32[]{:S(2)}, u32[]{:S(2)}) collective-permute-start(bf16[24,256]{1,0:T(8,128)(2,1)} %get-tuple-element.28), channel_id=1, source_target_pairs={{0,3},{1,2},{2,1},{3,0},{4,7},{5,6},{6,5},{7,4},{8,11},{9,10},{10,... | collective-permute-start | bytes 36872 | tf_op jit(solution)/shard_map/ppermute | solution.py:258
  49.2 3.1 %copy-start.11 = (bf16[24,256]{1,0:T(8,128)(2,1)}, bf16[24,256]{1,0:T(8,128)(2,1)S(1)}, u32[]{:S(2)}) copy-start(bf16[24,256]{1,0:T(8,128)(2,1)S(1)} %collective-permute-done.13.refs_1_) | copy-start | bytes 36868
  50.7 1.6 %copy-start.12 = (bf16[24,256]{1,0:T(8,128)(2,1)}, bf16[24,256]{1,0:T(8,128)(2,1)S(1)}, u32[]{:S(2)}) copy-start(bf16[24,256]{1,0:T(8,128)(2,1)S(1)} %collective-permute-done.14.refs_2_) | copy-start | bytes 36868
  52.3 0.6 %copy-start.13 = (bf16[24,256]{1,0:T(8,128)(2,1)}, bf16[24,256]{1,0:T(8,128)(2,1)S(1)}, u32[]{:S(2)}) copy-start(bf16[24,256]{1,0:T(8,128)(2,1)S(1)} %collective-permute-done.15.refs_3_) | copy-start | bytes 36868

commit v2 on v1

--- a/solution.py
+++ b/solution.py
@@ -10,6 +10,7 @@
 
 HEADS = 4
 VMEM_BYTES = 60 * 1024 * 1024
+HELD_BYTES = 3 * 512 * 1024
 UNROLLED_CHUNKS = 16
 F32 = jnp.float32
 BF16 = jnp.bfloat16
@@ -26,6 +27,12 @@
     scalar = pl.BlockSpec(memory_space=pltpu.SMEM)
 
     def run(*operands):
+        operands = operands[:scalars] + tuple(
+            pltpu.with_memory_space_constraint(operand, pltpu.VMEM)
+            if operand.size * operand.dtype.itemsize <= HELD_BYTES
+            else operand
+            for operand in operands[scalars:]
+        )
         return pl.pallas_call(
             kernel,
             out_shape=out_shape,
@@ -36,6 +43,11 @@
         )(*operands)
 
     return run
+
+
+def held(shape, dtype):
+    small = np.prod(shape) * np.dtype(dtype).itemsize <= HELD_BYTES
+    return (pltpu.VMEM if small else jax.ShapeDtypeStruct)(shape, dtype)
 
 
 def pad8(amount):
@@ -293,14 +305,14 @@
     select = shift_selector(rows + 2, cols, n_col)
     middle = shift_selector(rows, cols, n_col)[1]
     padded = pad8(cols)
-    block = jax.ShapeDtypeStruct((chips, pairs, strip, lanes), BF16)
+    block = held((chips, pairs, strip, lanes), BF16)
     dkv_own, dkv_other, dq, grad_z = call(
         functools.partial(strip_kernel, n_col, per_sample),
         (
             block,
             block,
-            jax.ShapeDtypeStruct((strip, lanes), F32),
-            jax.ShapeDtypeStruct((strip, channels), BF16),
+            held((strip, lanes), F32),
+            held((strip, channels), BF16),
         ),
         (
             pltpu.VMEM((n_col, rows + 2, padded, channels), F32),
@@ -324,12 +336,12 @@
 
     sums = call(
         core_sum_kernel,
-        [jax.ShapeDtypeStruct((pairs, strip, lanes), BF16) for _ in range(chips)],
+        [held((pairs, strip, lanes), BF16) for _ in range(chips)],
         scalars=0,
     )(dkv_own, to_core(dkv_other))
     parts = [sums[0]] + [to_chip(sums[k], k) for k in range(1, chips)]
 
-    tile = jax.ShapeDtypeStruct((rows * padded, channels), BF16)
+    tile = held((rows * padded, channels), BF16)
     cut = call(functools.partial(project_kernel, n_col, per_sample), [tile] * n_col)(
         place,
         *parts,
@@ -341,7 +353,7 @@
     returned = [cut[0]] + [to_col(cut[k], k) for k in range(1, n_col)]
     return call(
         functools.partial(output_kernel, per_sample),
-        jax.ShapeDtypeStruct((samples, rows, cols, channels), BF16),
+        held((samples, rows, cols, channels), BF16),
     )(place, *returned)
 
 

time: 56.5 us -> 48.1 us (0.85)
  Pallas kernels: 10 us -> 4.98 us
  local copies, waits for them, and re-layouts: 8 us -> 5.03 us
  starting transfers between devices: 22.3 us -> 23.3 us
  other arithmetic: 1.5 us -> 0.89 us
  waiting for transfers between devices: 13.6 us -> 13 us
    pallas_call x4, Pallas kernels: 10 us -> 4.98 us  [run(): pl.pallas_call(kernel, out_shape=out_shape, in_specs=[scalar] * scalars +...]
    unnamed x34 -> x18, local copies, waits for them, and re-layouts: 3.06 us -> 1.32 us
    pallas_call x1, local copies, waits for them, and re-layouts: 1.36 us -> 0.62 us  [run(): pl.pallas_call(kernel, out_shape=out_shape, in_specs=[scalar] * scalars +...]
    ppermute x6, starting transfers between devices: 7.47 us -> 8.14 us  [to_col(): return lax.ppermute(array, 'col', [(i, i ^ k) for i in range(n_col)])]
    concatenate x1, other arithmetic: 0.7 us -> 0.08 us  [shards(): queries = jnp.concatenate([query_heads[1], query_heads[0]], -1)]
    another operation x1, local copies, waits for them, and re-layouts: 1.36 us -> 0.75 us  [shards(): both = jnp.stack([out_grad, pre_silu])]
  transfers between devices with their start and end apart: 16 -> 16, of which waited for: 9 -> 9; matrix products, arithmetic and copies ran while one was open for 7% -> 5% of each run, Pallas kernels for 0% -> 0%
where the time goes in v2:
time: 48.1 us; the launch traced here: 47.4 us
  starting transfers between devices  23.3 us (48%)
  waiting for transfers between devices  13 us (27%)
  local copies, waits for them, and re-layouts  5.03 us (10%)
  Pallas kernels  4.98 us (10%)
  other arithmetic  0.89 us (2%)
    ppermute x6, starting transfers between devices, to_chip(): return lax.ppermute(array, 'row', [(i, i ^ 2 * k) for i in range(n_row)])  10.2 us
    ppermute x6, starting transfers between devices, to_col(): return lax.ppermute(array, 'col', [(i, i ^ k) for i in range(n_col)])  8.14 us
    ppermute x6, waiting for transfers between devices, to_col(): return lax.ppermute(array, 'col', [(i, i ^ k) for i in range(n_col)])  6.43 us
    ppermute x6, waiting for transfers between devices, to_chip(): return lax.ppermute(array, 'row', [(i, i ^ 2 * k) for i in range(n_row)])  5.42 us
    pallas_call x4, Pallas kernels, run(): pl.pallas_call(kernel, out_shape=out_shape, in_specs=[scalar] * scalars +...  4.98 us
    ppermute x3, starting transfers between devices, to_core(): return lax.ppermute(array, 'row', [(i, i ^ 1) for i in range(n_row)])  4.17 us
    unnamed x18, local copies, waits for them, and re-layouts  1.32 us
    ppermute x3, waiting for transfers between devices, to_core(): return lax.ppermute(array, 'row', [(i, i ^ 1) for i in range(n_row)])  1.2 us
  transfers between devices with their start and end apart: 16, of which 9 were waited for; matrix products, arithmetic and copies ran while one was open for 5% of the time, Pallas kernels for 0%

profile of v2, /device:TPU:0, one launch (start us, length us, event | category | flops | bytes accessed | tf_op | source)
XLA Modules:
  0.0 47.4 jit_solution(11541746900247156322)
XLA Ops:
  0.0 0.9 %fusion.6 = (bf16[1,72,64]{1,2,0:T(8,128)(2,1)S(1)}, bf16[1,72,64]{1,2,0:T(8,128)(2,1)S(1)}) fusion(bf16[2,72,64]{1,2,0:T(8,128)(2,1)} %param.14), kind=kLoop, calls=%fused_computation.30 | loop fusion | bytes 36864 | tf_op jit(solution)/shard_map/slice | solution.py:291
  0.9 0.1 copy.24
  1.0 0.1 copy.25
  1.1 0.7 %fusion.5 = (bf16[1,72,64]{1,2,0:T(8,128)(2,1)S(1)}, bf16[1,72,64]{1,2,0:T(8,128)(2,1)S(1)}) fusion(bf16[2,72,64]{1,2,0:T(8,128)(2,1)} %param.15), kind=kLoop, calls=%fused_computation.29 | loop fusion | bytes 36864 | tf_op jit(solution)/shard_map/slice | solution.py:291
  1.8 0.1 copy.23
  1.9 0.1 copy.26
  2.0 0.1 maximum_bitcast_fusion
  2.1 4.1 %collective-permute-start.6 = (bf16[2,72,128]{2,1,0:T(8,128)(2,1)S(1)}, bf16[2,72,128]{2,1,0:T(8,128)(2,1)S(1)}, u32[]{:S(2)}, u32[]{:S(2)}) collective-permute-start(bf16[2,72,128]{2,1,0:T(8,128)(2,1)S(1)} %get-tuple-element.32), channel_id=1, source_target_pairs={{0,16},{4,20},{8,24},{12,28},{16,0},{20,4},{24,8},{28,12},{1,17},{... | collective-permute-start | bytes 110600 | tf_op jit(solution)/shard_map/ppermute | solution.py:273
  6.2 1.6 %collective-permute-start.5 = (bf16[2,72,128]{2,1,0:T(8,128)(2,1)S(1)}, bf16[2,72,128]{2,1,0:T(8,128)(2,1)S(1)}, u32[]{:S(2)}, u32[]{:S(2)}) collective-permute-start(bf16[2,72,128]{2,1,0:T(8,128)(2,1)S(1)} %get-tuple-element.32), channel_id=1, source_target_pairs={{0,8},{4,12},{8,0},{12,4},{16,24},{20,28},{24,16},{28,20},{1,9},{5... | collective-permute-start | bytes 110600 | tf_op jit(solution)/shard_map/ppermute | solution.py:273
  7.8 0.8 %copy_bitcast_fusion = (bf16[1,2,3,6,256]{4,3,2,1,0:T(8,128)(2,1)S(1)}, bf16[2,3,6,256]{3,2,1,0:T(8,128)(2,1)S(1)}, bf16[2,3,6,256]{3,2,1,0:T(8,128)(2,1)S(1)}, bf16[1,2,3,6,256]{4,3,2,1,0:T(8,128)(2,1)S(1)}) fusion(bf16[2,3,6,256]{3,0,2,1:T(2,128)(2,1)} %param.11, bf16[2,3,6,256]{3,0,2,1:T(2,128)(2,1)} %param.12), kind=kLoop, calls=%fused_computation.25 | loop fusion | bytes 110592 | tf_op jit(solution)/shard_map/stack | solution.py:282
  8.6 1.8 %collective-permute-start = (bf16[2,3,6,256]{3,2,1,0:T(8,128)(2,1)S(1)}, bf16[2,3,6,256]{3,2,1,0:T(8,128)(2,1)S(1)}, u32[]{:S(2)}, u32[]{:S(2)}) collective-permute-start(bf16[2,3,6,256]{3,2,1,0:T(8,128)(2,1)S(1)} %bitcast.46), channel_id=1, source_target_pairs={{0,1},{1,0},{2,3},{3,2},{4,5},{5,4},{6,7},{7,6},{8,9},{9,8},{10,11... | collective-permute-start | bytes 55304 | tf_op jit(solution)/shard_map/ppermute | solution.py:270
  10.4 1.5 %collective-permute-start.2 = (bf16[2,3,6,256]{3,2,1,0:T(8,128)(2,1)S(1)}, bf16[2,3,6,256]{3,2,1,0:T(8,128)(2,1)S(1)}, u32[]{:S(2)}, u32[]{:S(2)}) collective-permute-start(bf16[2,3,6,256]{3,2,1,0:T(8,128)(2,1)S(1)} %get-tuple-element.29), channel_id=1, source_target_pairs={{0,3},{1,2},{2,1},{3,0},{4,7},{5,6},{6,5},{7,4},{8,11},{9,10},{10,... | collective-permute-start | bytes 55304 | tf_op jit(solution)/shard_map/ppermute | solution.py:270
  11.9 0.7 %fusion.4 = (bf16[1,72,64]{1,2,0:T(8,128)(2,1)S(1)}, bf16[1,72,64]{1,2,0:T(8,128)(2,1)S(1)}) fusion(bf16[2,72,64]{1,2,0:T(8,128)(2,1)} %param.13), kind=kLoop, calls=%fused_computation.28 | loop fusion | bytes 36864 | tf_op jit(solution)/shard_map/slice | solution.py:297
  12.6 0.1 copy.27
  12.7 0.1 copy.28
  12.8 0.1 pad_maximum_fusion.2.refs_10_
  12.9 0.0 collective-permute-done.refs_3_
  12.9 1.3 %collective-permute-start.1 = (bf16[2,3,6,256]{3,2,1,0:T(8,128)(2,1)S(1)}, bf16[2,3,6,256]{3,2,1,0:T(8,128)(2,1)S(1)}, u32[]{:S(2)}, u32[]{:S(2)}) collective-permute-start(bf16[2,3,6,256]{3,2,1,0:T(8,128)(2,1)S(1)} %get-tuple-element.29), channel_id=1, source_target_pairs={{0,2},{1,3},{2,0},{3,1},{4,6},{5,7},{6,4},{7,5},{8,10},{9,11},{10,... | collective-permute-start | bytes 55304 | tf_op jit(solution)/shard_map/ppermute | solution.py:270
  14.2 0.9 %collective-permute-done.2.refs_5_ = bf16[2,3,6,256]{3,2,1,0:T(8,128)(2,1)S(1)} collective-permute-done((bf16[2,3,6,256]{3,2,1,0:T(8,128)(2,1)S(1)}, bf16[2,3,6,256]{3,2,1,0:T(8,128)(2,1)S(1)}, u32[]{:S(2)}, u32[]{:S(2)}) %collective-permute-start.2) | collective-permute-done | bytes 18464 | tf_op jit(solution)/shard_map/ppermute | solution.py:270
  15.1 1.7 %collective-permute-done.1.refs_4_ = bf16[2,3,6,256]{3,2,1,0:T(8,128)(2,1)S(1)} collective-permute-done((bf16[2,3,6,256]{3,2,1,0:T(8,128)(2,1)S(1)}, bf16[2,3,6,256]{3,2,1,0:T(8,128)(2,1)S(1)}, u32[]{:S(2)}, u32[]{:S(2)}) %collective-permute-start.1) | collective-permute-done | bytes 18464 | tf_op jit(solution)/shard_map/ppermute | solution.py:270
  16.8 0.0 collective-permute-done.6
  16.8 0.0 collective-permute-done.7
  16.8 0.1 collective-permute-start.8
  16.9 0.0 copy-start.1
  16.9 0.0 copy-start.4
  17.0 0.8 %collective-permute-start.4 = (bf16[4,6,256]{2,1,0:T(8,128)(2,1)S(1)}, bf16[4,6,256]{2,1,0:T(8,128)(2,1)S(1)}, u32[]{:S(2)}, u32[]{:S(2)}) collective-permute-start(bf16[4,6,256]{2,1,0:T(8,128)(2,1)S(1)} %get-tuple-element.39), channel_id=1, source_target_pairs={{4,8},{12,16},{20,24},{8,4},{16,12},{24,20},{5,9},{13,17},{21,25},... | collective-permute-start | bytes 36872 | tf_op jit(solution)/shard_map/ppermute | solution.py:280
  17.8 2.1 %collective-permute-start.3 = (bf16[4,6,256]{2,1,0:T(8,128)(2,1)S(1)}, bf16[4,6,256]{2,1,0:T(8,128)(2,1)S(1)}, u32[]{:S(2)}, u32[]{:S(2)}) collective-permute-start(bf16[4,6,256]{2,1,0:T(8,128)(2,1)S(1)} %get-tuple-element.40), channel_id=1, source_target_pairs={{0,4},{4,0},{8,12},{12,8},{16,20},{20,16},{24,28},{28,24},{1,5},{5... | collective-permute-start | bytes 36872 | tf_op jit(solution)/shard_map/ppermute | solution.py:276
  19.9 0.7 %pad_add_fusion.refs_0_.place = s32[2]{0:T(128)} fusion(s32[1]{0:T(128)} %bitcast.1, s32[1]{0:T(128)} %bitcast), kind=kLoop, calls=%fused_computation.24 | loop fusion | flops 2 | bytes 16 | tf_op jit(solution)/shard_map/stack | solution.py:267
  20.5 0.2 collective-permute-done.3.refs_6_
  20.7 0.0 copy-start.5
  20.7 0.7 %copy-done.5 = bf16[72,96]{1,0:T(8,128)(2,1)S(1)} copy-done((bf16[72,96]{1,0:T(8,128)(2,1)S(1)}, bf16[72,96]{1,0:T(8,128)(2,1)}, u32[]{:S(2)}) %copy-start.5) | copy-done | bytes 13848
  21.5 3.2 %shard_map.109 = (bf16[4,2,72,128]{3,2,1,0:T(8,128)(2,1)S(1)}, bf16[4,2,72,128]{3,2,1,0:T(8,128)(2,1)S(1)}, f32[72,128]{1,0:T(8,128)S(1)}, bf16[72,256]{1,0:T(8,128)(2,1)S(1)}) custom-call(s32[2]{0:T(128)} %pad_add_fusion.refs_0_.place, bf16[2,3,6,256]{3,2,1,0:T(8,128)(2,1)S(1)} %get-tuple-element.53.refs_1_, ...), custom_call_target="tpu_custom_call" | custom-call | tf_op jit(solution)/shard_map/pallas_call | solution.py:36
  24.7 2.0 %collective-permute-start.9 = (bf16[4,2,72,128]{3,2,1,0:T(8,128)(2,1)S(1)}, bf16[4,2,72,128]{3,2,1,0:T(8,128)(2,1)S(1)}, u32[]{:S(2)}, u32[]{:S(2)}) collective-permute-start(bf16[4,2,72,128]{3,2,1,0:T(8,128)(2,1)S(1)} %get-tuple-element.18), channel_id=1, source_target_pairs={{0,4},{4,0},{8,12},{12,8},{16,20},{20,16},{24,28},{28,24},{1,5},{5... | collective-permute-start | bytes 442376 | tf_op jit(solution)/shard_map/ppermute | solution.py:276
  26.7 1.0 %collective-permute-done.9.received = bf16[4,2,72,128]{3,2,1,0:T(8,128)(2,1)S(1)} collective-permute-done((bf16[4,2,72,128]{3,2,1,0:T(8,128)(2,1)S(1)}, bf16[4,2,72,128]{3,2,1,0:T(8,128)(2,1)S(1)}, u32[]{:S(2)}, u32[]{:S(2)}) %collective-permute-start.9) | collective-permute-done | bytes 147488 | tf_op jit(solution)/shard_map/ppermute | solution.py:276
  27.7 0.8 %collective-permute-start.10 = (bf16[2,72,128]{2,1,0:T(8,128)(2,1)S(1)}, bf16[2,72,128]{2,1,0:T(8,128)(2,1)S(1)}, u32[]{:S(2)}, u32[]{:S(2)}) collective-permute-start(bf16[2,72,128]{2,1,0:T(8,128)(2,1)S(1)} %get-tuple-element.20), channel_id=1, source_target_pairs={{0,8},{4,12},{8,0},{12,4},{16,24},{20,28},{24,16},{28,20},{1,9},{5... | collective-permute-start | bytes 110600 | tf_op jit(solution)/shard_map/ppermute | solution.py:273
  28.5 3.4 %collective-permute-start.11 = (bf16[2,72,128]{2,1,0:T(8,128)(2,1)S(1)}, bf16[2,72,128]{2,1,0:T(8,128)(2,1)S(1)}, u32[]{:S(2)}, u32[]{:S(2)}) collective-permute-start(bf16[2,72,128]{2,1,0:T(8,128)(2,1)S(1)} %get-tuple-element.21), channel_id=1, source_target_pairs={{0,16},{4,20},{8,24},{12,28},{16,0},{20,4},{24,8},{28,12},{1,17},{... | collective-permute-start | bytes 110600 | tf_op jit(solution)/shard_map/ppermute | solution.py:273
  31.9 0.3 collective-permute-start.12
  32.2 2.2 %collective-permute-done.11.refs_2_ = bf16[2,72,128]{2,1,0:T(8,128)(2,1)S(1)} collective-permute-done((bf16[2,72,128]{2,1,0:T(8,128)(2,1)S(1)}, bf16[2,72,128]{2,1,0:T(8,128)(2,1)S(1)}, u32[]{:S(2)}, u32[]{:S(2)}) %collective-permute-start.11) | collective-permute-done | bytes 36896 | tf_op jit(solution)/shard_map/ppermute | solution.py:273
  34.4 3.2 %collective-permute-done.12.refs_3_ = bf16[2,72,128]{2,1,0:T(8,128)(2,1)S(1)} collective-permute-done((bf16[2,72,128]{2,1,0:T(8,128)(2,1)S(1)}, bf16[2,72,128]{2,1,0:T(8,128)(2,1)S(1)}, u32[]{:S(2)}, u32[]{:S(2)}) %collective-permute-start.12) | collective-permute-done | bytes 36896 | tf_op jit(solution)/shard_map/ppermute | solution.py:273
  37.6 1.1 %shard_map.111 = (bf16[24,256]{1,0:T(8,128)(2,1)S(1)}, bf16[24,256]{1,0:T(8,128)(2,1)S(1)}, bf16[24,256]{1,0:T(8,128)(2,1)S(1)}, bf16[24,256]{1,0:T(8,128)(2,1)S(1)}) custom-call(s32[2]{0:T(128)} %pad_add_fusion.refs_0_.place, bf16[2,72,128]{2,1,0:T(8,128)(2,1)S(1)} %get-tuple-element.19.refs_0_, bf16[2,72,128]{2,1,0:T(8,128)(2,1)S(1)} %collective-permute-done.10.refs_1_, ...), custom_call_target="tpu_custom_call" | custom-call | tf_op jit(solution)/shard_map/pallas_call | solution.py:36
  38.7 1.6 %collective-permute-start.13 = (bf16[24,256]{1,0:T(8,128)(2,1)S(1)}, bf16[24,256]{1,0:T(8,128)(2,1)S(1)}, u32[]{:S(2)}, u32[]{:S(2)}) collective-permute-start(bf16[24,256]{1,0:T(8,128)(2,1)S(1)} %get-tuple-element.26), channel_id=1, source_target_pairs={{0,1},{1,0},{2,3},{3,2},{4,5},{5,4},{6,7},{7,6},{8,9},{9,8},{10,11... | collective-permute-start | bytes 36872 | tf_op jit(solution)/shard_map/ppermute | solution.py:270
  40.2 1.3 %collective-permute-start.14 = (bf16[24,256]{1,0:T(8,128)(2,1)S(1)}, bf16[24,256]{1,0:T(8,128)(2,1)S(1)}, u32[]{:S(2)}, u32[]{:S(2)}) collective-permute-start(bf16[24,256]{1,0:T(8,128)(2,1)S(1)} %get-tuple-element.27), channel_id=1, source_target_pairs={{0,2},{1,3},{2,0},{3,1},{4,6},{5,7},{6,4},{7,5},{8,10},{9,11},{10,... | collective-permute-start | bytes 36872 | tf_op jit(solution)/shard_map/ppermute | solution.py:270
  41.5 0.7 %collective-permute-start.15 = (bf16[24,256]{1,0:T(8,128)(2,1)S(1)}, bf16[24,256]{1,0:T(8,128)(2,1)S(1)}, u32[]{:S(2)}, u32[]{:S(2)}) collective-permute-start(bf16[24,256]{1,0:T(8,128)(2,1)S(1)} %get-tuple-element.28), channel_id=1, source_target_pairs={{0,3},{1,2},{2,1},{3,0},{4,7},{5,6},{6,5},{7,4},{8,11},{9,10},{10,... | collective-permute-start | bytes 36872 | tf_op jit(solution)/shard_map/ppermute | solution.py:270
  42.2 0.2 collective-permute-done.13.refs_1_
  42.4 1.5 %collective-permute-done.14.refs_2_ = bf16[24,256]{1,0:T(8,128)(2,1)S(1)} collective-permute-done((bf16[24,256]{1,0:T(8,128)(2,1)S(1)}, bf16[24,256]{1,0:T(8,128)(2,1)S(1)}, u32[]{:S(2)}, u32[]{:S(2)}) %collective-permute-start.14) | collective-permute-done | bytes 12320 | tf_op jit(solution)/shard_map/ppermute | solution.py:270
  43.9 2.2 %collective-permute-done.15.refs_3_ = bf16[24,256]{1,0:T(8,128)(2,1)S(1)} collective-permute-done((bf16[24,256]{1,0:T(8,128)(2,1)S(1)}, bf16[24,256]{1,0:T(8,128)(2,1)S(1)}, u32[]{:S(2)}, u32[]{:S(2)}) %collective-permute-start.15) | collective-permute-done | bytes 12320 | tf_op jit(solution)/shard_map/ppermute | solution.py:270
  46.1 0.7 %shard_map.112 = bf16[2,3,6,256]{3,2,1,0:T(8,128)(2,1)S(1)} custom-call(s32[2]{0:T(128)} %pad_add_fusion.refs_0_.place, bf16[24,256]{1,0:T(8,128)(2,1)S(1)} %get-tuple-element.25.refs_0_, bf16[24,256]{1,0:T(8,128)(2,1)S(1)} %collective-permute-done.13.refs_1_, bf16[24,256]{1,0:T(8,128)(2,1)S(1)} %collective-permute-done.14.refs_2_, ...), custom_call_target="tpu_custom_call" | custom-call | tf_op jit(solution)/shard_map/pallas_call | solution.py:36
  46.8 0.6 %copy.22 = bf16[2,3,6,256]{3,0,2,1:T(2,128)(2,1)} copy(bf16[2,3,6,256]{3,2,1,0:T(8,128)(2,1)S(1)} %shard_map.112) | data formatting | bytes 36864 | tf_op jit(solution)/shard_map/pallas_call | solution.py:36
  (22 shorter events, 0.1 us)
Async XLA Ops:
  0.0 20.7 %copy-start.2 = (bf16[3,120,160]{2,1,0:T(8,128)(2,1)S(1)}, bf16[3,120,160]{2,1,0:T(8,128)(2,1)}, u32[]{:S(2)}) copy-start(bf16[3,120,160]{2,1,0:T(8,128)(2,1)} %constant.47.clone.refs_13_) | copy-start | bytes 345604
  0.0 20.7 %copy-start.3 = (bf16[256,256]{1,0:T(8,128)(2,1)S(1)}, bf16[256,256]{1,0:T(8,128)(2,1)}, u32[]{:S(2)}) copy-start(bf16[256,256]{1,0:T(8,128)(2,1)} %refs_12_.1) | copy-start | bytes 393220
  0.0 20.7 %copy-start = (bf16[3,3,256,256]{3,2,1,0:T(8,128)(2,1)S(1)}, bf16[3,3,256,256]{3,2,1,0:T(8,128)(2,1)}, u32[]{:S(2)}) copy-start(bf16[3,3,256,256]{3,2,1,0:T(8,128)(2,1)} %refs_11_.1) | copy-start | bytes 3538948
  2.1 14.7 %collective-permute-start.6 = (bf16[2,72,128]{2,1,0:T(8,128)(2,1)S(1)}, bf16[2,72,128]{2,1,0:T(8,128)(2,1)S(1)}, u32[]{:S(2)}, u32[]{:S(2)}) collective-permute-start(bf16[2,72,128]{2,1,0:T(8,128)(2,1)S(1)} %get-tuple-element.32), channel_id=1, source_target_pairs={{0,16},{4,20},{8,24},{12,28},{16,0},{20,4},{24,8},{28,12},{1,17},{... | collective-permute-start | bytes 110600 | tf_op jit(solution)/shard_map/ppermute | solution.py:273
  6.2 10.6 %collective-permute-start.5 = (bf16[2,72,128]{2,1,0:T(8,128)(2,1)S(1)}, bf16[2,72,128]{2,1,0:T(8,128)(2,1)S(1)}, u32[]{:S(2)}, u32[]{:S(2)}) collective-permute-start(bf16[2,72,128]{2,1,0:T(8,128)(2,1)S(1)} %get-tuple-element.32), channel_id=1, source_target_pairs={{0,8},{4,12},{8,0},{12,4},{16,24},{20,28},{24,16},{28,20},{1,9},{5... | collective-permute-start | bytes 110600 | tf_op jit(solution)/shard_map/ppermute | solution.py:273
  7.8 9.0 %collective-permute-start.7 = (bf16[2,72,128]{2,1,0:T(8,128)(2,1)S(1)}, bf16[2,72,128]{2,1,0:T(8,128)(2,1)S(1)}, u32[]{:S(2)}, u32[]{:S(2)}) collective-permute-start(bf16[2,72,128]{2,1,0:T(8,128)(2,1)S(1)} %get-tuple-element.32), channel_id=1, source_target_pairs={{0,24},{4,28},{8,16},{12,20},{16,8},{20,12},{24,0},{28,4},{1,25},{... | collective-permute-start | bytes 110600 | tf_op jit(solution)/shard_map/ppermute | solution.py:273
  8.6 4.3 %collective-permute-start = (bf16[2,3,6,256]{3,2,1,0:T(8,128)(2,1)S(1)}, bf16[2,3,6,256]{3,2,1,0:T(8,128)(2,1)S(1)}, u32[]{:S(2)}, u32[]{:S(2)}) collective-permute-start(bf16[2,3,6,256]{3,2,1,0:T(8,128)(2,1)S(1)} %bitcast.46), channel_id=1, source_target_pairs={{0,1},{1,0},{2,3},{3,2},{4,5},{5,4},{6,7},{7,6},{8,9},{9,8},{10,11... | collective-permute-start | bytes 55304 | tf_op jit(solution)/shard_map/ppermute | solution.py:270
  10.4 4.7 %collective-permute-start.2 = (bf16[2,3,6,256]{3,2,1,0:T(8,128)(2,1)S(1)}, bf16[2,3,6,256]{3,2,1,0:T(8,128)(2,1)S(1)}, u32[]{:S(2)}, u32[]{:S(2)}) collective-permute-start(bf16[2,3,6,256]{3,2,1,0:T(8,128)(2,1)S(1)} %get-tuple-element.29), channel_id=1, source_target_pairs={{0,3},{1,2},{2,1},{3,0},{4,7},{5,6},{6,5},{7,4},{8,11},{9,10},{10,... | collective-permute-start | bytes 55304 | tf_op jit(solution)/shard_map/ppermute | solution.py:270
  12.9 3.9 %collective-permute-start.1 = (bf16[2,3,6,256]{3,2,1,0:T(8,128)(2,1)S(1)}, bf16[2,3,6,256]{3,2,1,0:T(8,128)(2,1)S(1)}, u32[]{:S(2)}, u32[]{:S(2)}) collective-permute-start(bf16[2,3,6,256]{3,2,1,0:T(8,128)(2,1)S(1)} %get-tuple-element.29), channel_id=1, source_target_pairs={{0,2},{1,3},{2,0},{3,1},{4,6},{5,7},{6,4},{7,5},{8,10},{9,11},{10,... | collective-permute-start | bytes 55304 | tf_op jit(solution)/shard_map/ppermute | solution.py:270
  16.8 3.9 %collective-permute-start.8 = (bf16[4,2,72,128]{3,2,1,0:T(8,128)(2,1)S(1)}, bf16[4,2,72,128]{3,2,1,0:T(8,128)(2,1)S(1)}, u32[]{:S(2)}, u32[]{:S(2)}) collective-permute-start(bf16[4,2,72,128]{3,2,1,0:T(8,128)(2,1)S(1)} %pad_maximum_fusion.refs_8_), channel_id=1, source_target_pairs={{0,4},{4,0},{8,12},{12,8},{16,20},{20,16},{24,28},{28,24},{1,5},{5... | collective-permute-start | bytes 442376 | tf_op jit(solution)/shard_map/ppermute | solution.py:276
  16.9 20.7 %copy-start.1 = (bf16[256,768]{1,0:T(8,128)(2,1)S(1)}, bf16[256,768]{1,0:T(8,128)(2,1)}, u32[]{:S(2)}) copy-start(bf16[256,768]{1,0:T(8,128)(2,1)} %refs_6_.1) | copy-start | bytes 1179652
  16.9 20.7 %copy-start.4 = (bf16[4,24,72]{2,1,0:T(8,128)(2,1)S(1)}, bf16[4,24,72]{2,1,0:T(8,128)(2,1)}, u32[]{:S(2)}) copy-start(bf16[4,24,72]{2,1,0:T(8,128)(2,1)} %constant.49.clone.refs_7_) | copy-start | bytes 41476
  17.0 3.6 %collective-permute-start.4 = (bf16[4,6,256]{2,1,0:T(8,128)(2,1)S(1)}, bf16[4,6,256]{2,1,0:T(8,128)(2,1)S(1)}, u32[]{:S(2)}, u32[]{:S(2)}) collective-permute-start(bf16[4,6,256]{2,1,0:T(8,128)(2,1)S(1)} %get-tuple-element.39), channel_id=1, source_target_pairs={{4,8},{12,16},{20,24},{8,4},{16,12},{24,20},{5,9},{13,17},{21,25},... | collective-permute-start | bytes 36872 | tf_op jit(solution)/shard_map/ppermute | solution.py:280
  17.8 2.9 %collective-permute-start.3 = (bf16[4,6,256]{2,1,0:T(8,128)(2,1)S(1)}, bf16[4,6,256]{2,1,0:T(8,128)(2,1)S(1)}, u32[]{:S(2)}, u32[]{:S(2)}) collective-permute-start(bf16[4,6,256]{2,1,0:T(8,128)(2,1)S(1)} %get-tuple-element.40), channel_id=1, source_target_pairs={{0,4},{4,0},{8,12},{12,8},{16,20},{20,16},{24,28},{28,24},{1,5},{5... | collective-permute-start | bytes 36872 | tf_op jit(solution)/shard_map/ppermute | solution.py:276
  20.7 0.7 %copy-start.5 = (bf16[72,96]{1,0:T(8,128)(2,1)S(1)}, bf16[72,96]{1,0:T(8,128)(2,1)}, u32[]{:S(2)}) copy-start(bf16[72,96]{1,0:T(8,128)(2,1)} %constant.48.clone.refs_14_) | copy-start | bytes 41476
  24.7 3.0 %collective-permute-start.9 = (bf16[4,2,72,128]{3,2,1,0:T(8,128)(2,1)S(1)}, bf16[4,2,72,128]{3,2,1,0:T(8,128)(2,1)S(1)}, u32[]{:S(2)}, u32[]{:S(2)}) collective-permute-start(bf16[4,2,72,128]{3,2,1,0:T(8,128)(2,1)S(1)} %get-tuple-element.18), channel_id=1, source_target_pairs={{0,4},{4,0},{8,12},{12,8},{16,20},{20,16},{24,28},{28,24},{1,5},{5... | collective-permute-start | bytes 442376 | tf_op jit(solution)/shard_map/ppermute | solution.py:276
  27.7 4.5 %collective-permute-start.10 = (bf16[2,72,128]{2,1,0:T(8,128)(2,1)S(1)}, bf16[2,72,128]{2,1,0:T(8,128)(2,1)S(1)}, u32[]{:S(2)}, u32[]{:S(2)}) collective-permute-start(bf16[2,72,128]{2,1,0:T(8,128)(2,1)S(1)} %get-tuple-element.20), channel_id=1, source_target_pairs={{0,8},{4,12},{8,0},{12,4},{16,24},{20,28},{24,16},{28,20},{1,9},{5... | collective-permute-start | bytes 110600 | tf_op jit(solution)/shard_map/ppermute | solution.py:273
  28.5 5.9 %collective-permute-start.11 = (bf16[2,72,128]{2,1,0:T(8,128)(2,1)S(1)}, bf16[2,72,128]{2,1,0:T(8,128)(2,1)S(1)}, u32[]{:S(2)}, u32[]{:S(2)}) collective-permute-start(bf16[2,72,128]{2,1,0:T(8,128)(2,1)S(1)} %get-tuple-element.21), channel_id=1, source_target_pairs={{0,16},{4,20},{8,24},{12,28},{16,0},{20,4},{24,8},{28,12},{1,17},{... | collective-permute-start | bytes 110600 | tf_op jit(solution)/shard_map/ppermute | solution.py:273
  31.9 5.8 %collective-permute-start.12 = (bf16[2,72,128]{2,1,0:T(8,128)(2,1)S(1)}, bf16[2,72,128]{2,1,0:T(8,128)(2,1)S(1)}, u32[]{:S(2)}, u32[]{:S(2)}) collective-permute-start(bf16[2,72,128]{2,1,0:T(8,128)(2,1)S(1)} %get-tuple-element.22), channel_id=1, source_target_pairs={{0,24},{4,28},{8,16},{12,20},{16,8},{20,12},{24,0},{28,4},{1,25},{... | collective-permute-start | bytes 110600 | tf_op jit(solution)/shard_map/ppermute | solution.py:273
  38.7 3.8 %collective-permute-start.13 = (bf16[24,256]{1,0:T(8,128)(2,1)S(1)}, bf16[24,256]{1,0:T(8,128)(2,1)S(1)}, u32[]{:S(2)}, u32[]{:S(2)}) collective-permute-start(bf16[24,256]{1,0:T(8,128)(2,1)S(1)} %get-tuple-element.26), channel_id=1, source_target_pairs={{0,1},{1,0},{2,3},{3,2},{4,5},{5,4},{6,7},{7,6},{8,9},{9,8},{10,11... | collective-permute-start | bytes 36872 | tf_op jit(solution)/shard_map/ppermute | solution.py:270
  40.2 3.7 %collective-permute-start.14 = (bf16[24,256]{1,0:T(8,128)(2,1)S(1)}, bf16[24,256]{1,0:T(8,128)(2,1)S(1)}, u32[]{:S(2)}, u32[]{:S(2)}) collective-permute-start(bf16[24,256]{1,0:T(8,128)(2,1)S(1)} %get-tuple-element.27), channel_id=1, source_target_pairs={{0,2},{1,3},{2,0},{3,1},{4,6},{5,7},{6,4},{7,5},{8,10},{9,11},{10,... | collective-permute-start | bytes 36872 | tf_op jit(solution)/shard_map/ppermute | solution.py:270
  41.5 4.6 %collective-permute-start.15 = (bf16[24,256]{1,0:T(8,128)(2,1)S(1)}, bf16[24,256]{1,0:T(8,128)(2,1)S(1)}, u32[]{:S(2)}, u32[]{:S(2)}) collective-permute-start(bf16[24,256]{1,0:T(8,128)(2,1)S(1)} %get-tuple-element.28), channel_id=1, source_target_pairs={{0,3},{1,2},{2,1},{3,0},{4,7},{5,6},{6,5},{7,4},{8,11},{9,10},{10,... | collective-permute-start | bytes 36872 | tf_op jit(solution)/shard_map/ppermute | solution.py:270

commit v3 on v2

v3 whole, which is shorter than its diff:
```python
import functools

import jax
import jax.numpy as jnp
import numpy as np
from jax import lax
from jax.experimental import pallas as pl
from jax.experimental.pallas import tpu as pltpu
from jax.sharding import PartitionSpec as P

HEADS = 4
VMEM_BYTES = 32 * 1024 * 1024
HELD_BYTES = 3 * 512 * 1024
UNROLLED_CHUNKS = 16
F32 = jnp.float32
BF16 = jnp.bfloat16


def dot(left, right, left_dim=1, right_dim=0):
    return lax.dot_general(
        left, right, (((left_dim,), (right_dim,)), ((), ())), preferred_element_type=F32
    )


def call(kernel, out_shape, scratch=(), far=()):
    def run(*operands):
        specs = [pl.BlockSpec(memory_space=pltpu.VMEM)] * len(operands)
        operands = list(operands)
        for i, operand in enumerate(operands):
            if i in far:
                specs[i] = pl.BlockSpec(memory_space=pltpu.HBM)
                operands[i] = pltpu.with_memory_space_constraint(operand, pltpu.HBM)
            elif operand.size * operand.dtype.itemsize <= HELD_BYTES:
                operands[i] = pltpu.with_memory_space_constraint(operand, pltpu.VMEM)
        return pl.pallas_call(
            kernel,
            out_shape=out_shape,
            in_specs=specs,
            out_specs=jax.tree.map(lambda _: pl.BlockSpec(memory_space=pltpu.VMEM), out_shape),
            scratch_shapes=list(scratch),
            compiler_params=pltpu.CompilerParams(vmem_limit_bytes=VMEM_BYTES),
        )(*operands)

    return run


def held(shape, dtype):
    small = np.prod(shape) * np.dtype(dtype).itemsize <= HELD_BYTES
    return (pltpu.VMEM if small else jax.ShapeDtypeStruct)(shape, dtype)


def pad8(amount):
    return -(-amount // 8) * 8


def shift_selector(rows, cols, tiles):
    width, padded = tiles * cols, pad8(cols)
    select = np.zeros((3, rows, width, tiles, rows, padded), np.float32)
    for shift in (-1, 0, 1):
        for j in range(max(0, shift), min(width, width + shift)):
            tile, inner = divmod(j - shift, cols)
            for i in range(rows):
                select[shift + 1, i, j, tile, i, inner] = 1
    return select.reshape(3, rows * width, tiles * rows * padded)


def tile_selector(rows, cols, tiles):
    width, padded = tiles * cols, pad8(cols)
    select = np.zeros((tiles, rows, padded, rows, width), np.float32)
    for tile in range(tiles):
        for i in range(rows):
            for inner in range(cols):
                select[tile, i, inner, i, tile * cols + inner] = 1
    return select.reshape(tiles, rows * padded, rows * width)


def start_copies(pairs, sems):
    copies = [
        pltpu.make_async_copy(src, dst, sems.at[i]) for i, (src, dst) in enumerate(pairs)
    ]
    for copy in copies:
        copy.start()
    return copies


def pack_kernel(out_grad, pre_silu, queries, keys, values, tile, kv, query, q_ref, k_ref, v_ref, sems):
    copies = start_copies(
        [
            (values, v_ref),
            (keys, k_ref),
            (queries, q_ref),
            (out_grad, tile.at[0]),
            (pre_silu, tile.at[1]),
        ],
        sems,
    )

    def beside(left, right):
        return jnp.concatenate([left.astype(F32), right.astype(F32)], 0).T.astype(BF16)

    copies[0].wait()
    copies[1].wait()
    kv[0] = beside(v_ref[0], k_ref[0])
    kv[1] = beside(k_ref[1], v_ref[1])
    copies[2].wait()
    query[...] = beside(q_ref[1], q_ref[0]) * jnp.asarray(q_ref.shape[1] ** -0.5, BF16)
    copies[3].wait()
    copies[4].wait()


def middle_kernel(n_col, *refs):
    tiles, parts = refs[:n_col], refs[n_col:-4]
    query, to_core, to_chip, joined = refs[-4:]
    rows = tiles[0].shape[1]
    inner = jnp.where(lax.axis_index("row") % 2 == 1, rows - 1, 0)
    for k, tile in enumerate(tiles):
        to_core[k] = tile[0, inner]
        to_chip[k] = tile[0, rows - 1 - inner]
    heads = parts[0].shape[0]
    for j, part in enumerate(parts):
        for head in range(heads):
            joined[heads * j + head] = part[head]
    joined[heads * len(parts)] = query[...]


def strip_kernel(n_col, per_sample, *refs):
    tiles, rest = refs[:n_col], refs[n_col:]
    (
        halo_core,
        halo_chip,
        kv_sent,
        kv_kept,
        *far,
        dkv_sent,
        dkv_kept,
        dq_ref,
        gz_ref,
        grads,
        silus,
        conv_weight,
        out_weight,
        shifts,
        middle,
        sems,
    ) = rest
    copies = start_copies(list(zip(far, (shifts, middle, conv_weight, out_weight))), sems)
    col, core = lax.axis_index("col"), lax.axis_index("row") % 2
    sample = col // per_sample
    _, rows, cols, samples, channels = tiles[0].shape
    width = n_col * cols
    strip = rows * width
    chosen = lax.broadcasted_iota(jnp.int32, (cols, samples, channels), 1) == sample

    def pick(cells):
        return jnp.sum(jnp.where(chosen, cells.astype(F32), 0.0), axis=1)

    grads[...] = jnp.zeros_like(grads)
    silus[...] = jnp.zeros_like(silus)
    lower = jnp.where(core == 1, rows + 1, 0)
    upper = jnp.where(core == 1, 0, rows + 1)
    for k in range(n_col):
        tile = col ^ k
        for i in range(rows):
            grads[tile, i + 1, :cols] = pick(tiles[k][0, i])
            silus[tile, i, :cols] = pick(tiles[k][1, i])
        grads[tile, lower, :cols] = pick(halo_core[k])
        grads[tile, upper, :cols] = pick(halo_chip[k])
    lanes = kv_sent.shape[2]
    half = lanes // 2
    factor = half**-0.5
    low = lax.broadcasted_iota(jnp.int32, (strip, lanes), 1) < half
    query = kv_kept[kv_kept.shape[0] - 1]
    none = jnp.zeros_like(query)
    asked = (jnp.where(low, none, query), jnp.where(low, query, none))
    blocks = dkv_kept.shape[0]
    sources = ((kv_sent, dkv_sent), (kv_kept, dkv_kept))
    small = 2 * blocks <= UNROLLED_CHUNKS
    chunks = [(src, dst, j) for src, dst in sources for j in range(blocks)]

    def softmax(head):
        scores = [dot(src[2 * j + head], asked[head], 1, 1) for src, _, j in chunks]
        top = jnp.max(functools.reduce(jnp.maximum, scores), axis=0, keepdims=True)
        exps = [jnp.exp(s - top) for s in scores]
        scale = 1.0 / jnp.sum(sum(exps), axis=0, keepdims=True)
        return [e * scale for e in exps]

    if small:
        probs = [softmax(head) for head in (0, 1)]

    for copy in copies:
        copy.wait()
    flat = grads[...].reshape(-1, channels).astype(BF16)
    conv = jnp.zeros((strip, channels), F32)
    for b in (-1, 0, 1):
        shifted = dot(shifts[b + 1], flat)
        for a in (-1, 0, 1):
            window = shifted[(1 - a) * width : (1 - a) * width + strip].astype(BF16)
            conv = conv + dot(window, conv_weight[a + 1, b + 1], 1, 1)
    z = dot(middle[...], silus[...].reshape(-1, channels).astype(BF16))
    sigma = 1.0 / (1.0 + jnp.exp(-z))
    grad_z = (conv * sigma * (1.0 + z * (1.0 - sigma))).astype(BF16)
    gz_ref[...] = grad_z

    first = col % per_sample * lanes
    grad_out = dot(grad_z, out_weight[pl.ds(pl.multiple_of(first, lanes), lanes), :], 1, 1)
    grad_out = grad_out.astype(BF16)
    cotangent = (jnp.where(low, grad_out, none), jnp.where(low, none, grad_out))

    grad_query = []
    for head in (0, 1):
        ask, cot = asked[head], cotangent[head]

        def finish(kv, chunk_probs, probs_grad, row_dot):
            grad_scores = (chunk_probs * (probs_grad - row_dot)).astype(BF16)
            dkv = dot(grad_scores, ask) + dot(chunk_probs.astype(BF16), cot)
            return dkv.astype(BF16), dot(grad_scores, kv, 0, 0)

        total = jnp.zeros((strip, lanes), F32)
        if small:
            probs_grads = [dot(src[2 * j + head], cot, 1, 1) for src, _, j in chunks]
            weighted = sum(p * g for p, g in zip(probs[head], probs_grads))
            row_dot = jnp.sum(weighted, axis=0, keepdims=True)
            for (src, dst, j), p, g in zip(chunks, probs[head], probs_grads):
                dst[j, head], dq = finish(src[2 * j + head], p, g, row_dot)
                total = total + dq
        else:
            stats = (
                jnp.full((1, strip), -jnp.inf, F32),
                jnp.zeros((1, strip), F32),
                jnp.zeros((1, strip), F32),
            )
            for src, _ in sources:

                def gather(j, carry, src=src):
                    top, norm, weighted = carry
                    kv = src[2 * j + head]
                    scores = dot(kv, ask, 1, 1)
                    new = jnp.maximum(top, jnp.max(scores, axis=0, keepdims=True))
                    exps = jnp.exp(scores - new)
                    rescale = jnp.exp(top - new)
                    weights = jnp.sum(exps * dot(kv, cot, 1, 1), axis=0, keepdims=True)
                    return (
                        new,
                        norm * rescale + jnp.sum(exps, axis=0, keepdims=True),
                        weighted * rescale + weights,
                    )

                stats = lax.fori_loop(0, blocks, gather, stats)
            top, norm, weighted = stats
            scale = 1.0 / norm
            row_dot = weighted * scale
            for src, dst in sources:

                def spread(j, total, src=src, dst=dst):
                    kv = src[2 * j + head]
                    chunk_probs = jnp.exp(dot(kv, ask, 1, 1) - top) * scale
                    dst[j, head], dq = finish(kv, chunk_probs, dot(kv, cot, 1, 1), row_dot)
                    return total + dq

                total = lax.fori_loop(0, blocks, spread, total)
        grad_query.append(total)
    dq_ref[...] = jnp.where(low, grad_query[1], grad_query[0]) * factor


def core_sum_kernel(own, received, *outs):
    for j, out in enumerate(outs):
        out[...] = (own[j].astype(F32) + received[j].astype(F32)).astype(BF16)


def project_kernel(n_col, per_sample, *refs):
    n_in = len(refs) - n_col
    *parts, dq_ref, gz_ref, input_weight, tiles = refs[:n_in]
    outs = refs[n_in:]
    col = lax.axis_index("col")
    part = col % per_sample
    total = sum(ref[...].astype(F32) for ref in parts)
    strip, lanes = dq_ref.shape
    half = lanes // 2
    channels = gz_ref.shape[1]
    low = lax.broadcasted_iota(jnp.int32, (strip, lanes), 1) < half
    dv = jnp.where(low, total[0], total[1])
    dk = pltpu.roll(jnp.where(low, total[1], total[0]), half, 1)
    dq = pltpu.roll(dq_ref[...], half, 1)
    grad = jnp.where(part == 0, gz_ref[...].astype(F32), 0.0)
    for kind, value in enumerate((dq, dk, dv)):
        first = pl.multiple_of(kind * channels + part * lanes, lanes)
        weight = input_weight[:, pl.ds(first, lanes)]
        grad = grad + dot(value.astype(BF16), weight, 1, 1)
    grad = grad.astype(BF16)
    for k, out in enumerate(outs):
        out[...] = dot(tiles[col ^ k], grad).astype(BF16)


def output_kernel(per_sample, *refs):
    *parts, out = refs
    rows, cols, samples, channels = out.shape
    padded = pad8(cols)
    sample = lax.axis_index("col") // per_sample
    place = lax.broadcasted_iota(jnp.int32, (cols, samples, channels), 1)
    for i in range(rows):
        cells = jnp.zeros((cols, samples, channels), F32)
        for group in range(samples):
            total = sum(
                ref[...][i * padded : i * padded + cols].astype(F32)
                for ref in parts[group * per_sample : (group + 1) * per_sample]
            )
            cells = jnp.where(place == (sample ^ group), total[:, None, :], cells)
        out[i] = cells.astype(BF16)


def shards(
    pre_silu, out_grad, query_heads, key_heads, value_heads, conv_weight, out_weight, input_weight
):
    samples, rows, cols, channels = pre_silu.shape
    pairs, strip, head_dim = query_heads.shape
    n_row, n_col = lax.axis_size("row"), lax.axis_size("col")
    chips = n_row // 2
    per_sample = HEADS // pairs
    lanes = pairs * head_dim

    def to_col(array, k):
        pairs_of = [
            (r * n_col + c, (r ^ 1) * n_col + (c ^ k)) for r in range(n_row) for c in range(n_col)
        ]
        return lax.ppermute(array, ("row", "col"), pairs_of)

    def to_chip(array, k):
        return lax.ppermute(array, "row", [(i, i ^ (2 * k + 1)) for i in range(n_row)])

    def to_core(array):
        return lax.ppermute(array, "row", [(i, i ^ 1) for i in range(n_row)])

    def to_next_chip(array):
        edge = [(i, i + 3) for i in range(0, n_row - 2, 2)]
        return lax.ppermute(array, "row", edge + [(j, i) for i, j in edge])

    def cells(array):
        return jnp.transpose(array, (1, 2, 0, 3))

    def turned(array):
        return jnp.transpose(array, (0, 2, 1))

    saved = pltpu.VMEM((pairs, head_dim, strip), BF16)
    tile, kv, query = call(
        pack_kernel,
        (
            held((2, rows, cols, samples, channels), BF16),
            held((pairs, strip, lanes), BF16),
            held((strip, lanes), BF16),
        ),
        (saved, saved, saved, pltpu.SemaphoreType.DMA((5,))),
        range(5),
    )(cells(out_grad), cells(pre_silu), turned(query_heads), turned(key_heads), turned(value_heads))
    kv_parts = [kv] + [to_chip(kv, k) for k in range(1, chips)]
    tiles = [to_col(tile, k) for k in range(n_col)]

    rim = held((n_col, cols, samples, channels), BF16)
    rim_core, rim_chip, kv_sent = call(
        functools.partial(middle_kernel, n_col),
        (rim, rim, held((pairs * chips + 1, strip, lanes), BF16)),
    )(*tiles, *kv_parts, query)
    halo_core, halo_chip, kv_kept = to_core(rim_core), to_next_chip(rim_chip), to_core(kv_sent)

    padded = pad8(cols)
    shifts = jnp.asarray(shift_selector(rows + 2, cols, n_col), BF16)
    middle = jnp.asarray(shift_selector(rows, cols, n_col)[1], BF16)
    far = (shifts, middle, conv_weight, out_weight)
    block = held((chips, pairs, strip, lanes), BF16)
    dkv_sent, dkv_kept, dq, grad_z = call(
        functools.partial(strip_kernel, n_col, per_sample),
        (block, block, held((strip, lanes), F32), held((strip, channels), BF16)),
        (
            pltpu.VMEM((n_col, rows + 2, padded, channels), F32),
            pltpu.VMEM((n_col, rows, padded, channels), F32),
            pltpu.VMEM(conv_weight.shape, BF16),
            pltpu.VMEM(out_weight.shape, BF16),
            pltpu.VMEM(shifts.shape, BF16),
            pltpu.VMEM(middle.shape, BF16),
            pltpu.SemaphoreType.DMA((4,)),
        ),
        range(n_col + 4, n_col + 8),
    )(*tiles, halo_core, halo_chip, kv_sent, kv_kept, *far)

    sums = call(core_sum_kernel, [held((pairs, strip, lanes), BF16) for _ in range(chips)])(
        dkv_kept, to_core(dkv_sent)
    )
    parts = [sums[0]] + [to_chip(sums[k], k) for k in range(1, chips)]

    cut = call(
        functools.partial(project_kernel, n_col, per_sample),
        [held((rows * padded, channels), BF16)] * n_col,
    )(*parts, dq, grad_z, input_weight, jnp.asarray(tile_selector(rows, cols, n_col), BF16))
    grad_input = call(
        functools.partial(output_kernel, per_sample), held((rows, cols, samples, channels), BF16)
    )(*[to_col(cut[k], k) for k in range(n_col)])
    return jnp.transpose(grad_input, (2, 0, 1, 3))


def solution(mesh):
    tile = P(None, "row", "col", None)
    heads = P("col", "row", None)
    return jax.shard_map(
        shards,
        mesh=mesh,
        in_specs=(tile, tile, heads, heads, heads, P(), P(), P()),
        out_specs=tile,
        check_vma=False,
    )
```

time: 48.1 us -> 41.8 us (0.87); the launches traced: 47.4 us -> 41.6 us
  local copies, waits for them, and re-layouts: 5.03 us -> 0.62 us
  starting transfers between devices: 23.3 us -> 20.7 us
  waiting for transfers between devices: 13 us -> 14.4 us
  other arithmetic: 0.89 us -> 0 us
  Pallas kernels: 4.98 us -> 5.72 us
    ppermute x3, starting transfers between devices: 4.17 us -> 0.7 us  [to_core(): return lax.ppermute(array, 'row', [(i, i ^ 1) for i in range(n_row)])]
    ppermute x1, waiting for transfers between devices: 0.01 us -> 2.4 us  [to_next_chip(): return lax.ppermute(array, 'row', edge + [(j, i) for i, j in edge])]
    slice x7 -> x0, local copies, waits for them, and re-layouts: 2.34 us -> none  [the longest x1 0.85 us: shards(): key_heads[0]]
    ppermute x1, starting transfers between devices: 0.79 us -> 2.72 us  [to_next_chip(): return lax.ppermute(array, 'row', edge + [(j, i) for i, j in edge])]
    ppermute x12 -> x14, waiting for transfers between devices: 11.9 us -> 10.6 us  [the longest x6 6.85 us: to_chip(): lax.ppermute(array, 'row', [(i, i ^ 2 * k + 1) for i in range(n_row)])]
    ppermute x12 -> x14, starting transfers between devices: 18.3 us -> 17.3 us  [the longest x6 9.61 us: to_chip(): lax.ppermute(array, 'row', [(i, i ^ 2 * k + 1) for i in range(n_row)])]
    another operation x4 -> x0, other arithmetic: 0.77 us -> none  [the longest x1 0.65 us: shards(): place = jnp.stack([col, core]).astype(jnp.int32)]
    another operation x1 -> x0, local copies, waits for them, and re-layouts: 0.75 us -> none  [shards(): both = jnp.stack([out_grad, pre_silu])]
  transfers between devices with their start and end apart: 16 -> 18, of which waited for: 9 -> 8; matrix products, arithmetic and copies ran while one was open for 5% -> 0% of each run, Pallas kernels for 0% -> 0%
where the time goes in v3:
time: 41.8 us; the launch traced here: 41.6 us
  starting transfers between devices  20.7 us (50%)
  waiting for transfers between devices  14.4 us (34%)
  Pallas kernels  5.72 us (14%)
  local copies, waits for them, and re-layouts  0.62 us (1%)
    ppermute x6, starting transfers between devices, to_chip(): lax.ppermute(array, 'row', [(i, i ^ 2 * k + 1) for i in range(n_row)])  9.61 us
    ppermute x8, starting transfers between devices, to_col(): return lax.ppermute(array, ('row', 'col'), pairs_of)  7.71 us
    ppermute x6, waiting for transfers between devices, to_chip(): lax.ppermute(array, 'row', [(i, i ^ 2 * k + 1) for i in range(n_row)])  6.85 us
    pallas_call x6, Pallas kernels, run(): pl.pallas_call(kernel, out_shape=out_shape, in_specs=specs, out_specs=jax...  5.72 us
    ppermute x8, waiting for transfers between devices, to_col(): return lax.ppermute(array, ('row', 'col'), pairs_of)  3.8 us
    ppermute x1, starting transfers between devices, to_next_chip(): return lax.ppermute(array, 'row', edge + [(j, i) for i, j in edge])  2.72 us
    ppermute x1, waiting for transfers between devices, to_next_chip(): return lax.ppermute(array, 'row', edge + [(j, i) for i, j in edge])  2.4 us
    ppermute x3, waiting for transfers between devices, to_core(): return lax.ppermute(array, 'row', [(i, i ^ 1) for i in range(n_row)])  1.36 us
  transfers between devices with their start and end apart: 18, of which 8 were waited for; matrix products, arithmetic and copies ran while one was open for 0% of the time, Pallas kernels for 0%

profile of v3, /device:TPU:0, one launch (start us, length us, event | category | flops | bytes accessed | tf_op | source)
XLA Modules:
  0.0 41.6 jit_solution(6531361162479251205)
XLA Ops:
  0.0 1.0 %shard_map.109 = (bf16[2,3,6,2,256]{4,3,2,1,0:T(2,128)(2,1)S(1)}, bf16[2,72,128]{2,1,0:T(8,128)(2,1)S(1)}, bf16[72,128]{1,0:T(8,128)(2,1)S(1)}) custom-call(bf16[3,6,2,256]{3,2,1,0:T(2,128)(2,1)} %bitcast.10, bf16[3,6,2,256]{3,2,1,0:T(2,128)(2,1)} %bitcast.11, bf16[2,64,72]{2,1,0:T(8,128)(2,1)} %bitcast.7, bf16[2,64,72]{2,1,0:T(8,128)(2,1)} %bitcast.8, ...), custom_call_target="tpu_custom_call" | custom-call | tf_op jit(solution)/shard_map/pallas_call | solution.py:35
  1.0 3.4 %collective-permute-start.3 = (bf16[2,3,6,2,256]{4,3,2,1,0:T(2,128)(2,1)S(1)}, bf16[2,3,6,2,256]{4,3,2,1,0:T(2,128)(2,1)S(1)}, u32[]{:S(2)}, u32[]{:S(2)}) collective-permute-start(bf16[2,3,6,2,256]{4,3,2,1,0:T(2,128)(2,1)S(1)} %get-tuple-element.23), channel_id=1, source_target_pairs={{0,7},{1,6},{2,5},{3,4},{4,3},{5,2},{6,1},{7,0},{8,15},{9,14},{10,... | collective-permute-start | bytes 110600 | tf_op jit(solution)/shard_map/ppermute | solution.py:325
  4.4 0.8 %collective-permute-start.2 = (bf16[2,3,6,2,256]{4,3,2,1,0:T(2,128)(2,1)S(1)}, bf16[2,3,6,2,256]{4,3,2,1,0:T(2,128)(2,1)S(1)}, u32[]{:S(2)}, u32[]{:S(2)}) collective-permute-start(bf16[2,3,6,2,256]{4,3,2,1,0:T(2,128)(2,1)S(1)} %get-tuple-element.23), channel_id=1, source_target_pairs={{0,6},{1,7},{2,4},{3,5},{4,2},{5,3},{6,0},{7,1},{8,14},{9,15},{10,... | collective-permute-start | bytes 110600 | tf_op jit(solution)/shard_map/ppermute | solution.py:325
  5.2 0.1 collective-permute-start.1
  5.3 0.0 collective-permute-start
  5.3 3.7 %collective-permute-start.6 = (bf16[2,72,128]{2,1,0:T(8,128)(2,1)S(1)}, bf16[2,72,128]{2,1,0:T(8,128)(2,1)S(1)}, u32[]{:S(2)}, u32[]{:S(2)}) collective-permute-start(bf16[2,72,128]{2,1,0:T(8,128)(2,1)S(1)} %get-tuple-element.24.refs_4_), channel_id=1, source_target_pairs={{0,28},{4,24},{8,20},{12,16},{16,12},{20,8},{24,4},{28,0},{1,29},{... | collective-permute-start | bytes 110600 | tf_op jit(solution)/shard_map/ppermute | solution.py:328
  9.1 0.0 collective-permute-done.3.refs_3_
  9.1 0.3 collective-permute-start.5
  9.4 0.0 collective-permute-done.2.refs_2_
  9.4 1.6 %collective-permute-start.4 = (bf16[2,72,128]{2,1,0:T(8,128)(2,1)S(1)}, bf16[2,72,128]{2,1,0:T(8,128)(2,1)S(1)}, u32[]{:S(2)}, u32[]{:S(2)}) collective-permute-start(bf16[2,72,128]{2,1,0:T(8,128)(2,1)S(1)} %get-tuple-element.24.refs_4_), channel_id=1, source_target_pairs={{0,12},{4,8},{8,4},{12,0},{16,28},{20,24},{24,20},{28,16},{1,13},{... | collective-permute-start | bytes 110600 | tf_op jit(solution)/shard_map/ppermute | solution.py:328
  11.0 0.0 collective-permute-done.1.refs_1_
  11.0 0.0 collective-permute-done.refs_0_
  11.0 0.0 collective-permute-done.6.refs_7_
  11.0 2.5 %collective-permute-done.5.refs_6_ = bf16[2,72,128]{2,1,0:T(8,128)(2,1)S(1)} collective-permute-done((bf16[2,72,128]{2,1,0:T(8,128)(2,1)S(1)}, bf16[2,72,128]{2,1,0:T(8,128)(2,1)S(1)}, u32[]{:S(2)}, u32[]{:S(2)}) %collective-permute-start.5) | collective-permute-done | bytes 36896 | tf_op jit(solution)/shard_map/ppermute | solution.py:328
  13.5 0.0 collective-permute-done.4.refs_5_
  13.6 0.0 copy-start
  13.6 0.0 copy-start.1
  13.6 0.6 %collective-permute-start.9 = (bf16[9,72,128]{2,1,0:T(8,128)(2,1)S(1)}, bf16[9,72,128]{2,1,0:T(8,128)(2,1)S(1)}, u32[]{:S(2)}, u32[]{:S(2)}) collective-permute-start(bf16[9,72,128]{2,1,0:T(8,128)(2,1)S(1)} %get-tuple-element.28.refs_6_), channel_id=1, source_target_pairs={{0,4},{4,0},{8,12},{12,8},{16,20},{20,16},{24,28},{28,24},{1,5},{5... | collective-permute-start | bytes 497672 | tf_op jit(solution)/shard_map/ppermute | solution.py:331
  14.1 0.1 collective-permute-start.7
  14.2 2.7 %collective-permute-start.8 = (bf16[4,6,2,256]{3,2,1,0:T(2,128)(2,1)S(1)}, bf16[4,6,2,256]{3,2,1,0:T(2,128)(2,1)S(1)}, u32[]{:S(2)}, u32[]{:S(2)}) collective-permute-start(bf16[4,6,2,256]{3,2,1,0:T(2,128)(2,1)S(1)} %get-tuple-element.27), channel_id=1, source_target_pairs={{0,12},{8,20},{16,28},{12,0},{20,8},{28,16},{1,13},{9,21},{17,29},... | collective-permute-start | bytes 73736 | tf_op jit(solution)/shard_map/ppermute | solution.py:335
  16.9 0.0 collective-permute-done.7.refs_4_
  16.9 2.4 %collective-permute-done.8.refs_5_ = bf16[4,6,2,256]{3,2,1,0:T(2,128)(2,1)S(1)} collective-permute-done((bf16[4,6,2,256]{3,2,1,0:T(2,128)(2,1)S(1)}, bf16[4,6,2,256]{3,2,1,0:T(2,128)(2,1)S(1)}, u32[]{:S(2)}, u32[]{:S(2)}) %collective-permute-start.8) | collective-permute-done | bytes 24608 | tf_op jit(solution)/shard_map/ppermute | solution.py:335
  19.3 0.0 collective-permute-done.9.refs_7_
  19.3 4.2 %shard_map.111 = (bf16[4,2,72,128]{3,2,1,0:T(8,128)(2,1)S(1)}, bf16[4,2,72,128]{3,2,1,0:T(8,128)(2,1)S(1)}, f32[72,128]{1,0:T(8,128)S(1)}, bf16[72,256]{1,0:T(8,128)(2,1)S(1)}) custom-call(bf16[2,3,6,2,256]{4,3,2,1,0:T(2,128)(2,1)S(1)} %collective-permute-done.refs_0_, bf16[2,3,6,2,256]{4,3,2,1,0:T(2,128)(2,1)S(1)} %collective-permute-done.1.refs_1_, ...), custom_call_target="tpu_custom_call" | custom-call | tf_op jit(solution)/shard_map/pallas_call | solution.py:35
  23.6 0.1 collective-permute-start.10
  23.7 1.4 %collective-permute-done.10.received = bf16[4,2,72,128]{3,2,1,0:T(8,128)(2,1)S(1)} collective-permute-done((bf16[4,2,72,128]{3,2,1,0:T(8,128)(2,1)S(1)}, bf16[4,2,72,128]{3,2,1,0:T(8,128)(2,1)S(1)}, u32[]{:S(2)}, u32[]{:S(2)}) %collective-permute-start.10) | collective-permute-done | bytes 147488 | tf_op jit(solution)/shard_map/ppermute | solution.py:331
  25.1 0.9 %collective-permute-start.11 = (bf16[2,72,128]{2,1,0:T(8,128)(2,1)S(1)}, bf16[2,72,128]{2,1,0:T(8,128)(2,1)S(1)}, u32[]{:S(2)}, u32[]{:S(2)}) collective-permute-start(bf16[2,72,128]{2,1,0:T(8,128)(2,1)S(1)} %get-tuple-element.32), channel_id=1, source_target_pairs={{0,12},{4,8},{8,4},{12,0},{16,28},{20,24},{24,20},{28,16},{1,13},{... | collective-permute-start | bytes 110600 | tf_op jit(solution)/shard_map/ppermute | solution.py:328
  25.9 2.2 %collective-permute-start.12 = (bf16[2,72,128]{2,1,0:T(8,128)(2,1)S(1)}, bf16[2,72,128]{2,1,0:T(8,128)(2,1)S(1)}, u32[]{:S(2)}, u32[]{:S(2)}) collective-permute-start(bf16[2,72,128]{2,1,0:T(8,128)(2,1)S(1)} %get-tuple-element.33), channel_id=1, source_target_pairs={{0,20},{4,16},{8,28},{12,24},{16,4},{20,0},{24,12},{28,8},{1,21},{... | collective-permute-start | bytes 110600 | tf_op jit(solution)/shard_map/ppermute | solution.py:328
  28.2 0.8 %collective-permute-start.13 = (bf16[2,72,128]{2,1,0:T(8,128)(2,1)S(1)}, bf16[2,72,128]{2,1,0:T(8,128)(2,1)S(1)}, u32[]{:S(2)}, u32[]{:S(2)}) collective-permute-start(bf16[2,72,128]{2,1,0:T(8,128)(2,1)S(1)} %get-tuple-element.34), channel_id=1, source_target_pairs={{0,28},{4,24},{8,20},{12,16},{16,12},{20,8},{24,4},{28,0},{1,29},{... | collective-permute-start | bytes 110600 | tf_op jit(solution)/shard_map/ppermute | solution.py:328
  29.0 0.0 collective-permute-done.11.refs_1_
  29.0 1.3 %collective-permute-done.12.refs_2_ = bf16[2,72,128]{2,1,0:T(8,128)(2,1)S(1)} collective-permute-done((bf16[2,72,128]{2,1,0:T(8,128)(2,1)S(1)}, bf16[2,72,128]{2,1,0:T(8,128)(2,1)S(1)}, u32[]{:S(2)}, u32[]{:S(2)}) %collective-permute-start.12) | collective-permute-done | bytes 36896 | tf_op jit(solution)/shard_map/ppermute | solution.py:328
  30.3 3.0 %collective-permute-done.13.refs_3_ = bf16[2,72,128]{2,1,0:T(8,128)(2,1)S(1)} collective-permute-done((bf16[2,72,128]{2,1,0:T(8,128)(2,1)S(1)}, bf16[2,72,128]{2,1,0:T(8,128)(2,1)S(1)}, u32[]{:S(2)}, u32[]{:S(2)}) %collective-permute-start.13) | collective-permute-done | bytes 36896 | tf_op jit(solution)/shard_map/ppermute | solution.py:328
  33.3 0.0 copy-done
  33.4 0.0 copy-done.1
  33.4 0.4 shard_map.113
  33.8 0.4 collective-permute-start.14
  34.2 1.3 %collective-permute-start.15 = (bf16[24,256]{1,0:T(8,128)(2,1)S(1)}, bf16[24,256]{1,0:T(8,128)(2,1)S(1)}, u32[]{:S(2)}, u32[]{:S(2)}) collective-permute-start(bf16[24,256]{1,0:T(8,128)(2,1)S(1)} %get-tuple-element.38), channel_id=1, source_target_pairs={{0,5},{1,4},{2,7},{3,6},{4,1},{5,0},{6,3},{7,2},{8,13},{9,12},{10,... | collective-permute-start | bytes 36872 | tf_op jit(solution)/shard_map/ppermute | solution.py:325
  35.4 1.5 %collective-permute-start.16 = (bf16[24,256]{1,0:T(8,128)(2,1)S(1)}, bf16[24,256]{1,0:T(8,128)(2,1)S(1)}, u32[]{:S(2)}, u32[]{:S(2)}) collective-permute-start(bf16[24,256]{1,0:T(8,128)(2,1)S(1)} %get-tuple-element.39), channel_id=1, source_target_pairs={{0,6},{1,7},{2,4},{3,5},{4,2},{5,3},{6,0},{7,1},{8,14},{9,15},{10,... | collective-permute-start | bytes 36872 | tf_op jit(solution)/shard_map/ppermute | solution.py:325
  36.9 0.2 collective-permute-start.17
  37.1 0.0 collective-permute-done.14.refs_0_
  37.1 0.1 collective-permute-done.15.refs_1_
  37.3 1.3 %collective-permute-done.16.refs_2_ = bf16[24,256]{1,0:T(8,128)(2,1)S(1)} collective-permute-done((bf16[24,256]{1,0:T(8,128)(2,1)S(1)}, bf16[24,256]{1,0:T(8,128)(2,1)S(1)}, u32[]{:S(2)}, u32[]{:S(2)}) %collective-permute-start.16) | collective-permute-done | bytes 12320 | tf_op jit(solution)/shard_map/ppermute | solution.py:325
  38.6 2.4 %collective-permute-done.17.refs_3_ = bf16[24,256]{1,0:T(8,128)(2,1)S(1)} collective-permute-done((bf16[24,256]{1,0:T(8,128)(2,1)S(1)}, bf16[24,256]{1,0:T(8,128)(2,1)S(1)}, u32[]{:S(2)}, u32[]{:S(2)}) %collective-permute-start.17) | collective-permute-done | bytes 12320 | tf_op jit(solution)/shard_map/ppermute | solution.py:325
  41.0 0.6 %copy.12 = bf16[2,3,6,256]{3,0,2,1:T(2,128)(2,1)} copy(bf16[2,3,6,256]{3,0,2,1:T(2,128)(2,1)S(1)} %bitcast.6) | data formatting | bytes 36864
  (3 shorter events, 0.1 us)
Async XLA Ops:
  1.0 8.1 %collective-permute-start.3 = (bf16[2,3,6,2,256]{4,3,2,1,0:T(2,128)(2,1)S(1)}, bf16[2,3,6,2,256]{4,3,2,1,0:T(2,128)(2,1)S(1)}, u32[]{:S(2)}, u32[]{:S(2)}) collective-permute-start(bf16[2,3,6,2,256]{4,3,2,1,0:T(2,128)(2,1)S(1)} %get-tuple-element.23), channel_id=1, source_target_pairs={{0,7},{1,6},{2,5},{3,4},{4,3},{5,2},{6,1},{7,0},{8,15},{9,14},{10,... | collective-permute-start | bytes 110600 | tf_op jit(solution)/shard_map/ppermute | solution.py:325
  4.4 5.0 %collective-permute-start.2 = (bf16[2,3,6,2,256]{4,3,2,1,0:T(2,128)(2,1)S(1)}, bf16[2,3,6,2,256]{4,3,2,1,0:T(2,128)(2,1)S(1)}, u32[]{:S(2)}, u32[]{:S(2)}) collective-permute-start(bf16[2,3,6,2,256]{4,3,2,1,0:T(2,128)(2,1)S(1)} %get-tuple-element.23), channel_id=1, source_target_pairs={{0,6},{1,7},{2,4},{3,5},{4,2},{5,3},{6,0},{7,1},{8,14},{9,15},{10,... | collective-permute-start | bytes 110600 | tf_op jit(solution)/shard_map/ppermute | solution.py:325
  5.2 5.8 %collective-permute-start.1 = (bf16[2,3,6,2,256]{4,3,2,1,0:T(2,128)(2,1)S(1)}, bf16[2,3,6,2,256]{4,3,2,1,0:T(2,128)(2,1)S(1)}, u32[]{:S(2)}, u32[]{:S(2)}) collective-permute-start(bf16[2,3,6,2,256]{4,3,2,1,0:T(2,128)(2,1)S(1)} %get-tuple-element.23), channel_id=1, source_target_pairs={{0,5},{1,4},{2,7},{3,6},{4,1},{5,0},{6,3},{7,2},{8,13},{9,12},{10,... | collective-permute-start | bytes 110600 | tf_op jit(solution)/shard_map/ppermute | solution.py:325
  5.3 5.7 %collective-permute-start = (bf16[2,3,6,2,256]{4,3,2,1,0:T(2,128)(2,1)S(1)}, bf16[2,3,6,2,256]{4,3,2,1,0:T(2,128)(2,1)S(1)}, u32[]{:S(2)}, u32[]{:S(2)}) collective-permute-start(bf16[2,3,6,2,256]{4,3,2,1,0:T(2,128)(2,1)S(1)} %get-tuple-element.23), channel_id=1, source_target_pairs={{0,4},{1,5},{2,6},{3,7},{4,0},{5,1},{6,2},{7,3},{8,12},{9,13},{10,... | collective-permute-start | bytes 110600 | tf_op jit(solution)/shard_map/ppermute | solution.py:325
  5.3 5.7 %collective-permute-start.6 = (bf16[2,72,128]{2,1,0:T(8,128)(2,1)S(1)}, bf16[2,72,128]{2,1,0:T(8,128)(2,1)S(1)}, u32[]{:S(2)}, u32[]{:S(2)}) collective-permute-start(bf16[2,72,128]{2,1,0:T(8,128)(2,1)S(1)} %get-tuple-element.24.refs_4_), channel_id=1, source_target_pairs={{0,28},{4,24},{8,20},{12,16},{16,12},{20,8},{24,4},{28,0},{1,29},{... | collective-permute-start | bytes 110600 | tf_op jit(solution)/shard_map/ppermute | solution.py:328
  9.1 4.5 %collective-permute-start.5 = (bf16[2,72,128]{2,1,0:T(8,128)(2,1)S(1)}, bf16[2,72,128]{2,1,0:T(8,128)(2,1)S(1)}, u32[]{:S(2)}, u32[]{:S(2)}) collective-permute-start(bf16[2,72,128]{2,1,0:T(8,128)(2,1)S(1)} %get-tuple-element.24.refs_4_), channel_id=1, source_target_pairs={{0,20},{4,16},{8,28},{12,24},{16,4},{20,0},{24,12},{28,8},{1,21},{... | collective-permute-start | bytes 110600 | tf_op jit(solution)/shard_map/ppermute | solution.py:328
  9.4 4.1 %collective-permute-start.4 = (bf16[2,72,128]{2,1,0:T(8,128)(2,1)S(1)}, bf16[2,72,128]{2,1,0:T(8,128)(2,1)S(1)}, u32[]{:S(2)}, u32[]{:S(2)}) collective-permute-start(bf16[2,72,128]{2,1,0:T(8,128)(2,1)S(1)} %get-tuple-element.24.refs_4_), channel_id=1, source_target_pairs={{0,12},{4,8},{8,4},{12,0},{16,28},{20,24},{24,20},{28,16},{1,13},{... | collective-permute-start | bytes 110600 | tf_op jit(solution)/shard_map/ppermute | solution.py:328
  13.6 19.8 %copy-start = (bf16[256,768]{1,0:T(8,128)(2,1)S(1)}, bf16[256,768]{1,0:T(8,128)(2,1)}, u32[]{:S(2)}) copy-start(bf16[256,768]{1,0:T(8,128)(2,1)} %refs_6_.1) | copy-start | bytes 1179652
  13.6 19.8 %copy-start.1 = (bf16[4,24,72]{2,1,0:T(8,128)(2,1)S(1)}, bf16[4,24,72]{2,1,0:T(8,128)(2,1)}, u32[]{:S(2)}) copy-start(bf16[4,24,72]{2,1,0:T(8,128)(2,1)} %constant.8.clone.refs_7_) | copy-start | bytes 41476
  13.6 5.8 %collective-permute-start.9 = (bf16[9,72,128]{2,1,0:T(8,128)(2,1)S(1)}, bf16[9,72,128]{2,1,0:T(8,128)(2,1)S(1)}, u32[]{:S(2)}, u32[]{:S(2)}) collective-permute-start(bf16[9,72,128]{2,1,0:T(8,128)(2,1)S(1)} %get-tuple-element.28.refs_6_), channel_id=1, source_target_pairs={{0,4},{4,0},{8,12},{12,8},{16,20},{20,16},{24,28},{28,24},{1,5},{5... | collective-permute-start | bytes 497672 | tf_op jit(solution)/shard_map/ppermute | solution.py:331
  14.1 2.8 %collective-permute-start.7 = (bf16[4,6,2,256]{3,2,1,0:T(2,128)(2,1)S(1)}, bf16[4,6,2,256]{3,2,1,0:T(2,128)(2,1)S(1)}, u32[]{:S(2)}, u32[]{:S(2)}) collective-permute-start(bf16[4,6,2,256]{3,2,1,0:T(2,128)(2,1)S(1)} %get-tuple-element.26), channel_id=1, source_target_pairs={{0,4},{4,0},{8,12},{12,8},{16,20},{20,16},{24,28},{28,24},{1,5},{5... | collective-permute-start | bytes 73736 | tf_op jit(solution)/shard_map/ppermute | solution.py:331
  14.2 5.1 %collective-permute-start.8 = (bf16[4,6,2,256]{3,2,1,0:T(2,128)(2,1)S(1)}, bf16[4,6,2,256]{3,2,1,0:T(2,128)(2,1)S(1)}, u32[]{:S(2)}, u32[]{:S(2)}) collective-permute-start(bf16[4,6,2,256]{3,2,1,0:T(2,128)(2,1)S(1)} %get-tuple-element.27), channel_id=1, source_target_pairs={{0,12},{8,20},{16,28},{12,0},{20,8},{28,16},{1,13},{9,21},{17,29},... | collective-permute-start | bytes 73736 | tf_op jit(solution)/shard_map/ppermute | solution.py:335
  23.6 1.4 %collective-permute-start.10 = (bf16[4,2,72,128]{3,2,1,0:T(8,128)(2,1)S(1)}, bf16[4,2,72,128]{3,2,1,0:T(8,128)(2,1)S(1)}, u32[]{:S(2)}, u32[]{:S(2)}) collective-permute-start(bf16[4,2,72,128]{3,2,1,0:T(8,128)(2,1)S(1)} %get-tuple-element.30), channel_id=1, source_target_pairs={{0,4},{4,0},{8,12},{12,8},{16,20},{20,16},{24,28},{28,24},{1,5},{5... | collective-permute-start | bytes 442376 | tf_op jit(solution)/shard_map/ppermute | solution.py:331
  25.1 3.9 %collective-permute-start.11 = (bf16[2,72,128]{2,1,0:T(8,128)(2,1)S(1)}, bf16[2,72,128]{2,1,0:T(8,128)(2,1)S(1)}, u32[]{:S(2)}, u32[]{:S(2)}) collective-permute-start(bf16[2,72,128]{2,1,0:T(8,128)(2,1)S(1)} %get-tuple-element.32), channel_id=1, source_target_pairs={{0,12},{4,8},{8,4},{12,0},{16,28},{20,24},{24,20},{28,16},{1,13},{... | collective-permute-start | bytes 110600 | tf_op jit(solution)/shard_map/ppermute | solution.py:328
  25.9 4.4 %collective-permute-start.12 = (bf16[2,72,128]{2,1,0:T(8,128)(2,1)S(1)}, bf16[2,72,128]{2,1,0:T(8,128)(2,1)S(1)}, u32[]{:S(2)}, u32[]{:S(2)}) collective-permute-start(bf16[2,72,128]{2,1,0:T(8,128)(2,1)S(1)} %get-tuple-element.33), channel_id=1, source_target_pairs={{0,20},{4,16},{8,28},{12,24},{16,4},{20,0},{24,12},{28,8},{1,21},{... | collective-permute-start | bytes 110600 | tf_op jit(solution)/shard_map/ppermute | solution.py:328
  28.2 5.2 %collective-permute-start.13 = (bf16[2,72,128]{2,1,0:T(8,128)(2,1)S(1)}, bf16[2,72,128]{2,1,0:T(8,128)(2,1)S(1)}, u32[]{:S(2)}, u32[]{:S(2)}) collective-permute-start(bf16[2,72,128]{2,1,0:T(8,128)(2,1)S(1)} %get-tuple-element.34), channel_id=1, source_target_pairs={{0,28},{4,24},{8,20},{12,16},{16,12},{20,8},{24,4},{28,0},{1,29},{... | collective-permute-start | bytes 110600 | tf_op jit(solution)/shard_map/ppermute | solution.py:328
  33.8 3.4 %collective-permute-start.14 = (bf16[24,256]{1,0:T(8,128)(2,1)S(1)}, bf16[24,256]{1,0:T(8,128)(2,1)S(1)}, u32[]{:S(2)}, u32[]{:S(2)}) collective-permute-start(bf16[24,256]{1,0:T(8,128)(2,1)S(1)} %get-tuple-element.37), channel_id=1, source_target_pairs={{0,4},{1,5},{2,6},{3,7},{4,0},{5,1},{6,2},{7,3},{8,12},{9,13},{10,... | collective-permute-start | bytes 36872 | tf_op jit(solution)/shard_map/ppermute | solution.py:325
  34.2 3.1 %collective-permute-start.15 = (bf16[24,256]{1,0:T(8,128)(2,1)S(1)}, bf16[24,256]{1,0:T(8,128)(2,1)S(1)}, u32[]{:S(2)}, u32[]{:S(2)}) collective-permute-start(bf16[24,256]{1,0:T(8,128)(2,1)S(1)} %get-tuple-element.38), channel_id=1, source_target_pairs={{0,5},{1,4},{2,7},{3,6},{4,1},{5,0},{6,3},{7,2},{8,13},{9,12},{10,... | collective-permute-start | bytes 36872 | tf_op jit(solution)/shard_map/ppermute | solution.py:325
  35.4 3.1 %collective-permute-start.16 = (bf16[24,256]{1,0:T(8,128)(2,1)S(1)}, bf16[24,256]{1,0:T(8,128)(2,1)S(1)}, u32[]{:S(2)}, u32[]{:S(2)}) collective-permute-start(bf16[24,256]{1,0:T(8,128)(2,1)S(1)} %get-tuple-element.39), channel_id=1, source_target_pairs={{0,6},{1,7},{2,4},{3,5},{4,2},{5,3},{6,0},{7,1},{8,14},{9,15},{10,... | collective-permute-start | bytes 36872 | tf_op jit(solution)/shard_map/ppermute | solution.py:325
  36.9 4.0 %collective-permute-start.17 = (bf16[24,256]{1,0:T(8,128)(2,1)S(1)}, bf16[24,256]{1,0:T(8,128)(2,1)S(1)}, u32[]{:S(2)}, u32[]{:S(2)}) collective-permute-start(bf16[24,256]{1,0:T(8,128)(2,1)S(1)} %get-tuple-element.40), channel_id=1, source_target_pairs={{0,7},{1,6},{2,5},{3,4},{4,3},{5,2},{6,1},{7,0},{8,15},{9,14},{10,... | collective-permute-start | bytes 36872 | tf_op jit(solution)/shard_map/ppermute | solution.py:325

commit v4 on v3

--- a/solution.py
+++ b/solution.py
@@ -83,7 +83,9 @@
     return copies
 
 
-def pack_kernel(out_grad, pre_silu, queries, keys, values, tile, kv, query, q_ref, k_ref, v_ref, sems):
+def pack_kernel(
+    out_grad, pre_silu, queries, keys, values, tile, kv, query, q_ref, k_ref, v_ref, sems
+):
     copies = start_copies(
         [
             (values, v_ref),
@@ -108,39 +110,38 @@
     copies[4].wait()
 
 
-def middle_kernel(n_col, *refs):
-    tiles, parts = refs[:n_col], refs[n_col:-4]
-    query, to_core, to_chip, joined = refs[-4:]
+def rim_kernel(*refs):
+    *tiles, to_core, to_chip = refs
     rows = tiles[0].shape[1]
     inner = jnp.where(lax.axis_index("row") % 2 == 1, rows - 1, 0)
     for k, tile in enumerate(tiles):
         to_core[k] = tile[0, inner]
         to_chip[k] = tile[0, rows - 1 - inner]
-    heads = parts[0].shape[0]
-    for j, part in enumerate(parts):
-        for head in range(heads):
-            joined[heads * j + head] = part[head]
-    joined[heads * len(parts)] = query[...]
-
-
-def strip_kernel(n_col, per_sample, *refs):
+
+
+def join_kernel(*refs):
+    *parts, out = refs
+    first = 0
+    for part in parts:
+        for j in range(part.shape[0]):
+            out[first + j] = part[j]
+        first += part.shape[0]
+
+
+def conv_kernel(n_col, per_sample, *refs):
     tiles, rest = refs[:n_col], refs[n_col:]
     (
         halo_core,
         halo_chip,
-        kv_sent,
-        kv_kept,
         *far,
-        dkv_sent,
-        dkv_kept,
-        dq_ref,
         gz_ref,
+        go_ref,
         grads,
         silus,
+        shifts,
+        middle,
         conv_weight,
         out_weight,
-        shifts,
-        middle,
         sems,
     ) = rest
     copies = start_copies(list(zip(far, (shifts, middle, conv_weight, out_weight))), sems)
@@ -165,28 +166,6 @@
             silus[tile, i, :cols] = pick(tiles[k][1, i])
         grads[tile, lower, :cols] = pick(halo_core[k])
         grads[tile, upper, :cols] = pick(halo_chip[k])
-    lanes = kv_sent.shape[2]
-    half = lanes // 2
-    factor = half**-0.5
-    low = lax.broadcasted_iota(jnp.int32, (strip, lanes), 1) < half
-    query = kv_kept[kv_kept.shape[0] - 1]
-    none = jnp.zeros_like(query)
-    asked = (jnp.where(low, none, query), jnp.where(low, query, none))
-    blocks = dkv_kept.shape[0]
-    sources = ((kv_sent, dkv_sent), (kv_kept, dkv_kept))
-    small = 2 * blocks <= UNROLLED_CHUNKS
-    chunks = [(src, dst, j) for src, dst in sources for j in range(blocks)]
-
-    def softmax(head):
-        scores = [dot(src[2 * j + head], asked[head], 1, 1) for src, _, j in chunks]
-        top = jnp.max(functools.reduce(jnp.maximum, scores), axis=0, keepdims=True)
-        exps = [jnp.exp(s - top) for s in scores]
-        scale = 1.0 / jnp.sum(sum(exps), axis=0, keepdims=True)
-        return [e * scale for e in exps]
-
-    if small:
-        probs = [softmax(head) for head in (0, 1)]
-
     for copy in copies:
         copy.wait()
     flat = grads[...].reshape(-1, channels).astype(BF16)
@@ -200,64 +179,79 @@
     sigma = 1.0 / (1.0 + jnp.exp(-z))
     grad_z = (conv * sigma * (1.0 + z * (1.0 - sigma))).astype(BF16)
     gz_ref[...] = grad_z
-
-    first = col % per_sample * lanes
-    grad_out = dot(grad_z, out_weight[pl.ds(pl.multiple_of(first, lanes), lanes), :], 1, 1)
-    grad_out = grad_out.astype(BF16)
+    lanes = go_ref.shape[1]
+    first = pl.multiple_of(col % per_sample * lanes, lanes)
+    go_ref[...] = dot(grad_z, out_weight[pl.ds(first, lanes), :], 1, 1).astype(BF16)
+
+
+def attention_kernel(offsets, kv_sent, kv_kept, go_ref, dkv_sent, dkv_kept, dq_ref):
+    strip, lanes = go_ref.shape
+    half = lanes // 2
+    factor = half**-0.5
+    low = lax.broadcasted_iota(jnp.int32, (strip, lanes), 1) < half
+    query, grad_out = kv_kept[kv_kept.shape[0] - 1], go_ref[...]
+    none = jnp.zeros_like(query)
+    asked = (jnp.where(low, none, query), jnp.where(low, query, none))
     cotangent = (jnp.where(low, grad_out, none), jnp.where(low, none, grad_out))
+    chunks = []
+    for j, offset in enumerate(offsets):
+        even = offset != 0 and offset.bit_count() % 2 == 0
+        chunks.append((kv_sent, dkv_kept if even else dkv_sent, j, offset))
+        chunks.append((kv_kept, dkv_sent if even else dkv_kept, j, offset))
 
     grad_query = []
     for head in (0, 1):
         ask, cot = asked[head], cotangent[head]
 
-        def finish(kv, chunk_probs, probs_grad, row_dot):
-            grad_scores = (chunk_probs * (probs_grad - row_dot)).astype(BF16)
-            dkv = dot(grad_scores, ask) + dot(chunk_probs.astype(BF16), cot)
+        def finish(kv, probs, probs_grad, row_dot):
+            grad_scores = (probs * (probs_grad - row_dot)).astype(BF16)
+            dkv = dot(grad_scores, ask) + dot(probs.astype(BF16), cot)
             return dkv.astype(BF16), dot(grad_scores, kv, 0, 0)
 
         total = jnp.zeros((strip, lanes), F32)
-        if small:
-            probs_grads = [dot(src[2 * j + head], cot, 1, 1) for src, _, j in chunks]
-            weighted = sum(p * g for p, g in zip(probs[head], probs_grads))
+        if len(chunks) <= UNROLLED_CHUNKS:
+            scores = [dot(src[2 * j + head], ask, 1, 1) for src, _, j, _ in chunks]
+            top = jnp.max(functools.reduce(jnp.maximum, scores), axis=0, keepdims=True)
+            exps = [jnp.exp(s - top) for s in scores]
+            scale = 1.0 / jnp.sum(sum(exps), axis=0, keepdims=True)
+            probs = [e * scale for e in exps]
+            probs_grads = [dot(src[2 * j + head], cot, 1, 1) for src, _, j, _ in chunks]
+            weighted = sum(p * g for p, g in zip(probs, probs_grads))
             row_dot = jnp.sum(weighted, axis=0, keepdims=True)
-            for (src, dst, j), p, g in zip(chunks, probs[head], probs_grads):
-                dst[j, head], dq = finish(src[2 * j + head], p, g, row_dot)
+            for (src, dst, j, offset), p, g in zip(chunks, probs, probs_grads):
+                dst[offset, head], dq = finish(src[2 * j + head], p, g, row_dot)
                 total = total + dq
         else:
-            stats = (
-                jnp.full((1, strip), -jnp.inf, F32),
-                jnp.zeros((1, strip), F32),
-                jnp.zeros((1, strip), F32),
-            )
-            for src, _ in sources:
-
-                def gather(j, carry, src=src):
-                    top, norm, weighted = carry
-                    kv = src[2 * j + head]
-                    scores = dot(kv, ask, 1, 1)
-                    new = jnp.maximum(top, jnp.max(scores, axis=0, keepdims=True))
-                    exps = jnp.exp(scores - new)
-                    rescale = jnp.exp(top - new)
-                    weights = jnp.sum(exps * dot(kv, cot, 1, 1), axis=0, keepdims=True)
-                    return (
-                        new,
-                        norm * rescale + jnp.sum(exps, axis=0, keepdims=True),
-                        weighted * rescale + weights,
-                    )
-
-                stats = lax.fori_loop(0, blocks, gather, stats)
+
+            def gather(kv, carry):
+                top, norm, weighted = carry
+                scores = dot(kv, ask, 1, 1)
+                new = jnp.maximum(top, jnp.max(scores, axis=0, keepdims=True))
+                exps = jnp.exp(scores - new)
+                rescale = jnp.exp(top - new)
+                weights = jnp.sum(exps * dot(kv, cot, 1, 1), axis=0, keepdims=True)
+                return (
+                    new,
+                    norm * rescale + jnp.sum(exps, axis=0, keepdims=True),
+                    weighted * rescale + weights,
+                )
+
+            zero = jnp.zeros((1, strip), F32)
+            stats = (jnp.full((1, strip), -jnp.inf, F32), zero, zero)
+            for src in (kv_sent, kv_kept):
+                stats = lax.fori_loop(
+                    0,
+                    len(offsets),
+                    lambda j, carry, src=src: gather(src[2 * j + head], carry),
+                    stats,
+                )
             top, norm, weighted = stats
             scale = 1.0 / norm
-            row_dot = weighted * scale
-            for src, dst in sources:
-
-                def spread(j, total, src=src, dst=dst):
-                    kv = src[2 * j + head]
-                    chunk_probs = jnp.exp(dot(kv, ask, 1, 1) - top) * scale
-                    dst[j, head], dq = finish(kv, chunk_probs, dot(kv, cot, 1, 1), row_dot)
-                    return total + dq
-
-                total = lax.fori_loop(0, blocks, spread, total)
+            for src, dst, j, offset in chunks:
+                kv = src[2 * j + head]
+                probs = jnp.exp(dot(kv, ask, 1, 1) - top) * scale
+                dst[offset, head], dq = finish(kv, probs, dot(kv, cot, 1, 1), weighted * scale)
+                total = total + dq
         grad_query.append(total)
     dq_ref[...] = jnp.where(low, grad_query[1], grad_query[0]) * factor
 
@@ -351,35 +345,50 @@
         (saved, saved, saved, pltpu.SemaphoreType.DMA((5,))),
         range(5),
     )(cells(out_grad), cells(pre_silu), turned(query_heads), turned(key_heads), turned(value_heads))
-    kv_parts = [kv] + [to_chip(kv, k) for k in range(1, chips)]
     tiles = [to_col(tile, k) for k in range(n_col)]
 
+    def doubled(joined, received, *last):
+        parts = (joined, received, *last)
+        return call(join_kernel, held((sum(p.shape[0] for p in parts), strip, lanes), BF16))(*parts)
+
+    distances = [chips >> (i + 1) for i in range(chips.bit_length() - 1)]
+    offsets = [0]
+    for distance in distances:
+        offsets = offsets + [offset + distance for offset in offsets]
+    tiles, received = lax.optimization_barrier((tiles, to_chip(kv, distances[0])))
+    joined = doubled(kv, received)
+
     rim = held((n_col, cols, samples, channels), BF16)
-    rim_core, rim_chip, kv_sent = call(
-        functools.partial(middle_kernel, n_col),
-        (rim, rim, held((pairs * chips + 1, strip, lanes), BF16)),
-    )(*tiles, *kv_parts, query)
-    halo_core, halo_chip, kv_kept = to_core(rim_core), to_next_chip(rim_chip), to_core(kv_sent)
+    rim_core, rim_chip = call(rim_kernel, (rim, rim))(*tiles)
+    halo_chip, halo_core = to_next_chip(rim_chip), to_core(rim_core)
+    for distance in distances[1:-1]:
+        joined = doubled(joined, to_chip(joined, distance))
+    halo_chip, halo_core, received = lax.optimization_barrier(
+        (halo_chip, halo_core, to_chip(joined, distances[-1]))
+    )
+    joined = doubled(joined, received, query[None])
+    received = to_core(joined)
 
     padded = pad8(cols)
     shifts = jnp.asarray(shift_selector(rows + 2, cols, n_col), BF16)
     middle = jnp.asarray(shift_selector(rows, cols, n_col)[1], BF16)
     far = (shifts, middle, conv_weight, out_weight)
-    block = held((chips, pairs, strip, lanes), BF16)
-    dkv_sent, dkv_kept, dq, grad_z = call(
-        functools.partial(strip_kernel, n_col, per_sample),
-        (block, block, held((strip, lanes), F32), held((strip, channels), BF16)),
+    grad_z, grad_out = call(
+        functools.partial(conv_kernel, n_col, per_sample),
+        (held((strip, channels), BF16), held((strip, lanes), BF16)),
         (
             pltpu.VMEM((n_col, rows + 2, padded, channels), F32),
             pltpu.VMEM((n_col, rows, padded, channels), F32),
-            pltpu.VMEM(conv_weight.shape, BF16),
-            pltpu.VMEM(out_weight.shape, BF16),
-            pltpu.VMEM(shifts.shape, BF16),
-            pltpu.VMEM(middle.shape, BF16),
-            pltpu.SemaphoreType.DMA((4,)),
+            *(pltpu.VMEM(array.shape, BF16) for array in far),
+            pltpu.SemaphoreType.DMA((len(far),)),
         ),
-        range(n_col + 4, n_col + 8),
-    )(*tiles, halo_core, halo_chip, kv_sent, kv_kept, *far)
+        range(n_col + 2, n_col + 2 + len(far)),
+    )(*tiles, halo_core, halo_chip, *far)
+
+    block = held((chips, pairs, strip, lanes), BF16)
+    dkv_sent, dkv_kept, dq = call(
+        functools.partial(attention_kernel, offsets), (block, block, held((strip, lanes), F32))
+    )(joined, received, grad_out)
 
     sums = call(core_sum_kernel, [held((pairs, strip, lanes), BF16) for _ in range(chips)])(
         dkv_kept, to_core(dkv_sent)

time: 41.8 us -> 37.6 us (0.90)
  waiting for transfers between devices: 14.4 us -> 12.1 us
  starting transfers between devices: 20.7 us -> 19 us
    ppermute x6 -> x5, waiting for transfers between devices: 6.85 us -> 2.59 us  [to_chip(): lax.ppermute(array, 'row', [(i, i ^ 2 * k + 1) for i in range(n_row)])]
    ppermute x8, waiting for transfers between devices: 3.8 us -> 5.65 us  [to_col(): return lax.ppermute(array, ('row', 'col'), pairs_of)]
    ppermute x8, starting transfers between devices: 7.71 us -> 6.88 us  [to_col(): return lax.ppermute(array, ('row', 'col'), pairs_of)]
    ppermute x1, starting transfers between devices: 2.72 us -> 2.22 us  [to_next_chip(): return lax.ppermute(array, 'row', edge + [(j, i) for i, j in edge])]
    ppermute x6 -> x5, starting transfers between devices: 9.61 us -> 9.17 us  [to_chip(): lax.ppermute(array, 'row', [(i, i ^ 2 * k + 1) for i in range(n_row)])]
    ppermute x1, waiting for transfers between devices: 2.4 us -> 2.83 us  [to_next_chip(): return lax.ppermute(array, 'row', edge + [(j, i) for i, j in edge])]
    pallas_call x6 -> x9, Pallas kernels: 5.72 us -> 5.62 us  [run(): pl.pallas_call(kernel, out_shape=out_shape, in_specs=specs, out_specs=jax...]
  transfers between devices with their start and end apart: 18 -> 17, of which waited for: 8 -> 8; matrix products, arithmetic and copies ran while one was open for 0% -> 0% of each run, Pallas kernels for 0% -> 7%
where the time goes in v4:
time: 37.6 us; the launch traced here: 37.4 us
  starting transfers between devices  19 us (51%)
  waiting for transfers between devices  12.1 us (32%)
  Pallas kernels  5.62 us (15%)
  local copies, waits for them, and re-layouts  0.62 us (2%)
    ppermute x5, starting transfers between devices, to_chip(): lax.ppermute(array, 'row', [(i, i ^ 2 * k + 1) for i in range(n_row)])  9.17 us
    ppermute x8, starting transfers between devices, to_col(): return lax.ppermute(array, ('row', 'col'), pairs_of)  6.88 us
    ppermute x8, waiting for transfers between devices, to_col(): return lax.ppermute(array, ('row', 'col'), pairs_of)  5.65 us
    pallas_call x9, Pallas kernels, run(): pl.pallas_call(kernel, out_shape=out_shape, in_specs=specs, out_specs=jax...  5.62 us
    ppermute x1, waiting for transfers between devices, to_next_chip(): return lax.ppermute(array, 'row', edge + [(j, i) for i, j in edge])  2.83 us
    ppermute x5, waiting for transfers between devices, to_chip(): lax.ppermute(array, 'row', [(i, i ^ 2 * k + 1) for i in range(n_row)])  2.59 us
    ppermute x1, starting transfers between devices, to_next_chip(): return lax.ppermute(array, 'row', edge + [(j, i) for i, j in edge])  2.22 us
    ppermute x3, waiting for transfers between devices, to_core(): return lax.ppermute(array, 'row', [(i, i ^ 1) for i in range(n_row)])  1.01 us
  transfers between devices with their start and end apart: 17, of which 8 were waited for; matrix products, arithmetic and copies ran while one was open for 0% of the time, Pallas kernels for 7%

profile of v4, /device:TPU:0, one launch (start us, length us, event | category | flops | bytes accessed | tf_op | source)
XLA Modules:
  0.0 37.4 jit_solution(3001896067603237484)
XLA Ops:
  0.0 1.0 %shard_map.109 = (bf16[2,3,6,2,256]{4,3,2,1,0:T(2,128)(2,1)S(1)}, bf16[2,72,128]{2,1,0:T(8,128)(2,1)S(1)}, bf16[72,128]{1,0:T(8,128)(2,1)S(1)}) custom-call(bf16[3,6,2,256]{3,2,1,0:T(2,128)(2,1)} %bitcast.12, bf16[3,6,2,256]{3,2,1,0:T(2,128)(2,1)} %bitcast.13, bf16[2,64,72]{2,1,0:T(8,128)(2,1)} %bitcast.9, bf16[2,64,72]{2,1,0:T(8,128)(2,1)} %bitcast.10, ...), custom_call_target="tpu_custom_call" | custom-call | tf_op jit(solution)/shard_map/pallas_call | solution.py:35
  1.0 3.5 %collective-permute-start.4 = (bf16[2,72,128]{2,1,0:T(8,128)(2,1)S(1)}, bf16[2,72,128]{2,1,0:T(8,128)(2,1)S(1)}, u32[]{:S(2)}, u32[]{:S(2)}) collective-permute-start(bf16[2,72,128]{2,1,0:T(8,128)(2,1)S(1)} %get-tuple-element.31.refs_0_), channel_id=1, source_target_pairs={{0,20},{4,16},{8,28},{12,24},{16,4},{20,0},{24,12},{28,8},{1,21},{... | collective-permute-start | bytes 110600 | tf_op jit(solution)/shard_map/ppermute | solution.py:322
  4.5 2.7 %collective-permute-start.3 = (bf16[2,3,6,2,256]{4,3,2,1,0:T(2,128)(2,1)S(1)}, bf16[2,3,6,2,256]{4,3,2,1,0:T(2,128)(2,1)S(1)}, u32[]{:S(2)}, u32[]{:S(2)}) collective-permute-start(bf16[2,3,6,2,256]{4,3,2,1,0:T(2,128)(2,1)S(1)} %get-tuple-element.32), channel_id=1, source_target_pairs={{0,7},{1,6},{2,5},{3,4},{4,3},{5,2},{6,1},{7,0},{8,15},{9,14},{10,... | collective-permute-start | bytes 110600 | tf_op jit(solution)/shard_map/ppermute | solution.py:319
  7.3 0.0 collective-permute-start.2
  7.3 0.8 %collective-permute-start.1 = (bf16[2,3,6,2,256]{4,3,2,1,0:T(2,128)(2,1)S(1)}, bf16[2,3,6,2,256]{4,3,2,1,0:T(2,128)(2,1)S(1)}, u32[]{:S(2)}, u32[]{:S(2)}) collective-permute-start(bf16[2,3,6,2,256]{4,3,2,1,0:T(2,128)(2,1)S(1)} %get-tuple-element.32), channel_id=1, source_target_pairs={{0,5},{1,4},{2,7},{3,6},{4,1},{5,0},{6,3},{7,2},{8,13},{9,12},{10,... | collective-permute-start | bytes 110600 | tf_op jit(solution)/shard_map/ppermute | solution.py:319
  8.0 0.0 collective-permute-start
  8.0 0.0 collective-permute-done.4.refs_1_
  8.0 1.1 %collective-permute-done.3.refs_3_ = bf16[2,3,6,2,256]{4,3,2,1,0:T(2,128)(2,1)S(1)} collective-permute-done((bf16[2,3,6,2,256]{4,3,2,1,0:T(2,128)(2,1)S(1)}, bf16[2,3,6,2,256]{4,3,2,1,0:T(2,128)(2,1)S(1)}, u32[]{:S(2)}, u32[]{:S(2)}) %collective-permute-start.3) | collective-permute-done | bytes 36896 | tf_op jit(solution)/shard_map/ppermute | solution.py:319
  9.1 1.9 %collective-permute-done.2.refs_2_ = bf16[2,3,6,2,256]{4,3,2,1,0:T(2,128)(2,1)S(1)} collective-permute-done((bf16[2,3,6,2,256]{4,3,2,1,0:T(2,128)(2,1)S(1)}, bf16[2,3,6,2,256]{4,3,2,1,0:T(2,128)(2,1)S(1)}, u32[]{:S(2)}, u32[]{:S(2)}) %collective-permute-start.2) | collective-permute-done | bytes 36896 | tf_op jit(solution)/shard_map/ppermute | solution.py:319
  11.0 0.0 collective-permute-done.1.refs_1_
  11.0 0.0 collective-permute-done.refs_0_
  11.1 1.5 %collective-permute-start.7 = (bf16[4,72,128]{2,1,0:T(8,128)(2,1)S(1)}, bf16[4,72,128]{2,1,0:T(8,128)(2,1)S(1)}, u32[]{:S(2)}, u32[]{:S(2)}) collective-permute-start(bf16[4,72,128]{2,1,0:T(8,128)(2,1)S(1)} %shard_map.110.refs_0_), channel_id=1, source_target_pairs={{0,12},{4,8},{8,4},{12,0},{16,28},{20,24},{24,20},{28,16},{1,13},{... | collective-permute-start | bytes 221192 | tf_op jit(solution)/shard_map/ppermute | solution.py:322
  12.5 2.2 %collective-permute-start.5 = (bf16[4,6,2,256]{3,2,1,0:T(2,128)(2,1)S(1)}, bf16[4,6,2,256]{3,2,1,0:T(2,128)(2,1)S(1)}, u32[]{:S(2)}, u32[]{:S(2)}) collective-permute-start(bf16[4,6,2,256]{3,2,1,0:T(2,128)(2,1)S(1)} %get-tuple-element.38), channel_id=1, source_target_pairs={{0,12},{8,20},{16,28},{12,0},{20,8},{28,16},{1,13},{9,21},{17,29},... | collective-permute-start | bytes 73736 | tf_op jit(solution)/shard_map/ppermute | solution.py:329
  14.8 0.1 collective-permute-start.6
  14.9 2.8 %collective-permute-done.5.refs_5_ = bf16[4,6,2,256]{3,2,1,0:T(2,128)(2,1)S(1)} collective-permute-done((bf16[4,6,2,256]{3,2,1,0:T(2,128)(2,1)S(1)}, bf16[4,6,2,256]{3,2,1,0:T(2,128)(2,1)S(1)}, u32[]{:S(2)}, u32[]{:S(2)}) %collective-permute-start.5) | collective-permute-done | bytes 24608 | tf_op jit(solution)/shard_map/ppermute | solution.py:329
  17.7 0.0 collective-permute-done.6.refs_4_
  17.7 0.0 collective-permute-done.7.refs_1_
  17.7 0.0 copy-start
  17.7 0.0 copy-start.1
  17.7 0.1 collective-permute-start.8
  17.8 2.7 %shard_map.113 = (bf16[72,256]{1,0:T(8,128)(2,1)S(1)}, bf16[72,128]{1,0:T(8,128)(2,1)S(1)}) custom-call(bf16[2,3,6,2,256]{4,3,2,1,0:T(2,128)(2,1)S(1)} %collective-permute-done.refs_0_, bf16[2,3,6,2,256]{4,3,2,1,0:T(2,128)(2,1)S(1)} %collective-permute-done.1.refs_1_, bf16[2,3,6,2,256]{4,3,2,1,0:T(2,128)(2,1)S(1)} %collective-permute-done.2.refs_2_, ...), custom_call_target="tpu_custom_call" | custom-call | tf_op jit(solution)/shard_map/pallas_call | solution.py:35
  20.5 0.0 collective-permute-done.8.kv_kept
  20.6 1.4 %shard_map.114 = (bf16[4,2,72,128]{3,2,1,0:T(8,128)(2,1)S(1)}, bf16[4,2,72,128]{3,2,1,0:T(8,128)(2,1)S(1)}, f32[72,128]{1,0:T(8,128)S(1)}) custom-call(bf16[9,72,128]{2,1,0:T(8,128)(2,1)S(1)} %shard_map.112.kv_sent, bf16[9,72,128]{2,1,0:T(8,128)(2,1)S(1)} %collective-permute-done.8.kv_kept, bf16[72,128]{1,0:T(8,128)(2,1)S(1)} %get-tuple-element.44.go_ref), custom_call_target="tpu_custom_call" | custom-call | tf_op jit(solution)/shard_map/pallas_call | solution.py:35
  22.0 0.6 %collective-permute-start.9 = (bf16[4,2,72,128]{3,2,1,0:T(8,128)(2,1)S(1)}, bf16[4,2,72,128]{3,2,1,0:T(8,128)(2,1)S(1)}, u32[]{:S(2)}, u32[]{:S(2)}) collective-permute-start(bf16[4,2,72,128]{3,2,1,0:T(8,128)(2,1)S(1)} %get-tuple-element.46), channel_id=1, source_target_pairs={{0,4},{4,0},{8,12},{12,8},{16,20},{20,16},{24,28},{28,24},{1,5},{5... | collective-permute-start | bytes 442376 | tf_op jit(solution)/shard_map/ppermute | solution.py:325
  22.5 1.0 %collective-permute-done.9.received = bf16[4,2,72,128]{3,2,1,0:T(8,128)(2,1)S(1)} collective-permute-done((bf16[4,2,72,128]{3,2,1,0:T(8,128)(2,1)S(1)}, bf16[4,2,72,128]{3,2,1,0:T(8,128)(2,1)S(1)}, u32[]{:S(2)}, u32[]{:S(2)}) %collective-permute-start.9) | collective-permute-done | bytes 147488 | tf_op jit(solution)/shard_map/ppermute | solution.py:325
  23.6 0.5 %collective-permute-start.10 = (bf16[2,72,128]{2,1,0:T(8,128)(2,1)S(1)}, bf16[2,72,128]{2,1,0:T(8,128)(2,1)S(1)}, u32[]{:S(2)}, u32[]{:S(2)}) collective-permute-start(bf16[2,72,128]{2,1,0:T(8,128)(2,1)S(1)} %get-tuple-element.48), channel_id=1, source_target_pairs={{0,12},{4,8},{8,4},{12,0},{16,28},{20,24},{24,20},{28,16},{1,13},{... | collective-permute-start | bytes 110600 | tf_op jit(solution)/shard_map/ppermute | solution.py:322
  24.0 0.1 collective-permute-start.11
  24.2 3.5 %collective-permute-start.12 = (bf16[2,72,128]{2,1,0:T(8,128)(2,1)S(1)}, bf16[2,72,128]{2,1,0:T(8,128)(2,1)S(1)}, u32[]{:S(2)}, u32[]{:S(2)}) collective-permute-start(bf16[2,72,128]{2,1,0:T(8,128)(2,1)S(1)} %get-tuple-element.50), channel_id=1, source_target_pairs={{0,28},{4,24},{8,20},{12,16},{16,12},{20,8},{24,4},{28,0},{1,29},{... | collective-permute-start | bytes 110600 | tf_op jit(solution)/shard_map/ppermute | solution.py:322
  27.7 0.0 collective-permute-done.10.refs_1_
  27.7 0.6 %collective-permute-done.11.refs_2_ = bf16[2,72,128]{2,1,0:T(8,128)(2,1)S(1)} collective-permute-done((bf16[2,72,128]{2,1,0:T(8,128)(2,1)S(1)}, bf16[2,72,128]{2,1,0:T(8,128)(2,1)S(1)}, u32[]{:S(2)}, u32[]{:S(2)}) %collective-permute-start.11) | collective-permute-done | bytes 36896 | tf_op jit(solution)/shard_map/ppermute | solution.py:322
  28.3 2.0 %collective-permute-done.12.refs_3_ = bf16[2,72,128]{2,1,0:T(8,128)(2,1)S(1)} collective-permute-done((bf16[2,72,128]{2,1,0:T(8,128)(2,1)S(1)}, bf16[2,72,128]{2,1,0:T(8,128)(2,1)S(1)}, u32[]{:S(2)}, u32[]{:S(2)}) %collective-permute-start.12) | collective-permute-done | bytes 36896 | tf_op jit(solution)/shard_map/ppermute | solution.py:322
  30.3 0.0 copy-done
  30.3 0.0 copy-done.1
  30.3 0.4 %shard_map.116 = (bf16[24,256]{1,0:T(8,128)(2,1)S(1)}, bf16[24,256]{1,0:T(8,128)(2,1)S(1)}, bf16[24,256]{1,0:T(8,128)(2,1)S(1)}, bf16[24,256]{1,0:T(8,128)(2,1)S(1)}) custom-call(bf16[2,72,128]{2,1,0:T(8,128)(2,1)S(1)} %get-tuple-element.47.refs_0_, bf16[2,72,128]{2,1,0:T(8,128)(2,1)S(1)} %collective-permute-done.10.refs_1_, ...), custom_call_target="tpu_custom_call" | custom-call | tf_op jit(solution)/shard_map/pallas_call | solution.py:35
  30.7 0.3 collective-permute-start.13
  31.0 0.7 %collective-permute-start.14 = (bf16[24,256]{1,0:T(8,128)(2,1)S(1)}, bf16[24,256]{1,0:T(8,128)(2,1)S(1)}, u32[]{:S(2)}, u32[]{:S(2)}) collective-permute-start(bf16[24,256]{1,0:T(8,128)(2,1)S(1)} %get-tuple-element.54), channel_id=1, source_target_pairs={{0,5},{1,4},{2,7},{3,6},{4,1},{5,0},{6,3},{7,2},{8,13},{9,12},{10,... | collective-permute-start | bytes 36872 | tf_op jit(solution)/shard_map/ppermute | solution.py:319
  31.7 1.0 %collective-permute-start.15 = (bf16[24,256]{1,0:T(8,128)(2,1)S(1)}, bf16[24,256]{1,0:T(8,128)(2,1)S(1)}, u32[]{:S(2)}, u32[]{:S(2)}) collective-permute-start(bf16[24,256]{1,0:T(8,128)(2,1)S(1)} %get-tuple-element.55), channel_id=1, source_target_pairs={{0,6},{1,7},{2,4},{3,5},{4,2},{5,3},{6,0},{7,1},{8,14},{9,15},{10,... | collective-permute-start | bytes 36872 | tf_op jit(solution)/shard_map/ppermute | solution.py:319
  32.7 1.4 %collective-permute-start.16 = (bf16[24,256]{1,0:T(8,128)(2,1)S(1)}, bf16[24,256]{1,0:T(8,128)(2,1)S(1)}, u32[]{:S(2)}, u32[]{:S(2)}) collective-permute-start(bf16[24,256]{1,0:T(8,128)(2,1)S(1)} %get-tuple-element.56), channel_id=1, source_target_pairs={{0,7},{1,6},{2,5},{3,4},{4,3},{5,2},{6,1},{7,0},{8,15},{9,14},{10,... | collective-permute-start | bytes 36872 | tf_op jit(solution)/shard_map/ppermute | solution.py:319
  34.1 0.0 collective-permute-done.13.refs_0_
  34.1 0.0 collective-permute-done.14.refs_1_
  34.1 0.7 %collective-permute-done.15.refs_2_ = bf16[24,256]{1,0:T(8,128)(2,1)S(1)} collective-permute-done((bf16[24,256]{1,0:T(8,128)(2,1)S(1)}, bf16[24,256]{1,0:T(8,128)(2,1)S(1)}, u32[]{:S(2)}, u32[]{:S(2)}) %collective-permute-start.15) | collective-permute-done | bytes 12320 | tf_op jit(solution)/shard_map/ppermute | solution.py:319
  34.8 1.9 %collective-permute-done.16.refs_3_ = bf16[24,256]{1,0:T(8,128)(2,1)S(1)} collective-permute-done((bf16[24,256]{1,0:T(8,128)(2,1)S(1)}, bf16[24,256]{1,0:T(8,128)(2,1)S(1)}, u32[]{:S(2)}, u32[]{:S(2)}) %collective-permute-start.16) | collective-permute-done | bytes 12320 | tf_op jit(solution)/shard_map/ppermute | solution.py:319
  36.8 0.6 %copy.12 = bf16[2,3,6,256]{3,0,2,1:T(2,128)(2,1)} copy(bf16[2,3,6,256]{3,0,2,1:T(2,128)(2,1)S(1)} %bitcast.7) | data formatting | bytes 36864
  (5 shorter events, 0.1 us)
Async XLA Ops:
  1.0 7.0 %collective-permute-start.4 = (bf16[2,72,128]{2,1,0:T(8,128)(2,1)S(1)}, bf16[2,72,128]{2,1,0:T(8,128)(2,1)S(1)}, u32[]{:S(2)}, u32[]{:S(2)}) collective-permute-start(bf16[2,72,128]{2,1,0:T(8,128)(2,1)S(1)} %get-tuple-element.31.refs_0_), channel_id=1, source_target_pairs={{0,20},{4,16},{8,28},{12,24},{16,4},{20,0},{24,12},{28,8},{1,21},{... | collective-permute-start | bytes 110600 | tf_op jit(solution)/shard_map/ppermute | solution.py:322
  4.5 4.6 %collective-permute-start.3 = (bf16[2,3,6,2,256]{4,3,2,1,0:T(2,128)(2,1)S(1)}, bf16[2,3,6,2,256]{4,3,2,1,0:T(2,128)(2,1)S(1)}, u32[]{:S(2)}, u32[]{:S(2)}) collective-permute-start(bf16[2,3,6,2,256]{4,3,2,1,0:T(2,128)(2,1)S(1)} %get-tuple-element.32), channel_id=1, source_target_pairs={{0,7},{1,6},{2,5},{3,4},{4,3},{5,2},{6,1},{7,0},{8,15},{9,14},{10,... | collective-permute-start | bytes 110600 | tf_op jit(solution)/shard_map/ppermute | solution.py:319
  7.3 3.8 %collective-permute-start.2 = (bf16[2,3,6,2,256]{4,3,2,1,0:T(2,128)(2,1)S(1)}, bf16[2,3,6,2,256]{4,3,2,1,0:T(2,128)(2,1)S(1)}, u32[]{:S(2)}, u32[]{:S(2)}) collective-permute-start(bf16[2,3,6,2,256]{4,3,2,1,0:T(2,128)(2,1)S(1)} %get-tuple-element.32), channel_id=1, source_target_pairs={{0,6},{1,7},{2,4},{3,5},{4,2},{5,3},{6,0},{7,1},{8,14},{9,15},{10,... | collective-permute-start | bytes 110600 | tf_op jit(solution)/shard_map/ppermute | solution.py:319
  7.3 3.8 %collective-permute-start.1 = (bf16[2,3,6,2,256]{4,3,2,1,0:T(2,128)(2,1)S(1)}, bf16[2,3,6,2,256]{4,3,2,1,0:T(2,128)(2,1)S(1)}, u32[]{:S(2)}, u32[]{:S(2)}) collective-permute-start(bf16[2,3,6,2,256]{4,3,2,1,0:T(2,128)(2,1)S(1)} %get-tuple-element.32), channel_id=1, source_target_pairs={{0,5},{1,4},{2,7},{3,6},{4,1},{5,0},{6,3},{7,2},{8,13},{9,12},{10,... | collective-permute-start | bytes 110600 | tf_op jit(solution)/shard_map/ppermute | solution.py:319
  8.0 3.0 %collective-permute-start = (bf16[2,3,6,2,256]{4,3,2,1,0:T(2,128)(2,1)S(1)}, bf16[2,3,6,2,256]{4,3,2,1,0:T(2,128)(2,1)S(1)}, u32[]{:S(2)}, u32[]{:S(2)}) collective-permute-start(bf16[2,3,6,2,256]{4,3,2,1,0:T(2,128)(2,1)S(1)} %get-tuple-element.32), channel_id=1, source_target_pairs={{0,4},{1,5},{2,6},{3,7},{4,0},{5,1},{6,2},{7,3},{8,12},{9,13},{10,... | collective-permute-start | bytes 110600 | tf_op jit(solution)/shard_map/ppermute | solution.py:319
  11.1 6.6 %collective-permute-start.7 = (bf16[4,72,128]{2,1,0:T(8,128)(2,1)S(1)}, bf16[4,72,128]{2,1,0:T(8,128)(2,1)S(1)}, u32[]{:S(2)}, u32[]{:S(2)}) collective-permute-start(bf16[4,72,128]{2,1,0:T(8,128)(2,1)S(1)} %shard_map.110.refs_0_), channel_id=1, source_target_pairs={{0,12},{4,8},{8,4},{12,0},{16,28},{20,24},{24,20},{28,16},{1,13},{... | collective-permute-start | bytes 221192 | tf_op jit(solution)/shard_map/ppermute | solution.py:322
  12.5 5.1 %collective-permute-start.5 = (bf16[4,6,2,256]{3,2,1,0:T(2,128)(2,1)S(1)}, bf16[4,6,2,256]{3,2,1,0:T(2,128)(2,1)S(1)}, u32[]{:S(2)}, u32[]{:S(2)}) collective-permute-start(bf16[4,6,2,256]{3,2,1,0:T(2,128)(2,1)S(1)} %get-tuple-element.38), channel_id=1, source_target_pairs={{0,12},{8,20},{16,28},{12,0},{20,8},{28,16},{1,13},{9,21},{17,29},... | collective-permute-start | bytes 73736 | tf_op jit(solution)/shard_map/ppermute | solution.py:329
  14.8 2.9 %collective-permute-start.6 = (bf16[4,6,2,256]{3,2,1,0:T(2,128)(2,1)S(1)}, bf16[4,6,2,256]{3,2,1,0:T(2,128)(2,1)S(1)}, u32[]{:S(2)}, u32[]{:S(2)}) collective-permute-start(bf16[4,6,2,256]{3,2,1,0:T(2,128)(2,1)S(1)} %get-tuple-element.39), channel_id=1, source_target_pairs={{0,4},{4,0},{8,12},{12,8},{16,20},{20,16},{24,28},{28,24},{1,5},{5... | collective-permute-start | bytes 73736 | tf_op jit(solution)/shard_map/ppermute | solution.py:325
  17.7 12.6 %copy-start = (bf16[256,768]{1,0:T(8,128)(2,1)S(1)}, bf16[256,768]{1,0:T(8,128)(2,1)}, u32[]{:S(2)}) copy-start(bf16[256,768]{1,0:T(8,128)(2,1)} %refs_6_.2) | copy-start | bytes 1179652
  17.7 12.6 %copy-start.1 = (bf16[4,24,72]{2,1,0:T(8,128)(2,1)S(1)}, bf16[4,24,72]{2,1,0:T(8,128)(2,1)}, u32[]{:S(2)}) copy-start(bf16[4,24,72]{2,1,0:T(8,128)(2,1)} %constant.8.clone.refs_7_) | copy-start | bytes 41476
  17.7 2.8 %collective-permute-start.8 = (bf16[9,72,128]{2,1,0:T(8,128)(2,1)S(1)}, bf16[9,72,128]{2,1,0:T(8,128)(2,1)S(1)}, u32[]{:S(2)}, u32[]{:S(2)}) collective-permute-start(bf16[9,72,128]{2,1,0:T(8,128)(2,1)S(1)} %shard_map.112.kv_sent), channel_id=1, source_target_pairs={{0,4},{4,0},{8,12},{12,8},{16,20},{20,16},{24,28},{28,24},{1,5},{5... | collective-permute-start | bytes 497672 | tf_op jit(solution)/shard_map/ppermute | solution.py:325
  22.0 1.6 %collective-permute-start.9 = (bf16[4,2,72,128]{3,2,1,0:T(8,128)(2,1)S(1)}, bf16[4,2,72,128]{3,2,1,0:T(8,128)(2,1)S(1)}, u32[]{:S(2)}, u32[]{:S(2)}) collective-permute-start(bf16[4,2,72,128]{3,2,1,0:T(8,128)(2,1)S(1)} %get-tuple-element.46), channel_id=1, source_target_pairs={{0,4},{4,0},{8,12},{12,8},{16,20},{20,16},{24,28},{28,24},{1,5},{5... | collective-permute-start | bytes 442376 | tf_op jit(solution)/shard_map/ppermute | solution.py:325
  23.6 4.1 %collective-permute-start.10 = (bf16[2,72,128]{2,1,0:T(8,128)(2,1)S(1)}, bf16[2,72,128]{2,1,0:T(8,128)(2,1)S(1)}, u32[]{:S(2)}, u32[]{:S(2)}) collective-permute-start(bf16[2,72,128]{2,1,0:T(8,128)(2,1)S(1)} %get-tuple-element.48), channel_id=1, source_target_pairs={{0,12},{4,8},{8,4},{12,0},{16,28},{20,24},{24,20},{28,16},{1,13},{... | collective-permute-start | bytes 110600 | tf_op jit(solution)/shard_map/ppermute | solution.py:322
  24.0 4.3 %collective-permute-start.11 = (bf16[2,72,128]{2,1,0:T(8,128)(2,1)S(1)}, bf16[2,72,128]{2,1,0:T(8,128)(2,1)S(1)}, u32[]{:S(2)}, u32[]{:S(2)}) collective-permute-start(bf16[2,72,128]{2,1,0:T(8,128)(2,1)S(1)} %get-tuple-element.49), channel_id=1, source_target_pairs={{0,20},{4,16},{8,28},{12,24},{16,4},{20,0},{24,12},{28,8},{1,21},{... | collective-permute-start | bytes 110600 | tf_op jit(solution)/shard_map/ppermute | solution.py:322
  24.2 6.1 %collective-permute-start.12 = (bf16[2,72,128]{2,1,0:T(8,128)(2,1)S(1)}, bf16[2,72,128]{2,1,0:T(8,128)(2,1)S(1)}, u32[]{:S(2)}, u32[]{:S(2)}) collective-permute-start(bf16[2,72,128]{2,1,0:T(8,128)(2,1)S(1)} %get-tuple-element.50), channel_id=1, source_target_pairs={{0,28},{4,24},{8,20},{12,16},{16,12},{20,8},{24,4},{28,0},{1,29},{... | collective-permute-start | bytes 110600 | tf_op jit(solution)/shard_map/ppermute | solution.py:322
  30.7 3.4 %collective-permute-start.13 = (bf16[24,256]{1,0:T(8,128)(2,1)S(1)}, bf16[24,256]{1,0:T(8,128)(2,1)S(1)}, u32[]{:S(2)}, u32[]{:S(2)}) collective-permute-start(bf16[24,256]{1,0:T(8,128)(2,1)S(1)} %get-tuple-element.53), channel_id=1, source_target_pairs={{0,4},{1,5},{2,6},{3,7},{4,0},{5,1},{6,2},{7,3},{8,12},{9,13},{10,... | collective-permute-start | bytes 36872 | tf_op jit(solution)/shard_map/ppermute | solution.py:319
  31.0 3.1 %collective-permute-start.14 = (bf16[24,256]{1,0:T(8,128)(2,1)S(1)}, bf16[24,256]{1,0:T(8,128)(2,1)S(1)}, u32[]{:S(2)}, u32[]{:S(2)}) collective-permute-start(bf16[24,256]{1,0:T(8,128)(2,1)S(1)} %get-tuple-element.54), channel_id=1, source_target_pairs={{0,5},{1,4},{2,7},{3,6},{4,1},{5,0},{6,3},{7,2},{8,13},{9,12},{10,... | collective-permute-start | bytes 36872 | tf_op jit(solution)/shard_map/ppermute | solution.py:319
  31.7 3.1 %collective-permute-start.15 = (bf16[24,256]{1,0:T(8,128)(2,1)S(1)}, bf16[24,256]{1,0:T(8,128)(2,1)S(1)}, u32[]{:S(2)}, u32[]{:S(2)}) collective-permute-start(bf16[24,256]{1,0:T(8,128)(2,1)S(1)} %get-tuple-element.55), channel_id=1, source_target_pairs={{0,6},{1,7},{2,4},{3,5},{4,2},{5,3},{6,0},{7,1},{8,14},{9,15},{10,... | collective-permute-start | bytes 36872 | tf_op jit(solution)/shard_map/ppermute | solution.py:319
  32.7 4.0 %collective-permute-start.16 = (bf16[24,256]{1,0:T(8,128)(2,1)S(1)}, bf16[24,256]{1,0:T(8,128)(2,1)S(1)}, u32[]{:S(2)}, u32[]{:S(2)}) collective-permute-start(bf16[24,256]{1,0:T(8,128)(2,1)S(1)} %get-tuple-element.56), channel_id=1, source_target_pairs={{0,7},{1,6},{2,5},{3,4},{4,3},{5,2},{6,1},{7,0},{8,15},{9,14},{10,... | collective-permute-start | bytes 36872 | tf_op jit(solution)/shard_map/ppermute | solution.py:319

commit v5 on v4

--- a/solution.py
+++ b/solution.py
@@ -128,56 +128,66 @@
         first += part.shape[0]
 
 
+def load_kernel(*refs):
+    *copied, sems = refs
+    half = len(copied) // 2
+    for copy in start_copies(list(zip(copied[:half], copied[half:])), sems):
+        copy.wait()
+
+
+def pick(cells, sample):
+    place = lax.broadcasted_iota(jnp.int32, cells.shape, 1)
+    return jnp.sum(jnp.where(place == sample, cells.astype(F32), 0.0), axis=1)
+
+
 def conv_kernel(n_col, per_sample, *refs):
-    tiles, rest = refs[:n_col], refs[n_col:]
-    (
-        halo_core,
-        halo_chip,
-        *far,
-        gz_ref,
-        go_ref,
-        grads,
-        silus,
-        shifts,
-        middle,
-        conv_weight,
-        out_weight,
-        sems,
-    ) = rest
-    copies = start_copies(list(zip(far, (shifts, middle, conv_weight, out_weight))), sems)
+    tiles, (shifts, conv_weight, conv_ref, gate_ref, grads, silus) = refs[:n_col], refs[n_col:]
+    col = lax.axis_index("col")
+    sample = col // per_sample
+    _, rows, cols, _, channels = tiles[0].shape
+    width = n_col * cols
+    grads[...] = jnp.zeros_like(grads)
+    silus[...] = jnp.zeros_like(silus)
+    for k in range(n_col):
+        for i in range(rows):
+            grads[col ^ k, i, :cols] = pick(tiles[k][0, i], sample)
+            silus[col ^ k, i, :cols] = pick(tiles[k][1, i], sample)
+    flat = grads[...].reshape(-1, channels).astype(BF16)
+    none = jnp.zeros((width, channels), F32)
+    conv = jnp.zeros((rows * width, channels), F32)
+    for b in (-1, 0, 1):
+        here = dot(shifts[b + 1], flat)
+        above = jnp.concatenate([none, here[:-width]], 0)
+        below = jnp.concatenate([here[width:], none], 0)
+        for a, window in ((-1, below), (0, here), (1, above)):
+            conv = conv + dot(window.astype(BF16), conv_weight[a + 1, b + 1], 1, 1)
+    conv_ref[...] = conv
+    z = dot(shifts[1], silus[...].reshape(-1, channels).astype(BF16))
+    sigma = 1.0 / (1.0 + jnp.exp(-z))
+    gate_ref[...] = sigma * (1.0 + z * (1.0 - sigma))
+
+
+def rim_conv_kernel(per_sample, *refs):
+    halo_core, halo_chip, conv, gate, shifts, conv_weight, out_weight, gz_ref, go_ref, rims = refs
     col, core = lax.axis_index("col"), lax.axis_index("row") % 2
     sample = col // per_sample
-    _, rows, cols, samples, channels = tiles[0].shape
+    n_col, cols, _, channels = halo_core.shape
     width = n_col * cols
-    strip = rows * width
-    chosen = lax.broadcasted_iota(jnp.int32, (cols, samples, channels), 1) == sample
-
-    def pick(cells):
-        return jnp.sum(jnp.where(chosen, cells.astype(F32), 0.0), axis=1)
-
-    grads[...] = jnp.zeros_like(grads)
-    silus[...] = jnp.zeros_like(silus)
-    lower = jnp.where(core == 1, rows + 1, 0)
-    upper = jnp.where(core == 1, 0, rows + 1)
+    rims[...] = jnp.zeros_like(rims)
     for k in range(n_col):
-        tile = col ^ k
-        for i in range(rows):
-            grads[tile, i + 1, :cols] = pick(tiles[k][0, i])
-            silus[tile, i, :cols] = pick(tiles[k][1, i])
-        grads[tile, lower, :cols] = pick(halo_core[k])
-        grads[tile, upper, :cols] = pick(halo_chip[k])
-    for copy in copies:
-        copy.wait()
-    flat = grads[...].reshape(-1, channels).astype(BF16)
-    conv = jnp.zeros((strip, channels), F32)
-    for b in (-1, 0, 1):
-        shifted = dot(shifts[b + 1], flat)
-        for a in (-1, 0, 1):
-            window = shifted[(1 - a) * width : (1 - a) * width + strip].astype(BF16)
-            conv = conv + dot(window, conv_weight[a + 1, b + 1], 1, 1)
-    z = dot(middle[...], silus[...].reshape(-1, channels).astype(BF16))
-    sigma = 1.0 / (1.0 + jnp.exp(-z))
-    grad_z = (conv * sigma * (1.0 + z * (1.0 - sigma))).astype(BF16)
+        rims[core, col ^ k, :cols] = pick(halo_core[k], sample)
+        rims[1 - core, col ^ k, :cols] = pick(halo_chip[k], sample)
+    edges = []
+    for side, a in ((0, 1), (1, -1)):
+        flat = rims[side].reshape(-1, channels).astype(BF16)
+        edge = jnp.zeros((width, channels), F32)
+        for b in (-1, 0, 1):
+            window = dot(shifts[b + 1], flat).astype(BF16)
+            edge = edge + dot(window, conv_weight[a + 1, b + 1], 1, 1)
+        edges.append(edge)
+    between = jnp.zeros((conv.shape[0] - 2 * width, channels), F32)
+    total = conv[...] + jnp.concatenate([edges[0], between, edges[1]], 0)
+    grad_z = (total * gate[...]).astype(BF16)
     gz_ref[...] = grad_z
     lanes = go_ref.shape[1]
     first = pl.multiple_of(col % per_sample * lanes, lanes)
@@ -347,6 +357,20 @@
     )(cells(out_grad), cells(pre_silu), turned(query_heads), turned(key_heads), turned(value_heads))
     tiles = [to_col(tile, k) for k in range(n_col)]
 
+    padded = pad8(cols)
+    far = (
+        jnp.asarray(shift_selector(rows, cols, n_col), BF16),
+        jnp.asarray(shift_selector(1, cols, n_col), BF16),
+        conv_weight,
+        out_weight,
+    )
+    loaded = call(
+        load_kernel,
+        [held(array.shape, BF16) for array in far],
+        [pltpu.SemaphoreType.DMA((len(far),))],
+        range(len(far)),
+    )(*far)
+
     def doubled(joined, received, *last):
         parts = (joined, received, *last)
         return call(join_kernel, held((sum(p.shape[0] for p in parts), strip, lanes), BF16))(*parts)
@@ -355,7 +379,9 @@
     offsets = [0]
     for distance in distances:
         offsets = offsets + [offset + distance for offset in offsets]
-    tiles, received = lax.optimization_barrier((tiles, to_chip(kv, distances[0])))
+    tiles, received, (shifts, rim_shifts, conv_weight, out_weight) = lax.optimization_barrier(
+        (tiles, to_chip(kv, distances[0]), loaded)
+    )
     joined = doubled(kv, received)
 
     rim = held((n_col, cols, samples, channels), BF16)
@@ -363,27 +389,24 @@
     halo_chip, halo_core = to_next_chip(rim_chip), to_core(rim_core)
     for distance in distances[1:-1]:
         joined = doubled(joined, to_chip(joined, distance))
-    halo_chip, halo_core, received = lax.optimization_barrier(
-        (halo_chip, halo_core, to_chip(joined, distances[-1]))
+    received = to_chip(joined, distances[-1])
+
+    whole = held((strip, channels), F32)
+    conv, gate = call(
+        functools.partial(conv_kernel, n_col, per_sample),
+        (whole, whole),
+        [pltpu.VMEM((n_col, rows, padded, channels), F32)] * 2,
+    )(*tiles, shifts, conv_weight)
+    received, conv, halo_chip, halo_core = lax.optimization_barrier(
+        (received, conv, halo_chip, halo_core)
     )
     joined = doubled(joined, received, query[None])
     received = to_core(joined)
-
-    padded = pad8(cols)
-    shifts = jnp.asarray(shift_selector(rows + 2, cols, n_col), BF16)
-    middle = jnp.asarray(shift_selector(rows, cols, n_col)[1], BF16)
-    far = (shifts, middle, conv_weight, out_weight)
     grad_z, grad_out = call(
-        functools.partial(conv_kernel, n_col, per_sample),
+        functools.partial(rim_conv_kernel, per_sample),
         (held((strip, channels), BF16), held((strip, lanes), BF16)),
-        (
-            pltpu.VMEM((n_col, rows + 2, padded, channels), F32),
-            pltpu.VMEM((n_col, rows, padded, channels), F32),
-            *(pltpu.VMEM(array.shape, BF16) for array in far),
-            pltpu.SemaphoreType.DMA((len(far),)),
-        ),
-        range(n_col + 2, n_col + 2 + len(far)),
-    )(*tiles, halo_core, halo_chip, *far)
+        [pltpu.VMEM((2, n_col, padded, channels), F32)],
+    )(halo_core, halo_chip, conv, gate, rim_shifts, conv_weight, out_weight)
 
     block = held((chips, pairs, strip, lanes), BF16)
     dkv_sent, dkv_kept, dq = call(
@@ -393,7 +416,7 @@
     sums = call(core_sum_kernel, [held((pairs, strip, lanes), BF16) for _ in range(chips)])(
         dkv_kept, to_core(dkv_sent)
     )
-    parts = [sums[0]] + [to_chip(sums[k], k) for k in range(1, chips)]
+    parts = [to_chip(sums[k], k) for k in reversed(range(1, chips))] + [sums[0]]
 
     cut = call(
         functools.partial(project_kernel, n_col, per_sample),

time: 37.6 us -> 35.6 us (0.947)
  waiting for transfers between devices: 12.1 us -> 10.1 us
  starting transfers between devices: 19 us -> 18.4 us
  Pallas kernels: 5.62 us -> 6.15 us
    ppermute x8, waiting for transfers between devices: 5.65 us -> 4.24 us  [to_col(): return lax.ppermute(array, ('row', 'col'), pairs_of)]
    ppermute x1, waiting for transfers between devices: 2.83 us -> 1.64 us  [to_next_chip(): return lax.ppermute(array, 'row', edge + [(j, i) for i, j in edge])]
    ppermute x3, waiting for transfers between devices: 1.01 us -> 1.88 us  [to_core(): return lax.ppermute(array, 'row', [(i, i ^ 1) for i in range(n_row)])]
    pallas_call x9 -> x11, Pallas kernels: 5.62 us -> 6.15 us  [run(): pl.pallas_call(kernel, out_shape=out_shape, in_specs=specs, out_specs=jax...]
  transfers between devices with their start and end apart: 17 -> 17, of which waited for: 8 -> 8; matrix products, arithmetic and copies ran while one was open for 0% -> 0% of each run, Pallas kernels for 7% -> 9%
where the time goes in v5:
time: 35.6 us; the launch traced here: 35.4 us
  starting transfers between devices  18.4 us (52%)
  waiting for transfers between devices  10.1 us (28%)
  Pallas kernels  6.15 us (17%)
  local copies, waits for them, and re-layouts  0.62 us (2%)
    ppermute x5, starting transfers between devices, to_chip(): lax.ppermute(array, 'row', [(i, i ^ 2 * k + 1) for i in range(n_row)])  8.96 us
    ppermute x8, starting transfers between devices, to_col(): return lax.ppermute(array, ('row', 'col'), pairs_of)  6.88 us
    pallas_call x11, Pallas kernels, run(): pl.pallas_call(kernel, out_shape=out_shape, in_specs=specs, out_specs=jax...  6.15 us
    ppermute x8, waiting for transfers between devices, to_col(): return lax.ppermute(array, ('row', 'col'), pairs_of)  4.24 us
    ppermute x5, waiting for transfers between devices, to_chip(): lax.ppermute(array, 'row', [(i, i ^ 2 * k + 1) for i in range(n_row)])  2.29 us
    ppermute x1, starting transfers between devices, to_next_chip(): return lax.ppermute(array, 'row', edge + [(j, i) for i, j in edge])  2.22 us
    ppermute x3, waiting for transfers between devices, to_core(): return lax.ppermute(array, 'row', [(i, i ^ 1) for i in range(n_row)])  1.88 us
    ppermute x1, waiting for transfers between devices, to_next_chip(): return lax.ppermute(array, 'row', edge + [(j, i) for i, j in edge])  1.64 us
  transfers between devices with their start and end apart: 17, of which 8 were waited for; matrix products, arithmetic and copies ran while one was open for 0% of the time, Pallas kernels for 9%

profile of v5, /device:TPU:0, one launch (start us, length us, event | category | flops | bytes accessed | tf_op | source)
XLA Modules:
  0.0 35.4 jit_solution(13688044421257814935)
XLA Ops:
  0.0 1.0 %shard_map.109 = (bf16[2,3,6,2,256]{4,3,2,1,0:T(2,128)(2,1)S(1)}, bf16[2,72,128]{2,1,0:T(8,128)(2,1)S(1)}, bf16[72,128]{1,0:T(8,128)(2,1)S(1)}) custom-call(bf16[3,6,2,256]{3,2,1,0:T(2,128)(2,1)} %bitcast.12, bf16[3,6,2,256]{3,2,1,0:T(2,128)(2,1)} %bitcast.13, bf16[2,64,72]{2,1,0:T(8,128)(2,1)} %bitcast.9, bf16[2,64,72]{2,1,0:T(8,128)(2,1)} %bitcast.10, ...), custom_call_target="tpu_custom_call" | custom-call | tf_op jit(solution)/shard_map/pallas_call | solution.py:35
  1.0 3.5 %collective-permute-start.4 = (bf16[2,72,128]{2,1,0:T(8,128)(2,1)S(1)}, bf16[2,72,128]{2,1,0:T(8,128)(2,1)S(1)}, u32[]{:S(2)}, u32[]{:S(2)}) collective-permute-start(bf16[2,72,128]{2,1,0:T(8,128)(2,1)S(1)} %get-tuple-element.42.refs_0_), channel_id=1, source_target_pairs={{0,20},{4,16},{8,28},{12,24},{16,4},{20,0},{24,12},{28,8},{1,21},{... | collective-permute-start | bytes 110600 | tf_op jit(solution)/shard_map/ppermute | solution.py:332
  4.5 2.7 %collective-permute-start.3 = (bf16[2,3,6,2,256]{4,3,2,1,0:T(2,128)(2,1)S(1)}, bf16[2,3,6,2,256]{4,3,2,1,0:T(2,128)(2,1)S(1)}, u32[]{:S(2)}, u32[]{:S(2)}) collective-permute-start(bf16[2,3,6,2,256]{4,3,2,1,0:T(2,128)(2,1)S(1)} %get-tuple-element.43), channel_id=1, source_target_pairs={{0,7},{1,6},{2,5},{3,4},{4,3},{5,2},{6,1},{7,0},{8,15},{9,14},{10,... | collective-permute-start | bytes 110600 | tf_op jit(solution)/shard_map/ppermute | solution.py:329
  7.3 0.0 collective-permute-start.2
  7.3 0.8 %collective-permute-start.1 = (bf16[2,3,6,2,256]{4,3,2,1,0:T(2,128)(2,1)S(1)}, bf16[2,3,6,2,256]{4,3,2,1,0:T(2,128)(2,1)S(1)}, u32[]{:S(2)}, u32[]{:S(2)}) collective-permute-start(bf16[2,3,6,2,256]{4,3,2,1,0:T(2,128)(2,1)S(1)} %get-tuple-element.43), channel_id=1, source_target_pairs={{0,5},{1,4},{2,7},{3,6},{4,1},{5,0},{6,3},{7,2},{8,13},{9,12},{10,... | collective-permute-start | bytes 110600 | tf_op jit(solution)/shard_map/ppermute | solution.py:329
  8.0 0.0 collective-permute-start
  8.0 1.4 %shard_map.110 = (bf16[3,72,96]{2,1,0:T(8,128)(2,1)S(1)}, bf16[3,24,32]{2,1,0:T(8,128)(2,1)S(1)}, bf16[3,3,256,256]{3,2,1,0:T(8,128)(2,1)S(1)}, bf16[256,256]{1,0:T(8,128)(2,1)S(1)}) custom-call(bf16[3,72,96]{2,1,0:T(8,128)(2,1)} %constant.6.clone.refs_0_, bf16[3,24,32]{2,1,0:T(8,128)(2,1)} %constant.7.clone.refs_1_, bf16[3,3,256,256]{3,2,1,0:T(8,128)(2,1)} %refs_2_.1, ...), custom_call_target="tpu_custom_call" | custom-call | tf_op jit(solution)/shard_map/pallas_call | solution.py:35
  9.4 0.0 collective-permute-done.4.refs_1_
  9.4 0.0 collective-permute-done.3.refs_3_
  9.4 1.6 %collective-permute-done.2.refs_2_ = bf16[2,3,6,2,256]{4,3,2,1,0:T(2,128)(2,1)S(1)} collective-permute-done((bf16[2,3,6,2,256]{4,3,2,1,0:T(2,128)(2,1)S(1)}, bf16[2,3,6,2,256]{4,3,2,1,0:T(2,128)(2,1)S(1)}, u32[]{:S(2)}, u32[]{:S(2)}) %collective-permute-start.2) | collective-permute-done | bytes 36896 | tf_op jit(solution)/shard_map/ppermute | solution.py:329
  11.0 0.0 collective-permute-done.1.refs_1_
  11.0 0.0 collective-permute-done.refs_0_
  11.1 1.5 %collective-permute-start.5 = (bf16[4,72,128]{2,1,0:T(8,128)(2,1)S(1)}, bf16[4,72,128]{2,1,0:T(8,128)(2,1)S(1)}, u32[]{:S(2)}, u32[]{:S(2)}) collective-permute-start(bf16[4,72,128]{2,1,0:T(8,128)(2,1)S(1)} %shard_map.111.refs_0_), channel_id=1, source_target_pairs={{0,12},{4,8},{8,4},{12,0},{16,28},{20,24},{24,20},{28,16},{1,13},{... | collective-permute-start | bytes 221192 | tf_op jit(solution)/shard_map/ppermute | solution.py:332
  12.5 2.2 %collective-permute-start.6 = (bf16[4,6,2,256]{3,2,1,0:T(2,128)(2,1)S(1)}, bf16[4,6,2,256]{3,2,1,0:T(2,128)(2,1)S(1)}, u32[]{:S(2)}, u32[]{:S(2)}) collective-permute-start(bf16[4,6,2,256]{3,2,1,0:T(2,128)(2,1)S(1)} %get-tuple-element.56), channel_id=1, source_target_pairs={{0,12},{8,20},{16,28},{12,0},{20,8},{28,16},{1,13},{9,21},{17,29},... | collective-permute-start | bytes 73736 | tf_op jit(solution)/shard_map/ppermute | solution.py:339
  14.8 0.1 collective-permute-start.7
  14.9 1.2 %shard_map.112 = (f32[72,256]{1,0:T(8,128)S(1)}, f32[72,256]{1,0:T(8,128)S(1)}) custom-call(bf16[2,3,6,2,256]{4,3,2,1,0:T(2,128)(2,1)S(1)} %collective-permute-done.refs_0_, bf16[2,3,6,2,256]{4,3,2,1,0:T(2,128)(2,1)S(1)} %collective-permute-done.1.refs_1_, bf16[2,3,6,2,256]{4,3,2,1,0:T(2,128)(2,1)S(1)} %collective-permute-done.2.refs_2_, ...), custom_call_target="tpu_custom_call" | custom-call | tf_op jit(solution)/shard_map/pallas_call | solution.py:35
  16.0 1.6 %collective-permute-done.6.refs_1_ = bf16[4,6,2,256]{3,2,1,0:T(2,128)(2,1)S(1)} collective-permute-done((bf16[4,6,2,256]{3,2,1,0:T(2,128)(2,1)S(1)}, bf16[4,6,2,256]{3,2,1,0:T(2,128)(2,1)S(1)}, u32[]{:S(2)}, u32[]{:S(2)}) %collective-permute-start.6) | collective-permute-done | bytes 24608 | tf_op jit(solution)/shard_map/ppermute | solution.py:339
  17.7 0.0 collective-permute-done.7.refs_0_
  17.7 0.0 collective-permute-done.5.refs_1_
  17.7 0.0 copy-start
  17.7 0.0 copy-start.1
  17.7 0.1 collective-permute-start.8
  17.8 0.7 %shard_map.115 = (bf16[72,256]{1,0:T(8,128)(2,1)S(1)}, bf16[72,128]{1,0:T(8,128)(2,1)S(1)}) custom-call(bf16[4,6,2,256]{3,2,1,0:T(2,128)(2,1)S(1)} %collective-permute-done.7.refs_0_, bf16[4,6,2,256]{3,2,1,0:T(2,128)(2,1)S(1)} %collective-permute-done.6.refs_1_, f32[72,256]{1,0:T(8,128)S(1)} %get-tuple-element.62.refs_2_, ...), custom_call_target="tpu_custom_call" | custom-call | tf_op jit(solution)/shard_map/pallas_call | solution.py:35
  18.5 0.7 %collective-permute-done.8.kv_kept = bf16[9,72,128]{2,1,0:T(8,128)(2,1)S(1)} collective-permute-done((bf16[9,72,128]{2,1,0:T(8,128)(2,1)S(1)}, bf16[9,72,128]{2,1,0:T(8,128)(2,1)S(1)}, u32[]{:S(2)}, u32[]{:S(2)}) %collective-permute-start.8) | collective-permute-done | bytes 165920 | tf_op jit(solution)/shard_map/ppermute | solution.py:335
  19.2 1.4 %shard_map.116 = (bf16[4,2,72,128]{3,2,1,0:T(8,128)(2,1)S(1)}, bf16[4,2,72,128]{3,2,1,0:T(8,128)(2,1)S(1)}, f32[72,128]{1,0:T(8,128)S(1)}) custom-call(bf16[9,72,128]{2,1,0:T(8,128)(2,1)S(1)} %shard_map.114.kv_sent, bf16[9,72,128]{2,1,0:T(8,128)(2,1)S(1)} %collective-permute-done.8.kv_kept, bf16[72,128]{1,0:T(8,128)(2,1)S(1)} %get-tuple-element.66.go_ref), custom_call_target="tpu_custom_call" | custom-call | tf_op jit(solution)/shard_map/pallas_call | solution.py:35
  20.6 0.2 collective-permute-start.9
  20.8 1.2 %collective-permute-done.9.received = bf16[4,2,72,128]{3,2,1,0:T(8,128)(2,1)S(1)} collective-permute-done((bf16[4,2,72,128]{3,2,1,0:T(8,128)(2,1)S(1)}, bf16[4,2,72,128]{3,2,1,0:T(8,128)(2,1)S(1)}, u32[]{:S(2)}, u32[]{:S(2)}) %collective-permute-start.9) | collective-permute-done | bytes 147488 | tf_op jit(solution)/shard_map/ppermute | solution.py:335
  22.1 0.1 collective-permute-start.10
  22.1 1.6 %collective-permute-start.11 = (bf16[2,72,128]{2,1,0:T(8,128)(2,1)S(1)}, bf16[2,72,128]{2,1,0:T(8,128)(2,1)S(1)}, u32[]{:S(2)}, u32[]{:S(2)}) collective-permute-start(bf16[2,72,128]{2,1,0:T(8,128)(2,1)S(1)} %get-tuple-element.70), channel_id=1, source_target_pairs={{0,20},{4,16},{8,28},{12,24},{16,4},{20,0},{24,12},{28,8},{1,21},{... | collective-permute-start | bytes 110600 | tf_op jit(solution)/shard_map/ppermute | solution.py:332
  23.8 2.2 %collective-permute-start.12 = (bf16[2,72,128]{2,1,0:T(8,128)(2,1)S(1)}, bf16[2,72,128]{2,1,0:T(8,128)(2,1)S(1)}, u32[]{:S(2)}, u32[]{:S(2)}) collective-permute-start(bf16[2,72,128]{2,1,0:T(8,128)(2,1)S(1)} %get-tuple-element.71), channel_id=1, source_target_pairs={{0,12},{4,8},{8,4},{12,0},{16,28},{20,24},{24,20},{28,16},{1,13},{... | collective-permute-start | bytes 110600 | tf_op jit(solution)/shard_map/ppermute | solution.py:332
  26.0 1.4 %collective-permute-done.10.refs_0_ = bf16[2,72,128]{2,1,0:T(8,128)(2,1)S(1)} collective-permute-done((bf16[2,72,128]{2,1,0:T(8,128)(2,1)S(1)}, bf16[2,72,128]{2,1,0:T(8,128)(2,1)S(1)}, u32[]{:S(2)}, u32[]{:S(2)}) %collective-permute-start.10) | collective-permute-done | bytes 36896 | tf_op jit(solution)/shard_map/ppermute | solution.py:332
  27.4 0.0 collective-permute-done.11.refs_1_
  27.4 0.9 %collective-permute-done.12.refs_2_ = bf16[2,72,128]{2,1,0:T(8,128)(2,1)S(1)} collective-permute-done((bf16[2,72,128]{2,1,0:T(8,128)(2,1)S(1)}, bf16[2,72,128]{2,1,0:T(8,128)(2,1)S(1)}, u32[]{:S(2)}, u32[]{:S(2)}) %collective-permute-start.12) | collective-permute-done | bytes 36896 | tf_op jit(solution)/shard_map/ppermute | solution.py:332
  28.3 0.0 copy-done
  28.3 0.0 copy-done.1
  28.3 0.4 %shard_map.118 = (bf16[24,256]{1,0:T(8,128)(2,1)S(1)}, bf16[24,256]{1,0:T(8,128)(2,1)S(1)}, bf16[24,256]{1,0:T(8,128)(2,1)S(1)}, bf16[24,256]{1,0:T(8,128)(2,1)S(1)}) custom-call(bf16[2,72,128]{2,1,0:T(8,128)(2,1)S(1)} %collective-permute-done.10.refs_0_, bf16[2,72,128]{2,1,0:T(8,128)(2,1)S(1)} %collective-permute-done.11.refs_1_, ...), custom_call_target="tpu_custom_call" | custom-call | tf_op jit(solution)/shard_map/pallas_call | solution.py:35
  28.7 0.2 collective-permute-start.13
  28.9 0.9 %collective-permute-start.14 = (bf16[24,256]{1,0:T(8,128)(2,1)S(1)}, bf16[24,256]{1,0:T(8,128)(2,1)S(1)}, u32[]{:S(2)}, u32[]{:S(2)}) collective-permute-start(bf16[24,256]{1,0:T(8,128)(2,1)S(1)} %get-tuple-element.76), channel_id=1, source_target_pairs={{0,5},{1,4},{2,7},{3,6},{4,1},{5,0},{6,3},{7,2},{8,13},{9,12},{10,... | collective-permute-start | bytes 36872 | tf_op jit(solution)/shard_map/ppermute | solution.py:329
  29.8 0.9 %collective-permute-start.15 = (bf16[24,256]{1,0:T(8,128)(2,1)S(1)}, bf16[24,256]{1,0:T(8,128)(2,1)S(1)}, u32[]{:S(2)}, u32[]{:S(2)}) collective-permute-start(bf16[24,256]{1,0:T(8,128)(2,1)S(1)} %get-tuple-element.77), channel_id=1, source_target_pairs={{0,6},{1,7},{2,4},{3,5},{4,2},{5,3},{6,0},{7,1},{8,14},{9,15},{10,... | collective-permute-start | bytes 36872 | tf_op jit(solution)/shard_map/ppermute | solution.py:329
  30.7 1.4 %collective-permute-start.16 = (bf16[24,256]{1,0:T(8,128)(2,1)S(1)}, bf16[24,256]{1,0:T(8,128)(2,1)S(1)}, u32[]{:S(2)}, u32[]{:S(2)}) collective-permute-start(bf16[24,256]{1,0:T(8,128)(2,1)S(1)} %get-tuple-element.78), channel_id=1, source_target_pairs={{0,7},{1,6},{2,5},{3,4},{4,3},{5,2},{6,1},{7,0},{8,15},{9,14},{10,... | collective-permute-start | bytes 36872 | tf_op jit(solution)/shard_map/ppermute | solution.py:329
  32.1 0.0 collective-permute-done.13.refs_0_
  32.1 0.0 collective-permute-done.14.refs_1_
  32.1 0.9 %collective-permute-done.15.refs_2_ = bf16[24,256]{1,0:T(8,128)(2,1)S(1)} collective-permute-done((bf16[24,256]{1,0:T(8,128)(2,1)S(1)}, bf16[24,256]{1,0:T(8,128)(2,1)S(1)}, u32[]{:S(2)}, u32[]{:S(2)}) %collective-permute-start.15) | collective-permute-done | bytes 12320 | tf_op jit(solution)/shard_map/ppermute | solution.py:329
  33.0 1.8 %collective-permute-done.16.refs_3_ = bf16[24,256]{1,0:T(8,128)(2,1)S(1)} collective-permute-done((bf16[24,256]{1,0:T(8,128)(2,1)S(1)}, bf16[24,256]{1,0:T(8,128)(2,1)S(1)}, u32[]{:S(2)}, u32[]{:S(2)}) %collective-permute-start.16) | collective-permute-done | bytes 12320 | tf_op jit(solution)/shard_map/ppermute | solution.py:329
  34.8 0.6 %copy.12 = bf16[2,3,6,256]{3,0,2,1:T(2,128)(2,1)} copy(bf16[2,3,6,256]{3,0,2,1:T(2,128)(2,1)S(1)} %bitcast.7) | data formatting | bytes 36864
  (5 shorter events, 0.1 us)
Async XLA Ops:
  1.0 8.4 %collective-permute-start.4 = (bf16[2,72,128]{2,1,0:T(8,128)(2,1)S(1)}, bf16[2,72,128]{2,1,0:T(8,128)(2,1)S(1)}, u32[]{:S(2)}, u32[]{:S(2)}) collective-permute-start(bf16[2,72,128]{2,1,0:T(8,128)(2,1)S(1)} %get-tuple-element.42.refs_0_), channel_id=1, source_target_pairs={{0,20},{4,16},{8,28},{12,24},{16,4},{20,0},{24,12},{28,8},{1,21},{... | collective-permute-start | bytes 110600 | tf_op jit(solution)/shard_map/ppermute | solution.py:332
  4.5 4.9 %collective-permute-start.3 = (bf16[2,3,6,2,256]{4,3,2,1,0:T(2,128)(2,1)S(1)}, bf16[2,3,6,2,256]{4,3,2,1,0:T(2,128)(2,1)S(1)}, u32[]{:S(2)}, u32[]{:S(2)}) collective-permute-start(bf16[2,3,6,2,256]{4,3,2,1,0:T(2,128)(2,1)S(1)} %get-tuple-element.43), channel_id=1, source_target_pairs={{0,7},{1,6},{2,5},{3,4},{4,3},{5,2},{6,1},{7,0},{8,15},{9,14},{10,... | collective-permute-start | bytes 110600 | tf_op jit(solution)/shard_map/ppermute | solution.py:329
  7.3 3.8 %collective-permute-start.2 = (bf16[2,3,6,2,256]{4,3,2,1,0:T(2,128)(2,1)S(1)}, bf16[2,3,6,2,256]{4,3,2,1,0:T(2,128)(2,1)S(1)}, u32[]{:S(2)}, u32[]{:S(2)}) collective-permute-start(bf16[2,3,6,2,256]{4,3,2,1,0:T(2,128)(2,1)S(1)} %get-tuple-element.43), channel_id=1, source_target_pairs={{0,6},{1,7},{2,4},{3,5},{4,2},{5,3},{6,0},{7,1},{8,14},{9,15},{10,... | collective-permute-start | bytes 110600 | tf_op jit(solution)/shard_map/ppermute | solution.py:329
  7.3 3.8 %collective-permute-start.1 = (bf16[2,3,6,2,256]{4,3,2,1,0:T(2,128)(2,1)S(1)}, bf16[2,3,6,2,256]{4,3,2,1,0:T(2,128)(2,1)S(1)}, u32[]{:S(2)}, u32[]{:S(2)}) collective-permute-start(bf16[2,3,6,2,256]{4,3,2,1,0:T(2,128)(2,1)S(1)} %get-tuple-element.43), channel_id=1, source_target_pairs={{0,5},{1,4},{2,7},{3,6},{4,1},{5,0},{6,3},{7,2},{8,13},{9,12},{10,... | collective-permute-start | bytes 110600 | tf_op jit(solution)/shard_map/ppermute | solution.py:329
  8.0 3.0 %collective-permute-start = (bf16[2,3,6,2,256]{4,3,2,1,0:T(2,128)(2,1)S(1)}, bf16[2,3,6,2,256]{4,3,2,1,0:T(2,128)(2,1)S(1)}, u32[]{:S(2)}, u32[]{:S(2)}) collective-permute-start(bf16[2,3,6,2,256]{4,3,2,1,0:T(2,128)(2,1)S(1)} %get-tuple-element.43), channel_id=1, source_target_pairs={{0,4},{1,5},{2,6},{3,7},{4,0},{5,1},{6,2},{7,3},{8,12},{9,13},{10,... | collective-permute-start | bytes 110600 | tf_op jit(solution)/shard_map/ppermute | solution.py:329
  11.1 6.6 %collective-permute-start.5 = (bf16[4,72,128]{2,1,0:T(8,128)(2,1)S(1)}, bf16[4,72,128]{2,1,0:T(8,128)(2,1)S(1)}, u32[]{:S(2)}, u32[]{:S(2)}) collective-permute-start(bf16[4,72,128]{2,1,0:T(8,128)(2,1)S(1)} %shard_map.111.refs_0_), channel_id=1, source_target_pairs={{0,12},{4,8},{8,4},{12,0},{16,28},{20,24},{24,20},{28,16},{1,13},{... | collective-permute-start | bytes 221192 | tf_op jit(solution)/shard_map/ppermute | solution.py:332
  12.5 5.1 %collective-permute-start.6 = (bf16[4,6,2,256]{3,2,1,0:T(2,128)(2,1)S(1)}, bf16[4,6,2,256]{3,2,1,0:T(2,128)(2,1)S(1)}, u32[]{:S(2)}, u32[]{:S(2)}) collective-permute-start(bf16[4,6,2,256]{3,2,1,0:T(2,128)(2,1)S(1)} %get-tuple-element.56), channel_id=1, source_target_pairs={{0,12},{8,20},{16,28},{12,0},{20,8},{28,16},{1,13},{9,21},{17,29},... | collective-permute-start | bytes 73736 | tf_op jit(solution)/shard_map/ppermute | solution.py:339
  14.8 2.9 %collective-permute-start.7 = (bf16[4,6,2,256]{3,2,1,0:T(2,128)(2,1)S(1)}, bf16[4,6,2,256]{3,2,1,0:T(2,128)(2,1)S(1)}, u32[]{:S(2)}, u32[]{:S(2)}) collective-permute-start(bf16[4,6,2,256]{3,2,1,0:T(2,128)(2,1)S(1)} %get-tuple-element.57), channel_id=1, source_target_pairs={{0,4},{4,0},{8,12},{12,8},{16,20},{20,16},{24,28},{28,24},{1,5},{5... | collective-permute-start | bytes 73736 | tf_op jit(solution)/shard_map/ppermute | solution.py:335
  17.7 10.6 %copy-start = (bf16[256,768]{1,0:T(8,128)(2,1)S(1)}, bf16[256,768]{1,0:T(8,128)(2,1)}, u32[]{:S(2)}) copy-start(bf16[256,768]{1,0:T(8,128)(2,1)} %refs_6_.1) | copy-start | bytes 1179652
  17.7 10.6 %copy-start.1 = (bf16[4,24,72]{2,1,0:T(8,128)(2,1)S(1)}, bf16[4,24,72]{2,1,0:T(8,128)(2,1)}, u32[]{:S(2)}) copy-start(bf16[4,24,72]{2,1,0:T(8,128)(2,1)} %constant.8.clone.refs_7_) | copy-start | bytes 41476
  17.7 1.5 %collective-permute-start.8 = (bf16[9,72,128]{2,1,0:T(8,128)(2,1)S(1)}, bf16[9,72,128]{2,1,0:T(8,128)(2,1)S(1)}, u32[]{:S(2)}, u32[]{:S(2)}) collective-permute-start(bf16[9,72,128]{2,1,0:T(8,128)(2,1)S(1)} %shard_map.114.kv_sent), channel_id=1, source_target_pairs={{0,4},{4,0},{8,12},{12,8},{16,20},{20,16},{24,28},{28,24},{1,5},{5... | collective-permute-start | bytes 497672 | tf_op jit(solution)/shard_map/ppermute | solution.py:335
  20.6 1.4 %collective-permute-start.9 = (bf16[4,2,72,128]{3,2,1,0:T(8,128)(2,1)S(1)}, bf16[4,2,72,128]{3,2,1,0:T(8,128)(2,1)S(1)}, u32[]{:S(2)}, u32[]{:S(2)}) collective-permute-start(bf16[4,2,72,128]{3,2,1,0:T(8,128)(2,1)S(1)} %get-tuple-element.68), channel_id=1, source_target_pairs={{0,4},{4,0},{8,12},{12,8},{16,20},{20,16},{24,28},{28,24},{1,5},{5... | collective-permute-start | bytes 442376 | tf_op jit(solution)/shard_map/ppermute | solution.py:335
  22.1 5.3 %collective-permute-start.10 = (bf16[2,72,128]{2,1,0:T(8,128)(2,1)S(1)}, bf16[2,72,128]{2,1,0:T(8,128)(2,1)S(1)}, u32[]{:S(2)}, u32[]{:S(2)}) collective-permute-start(bf16[2,72,128]{2,1,0:T(8,128)(2,1)S(1)} %get-tuple-element.69), channel_id=1, source_target_pairs={{0,28},{4,24},{8,20},{12,16},{16,12},{20,8},{24,4},{28,0},{1,29},{... | collective-permute-start | bytes 110600 | tf_op jit(solution)/shard_map/ppermute | solution.py:332
  22.1 5.2 %collective-permute-start.11 = (bf16[2,72,128]{2,1,0:T(8,128)(2,1)S(1)}, bf16[2,72,128]{2,1,0:T(8,128)(2,1)S(1)}, u32[]{:S(2)}, u32[]{:S(2)}) collective-permute-start(bf16[2,72,128]{2,1,0:T(8,128)(2,1)S(1)} %get-tuple-element.70), channel_id=1, source_target_pairs={{0,20},{4,16},{8,28},{12,24},{16,4},{20,0},{24,12},{28,8},{1,21},{... | collective-permute-start | bytes 110600 | tf_op jit(solution)/shard_map/ppermute | solution.py:332
  23.8 4.5 %collective-permute-start.12 = (bf16[2,72,128]{2,1,0:T(8,128)(2,1)S(1)}, bf16[2,72,128]{2,1,0:T(8,128)(2,1)S(1)}, u32[]{:S(2)}, u32[]{:S(2)}) collective-permute-start(bf16[2,72,128]{2,1,0:T(8,128)(2,1)S(1)} %get-tuple-element.71), channel_id=1, source_target_pairs={{0,12},{4,8},{8,4},{12,0},{16,28},{20,24},{24,20},{28,16},{1,13},{... | collective-permute-start | bytes 110600 | tf_op jit(solution)/shard_map/ppermute | solution.py:332
  28.7 3.4 %collective-permute-start.13 = (bf16[24,256]{1,0:T(8,128)(2,1)S(1)}, bf16[24,256]{1,0:T(8,128)(2,1)S(1)}, u32[]{:S(2)}, u32[]{:S(2)}) collective-permute-start(bf16[24,256]{1,0:T(8,128)(2,1)S(1)} %get-tuple-element.75), channel_id=1, source_target_pairs={{0,4},{1,5},{2,6},{3,7},{4,0},{5,1},{6,2},{7,3},{8,12},{9,13},{10,... | collective-permute-start | bytes 36872 | tf_op jit(solution)/shard_map/ppermute | solution.py:329
  28.9 3.2 %collective-permute-start.14 = (bf16[24,256]{1,0:T(8,128)(2,1)S(1)}, bf16[24,256]{1,0:T(8,128)(2,1)S(1)}, u32[]{:S(2)}, u32[]{:S(2)}) collective-permute-start(bf16[24,256]{1,0:T(8,128)(2,1)S(1)} %get-tuple-element.76), channel_id=1, source_target_pairs={{0,5},{1,4},{2,7},{3,6},{4,1},{5,0},{6,3},{7,2},{8,13},{9,12},{10,... | collective-permute-start | bytes 36872 | tf_op jit(solution)/shard_map/ppermute | solution.py:329
  29.8 3.1 %collective-permute-start.15 = (bf16[24,256]{1,0:T(8,128)(2,1)S(1)}, bf16[24,256]{1,0:T(8,128)(2,1)S(1)}, u32[]{:S(2)}, u32[]{:S(2)}) collective-permute-start(bf16[24,256]{1,0:T(8,128)(2,1)S(1)} %get-tuple-element.77), channel_id=1, source_target_pairs={{0,6},{1,7},{2,4},{3,5},{4,2},{5,3},{6,0},{7,1},{8,14},{9,15},{10,... | collective-permute-start | bytes 36872 | tf_op jit(solution)/shard_map/ppermute | solution.py:329
  30.7 4.0 %collective-permute-start.16 = (bf16[24,256]{1,0:T(8,128)(2,1)S(1)}, bf16[24,256]{1,0:T(8,128)(2,1)S(1)}, u32[]{:S(2)}, u32[]{:S(2)}) collective-permute-start(bf16[24,256]{1,0:T(8,128)(2,1)S(1)} %get-tuple-element.78), channel_id=1, source_target_pairs={{0,7},{1,6},{2,5},{3,4},{4,3},{5,2},{6,1},{7,0},{8,15},{9,14},{10,... | collective-permute-start | bytes 36872 | tf_op jit(solution)/shard_map/ppermute | solution.py:329

commit v6 on v5

--- a/solution.py
+++ b/solution.py
@@ -110,22 +110,33 @@
     copies[4].wait()
 
 
-def rim_kernel(*refs):
-    *tiles, to_core, to_chip = refs
+def rim_kernel(n_col, per_sample, *refs):
+    tiles, (*parts, to_core, to_chip, joined, rims) = refs[:n_col], refs[n_col:]
+    col = lax.axis_index("col")
     rows = tiles[0].shape[1]
+    lanes = to_core.shape[1]
+    used = rims.shape[1] * rims.shape[2]
     inner = jnp.where(lax.axis_index("row") % 2 == 1, rows - 1, 0)
-    for k, tile in enumerate(tiles):
-        to_core[k] = tile[0, inner]
-        to_chip[k] = tile[0, rows - 1 - inner]
-
-
-def join_kernel(*refs):
+    cols = tiles[0].shape[2]
+    rims[...] = jnp.zeros_like(rims)
+    for side, (row, out) in enumerate(((inner, to_core), (rows - 1 - inner, to_chip))):
+        for k, tile in enumerate(tiles):
+            rims[side, col ^ k, :cols] = pick(tile[0, row], col // per_sample)
+        flat = rims[side].reshape(used, -1).astype(BF16)
+        out[...] = jnp.zeros_like(out)
+        for part in range(flat.shape[1] // lanes):
+            out[part * used : (part + 1) * used] = flat[:, part * lanes : (part + 1) * lanes]
+    join_kernel([part.shape[0] for part in parts], *parts, joined)
+    joined[joined.shape[0] - 1] = to_chip[...]
+
+
+def join_kernel(counts, *refs):
     *parts, out = refs
     first = 0
-    for part in parts:
-        for j in range(part.shape[0]):
+    for part, count in zip(parts, counts):
+        for j in range(count):
             out[first + j] = part[j]
-        first += part.shape[0]
+        first += count
 
 
 def load_kernel(*refs):
@@ -167,29 +178,40 @@
     gate_ref[...] = sigma * (1.0 + z * (1.0 - sigma))
 
 
-def rim_conv_kernel(per_sample, *refs):
-    halo_core, halo_chip, conv, gate, shifts, conv_weight, out_weight, gz_ref, go_ref, rims = refs
-    col, core = lax.axis_index("col"), lax.axis_index("row") % 2
-    sample = col // per_sample
-    n_col, cols, _, channels = halo_core.shape
-    width = n_col * cols
-    rims[...] = jnp.zeros_like(rims)
-    for k in range(n_col):
-        rims[core, col ^ k, :cols] = pick(halo_core[k], sample)
-        rims[1 - core, col ^ k, :cols] = pick(halo_chip[k], sample)
+def rim_conv_kernel(halo_core, halo_last, halo_odd, conv, gate, *refs):
+    shifts, conv_weight, out_weight, gz_ref, go_ref = refs
+    col, row = lax.axis_index("col"), lax.axis_index("row")
+    core, chip = row % 2, row // 2
+    strip, channels = gz_ref.shape
+    lanes = go_ref.shape[1]
+    per_sample = out_weight.shape[0] // lanes
+    width = shifts.shape[1]
+    used = shifts.shape[2]
+    last = halo_last[halo_last.shape[0] - 1]
+    missing = jnp.logical_or(row == 1, row == lax.axis_size("row") - 2)
+    halo_chip = jnp.where(core == chip % 2, last, halo_odd[...])
+    halo_chip = jnp.where(missing, jnp.zeros_like(last), halo_chip)
+    inner = halo_core[...]
+    parts = channels // lanes
+
+    def spread(halo):
+        return jnp.concatenate([halo[p * used : (p + 1) * used] for p in range(parts)], 1)
+
+    rims = (
+        spread(jnp.where(core == 1, halo_chip, inner)),
+        spread(jnp.where(core == 1, inner, halo_chip)),
+    )
     edges = []
-    for side, a in ((0, 1), (1, -1)):
-        flat = rims[side].reshape(-1, channels).astype(BF16)
+    for flat, a in zip(rims, (1, -1)):
         edge = jnp.zeros((width, channels), F32)
         for b in (-1, 0, 1):
             window = dot(shifts[b + 1], flat).astype(BF16)
             edge = edge + dot(window, conv_weight[a + 1, b + 1], 1, 1)
         edges.append(edge)
-    between = jnp.zeros((conv.shape[0] - 2 * width, channels), F32)
+    between = jnp.zeros((strip - 2 * width, channels), F32)
     total = conv[...] + jnp.concatenate([edges[0], between, edges[1]], 0)
     grad_z = (total * gate[...]).astype(BF16)
     gz_ref[...] = grad_z
-    lanes = go_ref.shape[1]
     first = pl.multiple_of(col % per_sample * lanes, lanes)
     go_ref[...] = dot(grad_z, out_weight[pl.ds(first, lanes), :], 1, 1).astype(BF16)
 
@@ -297,6 +319,7 @@
 
 def output_kernel(per_sample, *refs):
     *parts, out = refs
+    parts = parts[::-1]
     rows, cols, samples, channels = out.shape
     padded = pad8(cols)
     sample = lax.axis_index("col") // per_sample
@@ -334,9 +357,11 @@
     def to_core(array):
         return lax.ppermute(array, "row", [(i, i ^ 1) for i in range(n_row)])
 
-    def to_next_chip(array):
-        edge = [(i, i + 3) for i in range(0, n_row - 2, 2)]
-        return lax.ppermute(array, "row", edge + [(j, i) for i, j in edge])
+    def to_odd_chip(array):
+        both = [(0, 1), (n_row - 2, n_row - 1)]
+        for i in range(2, n_row - 2, 4):
+            both += [(i, i + 3), (i + 1, i + 2)]
+        return lax.ppermute(array, "row", both + [(j, i) for i, j in both])
 
     def cells(array):
         return jnp.transpose(array, (1, 2, 0, 3))
@@ -371,9 +396,11 @@
         range(len(far)),
     )(*far)
 
-    def doubled(joined, received, *last):
-        parts = (joined, received, *last)
-        return call(join_kernel, held((sum(p.shape[0] for p in parts), strip, lanes), BF16))(*parts)
+    def doubled(*parts, counts=None):
+        counts = counts or [part.shape[0] for part in parts]
+        return call(
+            functools.partial(join_kernel, counts), held((sum(counts), strip, lanes), BF16)
+        )(*parts)
 
     distances = [chips >> (i + 1) for i in range(chips.bit_length() - 1)]
     offsets = [0]
@@ -382,14 +409,20 @@
     tiles, received, (shifts, rim_shifts, conv_weight, out_weight) = lax.optimization_barrier(
         (tiles, to_chip(kv, distances[0]), loaded)
     )
-    joined = doubled(kv, received)
-
-    rim = held((n_col, cols, samples, channels), BF16)
-    rim_core, rim_chip = call(rim_kernel, (rim, rim))(*tiles)
-    halo_chip, halo_core = to_next_chip(rim_chip), to_core(rim_core)
+    parts = (kv, received)
     for distance in distances[1:-1]:
-        joined = doubled(joined, to_chip(joined, distance))
-    received = to_chip(joined, distances[-1])
+        joined = doubled(*parts)
+        parts = (joined, to_chip(joined, distance))
+
+    rim = held((strip, lanes), BF16)
+    blocks = sum(part.shape[0] for part in parts)
+    rim_core, rim_chip, sent = call(
+        functools.partial(rim_kernel, n_col, per_sample),
+        (rim, rim, held((blocks + 1, strip, lanes), BF16)),
+        [pltpu.VMEM((2, n_col, padded, channels), F32)],
+    )(*tiles, *parts)
+    received = to_chip(sent, distances[-1])
+    halo_odd, halo_core = to_odd_chip(rim_chip), to_core(rim_core)
 
     whole = held((strip, channels), F32)
     conv, gate = call(
@@ -397,21 +430,20 @@
         (whole, whole),
         [pltpu.VMEM((n_col, rows, padded, channels), F32)] * 2,
     )(*tiles, shifts, conv_weight)
-    received, conv, halo_chip, halo_core = lax.optimization_barrier(
-        (received, conv, halo_chip, halo_core)
-    )
-    joined = doubled(joined, received, query[None])
-    received = to_core(joined)
+    received, conv, halo_odd, halo_core = lax.optimization_barrier(
+        (received, conv, halo_odd, halo_core)
+    )
+    joined = doubled(sent, received, query[None], counts=(blocks, blocks, 1))
+    other = to_core(joined)
     grad_z, grad_out = call(
-        functools.partial(rim_conv_kernel, per_sample),
+        rim_conv_kernel,
         (held((strip, channels), BF16), held((strip, lanes), BF16)),
-        [pltpu.VMEM((2, n_col, padded, channels), F32)],
-    )(halo_core, halo_chip, conv, gate, rim_shifts, conv_weight, out_weight)
+    )(halo_core, received, halo_odd, conv, gate, rim_shifts, conv_weight, out_weight)
 
     block = held((chips, pairs, strip, lanes), BF16)
     dkv_sent, dkv_kept, dq = call(
         functools.partial(attention_kernel, offsets), (block, block, held((strip, lanes), F32))
-    )(joined, received, grad_out)
+    )(joined, other, grad_out)
 
     sums = call(core_sum_kernel, [held((pairs, strip, lanes), BF16) for _ in range(chips)])(
         dkv_kept, to_core(dkv_sent)
@@ -424,7 +456,7 @@
     )(*parts, dq, grad_z, input_weight, jnp.asarray(tile_selector(rows, cols, n_col), BF16))
     grad_input = call(
         functools.partial(output_kernel, per_sample), held((rows, cols, samples, channels), BF16)
-    )(*[to_col(cut[k], k) for k in range(n_col)])
+    )(*[to_col(cut[k], k) for k in reversed(range(n_col))])
     return jnp.transpose(grad_input, (2, 0, 1, 3))
 
 

time: 35.6 us -> 34.2 us (0.961)
  starting transfers between devices: 18.4 us -> 16.8 us
    ppermute x5, waiting for transfers between devices: 2.29 us -> 4.84 us  [to_chip(): lax.ppermute(array, 'row', [(i, i ^ 2 * k + 1) for i in range(n_row)])]
    ppermute x1, starting transfers between devices: 2.22 us -> 0.27 us  [to_odd_chip(): return lax.ppermute(array, 'row', both + [(j, i) for i, j in both])]
    ppermute x1, waiting for transfers between devices: 1.64 us -> 0.01 us  [to_odd_chip(): return lax.ppermute(array, 'row', both + [(j, i) for i, j in both])]
    ppermute x8, waiting for transfers between devices: 4.24 us -> 3.58 us  [to_col(): return lax.ppermute(array, ('row', 'col'), pairs_of)]
    pallas_call x11 -> x10, Pallas kernels: 6.15 us -> 6.17 us  [run(): pl.pallas_call(kernel, out_shape=out_shape, in_specs=specs, out_specs=jax...]
where the time goes in v6:
time: 34.2 us; the launch traced here: 34 us
  starting transfers between devices  16.8 us (49%)
  waiting for transfers between devices  10.3 us (30%)
  Pallas kernels  6.17 us (18%)
  local copies, waits for them, and re-layouts  0.62 us (2%)
    ppermute x5, starting transfers between devices, to_chip(): lax.ppermute(array, 'row', [(i, i ^ 2 * k + 1) for i in range(n_row)])  8.97 us
    ppermute x8, starting transfers between devices, to_col(): return lax.ppermute(array, ('row', 'col'), pairs_of)  6.88 us
    pallas_call x10, Pallas kernels, run(): pl.pallas_call(kernel, out_shape=out_shape, in_specs=specs, out_specs=jax...  6.17 us
    ppermute x5, waiting for transfers between devices, to_chip(): lax.ppermute(array, 'row', [(i, i ^ 2 * k + 1) for i in range(n_row)])  4.84 us
    ppermute x8, waiting for transfers between devices, to_col(): return lax.ppermute(array, ('row', 'col'), pairs_of)  3.58 us
    ppermute x3, waiting for transfers between devices, to_core(): return lax.ppermute(array, 'row', [(i, i ^ 1) for i in range(n_row)])  1.84 us
    ppermute x3, starting transfers between devices, to_core(): return lax.ppermute(array, 'row', [(i, i ^ 1) for i in range(n_row)])  0.7 us
  transfers between devices with their start and end apart: 17, of which 8 were waited for; matrix products, arithmetic and copies ran while one was open for 0% of the time, Pallas kernels for 9%

profile of v6, /device:TPU:0, one launch (start us, length us, event | category | flops | bytes accessed | tf_op | source)
XLA Modules:
  0.0 34.0 jit_solution(256954024743378535)
XLA Ops:
  0.0 1.0 %shard_map.109 = (bf16[2,3,6,2,256]{4,3,2,1,0:T(2,128)(2,1)S(1)}, bf16[2,72,128]{2,1,0:T(8,128)(2,1)S(1)}, bf16[72,128]{1,0:T(8,128)(2,1)S(1)}) custom-call(bf16[3,6,2,256]{3,2,1,0:T(2,128)(2,1)} %bitcast.12, bf16[3,6,2,256]{3,2,1,0:T(2,128)(2,1)} %bitcast.13, bf16[2,64,72]{2,1,0:T(8,128)(2,1)} %bitcast.9, bf16[2,64,72]{2,1,0:T(8,128)(2,1)} %bitcast.10, ...), custom_call_target="tpu_custom_call" | custom-call | tf_op jit(solution)/shard_map/pallas_call | solution.py:35
  1.0 3.5 %collective-permute-start.4 = (bf16[2,72,128]{2,1,0:T(8,128)(2,1)S(1)}, bf16[2,72,128]{2,1,0:T(8,128)(2,1)S(1)}, u32[]{:S(2)}, u32[]{:S(2)}) collective-permute-start(bf16[2,72,128]{2,1,0:T(8,128)(2,1)S(1)} %get-tuple-element.44.refs_4_), channel_id=1, source_target_pairs={{0,20},{4,16},{8,28},{12,24},{16,4},{20,0},{24,12},{28,8},{1,21},{... | collective-permute-start | bytes 110600 | tf_op jit(solution)/shard_map/ppermute | solution.py:355
  4.5 2.7 %collective-permute-start.3 = (bf16[2,3,6,2,256]{4,3,2,1,0:T(2,128)(2,1)S(1)}, bf16[2,3,6,2,256]{4,3,2,1,0:T(2,128)(2,1)S(1)}, u32[]{:S(2)}, u32[]{:S(2)}) collective-permute-start(bf16[2,3,6,2,256]{4,3,2,1,0:T(2,128)(2,1)S(1)} %get-tuple-element.43), channel_id=1, source_target_pairs={{0,7},{1,6},{2,5},{3,4},{4,3},{5,2},{6,1},{7,0},{8,15},{9,14},{10,... | collective-permute-start | bytes 110600 | tf_op jit(solution)/shard_map/ppermute | solution.py:352
  7.3 0.0 collective-permute-start.2
  7.3 0.8 %collective-permute-start.1 = (bf16[2,3,6,2,256]{4,3,2,1,0:T(2,128)(2,1)S(1)}, bf16[2,3,6,2,256]{4,3,2,1,0:T(2,128)(2,1)S(1)}, u32[]{:S(2)}, u32[]{:S(2)}) collective-permute-start(bf16[2,3,6,2,256]{4,3,2,1,0:T(2,128)(2,1)S(1)} %get-tuple-element.43), channel_id=1, source_target_pairs={{0,5},{1,4},{2,7},{3,6},{4,1},{5,0},{6,3},{7,2},{8,13},{9,12},{10,... | collective-permute-start | bytes 110600 | tf_op jit(solution)/shard_map/ppermute | solution.py:352
  8.0 0.0 collective-permute-start
  8.0 1.4 %shard_map.110 = (bf16[3,72,96]{2,1,0:T(8,128)(2,1)S(1)}, bf16[3,24,32]{2,1,0:T(8,128)(2,1)S(1)}, bf16[3,3,256,256]{3,2,1,0:T(8,128)(2,1)S(1)}, bf16[256,256]{1,0:T(8,128)(2,1)S(1)}) custom-call(bf16[3,72,96]{2,1,0:T(8,128)(2,1)} %constant.6.clone.refs_0_, bf16[3,24,32]{2,1,0:T(8,128)(2,1)} %constant.7.clone.refs_1_, bf16[3,3,256,256]{3,2,1,0:T(8,128)(2,1)} %refs_2_.1, ...), custom_call_target="tpu_custom_call" | custom-call | tf_op jit(solution)/shard_map/pallas_call | solution.py:35
  9.4 0.0 collective-permute-done.4.refs_5_
  9.4 0.0 collective-permute-done.3.refs_3_
  9.4 1.6 %collective-permute-done.2.refs_2_ = bf16[2,3,6,2,256]{4,3,2,1,0:T(2,128)(2,1)S(1)} collective-permute-done((bf16[2,3,6,2,256]{4,3,2,1,0:T(2,128)(2,1)S(1)}, bf16[2,3,6,2,256]{4,3,2,1,0:T(2,128)(2,1)S(1)}, u32[]{:S(2)}, u32[]{:S(2)}) %collective-permute-start.2) | collective-permute-done | bytes 36896 | tf_op jit(solution)/shard_map/ppermute | solution.py:352
  11.0 0.0 collective-permute-done.1.refs_1_
  11.0 0.0 collective-permute-done.refs_0_
  11.0 0.2 shard_map.111
  11.2 1.5 %collective-permute-start.5 = (bf16[5,72,128]{2,1,0:T(8,128)(2,1)S(1)}, bf16[5,72,128]{2,1,0:T(8,128)(2,1)S(1)}, u32[]{:S(2)}, u32[]{:S(2)}) collective-permute-start(bf16[5,72,128]{2,1,0:T(8,128)(2,1)S(1)} %get-tuple-element.54.refs_0_), channel_id=1, source_target_pairs={{0,12},{4,8},{8,4},{12,0},{16,28},{20,24},{24,20},{28,16},{1,13},{... | collective-permute-start | bytes 276488 | tf_op jit(solution)/shard_map/ppermute | solution.py:355
  12.7 0.3 collective-permute-start.6
  13.0 0.2 collective-permute-start.7
  13.2 1.2 %shard_map.112 = (f32[72,256]{1,0:T(8,128)S(1)}, f32[72,256]{1,0:T(8,128)S(1)}) custom-call(bf16[2,3,6,2,256]{4,3,2,1,0:T(2,128)(2,1)S(1)} %collective-permute-done.refs_0_, bf16[2,3,6,2,256]{4,3,2,1,0:T(2,128)(2,1)S(1)} %collective-permute-done.1.refs_1_, bf16[2,3,6,2,256]{4,3,2,1,0:T(2,128)(2,1)S(1)} %collective-permute-done.2.refs_2_, ...), custom_call_target="tpu_custom_call" | custom-call | tf_op jit(solution)/shard_map/pallas_call | solution.py:35
  14.4 0.0 collective-permute-done.6.halo_odd
  14.4 0.0 collective-permute-done.7.halo_core
  14.4 1.5 %collective-permute-done.5.refs_1_.halo_last = bf16[5,72,128]{2,1,0:T(8,128)(2,1)S(1)} collective-permute-done((bf16[5,72,128]{2,1,0:T(8,128)(2,1)S(1)}, bf16[5,72,128]{2,1,0:T(8,128)(2,1)S(1)}, u32[]{:S(2)}, u32[]{:S(2)}) %collective-permute-start.5) | collective-permute-done | bytes 92192 | tf_op jit(solution)/shard_map/ppermute | solution.py:355
  15.9 0.0 copy-start
  15.9 0.0 copy-start.1
  15.9 0.2 collective-permute-start.8
  16.2 0.6 %shard_map.114 = (bf16[72,256]{1,0:T(8,128)(2,1)S(1)}, bf16[72,128]{1,0:T(8,128)(2,1)S(1)}) custom-call(bf16[72,128]{1,0:T(8,128)(2,1)S(1)} %collective-permute-done.7.halo_core, bf16[5,72,128]{2,1,0:T(8,128)(2,1)S(1)} %collective-permute-done.5.refs_1_.halo_last, bf16[72,128]{1,0:T(8,128)(2,1)S(1)} %collective-permute-done.6.halo_odd, ...), custom_call_target="tpu_custom_call" | custom-call | tf_op jit(solution)/shard_map/pallas_call | solution.py:35
  16.8 0.6 %collective-permute-done.8.kv_kept = bf16[9,72,128]{2,1,0:T(8,128)(2,1)S(1)} collective-permute-done((bf16[9,72,128]{2,1,0:T(8,128)(2,1)S(1)}, bf16[9,72,128]{2,1,0:T(8,128)(2,1)S(1)}, u32[]{:S(2)}, u32[]{:S(2)}) %collective-permute-start.8) | collective-permute-done | bytes 165920 | tf_op jit(solution)/shard_map/ppermute | solution.py:358
  17.4 1.4 %shard_map.115 = (bf16[4,2,72,128]{3,2,1,0:T(8,128)(2,1)S(1)}, bf16[4,2,72,128]{3,2,1,0:T(8,128)(2,1)S(1)}, f32[72,128]{1,0:T(8,128)S(1)}) custom-call(bf16[9,72,128]{2,1,0:T(8,128)(2,1)S(1)} %shard_map.113.kv_sent, bf16[9,72,128]{2,1,0:T(8,128)(2,1)S(1)} %collective-permute-done.8.kv_kept, bf16[72,128]{1,0:T(8,128)(2,1)S(1)} %get-tuple-element.68.go_ref), custom_call_target="tpu_custom_call" | custom-call | tf_op jit(solution)/shard_map/pallas_call | solution.py:35
  18.8 0.2 collective-permute-start.9
  19.0 1.2 %collective-permute-done.9.received = bf16[4,2,72,128]{3,2,1,0:T(8,128)(2,1)S(1)} collective-permute-done((bf16[4,2,72,128]{3,2,1,0:T(8,128)(2,1)S(1)}, bf16[4,2,72,128]{3,2,1,0:T(8,128)(2,1)S(1)}, u32[]{:S(2)}, u32[]{:S(2)}) %collective-permute-start.9) | collective-permute-done | bytes 147488 | tf_op jit(solution)/shard_map/ppermute | solution.py:358
  20.3 1.1 %collective-permute-start.10 = (bf16[2,72,128]{2,1,0:T(8,128)(2,1)S(1)}, bf16[2,72,128]{2,1,0:T(8,128)(2,1)S(1)}, u32[]{:S(2)}, u32[]{:S(2)}) collective-permute-start(bf16[2,72,128]{2,1,0:T(8,128)(2,1)S(1)} %get-tuple-element.71), channel_id=1, source_target_pairs={{0,28},{4,24},{8,20},{12,16},{16,12},{20,8},{24,4},{28,0},{1,29},{... | collective-permute-start | bytes 110600 | tf_op jit(solution)/shard_map/ppermute | solution.py:355
  21.4 1.7 %collective-permute-start.11 = (bf16[2,72,128]{2,1,0:T(8,128)(2,1)S(1)}, bf16[2,72,128]{2,1,0:T(8,128)(2,1)S(1)}, u32[]{:S(2)}, u32[]{:S(2)}) collective-permute-start(bf16[2,72,128]{2,1,0:T(8,128)(2,1)S(1)} %get-tuple-element.72), channel_id=1, source_target_pairs={{0,20},{4,16},{8,28},{12,24},{16,4},{20,0},{24,12},{28,8},{1,21},{... | collective-permute-start | bytes 110600 | tf_op jit(solution)/shard_map/ppermute | solution.py:355
  23.1 1.1 %collective-permute-start.12 = (bf16[2,72,128]{2,1,0:T(8,128)(2,1)S(1)}, bf16[2,72,128]{2,1,0:T(8,128)(2,1)S(1)}, u32[]{:S(2)}, u32[]{:S(2)}) collective-permute-start(bf16[2,72,128]{2,1,0:T(8,128)(2,1)S(1)} %get-tuple-element.73), channel_id=1, source_target_pairs={{0,12},{4,8},{8,4},{12,0},{16,28},{20,24},{24,20},{28,16},{1,13},{... | collective-permute-start | bytes 110600 | tf_op jit(solution)/shard_map/ppermute | solution.py:355
  24.2 1.5 %collective-permute-done.10.refs_0_ = bf16[2,72,128]{2,1,0:T(8,128)(2,1)S(1)} collective-permute-done((bf16[2,72,128]{2,1,0:T(8,128)(2,1)S(1)}, bf16[2,72,128]{2,1,0:T(8,128)(2,1)S(1)}, u32[]{:S(2)}, u32[]{:S(2)}) %collective-permute-start.10) | collective-permute-done | bytes 36896 | tf_op jit(solution)/shard_map/ppermute | solution.py:355
  25.7 1.9 %collective-permute-done.11.refs_1_ = bf16[2,72,128]{2,1,0:T(8,128)(2,1)S(1)} collective-permute-done((bf16[2,72,128]{2,1,0:T(8,128)(2,1)S(1)}, bf16[2,72,128]{2,1,0:T(8,128)(2,1)S(1)}, u32[]{:S(2)}, u32[]{:S(2)}) %collective-permute-start.11) | collective-permute-done | bytes 36896 | tf_op jit(solution)/shard_map/ppermute | solution.py:355
  27.6 0.0 collective-permute-done.12.refs_2_
  27.6 0.0 copy-done
  27.6 0.0 copy-done.1
  27.6 0.4 %shard_map.117 = (bf16[24,256]{1,0:T(8,128)(2,1)S(1)}, bf16[24,256]{1,0:T(8,128)(2,1)S(1)}, bf16[24,256]{1,0:T(8,128)(2,1)S(1)}, bf16[24,256]{1,0:T(8,128)(2,1)S(1)}) custom-call(bf16[2,72,128]{2,1,0:T(8,128)(2,1)S(1)} %collective-permute-done.10.refs_0_, bf16[2,72,128]{2,1,0:T(8,128)(2,1)S(1)} %collective-permute-done.11.refs_1_, ...), custom_call_target="tpu_custom_call" | custom-call | tf_op jit(solution)/shard_map/pallas_call | solution.py:35
  28.0 0.7 %collective-permute-start.13 = (bf16[24,256]{1,0:T(8,128)(2,1)S(1)}, bf16[24,256]{1,0:T(8,128)(2,1)S(1)}, u32[]{:S(2)}, u32[]{:S(2)}) collective-permute-start(bf16[24,256]{1,0:T(8,128)(2,1)S(1)} %get-tuple-element.77), channel_id=1, source_target_pairs={{0,7},{1,6},{2,5},{3,4},{4,3},{5,2},{6,1},{7,0},{8,15},{9,14},{10,... | collective-permute-start | bytes 36872 | tf_op jit(solution)/shard_map/ppermute | solution.py:352
  28.7 1.5 %collective-permute-start.14 = (bf16[24,256]{1,0:T(8,128)(2,1)S(1)}, bf16[24,256]{1,0:T(8,128)(2,1)S(1)}, u32[]{:S(2)}, u32[]{:S(2)}) collective-permute-start(bf16[24,256]{1,0:T(8,128)(2,1)S(1)} %get-tuple-element.78), channel_id=1, source_target_pairs={{0,6},{1,7},{2,4},{3,5},{4,2},{5,3},{6,0},{7,1},{8,14},{9,15},{10,... | collective-permute-start | bytes 36872 | tf_op jit(solution)/shard_map/ppermute | solution.py:352
  30.2 0.7 %collective-permute-start.15 = (bf16[24,256]{1,0:T(8,128)(2,1)S(1)}, bf16[24,256]{1,0:T(8,128)(2,1)S(1)}, u32[]{:S(2)}, u32[]{:S(2)}) collective-permute-start(bf16[24,256]{1,0:T(8,128)(2,1)S(1)} %get-tuple-element.79), channel_id=1, source_target_pairs={{0,5},{1,4},{2,7},{3,6},{4,1},{5,0},{6,3},{7,2},{8,13},{9,12},{10,... | collective-permute-start | bytes 36872 | tf_op jit(solution)/shard_map/ppermute | solution.py:352
  30.9 0.5 %collective-permute-start.16 = (bf16[24,256]{1,0:T(8,128)(2,1)S(1)}, bf16[24,256]{1,0:T(8,128)(2,1)S(1)}, u32[]{:S(2)}, u32[]{:S(2)}) collective-permute-start(bf16[24,256]{1,0:T(8,128)(2,1)S(1)} %get-tuple-element.80), channel_id=1, source_target_pairs={{0,4},{1,5},{2,6},{3,7},{4,0},{5,1},{6,2},{7,3},{8,12},{9,13},{10,... | collective-permute-start | bytes 36872 | tf_op jit(solution)/shard_map/ppermute | solution.py:352
  31.4 0.7 %collective-permute-done.13.refs_0_ = bf16[24,256]{1,0:T(8,128)(2,1)S(1)} collective-permute-done((bf16[24,256]{1,0:T(8,128)(2,1)S(1)}, bf16[24,256]{1,0:T(8,128)(2,1)S(1)}, u32[]{:S(2)}, u32[]{:S(2)}) %collective-permute-start.13) | collective-permute-done | bytes 12320 | tf_op jit(solution)/shard_map/ppermute | solution.py:352
  32.1 0.0 collective-permute-done.14.refs_1_
  32.1 1.3 %collective-permute-done.15.refs_2_ = bf16[24,256]{1,0:T(8,128)(2,1)S(1)} collective-permute-done((bf16[24,256]{1,0:T(8,128)(2,1)S(1)}, bf16[24,256]{1,0:T(8,128)(2,1)S(1)}, u32[]{:S(2)}, u32[]{:S(2)}) %collective-permute-start.15) | collective-permute-done | bytes 12320 | tf_op jit(solution)/shard_map/ppermute | solution.py:352
  33.3 0.0 collective-permute-done.16.refs_3_
  33.4 0.6 %copy.12 = bf16[2,3,6,256]{3,0,2,1:T(2,128)(2,1)} copy(bf16[2,3,6,256]{3,0,2,1:T(2,128)(2,1)S(1)} %bitcast.7) | data formatting | bytes 36864
  (3 shorter events, 0.1 us)
Async XLA Ops:
  1.0 8.4 %collective-permute-start.4 = (bf16[2,72,128]{2,1,0:T(8,128)(2,1)S(1)}, bf16[2,72,128]{2,1,0:T(8,128)(2,1)S(1)}, u32[]{:S(2)}, u32[]{:S(2)}) collective-permute-start(bf16[2,72,128]{2,1,0:T(8,128)(2,1)S(1)} %get-tuple-element.44.refs_4_), channel_id=1, source_target_pairs={{0,20},{4,16},{8,28},{12,24},{16,4},{20,0},{24,12},{28,8},{1,21},{... | collective-permute-start | bytes 110600 | tf_op jit(solution)/shard_map/ppermute | solution.py:355
  4.5 4.9 %collective-permute-start.3 = (bf16[2,3,6,2,256]{4,3,2,1,0:T(2,128)(2,1)S(1)}, bf16[2,3,6,2,256]{4,3,2,1,0:T(2,128)(2,1)S(1)}, u32[]{:S(2)}, u32[]{:S(2)}) collective-permute-start(bf16[2,3,6,2,256]{4,3,2,1,0:T(2,128)(2,1)S(1)} %get-tuple-element.43), channel_id=1, source_target_pairs={{0,7},{1,6},{2,5},{3,4},{4,3},{5,2},{6,1},{7,0},{8,15},{9,14},{10,... | collective-permute-start | bytes 110600 | tf_op jit(solution)/shard_map/ppermute | solution.py:352
  7.3 3.8 %collective-permute-start.2 = (bf16[2,3,6,2,256]{4,3,2,1,0:T(2,128)(2,1)S(1)}, bf16[2,3,6,2,256]{4,3,2,1,0:T(2,128)(2,1)S(1)}, u32[]{:S(2)}, u32[]{:S(2)}) collective-permute-start(bf16[2,3,6,2,256]{4,3,2,1,0:T(2,128)(2,1)S(1)} %get-tuple-element.43), channel_id=1, source_target_pairs={{0,6},{1,7},{2,4},{3,5},{4,2},{5,3},{6,0},{7,1},{8,14},{9,15},{10,... | collective-permute-start | bytes 110600 | tf_op jit(solution)/shard_map/ppermute | solution.py:352
  7.3 3.8 %collective-permute-start.1 = (bf16[2,3,6,2,256]{4,3,2,1,0:T(2,128)(2,1)S(1)}, bf16[2,3,6,2,256]{4,3,2,1,0:T(2,128)(2,1)S(1)}, u32[]{:S(2)}, u32[]{:S(2)}) collective-permute-start(bf16[2,3,6,2,256]{4,3,2,1,0:T(2,128)(2,1)S(1)} %get-tuple-element.43), channel_id=1, source_target_pairs={{0,5},{1,4},{2,7},{3,6},{4,1},{5,0},{6,3},{7,2},{8,13},{9,12},{10,... | collective-permute-start | bytes 110600 | tf_op jit(solution)/shard_map/ppermute | solution.py:352
  8.0 3.0 %collective-permute-start = (bf16[2,3,6,2,256]{4,3,2,1,0:T(2,128)(2,1)S(1)}, bf16[2,3,6,2,256]{4,3,2,1,0:T(2,128)(2,1)S(1)}, u32[]{:S(2)}, u32[]{:S(2)}) collective-permute-start(bf16[2,3,6,2,256]{4,3,2,1,0:T(2,128)(2,1)S(1)} %get-tuple-element.43), channel_id=1, source_target_pairs={{0,4},{1,5},{2,6},{3,7},{4,0},{5,1},{6,2},{7,3},{8,12},{9,13},{10,... | collective-permute-start | bytes 110600 | tf_op jit(solution)/shard_map/ppermute | solution.py:352
  11.2 4.7 %collective-permute-start.5 = (bf16[5,72,128]{2,1,0:T(8,128)(2,1)S(1)}, bf16[5,72,128]{2,1,0:T(8,128)(2,1)S(1)}, u32[]{:S(2)}, u32[]{:S(2)}) collective-permute-start(bf16[5,72,128]{2,1,0:T(8,128)(2,1)S(1)} %get-tuple-element.54.refs_0_), channel_id=1, source_target_pairs={{0,12},{4,8},{8,4},{12,0},{16,28},{20,24},{24,20},{28,16},{1,13},{... | collective-permute-start | bytes 276488 | tf_op jit(solution)/shard_map/ppermute | solution.py:355
  12.7 1.7 %collective-permute-start.6 = (bf16[72,128]{1,0:T(8,128)(2,1)S(1)}, bf16[72,128]{1,0:T(8,128)(2,1)S(1)}, u32[]{:S(2)}, u32[]{:S(2)}) collective-permute-start(bf16[72,128]{1,0:T(8,128)(2,1)S(1)} %get-tuple-element.58), channel_id=1, source_target_pairs={{0,4},{24,28},{8,20},{12,16},{4,0},{28,24},{20,8},{16,12},{1,5},{2... | collective-permute-start | bytes 55304 | tf_op jit(solution)/shard_map/ppermute | solution.py:364
  13.0 1.4 %collective-permute-start.7 = (bf16[72,128]{1,0:T(8,128)(2,1)S(1)}, bf16[72,128]{1,0:T(8,128)(2,1)S(1)}, u32[]{:S(2)}, u32[]{:S(2)}) collective-permute-start(bf16[72,128]{1,0:T(8,128)(2,1)S(1)} %get-tuple-element.59), channel_id=1, source_target_pairs={{0,4},{4,0},{8,12},{12,8},{16,20},{20,16},{24,28},{28,24},{1,5},{5... | collective-permute-start | bytes 55304 | tf_op jit(solution)/shard_map/ppermute | solution.py:358
  15.9 11.7 %copy-start = (bf16[256,768]{1,0:T(8,128)(2,1)S(1)}, bf16[256,768]{1,0:T(8,128)(2,1)}, u32[]{:S(2)}) copy-start(bf16[256,768]{1,0:T(8,128)(2,1)} %refs_6_.1) | copy-start | bytes 1179652
  15.9 11.6 %copy-start.1 = (bf16[4,24,72]{2,1,0:T(8,128)(2,1)S(1)}, bf16[4,24,72]{2,1,0:T(8,128)(2,1)}, u32[]{:S(2)}) copy-start(bf16[4,24,72]{2,1,0:T(8,128)(2,1)} %constant.8.clone.refs_7_) | copy-start | bytes 41476
  15.9 1.5 %collective-permute-start.8 = (bf16[9,72,128]{2,1,0:T(8,128)(2,1)S(1)}, bf16[9,72,128]{2,1,0:T(8,128)(2,1)S(1)}, u32[]{:S(2)}, u32[]{:S(2)}) collective-permute-start(bf16[9,72,128]{2,1,0:T(8,128)(2,1)S(1)} %shard_map.113.kv_sent), channel_id=1, source_target_pairs={{0,4},{4,0},{8,12},{12,8},{16,20},{20,16},{24,28},{28,24},{1,5},{5... | collective-permute-start | bytes 497672 | tf_op jit(solution)/shard_map/ppermute | solution.py:358
  18.8 1.4 %collective-permute-start.9 = (bf16[4,2,72,128]{3,2,1,0:T(8,128)(2,1)S(1)}, bf16[4,2,72,128]{3,2,1,0:T(8,128)(2,1)S(1)}, u32[]{:S(2)}, u32[]{:S(2)}) collective-permute-start(bf16[4,2,72,128]{3,2,1,0:T(8,128)(2,1)S(1)} %get-tuple-element.70), channel_id=1, source_target_pairs={{0,4},{4,0},{8,12},{12,8},{16,20},{20,16},{24,28},{28,24},{1,5},{5... | collective-permute-start | bytes 442376 | tf_op jit(solution)/shard_map/ppermute | solution.py:358
  20.3 5.4 %collective-permute-start.10 = (bf16[2,72,128]{2,1,0:T(8,128)(2,1)S(1)}, bf16[2,72,128]{2,1,0:T(8,128)(2,1)S(1)}, u32[]{:S(2)}, u32[]{:S(2)}) collective-permute-start(bf16[2,72,128]{2,1,0:T(8,128)(2,1)S(1)} %get-tuple-element.71), channel_id=1, source_target_pairs={{0,28},{4,24},{8,20},{12,16},{16,12},{20,8},{24,4},{28,0},{1,29},{... | collective-permute-start | bytes 110600 | tf_op jit(solution)/shard_map/ppermute | solution.py:355
  21.4 6.2 %collective-permute-start.11 = (bf16[2,72,128]{2,1,0:T(8,128)(2,1)S(1)}, bf16[2,72,128]{2,1,0:T(8,128)(2,1)S(1)}, u32[]{:S(2)}, u32[]{:S(2)}) collective-permute-start(bf16[2,72,128]{2,1,0:T(8,128)(2,1)S(1)} %get-tuple-element.72), channel_id=1, source_target_pairs={{0,20},{4,16},{8,28},{12,24},{16,4},{20,0},{24,12},{28,8},{1,21},{... | collective-permute-start | bytes 110600 | tf_op jit(solution)/shard_map/ppermute | solution.py:355
  23.1 4.5 %collective-permute-start.12 = (bf16[2,72,128]{2,1,0:T(8,128)(2,1)S(1)}, bf16[2,72,128]{2,1,0:T(8,128)(2,1)S(1)}, u32[]{:S(2)}, u32[]{:S(2)}) collective-permute-start(bf16[2,72,128]{2,1,0:T(8,128)(2,1)S(1)} %get-tuple-element.73), channel_id=1, source_target_pairs={{0,12},{4,8},{8,4},{12,0},{16,28},{20,24},{24,20},{28,16},{1,13},{... | collective-permute-start | bytes 110600 | tf_op jit(solution)/shard_map/ppermute | solution.py:355
  28.0 4.1 %collective-permute-start.13 = (bf16[24,256]{1,0:T(8,128)(2,1)S(1)}, bf16[24,256]{1,0:T(8,128)(2,1)S(1)}, u32[]{:S(2)}, u32[]{:S(2)}) collective-permute-start(bf16[24,256]{1,0:T(8,128)(2,1)S(1)} %get-tuple-element.77), channel_id=1, source_target_pairs={{0,7},{1,6},{2,5},{3,4},{4,3},{5,2},{6,1},{7,0},{8,15},{9,14},{10,... | collective-permute-start | bytes 36872 | tf_op jit(solution)/shard_map/ppermute | solution.py:352
  28.7 3.4 %collective-permute-start.14 = (bf16[24,256]{1,0:T(8,128)(2,1)S(1)}, bf16[24,256]{1,0:T(8,128)(2,1)S(1)}, u32[]{:S(2)}, u32[]{:S(2)}) collective-permute-start(bf16[24,256]{1,0:T(8,128)(2,1)S(1)} %get-tuple-element.78), channel_id=1, source_target_pairs={{0,6},{1,7},{2,4},{3,5},{4,2},{5,3},{6,0},{7,1},{8,14},{9,15},{10,... | collective-permute-start | bytes 36872 | tf_op jit(solution)/shard_map/ppermute | solution.py:352
  30.2 3.1 %collective-permute-start.15 = (bf16[24,256]{1,0:T(8,128)(2,1)S(1)}, bf16[24,256]{1,0:T(8,128)(2,1)S(1)}, u32[]{:S(2)}, u32[]{:S(2)}) collective-permute-start(bf16[24,256]{1,0:T(8,128)(2,1)S(1)} %get-tuple-element.79), channel_id=1, source_target_pairs={{0,5},{1,4},{2,7},{3,6},{4,1},{5,0},{6,3},{7,2},{8,13},{9,12},{10,... | collective-permute-start | bytes 36872 | tf_op jit(solution)/shard_map/ppermute | solution.py:352
  30.9 2.5 %collective-permute-start.16 = (bf16[24,256]{1,0:T(8,128)(2,1)S(1)}, bf16[24,256]{1,0:T(8,128)(2,1)S(1)}, u32[]{:S(2)}, u32[]{:S(2)}) collective-permute-start(bf16[24,256]{1,0:T(8,128)(2,1)S(1)} %get-tuple-element.80), channel_id=1, source_target_pairs={{0,4},{1,5},{2,6},{3,7},{4,0},{5,1},{6,2},{7,3},{8,12},{9,13},{10,... | collective-permute-start | bytes 36872 | tf_op jit(solution)/shard_map/ppermute | solution.py:352

commit v7 on v6

--- a/solution.py
+++ b/solution.py
@@ -36,7 +36,14 @@
             kernel,
             out_shape=out_shape,
             in_specs=specs,
-            out_specs=jax.tree.map(lambda _: pl.BlockSpec(memory_space=pltpu.VMEM), out_shape),
+            out_specs=jax.tree.map(
+                lambda out: pl.BlockSpec(
+                    memory_space=pltpu.HBM
+                    if getattr(out, "memory_space", None) == pltpu.HBM
+                    else pltpu.VMEM
+                ),
+                out_shape,
+            ),
             scratch_shapes=list(scratch),
             compiler_params=pltpu.CompilerParams(vmem_limit_bytes=VMEM_BYTES),
         )(*operands)
@@ -231,29 +238,33 @@
         chunks.append((kv_sent, dkv_kept if even else dkv_sent, j, offset))
         chunks.append((kv_kept, dkv_sent if even else dkv_kept, j, offset))
 
-    grad_query = []
-    for head in (0, 1):
-        ask, cot = asked[head], cotangent[head]
-
-        def finish(kv, probs, probs_grad, row_dot):
-            grad_scores = (probs * (probs_grad - row_dot)).astype(BF16)
-            dkv = dot(grad_scores, ask) + dot(probs.astype(BF16), cot)
-            return dkv.astype(BF16), dot(grad_scores, kv, 0, 0)
-
-        total = jnp.zeros((strip, lanes), F32)
-        if len(chunks) <= UNROLLED_CHUNKS:
-            scores = [dot(src[2 * j + head], ask, 1, 1) for src, _, j, _ in chunks]
-            top = jnp.max(functools.reduce(jnp.maximum, scores), axis=0, keepdims=True)
-            exps = [jnp.exp(s - top) for s in scores]
-            scale = 1.0 / jnp.sum(sum(exps), axis=0, keepdims=True)
-            probs = [e * scale for e in exps]
-            probs_grads = [dot(src[2 * j + head], cot, 1, 1) for src, _, j, _ in chunks]
-            weighted = sum(p * g for p, g in zip(probs, probs_grads))
-            row_dot = jnp.sum(weighted, axis=0, keepdims=True)
-            for (src, dst, j, offset), p, g in zip(chunks, probs, probs_grads):
-                dst[offset, head], dq = finish(src[2 * j + head], p, g, row_dot)
-                total = total + dq
-        else:
+    heads = (0, 1)
+    if len(chunks) <= UNROLLED_CHUNKS:
+        kvs = [
+            jnp.concatenate([src[2 * j + h].astype(F32) for src, _, j, _ in chunks], 0).astype(BF16)
+            for h in heads
+        ]
+        scores = [dot(kvs[h], asked[h], 1, 1) for h in heads]
+        probs_grads = [dot(kvs[h], cotangent[h], 1, 1) for h in heads]
+        exps = [jnp.exp(s - jnp.max(s, axis=0, keepdims=True)) for s in scores]
+        scales = [1.0 / jnp.sum(e, axis=0, keepdims=True) for e in exps]
+        row_dots = [
+            jnp.sum(e * g, axis=0, keepdims=True) * s for e, g, s in zip(exps, probs_grads, scales)
+        ]
+        probs = [e * s for e, s in zip(exps, scales)]
+        grad_scores = [
+            (p * (g - r)).astype(BF16) for p, g, r in zip(probs, probs_grads, row_dots)
+        ]
+        grad_query = [dot(grad_scores[h], kvs[h], 0, 0) for h in heads]
+        for h in heads:
+            given = jnp.concatenate([grad_scores[h], probs[h].astype(BF16)], 1)
+            dkv = dot(given, jnp.concatenate([asked[h], cotangent[h]], 0))
+            for i, (_, dst, _, offset) in enumerate(chunks):
+                dst[offset, h] = dkv[i * strip : (i + 1) * strip].astype(BF16)
+    else:
+        grad_query = []
+        for head in heads:
+            ask, cot = asked[head], cotangent[head]
 
             def gather(kv, carry):
                 top, norm, weighted = carry
@@ -279,12 +290,15 @@
                 )
             top, norm, weighted = stats
             scale = 1.0 / norm
+            total = jnp.zeros((strip, lanes), F32)
             for src, dst, j, offset in chunks:
                 kv = src[2 * j + head]
                 probs = jnp.exp(dot(kv, ask, 1, 1) - top) * scale
-                dst[offset, head], dq = finish(kv, probs, dot(kv, cot, 1, 1), weighted * scale)
-                total = total + dq
-        grad_query.append(total)
+                grad_scores = (probs * (dot(kv, cot, 1, 1) - weighted * scale)).astype(BF16)
+                dkv = dot(grad_scores, ask) + dot(probs.astype(BF16), cot)
+                dst[offset, head] = dkv.astype(BF16)
+                total = total + dot(grad_scores, kv, 0, 0)
+            grad_query.append(total)
     dq_ref[...] = jnp.where(low, grad_query[1], grad_query[0]) * factor
 
 
@@ -294,6 +308,7 @@
 
 
 def project_kernel(n_col, per_sample, *refs):
+    *refs, cut = refs
     n_in = len(refs) - n_col
     *parts, dq_ref, gz_ref, input_weight, tiles = refs[:n_in]
     outs = refs[n_in:]
@@ -312,13 +327,13 @@
         first = pl.multiple_of(kind * channels + part * lanes, lanes)
         weight = input_weight[:, pl.ds(first, lanes)]
         grad = grad + dot(value.astype(BF16), weight, 1, 1)
-    grad = grad.astype(BF16)
+    cut[...] = dot(tiles[...], grad.astype(BF16)).reshape(cut.shape)
     for k, out in enumerate(outs):
-        out[...] = dot(tiles[col ^ k], grad).astype(BF16)
+        out[...] = cut[col ^ k].astype(BF16)
 
 
 def output_kernel(per_sample, *refs):
-    *parts, out = refs
+    *parts, far_out, out, sem = refs
     parts = parts[::-1]
     rows, cols, samples, channels = out.shape
     padded = pad8(cols)
@@ -333,6 +348,9 @@
             )
             cells = jnp.where(place == (sample ^ group), total[:, None, :], cells)
         out[i] = cells.astype(BF16)
+    copy = pltpu.make_async_copy(out, far_out, sem)
+    copy.start()
+    copy.wait()
 
 
 def shards(
@@ -450,12 +468,16 @@
     )
     parts = [to_chip(sums[k], k) for k in reversed(range(1, chips))] + [sums[0]]
 
+    selected = tile_selector(rows, cols, n_col).reshape(n_col * rows * padded, -1)
     cut = call(
         functools.partial(project_kernel, n_col, per_sample),
         [held((rows * padded, channels), BF16)] * n_col,
-    )(*parts, dq, grad_z, input_weight, jnp.asarray(tile_selector(rows, cols, n_col), BF16))
+        [pltpu.VMEM((n_col, rows * padded, channels), F32)],
+    )(*parts, dq, grad_z, input_weight, jnp.asarray(selected, BF16))
     grad_input = call(
-        functools.partial(output_kernel, per_sample), held((rows, cols, samples, channels), BF16)
+        functools.partial(output_kernel, per_sample),
+        pltpu.HBM((rows, cols, samples, channels), BF16),
+        [pltpu.VMEM((rows, cols, samples, channels), BF16), pltpu.SemaphoreType.DMA],
     )(*[to_col(cut[k], k) for k in reversed(range(n_col))])
     return jnp.transpose(grad_input, (2, 0, 1, 3))
 

time: 34.2 us -> 33.7 us (0.985)
  local copies, waits for them, and re-layouts: 0.62 us -> 0.01 us
    unnamed x5 -> x4, local copies, waits for them, and re-layouts: 0.62 us -> 0.01 us
where the time goes in v7:
time: 33.7 us; the launch traced here: 33.5 us
  starting transfers between devices  16.8 us (50%)
  waiting for transfers between devices  10.3 us (31%)
  Pallas kernels  6.32 us (19%)
    ppermute x5, starting transfers between devices, to_chip(): lax.ppermute(array, 'row', [(i, i ^ 2 * k + 1) for i in range(n_row)])  8.96 us
    ppermute x8, starting transfers between devices, to_col(): return lax.ppermute(array, ('row', 'col'), pairs_of)  6.88 us
    pallas_call x10, Pallas kernels, run(): pl.pallas_call(kernel, out_shape=out_shape, in_specs=specs, out_specs=jax...  6.32 us
    ppermute x5, waiting for transfers between devices, to_chip(): lax.ppermute(array, 'row', [(i, i ^ 2 * k + 1) for i in range(n_row)])  4.8 us
    ppermute x8, waiting for transfers between devices, to_col(): return lax.ppermute(array, ('row', 'col'), pairs_of)  3.61 us
    ppermute x3, waiting for transfers between devices, to_core(): return lax.ppermute(array, 'row', [(i, i ^ 1) for i in range(n_row)])  1.85 us
    ppermute x3, starting transfers between devices, to_core(): return lax.ppermute(array, 'row', [(i, i ^ 1) for i in range(n_row)])  0.69 us
  transfers between devices with their start and end apart: 17, of which 8 were waited for; matrix products, arithmetic and copies ran while one was open for 0% of the time, Pallas kernels for 9%

profile of v7, /device:TPU:0, one launch (start us, length us, event | category | flops | bytes accessed | tf_op | source)
XLA Modules:
  0.0 33.5 jit_solution(14207676192438781481)
XLA Ops:
  0.0 1.0 %shard_map.109 = (bf16[2,3,6,2,256]{4,3,2,1,0:T(2,128)(2,1)S(1)}, bf16[2,72,128]{2,1,0:T(8,128)(2,1)S(1)}, bf16[72,128]{1,0:T(8,128)(2,1)S(1)}) custom-call(bf16[3,6,2,256]{3,2,1,0:T(2,128)(2,1)} %bitcast.11, bf16[3,6,2,256]{3,2,1,0:T(2,128)(2,1)} %bitcast.12, bf16[2,64,72]{2,1,0:T(8,128)(2,1)} %bitcast.8, bf16[2,64,72]{2,1,0:T(8,128)(2,1)} %bitcast.9, ...), custom_call_target="tpu_custom_call" | custom-call | tf_op jit(solution)/shard_map/pallas_call | solution.py:35
  1.0 3.5 %collective-permute-start.4 = (bf16[2,72,128]{2,1,0:T(8,128)(2,1)S(1)}, bf16[2,72,128]{2,1,0:T(8,128)(2,1)S(1)}, u32[]{:S(2)}, u32[]{:S(2)}) collective-permute-start(bf16[2,72,128]{2,1,0:T(8,128)(2,1)S(1)} %get-tuple-element.44.refs_4_), channel_id=1, source_target_pairs={{0,20},{4,16},{8,28},{12,24},{16,4},{20,0},{24,12},{28,8},{1,21},{... | collective-permute-start | bytes 110600 | tf_op jit(solution)/shard_map/ppermute | solution.py:373
  4.5 2.7 %collective-permute-start.3 = (bf16[2,3,6,2,256]{4,3,2,1,0:T(2,128)(2,1)S(1)}, bf16[2,3,6,2,256]{4,3,2,1,0:T(2,128)(2,1)S(1)}, u32[]{:S(2)}, u32[]{:S(2)}) collective-permute-start(bf16[2,3,6,2,256]{4,3,2,1,0:T(2,128)(2,1)S(1)} %get-tuple-element.43), channel_id=1, source_target_pairs={{0,7},{1,6},{2,5},{3,4},{4,3},{5,2},{6,1},{7,0},{8,15},{9,14},{10,... | collective-permute-start | bytes 110600 | tf_op jit(solution)/shard_map/ppermute | solution.py:370
  7.3 0.0 collective-permute-start.2
  7.3 0.8 %collective-permute-start.1 = (bf16[2,3,6,2,256]{4,3,2,1,0:T(2,128)(2,1)S(1)}, bf16[2,3,6,2,256]{4,3,2,1,0:T(2,128)(2,1)S(1)}, u32[]{:S(2)}, u32[]{:S(2)}) collective-permute-start(bf16[2,3,6,2,256]{4,3,2,1,0:T(2,128)(2,1)S(1)} %get-tuple-element.43), channel_id=1, source_target_pairs={{0,5},{1,4},{2,7},{3,6},{4,1},{5,0},{6,3},{7,2},{8,13},{9,12},{10,... | collective-permute-start | bytes 110600 | tf_op jit(solution)/shard_map/ppermute | solution.py:370
  8.0 0.0 collective-permute-start
  8.0 1.4 %shard_map.110 = (bf16[3,72,96]{2,1,0:T(8,128)(2,1)S(1)}, bf16[3,24,32]{2,1,0:T(8,128)(2,1)S(1)}, bf16[3,3,256,256]{3,2,1,0:T(8,128)(2,1)S(1)}, bf16[256,256]{1,0:T(8,128)(2,1)S(1)}) custom-call(bf16[3,72,96]{2,1,0:T(8,128)(2,1)} %constant.6.clone.refs_0_, bf16[3,24,32]{2,1,0:T(8,128)(2,1)} %constant.7.clone.refs_1_, bf16[3,3,256,256]{3,2,1,0:T(8,128)(2,1)} %refs_2_.1, ...), custom_call_target="tpu_custom_call" | custom-call | tf_op jit(solution)/shard_map/pallas_call | solution.py:35
  9.4 0.0 collective-permute-done.4.refs_5_
  9.4 0.0 collective-permute-done.3.refs_3_
  9.4 1.6 %collective-permute-done.2.refs_2_ = bf16[2,3,6,2,256]{4,3,2,1,0:T(2,128)(2,1)S(1)} collective-permute-done((bf16[2,3,6,2,256]{4,3,2,1,0:T(2,128)(2,1)S(1)}, bf16[2,3,6,2,256]{4,3,2,1,0:T(2,128)(2,1)S(1)}, u32[]{:S(2)}, u32[]{:S(2)}) %collective-permute-start.2) | collective-permute-done | bytes 36896 | tf_op jit(solution)/shard_map/ppermute | solution.py:370
  11.0 0.0 collective-permute-done.1.refs_1_
  11.0 0.0 collective-permute-done.refs_0_
  11.0 0.2 shard_map.111
  11.2 1.5 %collective-permute-start.5 = (bf16[5,72,128]{2,1,0:T(8,128)(2,1)S(1)}, bf16[5,72,128]{2,1,0:T(8,128)(2,1)S(1)}, u32[]{:S(2)}, u32[]{:S(2)}) collective-permute-start(bf16[5,72,128]{2,1,0:T(8,128)(2,1)S(1)} %get-tuple-element.54.refs_0_), channel_id=1, source_target_pairs={{0,12},{4,8},{8,4},{12,0},{16,28},{20,24},{24,20},{28,16},{1,13},{... | collective-permute-start | bytes 276488 | tf_op jit(solution)/shard_map/ppermute | solution.py:373
  12.7 0.3 collective-permute-start.6
  13.0 0.2 collective-permute-start.7
  13.2 1.2 %shard_map.112 = (f32[72,256]{1,0:T(8,128)S(1)}, f32[72,256]{1,0:T(8,128)S(1)}) custom-call(bf16[2,3,6,2,256]{4,3,2,1,0:T(2,128)(2,1)S(1)} %collective-permute-done.refs_0_, bf16[2,3,6,2,256]{4,3,2,1,0:T(2,128)(2,1)S(1)} %collective-permute-done.1.refs_1_, bf16[2,3,6,2,256]{4,3,2,1,0:T(2,128)(2,1)S(1)} %collective-permute-done.2.refs_2_, ...), custom_call_target="tpu_custom_call" | custom-call | tf_op jit(solution)/shard_map/pallas_call | solution.py:35
  14.4 0.0 collective-permute-done.6.halo_odd
  14.4 0.0 collective-permute-done.7.halo_core
  14.4 1.5 %collective-permute-done.5.refs_1_.halo_last = bf16[5,72,128]{2,1,0:T(8,128)(2,1)S(1)} collective-permute-done((bf16[5,72,128]{2,1,0:T(8,128)(2,1)S(1)}, bf16[5,72,128]{2,1,0:T(8,128)(2,1)S(1)}, u32[]{:S(2)}, u32[]{:S(2)}) %collective-permute-start.5) | collective-permute-done | bytes 92192 | tf_op jit(solution)/shard_map/ppermute | solution.py:373
  15.9 0.0 copy-start
  15.9 0.0 copy-start.1
  15.9 0.2 collective-permute-start.8
  16.2 0.6 %shard_map.114 = (bf16[72,256]{1,0:T(8,128)(2,1)S(1)}, bf16[72,128]{1,0:T(8,128)(2,1)S(1)}) custom-call(bf16[72,128]{1,0:T(8,128)(2,1)S(1)} %collective-permute-done.7.halo_core, bf16[5,72,128]{2,1,0:T(8,128)(2,1)S(1)} %collective-permute-done.5.refs_1_.halo_last, bf16[72,128]{1,0:T(8,128)(2,1)S(1)} %collective-permute-done.6.halo_odd, ...), custom_call_target="tpu_custom_call" | custom-call | tf_op jit(solution)/shard_map/pallas_call | solution.py:35
  16.8 0.6 %collective-permute-done.8.kv_kept = bf16[9,72,128]{2,1,0:T(8,128)(2,1)S(1)} collective-permute-done((bf16[9,72,128]{2,1,0:T(8,128)(2,1)S(1)}, bf16[9,72,128]{2,1,0:T(8,128)(2,1)S(1)}, u32[]{:S(2)}, u32[]{:S(2)}) %collective-permute-start.8) | collective-permute-done | bytes 165920 | tf_op jit(solution)/shard_map/ppermute | solution.py:376
  17.4 0.9 %shard_map.115 = (bf16[4,2,72,128]{3,2,1,0:T(8,128)(2,1)S(1)}, bf16[4,2,72,128]{3,2,1,0:T(8,128)(2,1)S(1)}, f32[72,128]{1,0:T(8,128)S(1)}) custom-call(bf16[9,72,128]{2,1,0:T(8,128)(2,1)S(1)} %shard_map.113.kv_sent, bf16[9,72,128]{2,1,0:T(8,128)(2,1)S(1)} %collective-permute-done.8.kv_kept, bf16[72,128]{1,0:T(8,128)(2,1)S(1)} %get-tuple-element.68.go_ref), custom_call_target="tpu_custom_call" | custom-call | tf_op jit(solution)/shard_map/pallas_call | solution.py:35
  18.3 0.2 collective-permute-start.9
  18.6 1.2 %collective-permute-done.9.received = bf16[4,2,72,128]{3,2,1,0:T(8,128)(2,1)S(1)} collective-permute-done((bf16[4,2,72,128]{3,2,1,0:T(8,128)(2,1)S(1)}, bf16[4,2,72,128]{3,2,1,0:T(8,128)(2,1)S(1)}, u32[]{:S(2)}, u32[]{:S(2)}) %collective-permute-start.9) | collective-permute-done | bytes 147488 | tf_op jit(solution)/shard_map/ppermute | solution.py:376
  19.8 1.1 %collective-permute-start.10 = (bf16[2,72,128]{2,1,0:T(8,128)(2,1)S(1)}, bf16[2,72,128]{2,1,0:T(8,128)(2,1)S(1)}, u32[]{:S(2)}, u32[]{:S(2)}) collective-permute-start(bf16[2,72,128]{2,1,0:T(8,128)(2,1)S(1)} %get-tuple-element.71), channel_id=1, source_target_pairs={{0,28},{4,24},{8,20},{12,16},{16,12},{20,8},{24,4},{28,0},{1,29},{... | collective-permute-start | bytes 110600 | tf_op jit(solution)/shard_map/ppermute | solution.py:373
  20.9 1.7 %collective-permute-start.11 = (bf16[2,72,128]{2,1,0:T(8,128)(2,1)S(1)}, bf16[2,72,128]{2,1,0:T(8,128)(2,1)S(1)}, u32[]{:S(2)}, u32[]{:S(2)}) collective-permute-start(bf16[2,72,128]{2,1,0:T(8,128)(2,1)S(1)} %get-tuple-element.72), channel_id=1, source_target_pairs={{0,20},{4,16},{8,28},{12,24},{16,4},{20,0},{24,12},{28,8},{1,21},{... | collective-permute-start | bytes 110600 | tf_op jit(solution)/shard_map/ppermute | solution.py:373
  22.6 1.1 %collective-permute-start.12 = (bf16[2,72,128]{2,1,0:T(8,128)(2,1)S(1)}, bf16[2,72,128]{2,1,0:T(8,128)(2,1)S(1)}, u32[]{:S(2)}, u32[]{:S(2)}) collective-permute-start(bf16[2,72,128]{2,1,0:T(8,128)(2,1)S(1)} %get-tuple-element.73), channel_id=1, source_target_pairs={{0,12},{4,8},{8,4},{12,0},{16,28},{20,24},{24,20},{28,16},{1,13},{... | collective-permute-start | bytes 110600 | tf_op jit(solution)/shard_map/ppermute | solution.py:373
  23.7 1.4 %collective-permute-done.10.refs_0_ = bf16[2,72,128]{2,1,0:T(8,128)(2,1)S(1)} collective-permute-done((bf16[2,72,128]{2,1,0:T(8,128)(2,1)S(1)}, bf16[2,72,128]{2,1,0:T(8,128)(2,1)S(1)}, u32[]{:S(2)}, u32[]{:S(2)}) %collective-permute-start.10) | collective-permute-done | bytes 36896 | tf_op jit(solution)/shard_map/ppermute | solution.py:373
  25.1 1.9 %collective-permute-done.11.refs_1_ = bf16[2,72,128]{2,1,0:T(8,128)(2,1)S(1)} collective-permute-done((bf16[2,72,128]{2,1,0:T(8,128)(2,1)S(1)}, bf16[2,72,128]{2,1,0:T(8,128)(2,1)S(1)}, u32[]{:S(2)}, u32[]{:S(2)}) %collective-permute-start.11) | collective-permute-done | bytes 36896 | tf_op jit(solution)/shard_map/ppermute | solution.py:373
  27.0 0.0 collective-permute-done.12.refs_2_
  27.1 0.0 copy-done
  27.1 0.0 copy-done.1
  27.1 0.4 %shard_map.117 = (bf16[24,256]{1,0:T(8,128)(2,1)S(1)}, bf16[24,256]{1,0:T(8,128)(2,1)S(1)}, bf16[24,256]{1,0:T(8,128)(2,1)S(1)}, bf16[24,256]{1,0:T(8,128)(2,1)S(1)}) custom-call(bf16[2,72,128]{2,1,0:T(8,128)(2,1)S(1)} %collective-permute-done.10.refs_0_, bf16[2,72,128]{2,1,0:T(8,128)(2,1)S(1)} %collective-permute-done.11.refs_1_, ...), custom_call_target="tpu_custom_call" | custom-call | tf_op jit(solution)/shard_map/pallas_call | solution.py:35
  27.5 0.7 %collective-permute-start.13 = (bf16[24,256]{1,0:T(8,128)(2,1)S(1)}, bf16[24,256]{1,0:T(8,128)(2,1)S(1)}, u32[]{:S(2)}, u32[]{:S(2)}) collective-permute-start(bf16[24,256]{1,0:T(8,128)(2,1)S(1)} %get-tuple-element.77), channel_id=1, source_target_pairs={{0,7},{1,6},{2,5},{3,4},{4,3},{5,2},{6,1},{7,0},{8,15},{9,14},{10,... | collective-permute-start | bytes 36872 | tf_op jit(solution)/shard_map/ppermute | solution.py:370
  28.2 1.5 %collective-permute-start.14 = (bf16[24,256]{1,0:T(8,128)(2,1)S(1)}, bf16[24,256]{1,0:T(8,128)(2,1)S(1)}, u32[]{:S(2)}, u32[]{:S(2)}) collective-permute-start(bf16[24,256]{1,0:T(8,128)(2,1)S(1)} %get-tuple-element.78), channel_id=1, source_target_pairs={{0,6},{1,7},{2,4},{3,5},{4,2},{5,3},{6,0},{7,1},{8,14},{9,15},{10,... | collective-permute-start | bytes 36872 | tf_op jit(solution)/shard_map/ppermute | solution.py:370
  29.7 0.7 %collective-permute-start.15 = (bf16[24,256]{1,0:T(8,128)(2,1)S(1)}, bf16[24,256]{1,0:T(8,128)(2,1)S(1)}, u32[]{:S(2)}, u32[]{:S(2)}) collective-permute-start(bf16[24,256]{1,0:T(8,128)(2,1)S(1)} %get-tuple-element.79), channel_id=1, source_target_pairs={{0,5},{1,4},{2,7},{3,6},{4,1},{5,0},{6,3},{7,2},{8,13},{9,12},{10,... | collective-permute-start | bytes 36872 | tf_op jit(solution)/shard_map/ppermute | solution.py:370
  30.4 0.4 %collective-permute-start.16 = (bf16[24,256]{1,0:T(8,128)(2,1)S(1)}, bf16[24,256]{1,0:T(8,128)(2,1)S(1)}, u32[]{:S(2)}, u32[]{:S(2)}) collective-permute-start(bf16[24,256]{1,0:T(8,128)(2,1)S(1)} %get-tuple-element.80), channel_id=1, source_target_pairs={{0,4},{1,5},{2,6},{3,7},{4,0},{5,1},{6,2},{7,3},{8,12},{9,13},{10,... | collective-permute-start | bytes 36872 | tf_op jit(solution)/shard_map/ppermute | solution.py:370
  30.9 0.7 %collective-permute-done.13.refs_0_ = bf16[24,256]{1,0:T(8,128)(2,1)S(1)} collective-permute-done((bf16[24,256]{1,0:T(8,128)(2,1)S(1)}, bf16[24,256]{1,0:T(8,128)(2,1)S(1)}, u32[]{:S(2)}, u32[]{:S(2)}) %collective-permute-start.13) | collective-permute-done | bytes 12320 | tf_op jit(solution)/shard_map/ppermute | solution.py:370
  31.6 0.0 collective-permute-done.14.refs_1_
  31.6 1.3 %collective-permute-done.15.refs_2_ = bf16[24,256]{1,0:T(8,128)(2,1)S(1)} collective-permute-done((bf16[24,256]{1,0:T(8,128)(2,1)S(1)}, bf16[24,256]{1,0:T(8,128)(2,1)S(1)}, u32[]{:S(2)}, u32[]{:S(2)}) %collective-permute-start.15) | collective-permute-done | bytes 12320 | tf_op jit(solution)/shard_map/ppermute | solution.py:370
  32.8 0.0 collective-permute-done.16.refs_3_
  32.9 0.7 %shard_map.118 = bf16[3,6,2,256]{3,2,1,0:T(2,128)(2,1)} custom-call(bf16[24,256]{1,0:T(8,128)(2,1)S(1)} %collective-permute-done.13.refs_0_, bf16[24,256]{1,0:T(8,128)(2,1)S(1)} %collective-permute-done.14.refs_1_, bf16[24,256]{1,0:T(8,128)(2,1)S(1)} %collective-permute-done.15.refs_2_, bf16[24,256]{1,0:T(8,128)(2,1)S(1)} %collective-permute-done.16.refs_3_), custom_call_target="tpu_custom_call" | custom-call | tf_op jit(solution)/shard_map/pallas_call | solution.py:35
  (2 shorter events, 0.0 us)
Async XLA Ops:
  1.0 8.4 %collective-permute-start.4 = (bf16[2,72,128]{2,1,0:T(8,128)(2,1)S(1)}, bf16[2,72,128]{2,1,0:T(8,128)(2,1)S(1)}, u32[]{:S(2)}, u32[]{:S(2)}) collective-permute-start(bf16[2,72,128]{2,1,0:T(8,128)(2,1)S(1)} %get-tuple-element.44.refs_4_), channel_id=1, source_target_pairs={{0,20},{4,16},{8,28},{12,24},{16,4},{20,0},{24,12},{28,8},{1,21},{... | collective-permute-start | bytes 110600 | tf_op jit(solution)/shard_map/ppermute | solution.py:373
  4.5 4.9 %collective-permute-start.3 = (bf16[2,3,6,2,256]{4,3,2,1,0:T(2,128)(2,1)S(1)}, bf16[2,3,6,2,256]{4,3,2,1,0:T(2,128)(2,1)S(1)}, u32[]{:S(2)}, u32[]{:S(2)}) collective-permute-start(bf16[2,3,6,2,256]{4,3,2,1,0:T(2,128)(2,1)S(1)} %get-tuple-element.43), channel_id=1, source_target_pairs={{0,7},{1,6},{2,5},{3,4},{4,3},{5,2},{6,1},{7,0},{8,15},{9,14},{10,... | collective-permute-start | bytes 110600 | tf_op jit(solution)/shard_map/ppermute | solution.py:370
  7.3 3.8 %collective-permute-start.2 = (bf16[2,3,6,2,256]{4,3,2,1,0:T(2,128)(2,1)S(1)}, bf16[2,3,6,2,256]{4,3,2,1,0:T(2,128)(2,1)S(1)}, u32[]{:S(2)}, u32[]{:S(2)}) collective-permute-start(bf16[2,3,6,2,256]{4,3,2,1,0:T(2,128)(2,1)S(1)} %get-tuple-element.43), channel_id=1, source_target_pairs={{0,6},{1,7},{2,4},{3,5},{4,2},{5,3},{6,0},{7,1},{8,14},{9,15},{10,... | collective-permute-start | bytes 110600 | tf_op jit(solution)/shard_map/ppermute | solution.py:370
  7.3 3.8 %collective-permute-start.1 = (bf16[2,3,6,2,256]{4,3,2,1,0:T(2,128)(2,1)S(1)}, bf16[2,3,6,2,256]{4,3,2,1,0:T(2,128)(2,1)S(1)}, u32[]{:S(2)}, u32[]{:S(2)}) collective-permute-start(bf16[2,3,6,2,256]{4,3,2,1,0:T(2,128)(2,1)S(1)} %get-tuple-element.43), channel_id=1, source_target_pairs={{0,5},{1,4},{2,7},{3,6},{4,1},{5,0},{6,3},{7,2},{8,13},{9,12},{10,... | collective-permute-start | bytes 110600 | tf_op jit(solution)/shard_map/ppermute | solution.py:370
  8.0 3.0 %collective-permute-start = (bf16[2,3,6,2,256]{4,3,2,1,0:T(2,128)(2,1)S(1)}, bf16[2,3,6,2,256]{4,3,2,1,0:T(2,128)(2,1)S(1)}, u32[]{:S(2)}, u32[]{:S(2)}) collective-permute-start(bf16[2,3,6,2,256]{4,3,2,1,0:T(2,128)(2,1)S(1)} %get-tuple-element.43), channel_id=1, source_target_pairs={{0,4},{1,5},{2,6},{3,7},{4,0},{5,1},{6,2},{7,3},{8,12},{9,13},{10,... | collective-permute-start | bytes 110600 | tf_op jit(solution)/shard_map/ppermute | solution.py:370
  11.2 4.7 %collective-permute-start.5 = (bf16[5,72,128]{2,1,0:T(8,128)(2,1)S(1)}, bf16[5,72,128]{2,1,0:T(8,128)(2,1)S(1)}, u32[]{:S(2)}, u32[]{:S(2)}) collective-permute-start(bf16[5,72,128]{2,1,0:T(8,128)(2,1)S(1)} %get-tuple-element.54.refs_0_), channel_id=1, source_target_pairs={{0,12},{4,8},{8,4},{12,0},{16,28},{20,24},{24,20},{28,16},{1,13},{... | collective-permute-start | bytes 276488 | tf_op jit(solution)/shard_map/ppermute | solution.py:373
  12.7 1.7 %collective-permute-start.6 = (bf16[72,128]{1,0:T(8,128)(2,1)S(1)}, bf16[72,128]{1,0:T(8,128)(2,1)S(1)}, u32[]{:S(2)}, u32[]{:S(2)}) collective-permute-start(bf16[72,128]{1,0:T(8,128)(2,1)S(1)} %get-tuple-element.58), channel_id=1, source_target_pairs={{0,4},{24,28},{8,20},{12,16},{4,0},{28,24},{20,8},{16,12},{1,5},{2... | collective-permute-start | bytes 55304 | tf_op jit(solution)/shard_map/ppermute | solution.py:382
  13.0 1.4 %collective-permute-start.7 = (bf16[72,128]{1,0:T(8,128)(2,1)S(1)}, bf16[72,128]{1,0:T(8,128)(2,1)S(1)}, u32[]{:S(2)}, u32[]{:S(2)}) collective-permute-start(bf16[72,128]{1,0:T(8,128)(2,1)S(1)} %get-tuple-element.59), channel_id=1, source_target_pairs={{0,4},{4,0},{8,12},{12,8},{16,20},{20,16},{24,28},{28,24},{1,5},{5... | collective-permute-start | bytes 55304 | tf_op jit(solution)/shard_map/ppermute | solution.py:376
  15.9 11.1 %copy-start = (bf16[256,768]{1,0:T(8,128)(2,1)S(1)}, bf16[256,768]{1,0:T(8,128)(2,1)}, u32[]{:S(2)}) copy-start(bf16[256,768]{1,0:T(8,128)(2,1)} %refs_6_.1) | copy-start | bytes 1179652
  15.9 11.1 %copy-start.1 = (bf16[96,72]{1,0:T(8,128)(2,1)S(1)}, bf16[96,72]{1,0:T(8,128)(2,1)}, u32[]{:S(2)}) copy-start(bf16[96,72]{1,0:T(8,128)(2,1)} %constant.8.clone.refs_7_) | copy-start | bytes 41476
  15.9 1.5 %collective-permute-start.8 = (bf16[9,72,128]{2,1,0:T(8,128)(2,1)S(1)}, bf16[9,72,128]{2,1,0:T(8,128)(2,1)S(1)}, u32[]{:S(2)}, u32[]{:S(2)}) collective-permute-start(bf16[9,72,128]{2,1,0:T(8,128)(2,1)S(1)} %shard_map.113.kv_sent), channel_id=1, source_target_pairs={{0,4},{4,0},{8,12},{12,8},{16,20},{20,16},{24,28},{28,24},{1,5},{5... | collective-permute-start | bytes 497672 | tf_op jit(solution)/shard_map/ppermute | solution.py:376
  18.3 1.4 %collective-permute-start.9 = (bf16[4,2,72,128]{3,2,1,0:T(8,128)(2,1)S(1)}, bf16[4,2,72,128]{3,2,1,0:T(8,128)(2,1)S(1)}, u32[]{:S(2)}, u32[]{:S(2)}) collective-permute-start(bf16[4,2,72,128]{3,2,1,0:T(8,128)(2,1)S(1)} %get-tuple-element.70), channel_id=1, source_target_pairs={{0,4},{4,0},{8,12},{12,8},{16,20},{20,16},{24,28},{28,24},{1,5},{5... | collective-permute-start | bytes 442376 | tf_op jit(solution)/shard_map/ppermute | solution.py:376
  19.8 5.3 %collective-permute-start.10 = (bf16[2,72,128]{2,1,0:T(8,128)(2,1)S(1)}, bf16[2,72,128]{2,1,0:T(8,128)(2,1)S(1)}, u32[]{:S(2)}, u32[]{:S(2)}) collective-permute-start(bf16[2,72,128]{2,1,0:T(8,128)(2,1)S(1)} %get-tuple-element.71), channel_id=1, source_target_pairs={{0,28},{4,24},{8,20},{12,16},{16,12},{20,8},{24,4},{28,0},{1,29},{... | collective-permute-start | bytes 110600 | tf_op jit(solution)/shard_map/ppermute | solution.py:373
  20.9 6.2 %collective-permute-start.11 = (bf16[2,72,128]{2,1,0:T(8,128)(2,1)S(1)}, bf16[2,72,128]{2,1,0:T(8,128)(2,1)S(1)}, u32[]{:S(2)}, u32[]{:S(2)}) collective-permute-start(bf16[2,72,128]{2,1,0:T(8,128)(2,1)S(1)} %get-tuple-element.72), channel_id=1, source_target_pairs={{0,20},{4,16},{8,28},{12,24},{16,4},{20,0},{24,12},{28,8},{1,21},{... | collective-permute-start | bytes 110600 | tf_op jit(solution)/shard_map/ppermute | solution.py:373
  22.6 4.4 %collective-permute-start.12 = (bf16[2,72,128]{2,1,0:T(8,128)(2,1)S(1)}, bf16[2,72,128]{2,1,0:T(8,128)(2,1)S(1)}, u32[]{:S(2)}, u32[]{:S(2)}) collective-permute-start(bf16[2,72,128]{2,1,0:T(8,128)(2,1)S(1)} %get-tuple-element.73), channel_id=1, source_target_pairs={{0,12},{4,8},{8,4},{12,0},{16,28},{20,24},{24,20},{28,16},{1,13},{... | collective-permute-start | bytes 110600 | tf_op jit(solution)/shard_map/ppermute | solution.py:373
  27.5 4.1 %collective-permute-start.13 = (bf16[24,256]{1,0:T(8,128)(2,1)S(1)}, bf16[24,256]{1,0:T(8,128)(2,1)S(1)}, u32[]{:S(2)}, u32[]{:S(2)}) collective-permute-start(bf16[24,256]{1,0:T(8,128)(2,1)S(1)} %get-tuple-element.77), channel_id=1, source_target_pairs={{0,7},{1,6},{2,5},{3,4},{4,3},{5,2},{6,1},{7,0},{8,15},{9,14},{10,... | collective-permute-start | bytes 36872 | tf_op jit(solution)/shard_map/ppermute | solution.py:370
  28.2 3.3 %collective-permute-start.14 = (bf16[24,256]{1,0:T(8,128)(2,1)S(1)}, bf16[24,256]{1,0:T(8,128)(2,1)S(1)}, u32[]{:S(2)}, u32[]{:S(2)}) collective-permute-start(bf16[24,256]{1,0:T(8,128)(2,1)S(1)} %get-tuple-element.78), channel_id=1, source_target_pairs={{0,6},{1,7},{2,4},{3,5},{4,2},{5,3},{6,0},{7,1},{8,14},{9,15},{10,... | collective-permute-start | bytes 36872 | tf_op jit(solution)/shard_map/ppermute | solution.py:370
  29.7 3.1 %collective-permute-start.15 = (bf16[24,256]{1,0:T(8,128)(2,1)S(1)}, bf16[24,256]{1,0:T(8,128)(2,1)S(1)}, u32[]{:S(2)}, u32[]{:S(2)}) collective-permute-start(bf16[24,256]{1,0:T(8,128)(2,1)S(1)} %get-tuple-element.79), channel_id=1, source_target_pairs={{0,5},{1,4},{2,7},{3,6},{4,1},{5,0},{6,3},{7,2},{8,13},{9,12},{10,... | collective-permute-start | bytes 36872 | tf_op jit(solution)/shard_map/ppermute | solution.py:370
  30.4 2.4 %collective-permute-start.16 = (bf16[24,256]{1,0:T(8,128)(2,1)S(1)}, bf16[24,256]{1,0:T(8,128)(2,1)S(1)}, u32[]{:S(2)}, u32[]{:S(2)}) collective-permute-start(bf16[24,256]{1,0:T(8,128)(2,1)S(1)} %get-tuple-element.80), channel_id=1, source_target_pairs={{0,4},{1,5},{2,6},{3,7},{4,0},{5,1},{6,2},{7,3},{8,12},{9,13},{10,... | collective-permute-start | bytes 36872 | tf_op jit(solution)/shard_map/ppermute | solution.py:370

commit v8 on v7

--- a/solution.py
+++ b/solution.py
@@ -466,7 +466,9 @@
     sums = call(core_sum_kernel, [held((pairs, strip, lanes), BF16) for _ in range(chips)])(
         dkv_kept, to_core(dkv_sent)
     )
-    parts = [to_chip(sums[k], k) for k in reversed(range(1, chips))] + [sums[0]]
+    far_near = [k for pair in zip(range(chips - 1, 0, -1), range(1, chips)) for k in pair]
+    order = list(dict.fromkeys(far_near))
+    parts = [to_chip(sums[k], k) for k in order] + [sums[0]]
 
     selected = tile_selector(rows, cols, n_col).reshape(n_col * rows * padded, -1)
     cut = call(

time: 33.7 us -> 32.7 us (0.970)
  waiting for transfers between devices: 10.3 us -> 9.27 us
    ppermute x5, waiting for transfers between devices: 4.8 us -> 3.76 us  [to_chip(): lax.ppermute(array, 'row', [(i, i ^ 2 * k + 1) for i in range(n_row)])]
  transfers between devices with their start and end apart: 17 -> 17, of which waited for: 8 -> 9; matrix products, arithmetic and copies ran while one was open for 0% -> 0% of each run, Pallas kernels for 9% -> 10%
where the time goes in v8:
time: 32.7 us; the launch traced here: 32.5 us
  starting transfers between devices  16.8 us (51%)
  waiting for transfers between devices  9.27 us (28%)
  Pallas kernels  6.32 us (19%)
    ppermute x5, starting transfers between devices, to_chip(): lax.ppermute(array, 'row', [(i, i ^ 2 * k + 1) for i in range(n_row)])  8.96 us
    ppermute x8, starting transfers between devices, to_col(): return lax.ppermute(array, ('row', 'col'), pairs_of)  6.88 us
    pallas_call x10, Pallas kernels, run(): pl.pallas_call(kernel, out_shape=out_shape, in_specs=specs, out_specs=jax...  6.32 us
    ppermute x5, waiting for transfers between devices, to_chip(): lax.ppermute(array, 'row', [(i, i ^ 2 * k + 1) for i in range(n_row)])  3.76 us
    ppermute x8, waiting for transfers between devices, to_col(): return lax.ppermute(array, ('row', 'col'), pairs_of)  3.66 us
    ppermute x3, waiting for transfers between devices, to_core(): return lax.ppermute(array, 'row', [(i, i ^ 1) for i in range(n_row)])  1.85 us
    ppermute x3, starting transfers between devices, to_core(): return lax.ppermute(array, 'row', [(i, i ^ 1) for i in range(n_row)])  0.69 us
  transfers between devices with their start and end apart: 17, of which 9 were waited for; matrix products, arithmetic and copies ran while one was open for 0% of the time, Pallas kernels for 10%

profile of v8, /device:TPU:0, one launch (start us, length us, event | category | flops | bytes accessed | tf_op | source)
XLA Modules:
  0.0 32.5 jit_solution(10608651959362471233)
XLA Ops:
  0.0 1.0 %shard_map.109 = (bf16[2,3,6,2,256]{4,3,2,1,0:T(2,128)(2,1)S(1)}, bf16[2,72,128]{2,1,0:T(8,128)(2,1)S(1)}, bf16[72,128]{1,0:T(8,128)(2,1)S(1)}) custom-call(bf16[3,6,2,256]{3,2,1,0:T(2,128)(2,1)} %bitcast.11, bf16[3,6,2,256]{3,2,1,0:T(2,128)(2,1)} %bitcast.12, bf16[2,64,72]{2,1,0:T(8,128)(2,1)} %bitcast.8, bf16[2,64,72]{2,1,0:T(8,128)(2,1)} %bitcast.9, ...), custom_call_target="tpu_custom_call" | custom-call | tf_op jit(solution)/shard_map/pallas_call | solution.py:35
  1.0 3.5 %collective-permute-start.4 = (bf16[2,72,128]{2,1,0:T(8,128)(2,1)S(1)}, bf16[2,72,128]{2,1,0:T(8,128)(2,1)S(1)}, u32[]{:S(2)}, u32[]{:S(2)}) collective-permute-start(bf16[2,72,128]{2,1,0:T(8,128)(2,1)S(1)} %get-tuple-element.44.refs_4_), channel_id=1, source_target_pairs={{0,20},{4,16},{8,28},{12,24},{16,4},{20,0},{24,12},{28,8},{1,21},{... | collective-permute-start | bytes 110600 | tf_op jit(solution)/shard_map/ppermute | solution.py:373
  4.5 2.7 %collective-permute-start.3 = (bf16[2,3,6,2,256]{4,3,2,1,0:T(2,128)(2,1)S(1)}, bf16[2,3,6,2,256]{4,3,2,1,0:T(2,128)(2,1)S(1)}, u32[]{:S(2)}, u32[]{:S(2)}) collective-permute-start(bf16[2,3,6,2,256]{4,3,2,1,0:T(2,128)(2,1)S(1)} %get-tuple-element.43), channel_id=1, source_target_pairs={{0,7},{1,6},{2,5},{3,4},{4,3},{5,2},{6,1},{7,0},{8,15},{9,14},{10,... | collective-permute-start | bytes 110600 | tf_op jit(solution)/shard_map/ppermute | solution.py:370
  7.3 0.0 collective-permute-start.2
  7.3 0.8 %collective-permute-start.1 = (bf16[2,3,6,2,256]{4,3,2,1,0:T(2,128)(2,1)S(1)}, bf16[2,3,6,2,256]{4,3,2,1,0:T(2,128)(2,1)S(1)}, u32[]{:S(2)}, u32[]{:S(2)}) collective-permute-start(bf16[2,3,6,2,256]{4,3,2,1,0:T(2,128)(2,1)S(1)} %get-tuple-element.43), channel_id=1, source_target_pairs={{0,5},{1,4},{2,7},{3,6},{4,1},{5,0},{6,3},{7,2},{8,13},{9,12},{10,... | collective-permute-start | bytes 110600 | tf_op jit(solution)/shard_map/ppermute | solution.py:370
  8.0 0.0 collective-permute-start
  8.0 1.4 %shard_map.110 = (bf16[3,72,96]{2,1,0:T(8,128)(2,1)S(1)}, bf16[3,24,32]{2,1,0:T(8,128)(2,1)S(1)}, bf16[3,3,256,256]{3,2,1,0:T(8,128)(2,1)S(1)}, bf16[256,256]{1,0:T(8,128)(2,1)S(1)}) custom-call(bf16[3,72,96]{2,1,0:T(8,128)(2,1)} %constant.6.clone.refs_0_, bf16[3,24,32]{2,1,0:T(8,128)(2,1)} %constant.7.clone.refs_1_, bf16[3,3,256,256]{3,2,1,0:T(8,128)(2,1)} %refs_2_.1, ...), custom_call_target="tpu_custom_call" | custom-call | tf_op jit(solution)/shard_map/pallas_call | solution.py:35
  9.4 0.0 collective-permute-done.4.refs_5_
  9.4 0.0 collective-permute-done.3.refs_3_
  9.4 1.6 %collective-permute-done.2.refs_2_ = bf16[2,3,6,2,256]{4,3,2,1,0:T(2,128)(2,1)S(1)} collective-permute-done((bf16[2,3,6,2,256]{4,3,2,1,0:T(2,128)(2,1)S(1)}, bf16[2,3,6,2,256]{4,3,2,1,0:T(2,128)(2,1)S(1)}, u32[]{:S(2)}, u32[]{:S(2)}) %collective-permute-start.2) | collective-permute-done | bytes 36896 | tf_op jit(solution)/shard_map/ppermute | solution.py:370
  11.0 0.0 collective-permute-done.1.refs_1_
  11.0 0.0 collective-permute-done.refs_0_
  11.0 0.2 shard_map.111
  11.2 1.5 %collective-permute-start.5 = (bf16[5,72,128]{2,1,0:T(8,128)(2,1)S(1)}, bf16[5,72,128]{2,1,0:T(8,128)(2,1)S(1)}, u32[]{:S(2)}, u32[]{:S(2)}) collective-permute-start(bf16[5,72,128]{2,1,0:T(8,128)(2,1)S(1)} %get-tuple-element.54.refs_0_), channel_id=1, source_target_pairs={{0,12},{4,8},{8,4},{12,0},{16,28},{20,24},{24,20},{28,16},{1,13},{... | collective-permute-start | bytes 276488 | tf_op jit(solution)/shard_map/ppermute | solution.py:373
  12.7 0.3 collective-permute-start.6
  13.0 0.2 collective-permute-start.7
  13.2 1.2 %shard_map.112 = (f32[72,256]{1,0:T(8,128)S(1)}, f32[72,256]{1,0:T(8,128)S(1)}) custom-call(bf16[2,3,6,2,256]{4,3,2,1,0:T(2,128)(2,1)S(1)} %collective-permute-done.refs_0_, bf16[2,3,6,2,256]{4,3,2,1,0:T(2,128)(2,1)S(1)} %collective-permute-done.1.refs_1_, bf16[2,3,6,2,256]{4,3,2,1,0:T(2,128)(2,1)S(1)} %collective-permute-done.2.refs_2_, ...), custom_call_target="tpu_custom_call" | custom-call | tf_op jit(solution)/shard_map/pallas_call | solution.py:35
  14.4 0.0 collective-permute-done.6.halo_odd
  14.4 0.0 collective-permute-done.7.halo_core
  14.4 1.5 %collective-permute-done.5.refs_1_.halo_last = bf16[5,72,128]{2,1,0:T(8,128)(2,1)S(1)} collective-permute-done((bf16[5,72,128]{2,1,0:T(8,128)(2,1)S(1)}, bf16[5,72,128]{2,1,0:T(8,128)(2,1)S(1)}, u32[]{:S(2)}, u32[]{:S(2)}) %collective-permute-start.5) | collective-permute-done | bytes 92192 | tf_op jit(solution)/shard_map/ppermute | solution.py:373
  15.9 0.0 copy-start
  15.9 0.0 copy-start.1
  15.9 0.2 collective-permute-start.8
  16.2 0.6 %shard_map.114 = (bf16[72,256]{1,0:T(8,128)(2,1)S(1)}, bf16[72,128]{1,0:T(8,128)(2,1)S(1)}) custom-call(bf16[72,128]{1,0:T(8,128)(2,1)S(1)} %collective-permute-done.7.halo_core, bf16[5,72,128]{2,1,0:T(8,128)(2,1)S(1)} %collective-permute-done.5.refs_1_.halo_last, bf16[72,128]{1,0:T(8,128)(2,1)S(1)} %collective-permute-done.6.halo_odd, ...), custom_call_target="tpu_custom_call" | custom-call | tf_op jit(solution)/shard_map/pallas_call | solution.py:35
  16.8 0.6 %collective-permute-done.8.kv_kept = bf16[9,72,128]{2,1,0:T(8,128)(2,1)S(1)} collective-permute-done((bf16[9,72,128]{2,1,0:T(8,128)(2,1)S(1)}, bf16[9,72,128]{2,1,0:T(8,128)(2,1)S(1)}, u32[]{:S(2)}, u32[]{:S(2)}) %collective-permute-start.8) | collective-permute-done | bytes 165920 | tf_op jit(solution)/shard_map/ppermute | solution.py:376
  17.4 0.9 %shard_map.115 = (bf16[4,2,72,128]{3,2,1,0:T(8,128)(2,1)S(1)}, bf16[4,2,72,128]{3,2,1,0:T(8,128)(2,1)S(1)}, f32[72,128]{1,0:T(8,128)S(1)}) custom-call(bf16[9,72,128]{2,1,0:T(8,128)(2,1)S(1)} %shard_map.113.kv_sent, bf16[9,72,128]{2,1,0:T(8,128)(2,1)S(1)} %collective-permute-done.8.kv_kept, bf16[72,128]{1,0:T(8,128)(2,1)S(1)} %get-tuple-element.68.go_ref), custom_call_target="tpu_custom_call" | custom-call | tf_op jit(solution)/shard_map/pallas_call | solution.py:35
  18.3 0.2 collective-permute-start.9
  18.6 1.2 %collective-permute-done.9.received = bf16[4,2,72,128]{3,2,1,0:T(8,128)(2,1)S(1)} collective-permute-done((bf16[4,2,72,128]{3,2,1,0:T(8,128)(2,1)S(1)}, bf16[4,2,72,128]{3,2,1,0:T(8,128)(2,1)S(1)}, u32[]{:S(2)}, u32[]{:S(2)}) %collective-permute-start.9) | collective-permute-done | bytes 147488 | tf_op jit(solution)/shard_map/ppermute | solution.py:376
  19.8 1.1 %collective-permute-start.10 = (bf16[2,72,128]{2,1,0:T(8,128)(2,1)S(1)}, bf16[2,72,128]{2,1,0:T(8,128)(2,1)S(1)}, u32[]{:S(2)}, u32[]{:S(2)}) collective-permute-start(bf16[2,72,128]{2,1,0:T(8,128)(2,1)S(1)} %get-tuple-element.71), channel_id=1, source_target_pairs={{0,28},{4,24},{8,20},{12,16},{16,12},{20,8},{24,4},{28,0},{1,29},{... | collective-permute-start | bytes 110600 | tf_op jit(solution)/shard_map/ppermute | solution.py:373
  20.9 0.4 %collective-permute-start.11 = (bf16[2,72,128]{2,1,0:T(8,128)(2,1)S(1)}, bf16[2,72,128]{2,1,0:T(8,128)(2,1)S(1)}, u32[]{:S(2)}, u32[]{:S(2)}) collective-permute-start(bf16[2,72,128]{2,1,0:T(8,128)(2,1)S(1)} %get-tuple-element.72), channel_id=1, source_target_pairs={{0,12},{4,8},{8,4},{12,0},{16,28},{20,24},{24,20},{28,16},{1,13},{... | collective-permute-start | bytes 110600 | tf_op jit(solution)/shard_map/ppermute | solution.py:373
  21.3 2.5 %collective-permute-start.12 = (bf16[2,72,128]{2,1,0:T(8,128)(2,1)S(1)}, bf16[2,72,128]{2,1,0:T(8,128)(2,1)S(1)}, u32[]{:S(2)}, u32[]{:S(2)}) collective-permute-start(bf16[2,72,128]{2,1,0:T(8,128)(2,1)S(1)} %get-tuple-element.73), channel_id=1, source_target_pairs={{0,20},{4,16},{8,28},{12,24},{16,4},{20,0},{24,12},{28,8},{1,21},{... | collective-permute-start | bytes 110600 | tf_op jit(solution)/shard_map/ppermute | solution.py:373
  23.7 1.4 %collective-permute-done.10.refs_0_ = bf16[2,72,128]{2,1,0:T(8,128)(2,1)S(1)} collective-permute-done((bf16[2,72,128]{2,1,0:T(8,128)(2,1)S(1)}, bf16[2,72,128]{2,1,0:T(8,128)(2,1)S(1)}, u32[]{:S(2)}, u32[]{:S(2)}) %collective-permute-start.10) | collective-permute-done | bytes 36896 | tf_op jit(solution)/shard_map/ppermute | solution.py:373
  25.1 0.0 collective-permute-done.11.refs_1_
  25.1 0.9 %collective-permute-done.12.refs_2_ = bf16[2,72,128]{2,1,0:T(8,128)(2,1)S(1)} collective-permute-done((bf16[2,72,128]{2,1,0:T(8,128)(2,1)S(1)}, bf16[2,72,128]{2,1,0:T(8,128)(2,1)S(1)}, u32[]{:S(2)}, u32[]{:S(2)}) %collective-permute-start.12) | collective-permute-done | bytes 36896 | tf_op jit(solution)/shard_map/ppermute | solution.py:373
  26.0 0.0 copy-done
  26.0 0.0 copy-done.1
  26.0 0.4 %shard_map.117 = (bf16[24,256]{1,0:T(8,128)(2,1)S(1)}, bf16[24,256]{1,0:T(8,128)(2,1)S(1)}, bf16[24,256]{1,0:T(8,128)(2,1)S(1)}, bf16[24,256]{1,0:T(8,128)(2,1)S(1)}) custom-call(bf16[2,72,128]{2,1,0:T(8,128)(2,1)S(1)} %collective-permute-done.10.refs_0_, bf16[2,72,128]{2,1,0:T(8,128)(2,1)S(1)} %collective-permute-done.11.refs_1_, ...), custom_call_target="tpu_custom_call" | custom-call | tf_op jit(solution)/shard_map/pallas_call | solution.py:35
  26.4 1.6 %collective-permute-start.13 = (bf16[24,256]{1,0:T(8,128)(2,1)S(1)}, bf16[24,256]{1,0:T(8,128)(2,1)S(1)}, u32[]{:S(2)}, u32[]{:S(2)}) collective-permute-start(bf16[24,256]{1,0:T(8,128)(2,1)S(1)} %get-tuple-element.77), channel_id=1, source_target_pairs={{0,7},{1,6},{2,5},{3,4},{4,3},{5,2},{6,1},{7,0},{8,15},{9,14},{10,... | collective-permute-start | bytes 36872 | tf_op jit(solution)/shard_map/ppermute | solution.py:370
  28.0 0.7 %collective-permute-start.14 = (bf16[24,256]{1,0:T(8,128)(2,1)S(1)}, bf16[24,256]{1,0:T(8,128)(2,1)S(1)}, u32[]{:S(2)}, u32[]{:S(2)}) collective-permute-start(bf16[24,256]{1,0:T(8,128)(2,1)S(1)} %get-tuple-element.78), channel_id=1, source_target_pairs={{0,6},{1,7},{2,4},{3,5},{4,2},{5,3},{6,0},{7,1},{8,14},{9,15},{10,... | collective-permute-start | bytes 36872 | tf_op jit(solution)/shard_map/ppermute | solution.py:370
  28.7 0.8 %collective-permute-start.15 = (bf16[24,256]{1,0:T(8,128)(2,1)S(1)}, bf16[24,256]{1,0:T(8,128)(2,1)S(1)}, u32[]{:S(2)}, u32[]{:S(2)}) collective-permute-start(bf16[24,256]{1,0:T(8,128)(2,1)S(1)} %get-tuple-element.79), channel_id=1, source_target_pairs={{0,5},{1,4},{2,7},{3,6},{4,1},{5,0},{6,3},{7,2},{8,13},{9,12},{10,... | collective-permute-start | bytes 36872 | tf_op jit(solution)/shard_map/ppermute | solution.py:370
  29.6 0.3 collective-permute-start.16
  29.8 0.7 %collective-permute-done.13.refs_0_ = bf16[24,256]{1,0:T(8,128)(2,1)S(1)} collective-permute-done((bf16[24,256]{1,0:T(8,128)(2,1)S(1)}, bf16[24,256]{1,0:T(8,128)(2,1)S(1)}, u32[]{:S(2)}, u32[]{:S(2)}) %collective-permute-start.13) | collective-permute-done | bytes 12320 | tf_op jit(solution)/shard_map/ppermute | solution.py:370
  30.5 0.7 %collective-permute-done.14.refs_1_ = bf16[24,256]{1,0:T(8,128)(2,1)S(1)} collective-permute-done((bf16[24,256]{1,0:T(8,128)(2,1)S(1)}, bf16[24,256]{1,0:T(8,128)(2,1)S(1)}, u32[]{:S(2)}, u32[]{:S(2)}) %collective-permute-start.14) | collective-permute-done | bytes 12320 | tf_op jit(solution)/shard_map/ppermute | solution.py:370
  31.2 0.7 %collective-permute-done.15.refs_2_ = bf16[24,256]{1,0:T(8,128)(2,1)S(1)} collective-permute-done((bf16[24,256]{1,0:T(8,128)(2,1)S(1)}, bf16[24,256]{1,0:T(8,128)(2,1)S(1)}, u32[]{:S(2)}, u32[]{:S(2)}) %collective-permute-start.15) | collective-permute-done | bytes 12320 | tf_op jit(solution)/shard_map/ppermute | solution.py:370
  31.8 0.0 collective-permute-done.16.refs_3_
  31.9 0.7 %shard_map.118 = bf16[3,6,2,256]{3,2,1,0:T(2,128)(2,1)} custom-call(bf16[24,256]{1,0:T(8,128)(2,1)S(1)} %collective-permute-done.13.refs_0_, bf16[24,256]{1,0:T(8,128)(2,1)S(1)} %collective-permute-done.14.refs_1_, bf16[24,256]{1,0:T(8,128)(2,1)S(1)} %collective-permute-done.15.refs_2_, bf16[24,256]{1,0:T(8,128)(2,1)S(1)} %collective-permute-done.16.refs_3_), custom_call_target="tpu_custom_call" | custom-call | tf_op jit(solution)/shard_map/pallas_call | solution.py:35
  (2 shorter events, 0.0 us)
Async XLA Ops:
  1.0 8.4 %collective-permute-start.4 = (bf16[2,72,128]{2,1,0:T(8,128)(2,1)S(1)}, bf16[2,72,128]{2,1,0:T(8,128)(2,1)S(1)}, u32[]{:S(2)}, u32[]{:S(2)}) collective-permute-start(bf16[2,72,128]{2,1,0:T(8,128)(2,1)S(1)} %get-tuple-element.44.refs_4_), channel_id=1, source_target_pairs={{0,20},{4,16},{8,28},{12,24},{16,4},{20,0},{24,12},{28,8},{1,21},{... | collective-permute-start | bytes 110600 | tf_op jit(solution)/shard_map/ppermute | solution.py:373
  4.5 4.9 %collective-permute-start.3 = (bf16[2,3,6,2,256]{4,3,2,1,0:T(2,128)(2,1)S(1)}, bf16[2,3,6,2,256]{4,3,2,1,0:T(2,128)(2,1)S(1)}, u32[]{:S(2)}, u32[]{:S(2)}) collective-permute-start(bf16[2,3,6,2,256]{4,3,2,1,0:T(2,128)(2,1)S(1)} %get-tuple-element.43), channel_id=1, source_target_pairs={{0,7},{1,6},{2,5},{3,4},{4,3},{5,2},{6,1},{7,0},{8,15},{9,14},{10,... | collective-permute-start | bytes 110600 | tf_op jit(solution)/shard_map/ppermute | solution.py:370
  7.3 3.8 %collective-permute-start.2 = (bf16[2,3,6,2,256]{4,3,2,1,0:T(2,128)(2,1)S(1)}, bf16[2,3,6,2,256]{4,3,2,1,0:T(2,128)(2,1)S(1)}, u32[]{:S(2)}, u32[]{:S(2)}) collective-permute-start(bf16[2,3,6,2,256]{4,3,2,1,0:T(2,128)(2,1)S(1)} %get-tuple-element.43), channel_id=1, source_target_pairs={{0,6},{1,7},{2,4},{3,5},{4,2},{5,3},{6,0},{7,1},{8,14},{9,15},{10,... | collective-permute-start | bytes 110600 | tf_op jit(solution)/shard_map/ppermute | solution.py:370
  7.3 3.8 %collective-permute-start.1 = (bf16[2,3,6,2,256]{4,3,2,1,0:T(2,128)(2,1)S(1)}, bf16[2,3,6,2,256]{4,3,2,1,0:T(2,128)(2,1)S(1)}, u32[]{:S(2)}, u32[]{:S(2)}) collective-permute-start(bf16[2,3,6,2,256]{4,3,2,1,0:T(2,128)(2,1)S(1)} %get-tuple-element.43), channel_id=1, source_target_pairs={{0,5},{1,4},{2,7},{3,6},{4,1},{5,0},{6,3},{7,2},{8,13},{9,12},{10,... | collective-permute-start | bytes 110600 | tf_op jit(solution)/shard_map/ppermute | solution.py:370
  8.0 3.0 %collective-permute-start = (bf16[2,3,6,2,256]{4,3,2,1,0:T(2,128)(2,1)S(1)}, bf16[2,3,6,2,256]{4,3,2,1,0:T(2,128)(2,1)S(1)}, u32[]{:S(2)}, u32[]{:S(2)}) collective-permute-start(bf16[2,3,6,2,256]{4,3,2,1,0:T(2,128)(2,1)S(1)} %get-tuple-element.43), channel_id=1, source_target_pairs={{0,4},{1,5},{2,6},{3,7},{4,0},{5,1},{6,2},{7,3},{8,12},{9,13},{10,... | collective-permute-start | bytes 110600 | tf_op jit(solution)/shard_map/ppermute | solution.py:370
  11.2 4.7 %collective-permute-start.5 = (bf16[5,72,128]{2,1,0:T(8,128)(2,1)S(1)}, bf16[5,72,128]{2,1,0:T(8,128)(2,1)S(1)}, u32[]{:S(2)}, u32[]{:S(2)}) collective-permute-start(bf16[5,72,128]{2,1,0:T(8,128)(2,1)S(1)} %get-tuple-element.54.refs_0_), channel_id=1, source_target_pairs={{0,12},{4,8},{8,4},{12,0},{16,28},{20,24},{24,20},{28,16},{1,13},{... | collective-permute-start | bytes 276488 | tf_op jit(solution)/shard_map/ppermute | solution.py:373
  12.7 1.7 %collective-permute-start.6 = (bf16[72,128]{1,0:T(8,128)(2,1)S(1)}, bf16[72,128]{1,0:T(8,128)(2,1)S(1)}, u32[]{:S(2)}, u32[]{:S(2)}) collective-permute-start(bf16[72,128]{1,0:T(8,128)(2,1)S(1)} %get-tuple-element.58), channel_id=1, source_target_pairs={{0,4},{24,28},{8,20},{12,16},{4,0},{28,24},{20,8},{16,12},{1,5},{2... | collective-permute-start | bytes 55304 | tf_op jit(solution)/shard_map/ppermute | solution.py:382
  13.0 1.4 %collective-permute-start.7 = (bf16[72,128]{1,0:T(8,128)(2,1)S(1)}, bf16[72,128]{1,0:T(8,128)(2,1)S(1)}, u32[]{:S(2)}, u32[]{:S(2)}) collective-permute-start(bf16[72,128]{1,0:T(8,128)(2,1)S(1)} %get-tuple-element.59), channel_id=1, source_target_pairs={{0,4},{4,0},{8,12},{12,8},{16,20},{20,16},{24,28},{28,24},{1,5},{5... | collective-permute-start | bytes 55304 | tf_op jit(solution)/shard_map/ppermute | solution.py:376
  15.9 10.1 %copy-start = (bf16[256,768]{1,0:T(8,128)(2,1)S(1)}, bf16[256,768]{1,0:T(8,128)(2,1)}, u32[]{:S(2)}) copy-start(bf16[256,768]{1,0:T(8,128)(2,1)} %refs_6_.1) | copy-start | bytes 1179652
  15.9 10.1 %copy-start.1 = (bf16[96,72]{1,0:T(8,128)(2,1)S(1)}, bf16[96,72]{1,0:T(8,128)(2,1)}, u32[]{:S(2)}) copy-start(bf16[96,72]{1,0:T(8,128)(2,1)} %constant.8.clone.refs_7_) | copy-start | bytes 41476
  15.9 1.5 %collective-permute-start.8 = (bf16[9,72,128]{2,1,0:T(8,128)(2,1)S(1)}, bf16[9,72,128]{2,1,0:T(8,128)(2,1)S(1)}, u32[]{:S(2)}, u32[]{:S(2)}) collective-permute-start(bf16[9,72,128]{2,1,0:T(8,128)(2,1)S(1)} %shard_map.113.kv_sent), channel_id=1, source_target_pairs={{0,4},{4,0},{8,12},{12,8},{16,20},{20,16},{24,28},{28,24},{1,5},{5... | collective-permute-start | bytes 497672 | tf_op jit(solution)/shard_map/ppermute | solution.py:376
  18.3 1.4 %collective-permute-start.9 = (bf16[4,2,72,128]{3,2,1,0:T(8,128)(2,1)S(1)}, bf16[4,2,72,128]{3,2,1,0:T(8,128)(2,1)S(1)}, u32[]{:S(2)}, u32[]{:S(2)}) collective-permute-start(bf16[4,2,72,128]{3,2,1,0:T(8,128)(2,1)S(1)} %get-tuple-element.70), channel_id=1, source_target_pairs={{0,4},{4,0},{8,12},{12,8},{16,20},{20,16},{24,28},{28,24},{1,5},{5... | collective-permute-start | bytes 442376 | tf_op jit(solution)/shard_map/ppermute | solution.py:376
  19.8 5.3 %collective-permute-start.10 = (bf16[2,72,128]{2,1,0:T(8,128)(2,1)S(1)}, bf16[2,72,128]{2,1,0:T(8,128)(2,1)S(1)}, u32[]{:S(2)}, u32[]{:S(2)}) collective-permute-start(bf16[2,72,128]{2,1,0:T(8,128)(2,1)S(1)} %get-tuple-element.71), channel_id=1, source_target_pairs={{0,28},{4,24},{8,20},{12,16},{16,12},{20,8},{24,4},{28,0},{1,29},{... | collective-permute-start | bytes 110600 | tf_op jit(solution)/shard_map/ppermute | solution.py:373
  20.9 4.3 %collective-permute-start.11 = (bf16[2,72,128]{2,1,0:T(8,128)(2,1)S(1)}, bf16[2,72,128]{2,1,0:T(8,128)(2,1)S(1)}, u32[]{:S(2)}, u32[]{:S(2)}) collective-permute-start(bf16[2,72,128]{2,1,0:T(8,128)(2,1)S(1)} %get-tuple-element.72), channel_id=1, source_target_pairs={{0,12},{4,8},{8,4},{12,0},{16,28},{20,24},{24,20},{28,16},{1,13},{... | collective-permute-start | bytes 110600 | tf_op jit(solution)/shard_map/ppermute | solution.py:373
  21.3 4.7 %collective-permute-start.12 = (bf16[2,72,128]{2,1,0:T(8,128)(2,1)S(1)}, bf16[2,72,128]{2,1,0:T(8,128)(2,1)S(1)}, u32[]{:S(2)}, u32[]{:S(2)}) collective-permute-start(bf16[2,72,128]{2,1,0:T(8,128)(2,1)S(1)} %get-tuple-element.73), channel_id=1, source_target_pairs={{0,20},{4,16},{8,28},{12,24},{16,4},{20,0},{24,12},{28,8},{1,21},{... | collective-permute-start | bytes 110600 | tf_op jit(solution)/shard_map/ppermute | solution.py:373
  26.4 4.1 %collective-permute-start.13 = (bf16[24,256]{1,0:T(8,128)(2,1)S(1)}, bf16[24,256]{1,0:T(8,128)(2,1)S(1)}, u32[]{:S(2)}, u32[]{:S(2)}) collective-permute-start(bf16[24,256]{1,0:T(8,128)(2,1)S(1)} %get-tuple-element.77), channel_id=1, source_target_pairs={{0,7},{1,6},{2,5},{3,4},{4,3},{5,2},{6,1},{7,0},{8,15},{9,14},{10,... | collective-permute-start | bytes 36872 | tf_op jit(solution)/shard_map/ppermute | solution.py:370
  28.0 3.1 %collective-permute-start.14 = (bf16[24,256]{1,0:T(8,128)(2,1)S(1)}, bf16[24,256]{1,0:T(8,128)(2,1)S(1)}, u32[]{:S(2)}, u32[]{:S(2)}) collective-permute-start(bf16[24,256]{1,0:T(8,128)(2,1)S(1)} %get-tuple-element.78), channel_id=1, source_target_pairs={{0,6},{1,7},{2,4},{3,5},{4,2},{5,3},{6,0},{7,1},{8,14},{9,15},{10,... | collective-permute-start | bytes 36872 | tf_op jit(solution)/shard_map/ppermute | solution.py:370
  28.7 3.1 %collective-permute-start.15 = (bf16[24,256]{1,0:T(8,128)(2,1)S(1)}, bf16[24,256]{1,0:T(8,128)(2,1)S(1)}, u32[]{:S(2)}, u32[]{:S(2)}) collective-permute-start(bf16[24,256]{1,0:T(8,128)(2,1)S(1)} %get-tuple-element.79), channel_id=1, source_target_pairs={{0,5},{1,4},{2,7},{3,6},{4,1},{5,0},{6,3},{7,2},{8,13},{9,12},{10,... | collective-permute-start | bytes 36872 | tf_op jit(solution)/shard_map/ppermute | solution.py:370
  29.6 2.3 %collective-permute-start.16 = (bf16[24,256]{1,0:T(8,128)(2,1)S(1)}, bf16[24,256]{1,0:T(8,128)(2,1)S(1)}, u32[]{:S(2)}, u32[]{:S(2)}) collective-permute-start(bf16[24,256]{1,0:T(8,128)(2,1)S(1)} %get-tuple-element.80), channel_id=1, source_target_pairs={{0,4},{1,5},{2,6},{3,7},{4,0},{5,1},{6,2},{7,3},{8,12},{9,13},{10,... | collective-permute-start | bytes 36872 | tf_op jit(solution)/shard_map/ppermute | solution.py:370

commit v9 on v8

--- a/solution.py
+++ b/solution.py
@@ -118,15 +118,16 @@
 
 
 def rim_kernel(n_col, per_sample, *refs):
-    tiles, (*parts, to_core, to_chip, joined, rims) = refs[:n_col], refs[n_col:]
+    tiles, (*parts, query, to_core, to_chip, joined, rims) = refs[:n_col], refs[n_col:]
     col = lax.axis_index("col")
     rows = tiles[0].shape[1]
-    lanes = to_core.shape[1]
+    lanes = to_chip.shape[1]
     used = rims.shape[1] * rims.shape[2]
     inner = jnp.where(lax.axis_index("row") % 2 == 1, rows - 1, 0)
     cols = tiles[0].shape[2]
     rims[...] = jnp.zeros_like(rims)
-    for side, (row, out) in enumerate(((inner, to_core), (rows - 1 - inner, to_chip))):
+    to_core[1] = query[...]
+    for side, (row, out) in enumerate(((inner, to_core.at[0]), (rows - 1 - inner, to_chip))):
         for k, tile in enumerate(tiles):
             rims[side, col ^ k, :cols] = pick(tile[0, row], col // per_sample)
         flat = rims[side].reshape(used, -1).astype(BF16)
@@ -198,7 +199,7 @@
     missing = jnp.logical_or(row == 1, row == lax.axis_size("row") - 2)
     halo_chip = jnp.where(core == chip % 2, last, halo_odd[...])
     halo_chip = jnp.where(missing, jnp.zeros_like(last), halo_chip)
-    inner = halo_core[...]
+    inner = halo_core[0]
     parts = channels // lanes
 
     def spread(halo):
@@ -223,83 +224,145 @@
     go_ref[...] = dot(grad_z, out_weight[pl.ds(first, lanes), :], 1, 1).astype(BF16)
 
 
-def attention_kernel(offsets, kv_sent, kv_kept, go_ref, dkv_sent, dkv_kept, dq_ref):
-    strip, lanes = go_ref.shape
-    half = lanes // 2
-    factor = half**-0.5
-    low = lax.broadcasted_iota(jnp.int32, (strip, lanes), 1) < half
-    query, grad_out = kv_kept[kv_kept.shape[0] - 1], go_ref[...]
+def by_head(query, grad_out):
+    low = lax.broadcasted_iota(jnp.int32, query.shape, 1) < query.shape[1] // 2
     none = jnp.zeros_like(query)
     asked = (jnp.where(low, none, query), jnp.where(low, query, none))
-    cotangent = (jnp.where(low, grad_out, none), jnp.where(low, none, grad_out))
-    chunks = []
-    for j, offset in enumerate(offsets):
-        even = offset != 0 and offset.bit_count() % 2 == 0
-        chunks.append((kv_sent, dkv_kept if even else dkv_sent, j, offset))
-        chunks.append((kv_kept, dkv_sent if even else dkv_kept, j, offset))
-
+    return asked, (jnp.where(low, grad_out, none), jnp.where(low, none, grad_out))
+
+
+def chunks_of(offsets):
+    even = [offset != 0 and offset.bit_count() % 2 == 0 for offset in offsets]
+    sent = [(e, j, offset) for j, (e, offset) in enumerate(zip(even, offsets))]
+    return sent, [(not e, j, offset) for e, j, offset in sent]
+
+
+def all_keys(kv, head):
+    return jnp.concatenate(
+        [kv[2 * j + head].astype(F32) for j in range(kv.shape[0] // 2)], 0
+    ).astype(BF16)
+
+
+def score_kernel(kv, asker, grad_out, scores, probs_grads):
+    asked, cotangent = by_head(asker[1], grad_out[...])
+    for head in (0, 1):
+        keys = all_keys(kv, head)
+        scores[head] = dot(keys, asked[head], 1, 1)
+        probs_grads[head] = dot(keys, cotangent[head], 1, 1)
+
+
+def softmax_kernel(offsets, kv_kept, asker, grad_out, scores, probs_grads, *outs):
+    dkv_sent, grad_scores, kept_probs = outs
+    strip = grad_out.shape[0]
     heads = (0, 1)
-    if len(chunks) <= UNROLLED_CHUNKS:
-        kvs = [
-            jnp.concatenate([src[2 * j + h].astype(F32) for src, _, j, _ in chunks], 0).astype(BF16)
-            for h in heads
-        ]
-        scores = [dot(kvs[h], asked[h], 1, 1) for h in heads]
-        probs_grads = [dot(kvs[h], cotangent[h], 1, 1) for h in heads]
-        exps = [jnp.exp(s - jnp.max(s, axis=0, keepdims=True)) for s in scores]
-        scales = [1.0 / jnp.sum(e, axis=0, keepdims=True) for e in exps]
-        row_dots = [
-            jnp.sum(e * g, axis=0, keepdims=True) * s for e, g, s in zip(exps, probs_grads, scales)
-        ]
-        probs = [e * s for e, s in zip(exps, scales)]
-        grad_scores = [
-            (p * (g - r)).astype(BF16) for p, g, r in zip(probs, probs_grads, row_dots)
-        ]
-        grad_query = [dot(grad_scores[h], kvs[h], 0, 0) for h in heads]
-        for h in heads:
-            given = jnp.concatenate([grad_scores[h], probs[h].astype(BF16)], 1)
-            dkv = dot(given, jnp.concatenate([asked[h], cotangent[h]], 0))
-            for i, (_, dst, _, offset) in enumerate(chunks):
-                dst[offset, h] = dkv[i * strip : (i + 1) * strip].astype(BF16)
-    else:
-        grad_query = []
-        for head in heads:
-            ask, cot = asked[head], cotangent[head]
-
-            def gather(kv, carry):
-                top, norm, weighted = carry
-                scores = dot(kv, ask, 1, 1)
-                new = jnp.maximum(top, jnp.max(scores, axis=0, keepdims=True))
-                exps = jnp.exp(scores - new)
-                rescale = jnp.exp(top - new)
-                weights = jnp.sum(exps * dot(kv, cot, 1, 1), axis=0, keepdims=True)
-                return (
-                    new,
-                    norm * rescale + jnp.sum(exps, axis=0, keepdims=True),
-                    weighted * rescale + weights,
-                )
-
-            zero = jnp.zeros((1, strip), F32)
-            stats = (jnp.full((1, strip), -jnp.inf, F32), zero, zero)
-            for src in (kv_sent, kv_kept):
-                stats = lax.fori_loop(
-                    0,
-                    len(offsets),
-                    lambda j, carry, src=src: gather(src[2 * j + head], carry),
-                    stats,
-                )
-            top, norm, weighted = stats
-            scale = 1.0 / norm
-            total = jnp.zeros((strip, lanes), F32)
-            for src, dst, j, offset in chunks:
-                kv = src[2 * j + head]
+    asked, cotangent = by_head(asker[1], grad_out[...])
+    sent, kept = chunks_of(offsets)
+
+    def arranged(first, second):
+        return jnp.concatenate(
+            [
+                (second if late else first)[j * strip : (j + 1) * strip]
+                for late, j, _ in sent + kept
+            ],
+            0,
+        )
+
+    keys = [all_keys(kv_kept, h) for h in heads]
+    late_scores = [dot(keys[h], asked[h], 1, 1) for h in heads]
+    late_grads = [dot(keys[h], cotangent[h], 1, 1) for h in heads]
+    both = [arranged(scores[h], late_scores[h]) for h in heads]
+    grads = [arranged(probs_grads[h], late_grads[h]) for h in heads]
+    exps = [jnp.exp(x - jnp.max(x, axis=0, keepdims=True)) for x in both]
+    scales = [1.0 / jnp.sum(e, axis=0, keepdims=True) for e in exps]
+    row_dots = [jnp.sum(e * g, axis=0, keepdims=True) * s for e, g, s in zip(exps, grads, scales)]
+    probs = [(e * s) for e, s in zip(exps, scales)]
+    middle = len(sent) * strip
+    for h in heads:
+        grad = (probs[h] * (grads[h] - row_dots[h])).astype(BF16)
+        grad_scores[h] = grad
+        rounded = probs[h].astype(BF16)
+        kept_probs[h] = rounded[middle:]
+        given = jnp.concatenate([grad[:middle], rounded[:middle]], 1)
+        dkv = dot(given, jnp.concatenate([asked[h], cotangent[h]], 0))
+        for i, (_, _, offset) in enumerate(sent):
+            dkv_sent[offset, h] = dkv[i * strip : (i + 1) * strip].astype(BF16)
+
+
+def base(dq, gz_ref, input_weight):
+    strip, lanes = dq.shape
+    part = lax.axis_index("col") % (gz_ref.shape[1] // lanes)
+    first = pl.multiple_of(part * lanes, lanes)
+    grad = jnp.where(part == 0, gz_ref[...].astype(F32), 0.0)
+    query = pltpu.roll(dq * (lanes // 2) ** -0.5, lanes // 2, 1).astype(BF16)
+    return grad + dot(query, input_weight[:, pl.ds(first, lanes)], 1, 1)
+
+
+def finish_kernel(offsets, *refs):
+    kv_sent, kv_kept, asker, grad_out, grad_scores, kept_probs, gz_ref, input_weight = refs[:8]
+    dkv_kept, base_ref = refs[8:]
+    strip, lanes = grad_out.shape
+    asked, cotangent = by_head(asker[1], grad_out[...])
+    sent, kept = chunks_of(offsets)
+    middle = len(sent) * strip
+    query = []
+    for h in (0, 1):
+        given = jnp.concatenate([grad_scores[h, middle:], kept_probs[h]], 1)
+        dkv = dot(given, jnp.concatenate([asked[h], cotangent[h]], 0))
+        for i, (_, _, offset) in enumerate(kept):
+            dkv_kept[offset, h] = dkv[i * strip : (i + 1) * strip].astype(BF16)
+        keys = jnp.concatenate(
+            [(kv_kept if late else kv_sent)[2 * j + h].astype(F32) for late, j, _ in sent + kept], 0
+        )
+        query.append(dot(grad_scores[h], keys.astype(BF16), 0, 0))
+    low = lax.broadcasted_iota(jnp.int32, (strip, lanes), 1) < lanes // 2
+    base_ref[...] = base(jnp.where(low, query[1], query[0]), gz_ref, input_weight)
+
+
+def long_kernel(offsets, *refs):
+    kv_sent, kv_kept, asker, grad_out, gz_ref, input_weight, dkv_sent, dkv_kept, base_ref = refs
+    strip, lanes = grad_out.shape
+    asked, cotangent = by_head(asker[1], grad_out[...])
+    sent, kept = chunks_of(offsets)
+    query = []
+    for head in (0, 1):
+        ask, cot = asked[head], cotangent[head]
+
+        def gather(kv, carry):
+            top, norm, weighted = carry
+            scores = dot(kv, ask, 1, 1)
+            new = jnp.maximum(top, jnp.max(scores, axis=0, keepdims=True))
+            exps = jnp.exp(scores - new)
+            rescale = jnp.exp(top - new)
+            weights = jnp.sum(exps * dot(kv, cot, 1, 1), axis=0, keepdims=True)
+            return (
+                new,
+                norm * rescale + jnp.sum(exps, axis=0, keepdims=True),
+                weighted * rescale + weights,
+            )
+
+        zero = jnp.zeros((1, strip), F32)
+        stats = (jnp.full((1, strip), -jnp.inf, F32), zero, zero)
+        for src in (kv_sent, kv_kept):
+            stats = lax.fori_loop(
+                0,
+                len(offsets),
+                lambda j, carry, src=src: gather(src[2 * j + head], carry),
+                stats,
+            )
+        top, norm, weighted = stats
+        scale = 1.0 / norm
+        total = jnp.zeros((strip, lanes), F32)
+        for dst, chunks in ((dkv_sent, sent), (dkv_kept, kept)):
+            for late, j, offset in chunks:
+                kv = (kv_kept if late else kv_sent)[2 * j + head]
                 probs = jnp.exp(dot(kv, ask, 1, 1) - top) * scale
                 grad_scores = (probs * (dot(kv, cot, 1, 1) - weighted * scale)).astype(BF16)
                 dkv = dot(grad_scores, ask) + dot(probs.astype(BF16), cot)
                 dst[offset, head] = dkv.astype(BF16)
                 total = total + dot(grad_scores, kv, 0, 0)
-            grad_query.append(total)
-    dq_ref[...] = jnp.where(low, grad_query[1], grad_query[0]) * factor
+        query.append(total)
+    low = lax.broadcasted_iota(jnp.int32, (strip, lanes), 1) < lanes // 2
+    base_ref[...] = base(jnp.where(low, query[1], query[0]), gz_ref, input_weight)
 
 
 def core_sum_kernel(own, received, *outs):
@@ -310,20 +373,19 @@
 def project_kernel(n_col, per_sample, *refs):
     *refs, cut = refs
     n_in = len(refs) - n_col
-    *parts, dq_ref, gz_ref, input_weight, tiles = refs[:n_in]
+    *parts, base_ref, input_weight, tiles = refs[:n_in]
     outs = refs[n_in:]
     col = lax.axis_index("col")
     part = col % per_sample
     total = sum(ref[...].astype(F32) for ref in parts)
-    strip, lanes = dq_ref.shape
+    _, strip, lanes = parts[0].shape
     half = lanes // 2
-    channels = gz_ref.shape[1]
+    channels = base_ref.shape[1]
     low = lax.broadcasted_iota(jnp.int32, (strip, lanes), 1) < half
     dv = jnp.where(low, total[0], total[1])
     dk = pltpu.roll(jnp.where(low, total[1], total[0]), half, 1)
-    dq = pltpu.roll(dq_ref[...], half, 1)
-    grad = jnp.where(part == 0, gz_ref[...].astype(F32), 0.0)
-    for kind, value in enumerate((dq, dk, dv)):
+    grad = base_ref[...]
+    for kind, value in ((1, dk), (2, dv)):
         first = pl.multiple_of(kind * channels + part * lanes, lanes)
         weight = input_weight[:, pl.ds(first, lanes)]
         grad = grad + dot(value.astype(BF16), weight, 1, 1)
@@ -436,9 +498,9 @@
     blocks = sum(part.shape[0] for part in parts)
     rim_core, rim_chip, sent = call(
         functools.partial(rim_kernel, n_col, per_sample),
-        (rim, rim, held((blocks + 1, strip, lanes), BF16)),
+        (held((2, strip, lanes), BF16), rim, held((blocks + 1, strip, lanes), BF16)),
         [pltpu.VMEM((2, n_col, padded, channels), F32)],
-    )(*tiles, *parts)
+    )(*tiles, *parts, query)
     received = to_chip(sent, distances[-1])
     halo_odd, halo_core = to_odd_chip(rim_chip), to_core(rim_core)
 
@@ -451,7 +513,7 @@
     received, conv, halo_odd, halo_core = lax.optimization_barrier(
         (received, conv, halo_odd, halo_core)
     )
-    joined = doubled(sent, received, query[None], counts=(blocks, blocks, 1))
+    joined = doubled(sent, received, counts=(blocks, blocks))
     other = to_core(joined)
     grad_z, grad_out = call(
         rim_conv_kernel,
@@ -459,12 +521,29 @@
     )(halo_core, received, halo_odd, conv, gate, rim_shifts, conv_weight, out_weight)
 
     block = held((chips, pairs, strip, lanes), BF16)
-    dkv_sent, dkv_kept, dq = call(
-        functools.partial(attention_kernel, offsets), (block, block, held((strip, lanes), F32))
-    )(joined, other, grad_out)
+    if 2 * chips <= UNROLLED_CHUNKS:
+        half = held((pairs, chips * strip, strip), F32)
+        scores, probs_grads = call(score_kernel, (half, half))(joined, halo_core, grad_out)
+        dkv_sent, grad_scores, kept_probs = call(
+            functools.partial(softmax_kernel, offsets),
+            (
+                block,
+                held((pairs, 2 * chips * strip, strip), BF16),
+                held((pairs, chips * strip, strip), BF16),
+            ),
+        )(other, halo_core, grad_out, scores, probs_grads)
+        from_core = to_core(dkv_sent)
+        dkv_kept, complete = call(functools.partial(finish_kernel, offsets), (block, whole))(
+            joined, other, halo_core, grad_out, grad_scores, kept_probs, grad_z, input_weight
+        )
+    else:
+        dkv_sent, dkv_kept, complete = call(
+            functools.partial(long_kernel, offsets), (block, block, whole)
+        )(joined, other, halo_core, grad_out, grad_z, input_weight)
+        from_core = to_core(dkv_sent)
 
     sums = call(core_sum_kernel, [held((pairs, strip, lanes), BF16) for _ in range(chips)])(
-        dkv_kept, to_core(dkv_sent)
+        dkv_kept, from_core
     )
     far_near = [k for pair in zip(range(chips - 1, 0, -1), range(1, chips)) for k in pair]
     order = list(dict.fromkeys(far_near))
@@ -475,7 +554,7 @@
         functools.partial(project_kernel, n_col, per_sample),
         [held((rows * padded, channels), BF16)] * n_col,
         [pltpu.VMEM((n_col, rows * padded, channels), F32)],
-    )(*parts, dq, grad_z, input_weight, jnp.asarray(selected, BF16))
+    )(*parts, complete, input_weight, jnp.asarray(selected, BF16))
     grad_input = call(
         functools.partial(output_kernel, per_sample),
         pltpu.HBM((rows, cols, samples, channels), BF16),

time: 32.7 us -> 32.5 us (level)
  waiting for transfers between devices: 9.27 us -> 8.07 us
  Pallas kernels: 6.32 us -> 6.88 us
  starting transfers between devices: 16.8 us -> 17.2 us
    ppermute x3, waiting for transfers between devices: 1.85 us -> 1.01 us  [to_core(): return lax.ppermute(array, 'row', [(i, i ^ 1) for i in range(n_row)])]
    pallas_call x10 -> x12, Pallas kernels: 6.32 us -> 6.88 us  [run(): pl.pallas_call(kernel, out_shape=out_shape, in_specs=specs, out_specs=jax...]
    ppermute x8, waiting for transfers between devices: 3.66 us -> 3.29 us  [to_col(): return lax.ppermute(array, ('row', 'col'), pairs_of)]
    ppermute x8, starting transfers between devices: 6.88 us -> 7.25 us  [to_col(): return lax.ppermute(array, ('row', 'col'), pairs_of)]
  transfers between devices with their start and end apart: 17 -> 17, of which waited for: 9 -> 9; matrix products, arithmetic and copies ran while one was open for 0% -> 0% of each run, Pallas kernels for 10% -> 12%
where the time goes in v9:
time: 32.5 us; the launch traced here: 32.3 us
  starting transfers between devices  17.2 us (53%)
  waiting for transfers between devices  8.07 us (25%)
  Pallas kernels  6.88 us (21%)
    ppermute x5, starting transfers between devices, to_chip(): lax.ppermute(array, 'row', [(i, i ^ 2 * k + 1) for i in range(n_row)])  8.97 us
    ppermute x8, starting transfers between devices, to_col(): return lax.ppermute(array, ('row', 'col'), pairs_of)  7.25 us
    pallas_call x12, Pallas kernels, run(): pl.pallas_call(kernel, out_shape=out_shape, in_specs=specs, out_specs=jax...  6.88 us
    ppermute x5, waiting for transfers between devices, to_chip(): lax.ppermute(array, 'row', [(i, i ^ 2 * k + 1) for i in range(n_row)])  3.76 us
    ppermute x8, waiting for transfers between devices, to_col(): return lax.ppermute(array, ('row', 'col'), pairs_of)  3.29 us
    ppermute x3, waiting for transfers between devices, to_core(): return lax.ppermute(array, 'row', [(i, i ^ 1) for i in range(n_row)])  1.01 us
    ppermute x3, starting transfers between devices, to_core(): return lax.ppermute(array, 'row', [(i, i ^ 1) for i in range(n_row)])  0.73 us
  transfers between devices with their start and end apart: 17, of which 9 were waited for; matrix products, arithmetic and copies ran while one was open for 0% of the time, Pallas kernels for 12%

profile of v9, /device:TPU:0, one launch (start us, length us, event | category | flops | bytes accessed | tf_op | source)
XLA Modules:
  0.0 32.3 jit_solution(10430408592153899783)
XLA Ops:
  0.0 1.0 %shard_map.109 = (bf16[2,3,6,2,256]{4,3,2,1,0:T(2,128)(2,1)S(1)}, bf16[2,72,128]{2,1,0:T(8,128)(2,1)S(1)}, bf16[72,128]{1,0:T(8,128)(2,1)S(1)}) custom-call(bf16[3,6,2,256]{3,2,1,0:T(2,128)(2,1)} %bitcast.9, bf16[3,6,2,256]{3,2,1,0:T(2,128)(2,1)} %bitcast.10, bf16[2,64,72]{2,1,0:T(8,128)(2,1)} %bitcast.6, bf16[2,64,72]{2,1,0:T(8,128)(2,1)} %bitcast.7, ...), custom_call_target="tpu_custom_call" | custom-call | tf_op jit(solution)/shard_map/pallas_call | solution.py:35
  1.0 3.5 %collective-permute-start.4 = (bf16[2,72,128]{2,1,0:T(8,128)(2,1)S(1)}, bf16[2,72,128]{2,1,0:T(8,128)(2,1)S(1)}, u32[]{:S(2)}, u32[]{:S(2)}) collective-permute-start(bf16[2,72,128]{2,1,0:T(8,128)(2,1)S(1)} %get-tuple-element.48.refs_4_), channel_id=1, source_target_pairs={{0,20},{4,16},{8,28},{12,24},{16,4},{20,0},{24,12},{28,8},{1,21},{... | collective-permute-start | bytes 110600 | tf_op jit(solution)/shard_map/ppermute | solution.py:435
  4.5 2.7 %collective-permute-start.3 = (bf16[2,3,6,2,256]{4,3,2,1,0:T(2,128)(2,1)S(1)}, bf16[2,3,6,2,256]{4,3,2,1,0:T(2,128)(2,1)S(1)}, u32[]{:S(2)}, u32[]{:S(2)}) collective-permute-start(bf16[2,3,6,2,256]{4,3,2,1,0:T(2,128)(2,1)S(1)} %get-tuple-element.47), channel_id=1, source_target_pairs={{0,7},{1,6},{2,5},{3,4},{4,3},{5,2},{6,1},{7,0},{8,15},{9,14},{10,... | collective-permute-start | bytes 110600 | tf_op jit(solution)/shard_map/ppermute | solution.py:432
  7.3 0.0 collective-permute-start.2
  7.3 0.8 %collective-permute-start.1 = (bf16[2,3,6,2,256]{4,3,2,1,0:T(2,128)(2,1)S(1)}, bf16[2,3,6,2,256]{4,3,2,1,0:T(2,128)(2,1)S(1)}, u32[]{:S(2)}, u32[]{:S(2)}) collective-permute-start(bf16[2,3,6,2,256]{4,3,2,1,0:T(2,128)(2,1)S(1)} %get-tuple-element.47), channel_id=1, source_target_pairs={{0,5},{1,4},{2,7},{3,6},{4,1},{5,0},{6,3},{7,2},{8,13},{9,12},{10,... | collective-permute-start | bytes 110600 | tf_op jit(solution)/shard_map/ppermute | solution.py:432
  8.0 0.0 collective-permute-start
  8.0 1.4 %shard_map.110 = (bf16[3,72,96]{2,1,0:T(8,128)(2,1)S(1)}, bf16[3,24,32]{2,1,0:T(8,128)(2,1)S(1)}, bf16[3,3,256,256]{3,2,1,0:T(8,128)(2,1)S(1)}, bf16[256,256]{1,0:T(8,128)(2,1)S(1)}) custom-call(bf16[3,72,96]{2,1,0:T(8,128)(2,1)} %constant.6.clone.refs_0_, bf16[3,24,32]{2,1,0:T(8,128)(2,1)} %constant.7.clone.refs_1_, bf16[3,3,256,256]{3,2,1,0:T(8,128)(2,1)} %refs_2_.1, ...), custom_call_target="tpu_custom_call" | custom-call | tf_op jit(solution)/shard_map/pallas_call | solution.py:35
  9.4 0.0 collective-permute-done.4.refs_5_
  9.4 0.0 collective-permute-done.3.refs_3_
  9.4 1.6 %collective-permute-done.2.refs_2_ = bf16[2,3,6,2,256]{4,3,2,1,0:T(2,128)(2,1)S(1)} collective-permute-done((bf16[2,3,6,2,256]{4,3,2,1,0:T(2,128)(2,1)S(1)}, bf16[2,3,6,2,256]{4,3,2,1,0:T(2,128)(2,1)S(1)}, u32[]{:S(2)}, u32[]{:S(2)}) %collective-permute-start.2) | collective-permute-done | bytes 36896 | tf_op jit(solution)/shard_map/ppermute | solution.py:432
  11.0 0.0 collective-permute-done.1.refs_1_
  11.0 0.0 collective-permute-done.refs_0_
  11.0 0.2 shard_map.111
  11.2 1.5 %collective-permute-start.5 = (bf16[5,72,128]{2,1,0:T(8,128)(2,1)S(1)}, bf16[5,72,128]{2,1,0:T(8,128)(2,1)S(1)}, u32[]{:S(2)}, u32[]{:S(2)}) collective-permute-start(bf16[5,72,128]{2,1,0:T(8,128)(2,1)S(1)} %get-tuple-element.59.refs_0_), channel_id=1, source_target_pairs={{0,12},{4,8},{8,4},{12,0},{16,28},{20,24},{24,20},{28,16},{1,13},{... | collective-permute-start | bytes 276488 | tf_op jit(solution)/shard_map/ppermute | solution.py:435
  12.7 0.3 collective-permute-start.7
  13.0 0.2 collective-permute-start.6
  13.2 1.2 %shard_map.112 = (f32[72,256]{1,0:T(8,128)S(1)}, f32[72,256]{1,0:T(8,128)S(1)}) custom-call(bf16[2,3,6,2,256]{4,3,2,1,0:T(2,128)(2,1)S(1)} %collective-permute-done.refs_0_, bf16[2,3,6,2,256]{4,3,2,1,0:T(2,128)(2,1)S(1)} %collective-permute-done.1.refs_1_, bf16[2,3,6,2,256]{4,3,2,1,0:T(2,128)(2,1)S(1)} %collective-permute-done.2.refs_2_, ...), custom_call_target="tpu_custom_call" | custom-call | tf_op jit(solution)/shard_map/pallas_call | solution.py:35
  14.4 0.0 collective-permute-done.6.halo_odd
  14.4 0.0 collective-permute-done.7.halo_core.asker.refs_2_
  14.4 1.5 %collective-permute-done.5.refs_1_.halo_last = bf16[5,72,128]{2,1,0:T(8,128)(2,1)S(1)} collective-permute-done((bf16[5,72,128]{2,1,0:T(8,128)(2,1)S(1)}, bf16[5,72,128]{2,1,0:T(8,128)(2,1)S(1)}, u32[]{:S(2)}, u32[]{:S(2)}) %collective-permute-start.5) | collective-permute-done | bytes 92192 | tf_op jit(solution)/shard_map/ppermute | solution.py:435
  15.9 0.2 collective-permute-start.8
  16.1 0.0 copy-start
  16.1 0.6 %shard_map.114 = (bf16[72,256]{1,0:T(8,128)(2,1)S(1)}, bf16[72,128]{1,0:T(8,128)(2,1)S(1)}) custom-call(bf16[2,72,128]{2,1,0:T(8,128)(2,1)S(1)} %collective-permute-done.7.halo_core.asker.refs_2_, bf16[5,72,128]{2,1,0:T(8,128)(2,1)S(1)} %collective-permute-done.5.refs_1_.halo_last, bf16[72,128]{1,0:T(8,128)(2,1)S(1)} %collective-permute-done.6.halo_odd, ...), custom_call_target="tpu_custom_call" | custom-call | tf_op jit(solution)/shard_map/pallas_call | solution.py:35
  16.7 0.2 shard_map.115
  17.0 0.0 copy-start.1
  17.0 0.3 %collective-permute-done.8.kv_kept.refs_1_ = bf16[8,72,128]{2,1,0:T(8,128)(2,1)S(1)} collective-permute-done((bf16[8,72,128]{2,1,0:T(8,128)(2,1)S(1)}, bf16[8,72,128]{2,1,0:T(8,128)(2,1)S(1)}, u32[]{:S(2)}, u32[]{:S(2)}) %collective-permute-start.8) | collective-permute-done | bytes 147488 | tf_op jit(solution)/shard_map/ppermute | solution.py:438
  17.4 0.7 %shard_map.116 = (bf16[4,2,72,128]{3,2,1,0:T(8,128)(2,1)S(1)}, bf16[2,576,72]{2,1,0:T(8,128)(2,1)S(1)}, bf16[2,288,72]{2,1,0:T(8,128)(2,1)S(1)}) custom-call(bf16[8,72,128]{2,1,0:T(8,128)(2,1)S(1)} %collective-permute-done.8.kv_kept.refs_1_, bf16[2,72,128]{2,1,0:T(8,128)(2,1)S(1)} %collective-permute-done.7.halo_core.asker.refs_2_, ...), custom_call_target="tpu_custom_call" | custom-call | tf_op jit(solution)/shard_map/pallas_call | solution.py:35
  18.1 0.2 collective-permute-start.9
  18.3 0.0 copy-done
  18.3 0.5 %shard_map.117 = (bf16[4,2,72,128]{3,2,1,0:T(8,128)(2,1)S(1)}, f32[72,256]{1,0:T(8,128)S(1)}) custom-call(bf16[8,72,128]{2,1,0:T(8,128)(2,1)S(1)} %shard_map.113.kv.refs_0_, bf16[8,72,128]{2,1,0:T(8,128)(2,1)S(1)} %collective-permute-done.8.kv_kept.refs_1_, bf16[2,72,128]{2,1,0:T(8,128)(2,1)S(1)} %collective-permute-done.7.halo_core.asker.refs_2_, ...), custom_call_target="tpu_custom_call" | custom-call | tf_op jit(solution)/shard_map/pallas_call | solution.py:35
  18.9 0.7 %collective-permute-done.9.received = bf16[4,2,72,128]{3,2,1,0:T(8,128)(2,1)S(1)} collective-permute-done((bf16[4,2,72,128]{3,2,1,0:T(8,128)(2,1)S(1)}, bf16[4,2,72,128]{3,2,1,0:T(8,128)(2,1)S(1)}, u32[]{:S(2)}, u32[]{:S(2)}) %collective-permute-start.9) | collective-permute-done | bytes 147488 | tf_op jit(solution)/shard_map/ppermute | solution.py:438
  19.6 1.1 %collective-permute-start.10 = (bf16[2,72,128]{2,1,0:T(8,128)(2,1)S(1)}, bf16[2,72,128]{2,1,0:T(8,128)(2,1)S(1)}, u32[]{:S(2)}, u32[]{:S(2)}) collective-permute-start(bf16[2,72,128]{2,1,0:T(8,128)(2,1)S(1)} %get-tuple-element.80), channel_id=1, source_target_pairs={{0,28},{4,24},{8,20},{12,16},{16,12},{20,8},{24,4},{28,0},{1,29},{... | collective-permute-start | bytes 110600 | tf_op jit(solution)/shard_map/ppermute | solution.py:435
  20.6 0.4 %collective-permute-start.11 = (bf16[2,72,128]{2,1,0:T(8,128)(2,1)S(1)}, bf16[2,72,128]{2,1,0:T(8,128)(2,1)S(1)}, u32[]{:S(2)}, u32[]{:S(2)}) collective-permute-start(bf16[2,72,128]{2,1,0:T(8,128)(2,1)S(1)} %get-tuple-element.81), channel_id=1, source_target_pairs={{0,12},{4,8},{8,4},{12,0},{16,28},{20,24},{24,20},{28,16},{1,13},{... | collective-permute-start | bytes 110600 | tf_op jit(solution)/shard_map/ppermute | solution.py:435
  21.1 2.5 %collective-permute-start.12 = (bf16[2,72,128]{2,1,0:T(8,128)(2,1)S(1)}, bf16[2,72,128]{2,1,0:T(8,128)(2,1)S(1)}, u32[]{:S(2)}, u32[]{:S(2)}) collective-permute-start(bf16[2,72,128]{2,1,0:T(8,128)(2,1)S(1)} %get-tuple-element.82), channel_id=1, source_target_pairs={{0,20},{4,16},{8,28},{12,24},{16,4},{20,0},{24,12},{28,8},{1,21},{... | collective-permute-start | bytes 110600 | tf_op jit(solution)/shard_map/ppermute | solution.py:435
  23.5 1.4 %collective-permute-done.10.refs_0_ = bf16[2,72,128]{2,1,0:T(8,128)(2,1)S(1)} collective-permute-done((bf16[2,72,128]{2,1,0:T(8,128)(2,1)S(1)}, bf16[2,72,128]{2,1,0:T(8,128)(2,1)S(1)}, u32[]{:S(2)}, u32[]{:S(2)}) %collective-permute-start.10) | collective-permute-done | bytes 36896 | tf_op jit(solution)/shard_map/ppermute | solution.py:435
  24.9 0.0 collective-permute-done.11.refs_1_
  24.9 0.9 %collective-permute-done.12.refs_2_ = bf16[2,72,128]{2,1,0:T(8,128)(2,1)S(1)} collective-permute-done((bf16[2,72,128]{2,1,0:T(8,128)(2,1)S(1)}, bf16[2,72,128]{2,1,0:T(8,128)(2,1)S(1)}, u32[]{:S(2)}, u32[]{:S(2)}) %collective-permute-start.12) | collective-permute-done | bytes 36896 | tf_op jit(solution)/shard_map/ppermute | solution.py:435
  25.8 0.0 copy-done.1
  25.8 0.4 %shard_map.119 = (bf16[24,256]{1,0:T(8,128)(2,1)S(1)}, bf16[24,256]{1,0:T(8,128)(2,1)S(1)}, bf16[24,256]{1,0:T(8,128)(2,1)S(1)}, bf16[24,256]{1,0:T(8,128)(2,1)S(1)}) custom-call(bf16[2,72,128]{2,1,0:T(8,128)(2,1)S(1)} %collective-permute-done.10.refs_0_, bf16[2,72,128]{2,1,0:T(8,128)(2,1)S(1)} %collective-permute-done.11.refs_1_, ...), custom_call_target="tpu_custom_call" | custom-call | tf_op jit(solution)/shard_map/pallas_call | solution.py:35
  26.2 1.6 %collective-permute-start.13 = (bf16[24,256]{1,0:T(8,128)(2,1)S(1)}, bf16[24,256]{1,0:T(8,128)(2,1)S(1)}, u32[]{:S(2)}, u32[]{:S(2)}) collective-permute-start(bf16[24,256]{1,0:T(8,128)(2,1)S(1)} %get-tuple-element.85), channel_id=1, source_target_pairs={{0,7},{1,6},{2,5},{3,4},{4,3},{5,2},{6,1},{7,0},{8,15},{9,14},{10,... | collective-permute-start | bytes 36872 | tf_op jit(solution)/shard_map/ppermute | solution.py:432
  27.8 0.7 %collective-permute-start.14 = (bf16[24,256]{1,0:T(8,128)(2,1)S(1)}, bf16[24,256]{1,0:T(8,128)(2,1)S(1)}, u32[]{:S(2)}, u32[]{:S(2)}) collective-permute-start(bf16[24,256]{1,0:T(8,128)(2,1)S(1)} %get-tuple-element.86), channel_id=1, source_target_pairs={{0,6},{1,7},{2,4},{3,5},{4,2},{5,3},{6,0},{7,1},{8,14},{9,15},{10,... | collective-permute-start | bytes 36872 | tf_op jit(solution)/shard_map/ppermute | solution.py:432
  28.5 1.4 %collective-permute-start.15 = (bf16[24,256]{1,0:T(8,128)(2,1)S(1)}, bf16[24,256]{1,0:T(8,128)(2,1)S(1)}, u32[]{:S(2)}, u32[]{:S(2)}) collective-permute-start(bf16[24,256]{1,0:T(8,128)(2,1)S(1)} %get-tuple-element.87), channel_id=1, source_target_pairs={{0,5},{1,4},{2,7},{3,6},{4,1},{5,0},{6,3},{7,2},{8,13},{9,12},{10,... | collective-permute-start | bytes 36872 | tf_op jit(solution)/shard_map/ppermute | solution.py:432
  29.9 0.0 collective-permute-start.16
  29.9 0.3 %collective-permute-done.13.refs_0_ = bf16[24,256]{1,0:T(8,128)(2,1)S(1)} collective-permute-done((bf16[24,256]{1,0:T(8,128)(2,1)S(1)}, bf16[24,256]{1,0:T(8,128)(2,1)S(1)}, u32[]{:S(2)}, u32[]{:S(2)}) %collective-permute-start.13) | collective-permute-done | bytes 12320 | tf_op jit(solution)/shard_map/ppermute | solution.py:432
  30.3 0.6 %collective-permute-done.14.refs_1_ = bf16[24,256]{1,0:T(8,128)(2,1)S(1)} collective-permute-done((bf16[24,256]{1,0:T(8,128)(2,1)S(1)}, bf16[24,256]{1,0:T(8,128)(2,1)S(1)}, u32[]{:S(2)}, u32[]{:S(2)}) %collective-permute-start.14) | collective-permute-done | bytes 12320 | tf_op jit(solution)/shard_map/ppermute | solution.py:432
  30.9 0.7 %collective-permute-done.15.refs_2_ = bf16[24,256]{1,0:T(8,128)(2,1)S(1)} collective-permute-done((bf16[24,256]{1,0:T(8,128)(2,1)S(1)}, bf16[24,256]{1,0:T(8,128)(2,1)S(1)}, u32[]{:S(2)}, u32[]{:S(2)}) %collective-permute-start.15) | collective-permute-done | bytes 12320 | tf_op jit(solution)/shard_map/ppermute | solution.py:432
  31.6 0.0 collective-permute-done.16.refs_3_
  31.6 0.7 %shard_map.120 = bf16[3,6,2,256]{3,2,1,0:T(2,128)(2,1)} custom-call(bf16[24,256]{1,0:T(8,128)(2,1)S(1)} %collective-permute-done.13.refs_0_, bf16[24,256]{1,0:T(8,128)(2,1)S(1)} %collective-permute-done.14.refs_1_, bf16[24,256]{1,0:T(8,128)(2,1)S(1)} %collective-permute-done.15.refs_2_, bf16[24,256]{1,0:T(8,128)(2,1)S(1)} %collective-permute-done.16.refs_3_), custom_call_target="tpu_custom_call" | custom-call | tf_op jit(solution)/shard_map/pallas_call | solution.py:35
  (2 shorter events, 0.0 us)
Async XLA Ops:
  1.0 8.4 %collective-permute-start.4 = (bf16[2,72,128]{2,1,0:T(8,128)(2,1)S(1)}, bf16[2,72,128]{2,1,0:T(8,128)(2,1)S(1)}, u32[]{:S(2)}, u32[]{:S(2)}) collective-permute-start(bf16[2,72,128]{2,1,0:T(8,128)(2,1)S(1)} %get-tuple-element.48.refs_4_), channel_id=1, source_target_pairs={{0,20},{4,16},{8,28},{12,24},{16,4},{20,0},{24,12},{28,8},{1,21},{... | collective-permute-start | bytes 110600 | tf_op jit(solution)/shard_map/ppermute | solution.py:435
  4.5 4.9 %collective-permute-start.3 = (bf16[2,3,6,2,256]{4,3,2,1,0:T(2,128)(2,1)S(1)}, bf16[2,3,6,2,256]{4,3,2,1,0:T(2,128)(2,1)S(1)}, u32[]{:S(2)}, u32[]{:S(2)}) collective-permute-start(bf16[2,3,6,2,256]{4,3,2,1,0:T(2,128)(2,1)S(1)} %get-tuple-element.47), channel_id=1, source_target_pairs={{0,7},{1,6},{2,5},{3,4},{4,3},{5,2},{6,1},{7,0},{8,15},{9,14},{10,... | collective-permute-start | bytes 110600 | tf_op jit(solution)/shard_map/ppermute | solution.py:432
  7.3 3.8 %collective-permute-start.2 = (bf16[2,3,6,2,256]{4,3,2,1,0:T(2,128)(2,1)S(1)}, bf16[2,3,6,2,256]{4,3,2,1,0:T(2,128)(2,1)S(1)}, u32[]{:S(2)}, u32[]{:S(2)}) collective-permute-start(bf16[2,3,6,2,256]{4,3,2,1,0:T(2,128)(2,1)S(1)} %get-tuple-element.47), channel_id=1, source_target_pairs={{0,6},{1,7},{2,4},{3,5},{4,2},{5,3},{6,0},{7,1},{8,14},{9,15},{10,... | collective-permute-start | bytes 110600 | tf_op jit(solution)/shard_map/ppermute | solution.py:432
  7.3 3.8 %collective-permute-start.1 = (bf16[2,3,6,2,256]{4,3,2,1,0:T(2,128)(2,1)S(1)}, bf16[2,3,6,2,256]{4,3,2,1,0:T(2,128)(2,1)S(1)}, u32[]{:S(2)}, u32[]{:S(2)}) collective-permute-start(bf16[2,3,6,2,256]{4,3,2,1,0:T(2,128)(2,1)S(1)} %get-tuple-element.47), channel_id=1, source_target_pairs={{0,5},{1,4},{2,7},{3,6},{4,1},{5,0},{6,3},{7,2},{8,13},{9,12},{10,... | collective-permute-start | bytes 110600 | tf_op jit(solution)/shard_map/ppermute | solution.py:432
  8.0 3.0 %collective-permute-start = (bf16[2,3,6,2,256]{4,3,2,1,0:T(2,128)(2,1)S(1)}, bf16[2,3,6,2,256]{4,3,2,1,0:T(2,128)(2,1)S(1)}, u32[]{:S(2)}, u32[]{:S(2)}) collective-permute-start(bf16[2,3,6,2,256]{4,3,2,1,0:T(2,128)(2,1)S(1)} %get-tuple-element.47), channel_id=1, source_target_pairs={{0,4},{1,5},{2,6},{3,7},{4,0},{5,1},{6,2},{7,3},{8,12},{9,13},{10,... | collective-permute-start | bytes 110600 | tf_op jit(solution)/shard_map/ppermute | solution.py:432
  11.2 4.7 %collective-permute-start.5 = (bf16[5,72,128]{2,1,0:T(8,128)(2,1)S(1)}, bf16[5,72,128]{2,1,0:T(8,128)(2,1)S(1)}, u32[]{:S(2)}, u32[]{:S(2)}) collective-permute-start(bf16[5,72,128]{2,1,0:T(8,128)(2,1)S(1)} %get-tuple-element.59.refs_0_), channel_id=1, source_target_pairs={{0,12},{4,8},{8,4},{12,0},{16,28},{20,24},{24,20},{28,16},{1,13},{... | collective-permute-start | bytes 276488 | tf_op jit(solution)/shard_map/ppermute | solution.py:435
  12.7 1.7 %collective-permute-start.7 = (bf16[2,72,128]{2,1,0:T(8,128)(2,1)S(1)}, bf16[2,72,128]{2,1,0:T(8,128)(2,1)S(1)}, u32[]{:S(2)}, u32[]{:S(2)}) collective-permute-start(bf16[2,72,128]{2,1,0:T(8,128)(2,1)S(1)} %get-tuple-element.64), channel_id=1, source_target_pairs={{0,4},{4,0},{8,12},{12,8},{16,20},{20,16},{24,28},{28,24},{1,5},{5... | collective-permute-start | bytes 110600 | tf_op jit(solution)/shard_map/ppermute | solution.py:438
  13.0 1.4 %collective-permute-start.6 = (bf16[72,128]{1,0:T(8,128)(2,1)S(1)}, bf16[72,128]{1,0:T(8,128)(2,1)S(1)}, u32[]{:S(2)}, u32[]{:S(2)}) collective-permute-start(bf16[72,128]{1,0:T(8,128)(2,1)S(1)} %get-tuple-element.63), channel_id=1, source_target_pairs={{0,4},{24,28},{8,20},{12,16},{4,0},{28,24},{20,8},{16,12},{1,5},{2... | collective-permute-start | bytes 55304 | tf_op jit(solution)/shard_map/ppermute | solution.py:444
  15.9 1.4 %collective-permute-start.8 = (bf16[8,72,128]{2,1,0:T(8,128)(2,1)S(1)}, bf16[8,72,128]{2,1,0:T(8,128)(2,1)S(1)}, u32[]{:S(2)}, u32[]{:S(2)}) collective-permute-start(bf16[8,72,128]{2,1,0:T(8,128)(2,1)S(1)} %shard_map.113.kv.refs_0_), channel_id=1, source_target_pairs={{0,4},{4,0},{8,12},{12,8},{16,20},{20,16},{24,28},{28,24},{1,5},{5... | collective-permute-start | bytes 442376 | tf_op jit(solution)/shard_map/ppermute | solution.py:438
  16.1 2.2 %copy-start = (bf16[256,768]{1,0:T(8,128)(2,1)S(1)}, bf16[256,768]{1,0:T(8,128)(2,1)}, u32[]{:S(2)}) copy-start(bf16[256,768]{1,0:T(8,128)(2,1)} %refs_5_.1) | copy-start | bytes 1179652
  17.0 8.8 %copy-start.1 = (bf16[96,72]{1,0:T(8,128)(2,1)S(1)}, bf16[96,72]{1,0:T(8,128)(2,1)}, u32[]{:S(2)}) copy-start(bf16[96,72]{1,0:T(8,128)(2,1)} %constant.8.clone.refs_6_) | copy-start | bytes 41476
  18.1 1.4 %collective-permute-start.9 = (bf16[4,2,72,128]{3,2,1,0:T(8,128)(2,1)S(1)}, bf16[4,2,72,128]{3,2,1,0:T(8,128)(2,1)S(1)}, u32[]{:S(2)}, u32[]{:S(2)}) collective-permute-start(bf16[4,2,72,128]{3,2,1,0:T(8,128)(2,1)S(1)} %get-tuple-element.79), channel_id=1, source_target_pairs={{0,4},{4,0},{8,12},{12,8},{16,20},{20,16},{24,28},{28,24},{1,5},{5... | collective-permute-start | bytes 442376 | tf_op jit(solution)/shard_map/ppermute | solution.py:438
  19.6 5.3 %collective-permute-start.10 = (bf16[2,72,128]{2,1,0:T(8,128)(2,1)S(1)}, bf16[2,72,128]{2,1,0:T(8,128)(2,1)S(1)}, u32[]{:S(2)}, u32[]{:S(2)}) collective-permute-start(bf16[2,72,128]{2,1,0:T(8,128)(2,1)S(1)} %get-tuple-element.80), channel_id=1, source_target_pairs={{0,28},{4,24},{8,20},{12,16},{16,12},{20,8},{24,4},{28,0},{1,29},{... | collective-permute-start | bytes 110600 | tf_op jit(solution)/shard_map/ppermute | solution.py:435
  20.6 4.2 %collective-permute-start.11 = (bf16[2,72,128]{2,1,0:T(8,128)(2,1)S(1)}, bf16[2,72,128]{2,1,0:T(8,128)(2,1)S(1)}, u32[]{:S(2)}, u32[]{:S(2)}) collective-permute-start(bf16[2,72,128]{2,1,0:T(8,128)(2,1)S(1)} %get-tuple-element.81), channel_id=1, source_target_pairs={{0,12},{4,8},{8,4},{12,0},{16,28},{20,24},{24,20},{28,16},{1,13},{... | collective-permute-start | bytes 110600 | tf_op jit(solution)/shard_map/ppermute | solution.py:435
  21.1 4.7 %collective-permute-start.12 = (bf16[2,72,128]{2,1,0:T(8,128)(2,1)S(1)}, bf16[2,72,128]{2,1,0:T(8,128)(2,1)S(1)}, u32[]{:S(2)}, u32[]{:S(2)}) collective-permute-start(bf16[2,72,128]{2,1,0:T(8,128)(2,1)S(1)} %get-tuple-element.82), channel_id=1, source_target_pairs={{0,20},{4,16},{8,28},{12,24},{16,4},{20,0},{24,12},{28,8},{1,21},{... | collective-permute-start | bytes 110600 | tf_op jit(solution)/shard_map/ppermute | solution.py:435
  26.2 4.1 %collective-permute-start.13 = (bf16[24,256]{1,0:T(8,128)(2,1)S(1)}, bf16[24,256]{1,0:T(8,128)(2,1)S(1)}, u32[]{:S(2)}, u32[]{:S(2)}) collective-permute-start(bf16[24,256]{1,0:T(8,128)(2,1)S(1)} %get-tuple-element.85), channel_id=1, source_target_pairs={{0,7},{1,6},{2,5},{3,4},{4,3},{5,2},{6,1},{7,0},{8,15},{9,14},{10,... | collective-permute-start | bytes 36872 | tf_op jit(solution)/shard_map/ppermute | solution.py:432
  27.8 3.1 %collective-permute-start.14 = (bf16[24,256]{1,0:T(8,128)(2,1)S(1)}, bf16[24,256]{1,0:T(8,128)(2,1)S(1)}, u32[]{:S(2)}, u32[]{:S(2)}) collective-permute-start(bf16[24,256]{1,0:T(8,128)(2,1)S(1)} %get-tuple-element.86), channel_id=1, source_target_pairs={{0,6},{1,7},{2,4},{3,5},{4,2},{5,3},{6,0},{7,1},{8,14},{9,15},{10,... | collective-permute-start | bytes 36872 | tf_op jit(solution)/shard_map/ppermute | solution.py:432
  28.5 3.1 %collective-permute-start.15 = (bf16[24,256]{1,0:T(8,128)(2,1)S(1)}, bf16[24,256]{1,0:T(8,128)(2,1)S(1)}, u32[]{:S(2)}, u32[]{:S(2)}) collective-permute-start(bf16[24,256]{1,0:T(8,128)(2,1)S(1)} %get-tuple-element.87), channel_id=1, source_target_pairs={{0,5},{1,4},{2,7},{3,6},{4,1},{5,0},{6,3},{7,2},{8,13},{9,12},{10,... | collective-permute-start | bytes 36872 | tf_op jit(solution)/shard_map/ppermute | solution.py:432
  29.9 1.7 %collective-permute-start.16 = (bf16[24,256]{1,0:T(8,128)(2,1)S(1)}, bf16[24,256]{1,0:T(8,128)(2,1)S(1)}, u32[]{:S(2)}, u32[]{:S(2)}) collective-permute-start(bf16[24,256]{1,0:T(8,128)(2,1)S(1)} %get-tuple-element.88), channel_id=1, source_target_pairs={{0,4},{1,5},{2,6},{3,7},{4,0},{5,1},{6,2},{7,3},{8,12},{9,13},{10,... | collective-permute-start | bytes 36872 | tf_op jit(solution)/shard_map/ppermute | solution.py:432

commit v10 on v9

--- a/solution.py
+++ b/solution.py
@@ -90,31 +90,26 @@
     return copies
 
 
-def pack_kernel(
-    out_grad, pre_silu, queries, keys, values, tile, kv, query, q_ref, k_ref, v_ref, sems
-):
+def beside(left, right):
+    return jnp.concatenate([left.astype(F32), right.astype(F32)], 0).T.astype(BF16)
+
+
+def pack_kernel(out_grad, pre_silu, keys, values, tile, kv, k_ref, v_ref, sems):
     copies = start_copies(
         [
             (values, v_ref),
             (keys, k_ref),
-            (queries, q_ref),
             (out_grad, tile.at[0]),
             (pre_silu, tile.at[1]),
         ],
         sems,
     )
-
-    def beside(left, right):
-        return jnp.concatenate([left.astype(F32), right.astype(F32)], 0).T.astype(BF16)
-
     copies[0].wait()
     copies[1].wait()
     kv[0] = beside(v_ref[0], k_ref[0])
     kv[1] = beside(k_ref[1], v_ref[1])
     copies[2].wait()
-    query[...] = beside(q_ref[1], q_ref[0]) * jnp.asarray(q_ref.shape[1] ** -0.5, BF16)
     copies[3].wait()
-    copies[4].wait()
 
 
 def rim_kernel(n_col, per_sample, *refs):
@@ -147,10 +142,13 @@
         first += count
 
 
-def load_kernel(*refs):
-    *copied, sems = refs
+def load_kernel(queries, *refs):
+    *copied, query, q_ref, sems = refs
     half = len(copied) // 2
-    for copy in start_copies(list(zip(copied[:half], copied[half:])), sems):
+    copies = start_copies([(queries, q_ref), *zip(copied[:half], copied[half:])], sems)
+    copies[0].wait()
+    query[...] = beside(q_ref[1], q_ref[0]) * jnp.asarray(q_ref.shape[1] ** -0.5, BF16)
+    for copy in copies[1:]:
         copy.wait()
 
 
@@ -297,9 +295,20 @@
     return grad + dot(query, input_weight[:, pl.ds(first, lanes)], 1, 1)
 
 
+def turned_weight(channels, lanes, input_weight):
+    part = lax.axis_index("col") % (channels // lanes)
+    key, value = (
+        input_weight[:, pl.ds(pl.multiple_of(kind * channels + part * lanes, lanes), lanes)]
+        for kind in (1, 2)
+    )
+    key = pltpu.roll(key.astype(F32), lanes // 2, 1)
+    return jnp.concatenate([key, value.astype(F32)], 1).T.astype(BF16)
+
+
 def finish_kernel(offsets, *refs):
     kv_sent, kv_kept, asker, grad_out, grad_scores, kept_probs, gz_ref, input_weight = refs[:8]
-    dkv_kept, base_ref = refs[8:]
+    dkv_kept, base_ref, turned_ref = refs[8:]
+    turned_ref[...] = turned_weight(gz_ref.shape[1], asker.shape[2], input_weight)
     strip, lanes = grad_out.shape
     asked, cotangent = by_head(asker[1], grad_out[...])
     sent, kept = chunks_of(offsets)
@@ -319,7 +328,9 @@
 
 
 def long_kernel(offsets, *refs):
-    kv_sent, kv_kept, asker, grad_out, gz_ref, input_weight, dkv_sent, dkv_kept, base_ref = refs
+    kv_sent, kv_kept, asker, grad_out, gz_ref, input_weight = refs[:6]
+    dkv_sent, dkv_kept, base_ref, turned_ref = refs[6:]
+    turned_ref[...] = turned_weight(gz_ref.shape[1], asker.shape[2], input_weight)
     strip, lanes = grad_out.shape
     asked, cotangent = by_head(asker[1], grad_out[...])
     sent, kept = chunks_of(offsets)
@@ -373,7 +384,7 @@
 def project_kernel(n_col, per_sample, *refs):
     *refs, cut = refs
     n_in = len(refs) - n_col
-    *parts, base_ref, input_weight, tiles = refs[:n_in]
+    *parts, base_ref, weight, tiles = refs[:n_in]
     outs = refs[n_in:]
     col = lax.axis_index("col")
     part = col % per_sample
@@ -383,12 +394,9 @@
     channels = base_ref.shape[1]
     low = lax.broadcasted_iota(jnp.int32, (strip, lanes), 1) < half
     dv = jnp.where(low, total[0], total[1])
-    dk = pltpu.roll(jnp.where(low, total[1], total[0]), half, 1)
-    grad = base_ref[...]
-    for kind, value in ((1, dk), (2, dv)):
-        first = pl.multiple_of(kind * channels + part * lanes, lanes)
-        weight = input_weight[:, pl.ds(first, lanes)]
-        grad = grad + dot(value.astype(BF16), weight, 1, 1)
+    dk = jnp.where(low, total[1], total[0])
+    given = jnp.concatenate([dk, dv], 1).astype(BF16)
+    grad = base_ref[...] + dot(given, weight[...])
     cut[...] = dot(tiles[...], grad.astype(BF16)).reshape(cut.shape)
     for k, out in enumerate(outs):
         out[...] = cut[col ^ k].astype(BF16)
@@ -450,16 +458,15 @@
         return jnp.transpose(array, (0, 2, 1))
 
     saved = pltpu.VMEM((pairs, head_dim, strip), BF16)
-    tile, kv, query = call(
+    tile, kv = call(
         pack_kernel,
         (
             held((2, rows, cols, samples, channels), BF16),
             held((pairs, strip, lanes), BF16),
-            held((strip, lanes), BF16),
         ),
-        (saved, saved, saved, pltpu.SemaphoreType.DMA((5,))),
-        range(5),
-    )(cells(out_grad), cells(pre_silu), turned(query_heads), turned(key_heads), turned(value_heads))
+        (saved, saved, pltpu.SemaphoreType.DMA((4,))),
+        range(4),
+    )(cells(out_grad), cells(pre_silu), turned(key_heads), turned(value_heads))
     tiles = [to_col(tile, k) for k in range(n_col)]
 
     padded = pad8(cols)
@@ -469,12 +476,12 @@
         conv_weight,
         out_weight,
     )
-    loaded = call(
+    *loaded, query = call(
         load_kernel,
-        [held(array.shape, BF16) for array in far],
-        [pltpu.SemaphoreType.DMA((len(far),))],
-        range(len(far)),
-    )(*far)
+        [held(array.shape, BF16) for array in far] + [held((strip, lanes), BF16)],
+        [saved, pltpu.SemaphoreType.DMA((len(far) + 1,))],
+        range(len(far) + 1),
+    )(turned(query_heads), *far)
 
     def doubled(*parts, counts=None):
         counts = counts or [part.shape[0] for part in parts]
@@ -521,6 +528,7 @@
     )(halo_core, received, halo_odd, conv, gate, rim_shifts, conv_weight, out_weight)
 
     block = held((chips, pairs, strip, lanes), BF16)
+    given = held((2 * lanes, channels), BF16)
     if 2 * chips <= UNROLLED_CHUNKS:
         half = held((pairs, chips * strip, strip), F32)
         scores, probs_grads = call(score_kernel, (half, half))(joined, halo_core, grad_out)
@@ -533,12 +541,14 @@
             ),
         )(other, halo_core, grad_out, scores, probs_grads)
         from_core = to_core(dkv_sent)
-        dkv_kept, complete = call(functools.partial(finish_kernel, offsets), (block, whole))(
+        dkv_kept, complete, weight = call(
+            functools.partial(finish_kernel, offsets), (block, whole, given)
+        )(
             joined, other, halo_core, grad_out, grad_scores, kept_probs, grad_z, input_weight
         )
     else:
-        dkv_sent, dkv_kept, complete = call(
-            functools.partial(long_kernel, offsets), (block, block, whole)
+        dkv_sent, dkv_kept, complete, weight = call(
+            functools.partial(long_kernel, offsets), (block, block, whole, given)
         )(joined, other, halo_core, grad_out, grad_z, input_weight)
         from_core = to_core(dkv_sent)
 
@@ -554,7 +564,7 @@
         functools.partial(project_kernel, n_col, per_sample),
         [held((rows * padded, channels), BF16)] * n_col,
         [pltpu.VMEM((n_col, rows * padded, channels), F32)],
-    )(*parts, complete, input_weight, jnp.asarray(selected, BF16))
+    )(*parts, complete, weight, jnp.asarray(selected, BF16))
     grad_input = call(
         functools.partial(output_kernel, per_sample),
         pltpu.HBM((rows, cols, samples, channels), BF16),

time: 32.5 us -> 32.3 us (level)
  starting transfers between devices: 17.2 us -> 16.8 us
  waiting for transfers between devices: 8.07 us -> 8.4 us
    ppermute x8, starting transfers between devices: 7.25 us -> 6.88 us  [to_col(): return lax.ppermute(array, ('row', 'col'), pairs_of)]
    ppermute x8, waiting for transfers between devices: 3.29 us -> 3.62 us  [to_col(): return lax.ppermute(array, ('row', 'col'), pairs_of)]
where the time goes in v10:
time: 32.3 us; the launch traced here: 32.1 us
  starting transfers between devices  16.8 us (52%)
  waiting for transfers between devices  8.4 us (26%)
  Pallas kernels  6.75 us (21%)
    ppermute x5, starting transfers between devices, to_chip(): lax.ppermute(array, 'row', [(i, i ^ 2 * k + 1) for i in range(n_row)])  8.96 us
    ppermute x8, starting transfers between devices, to_col(): return lax.ppermute(array, ('row', 'col'), pairs_of)  6.88 us
    pallas_call x12, Pallas kernels, run(): pl.pallas_call(kernel, out_shape=out_shape, in_specs=specs, out_specs=jax...  6.75 us
    ppermute x5, waiting for transfers between devices, to_chip(): lax.ppermute(array, 'row', [(i, i ^ 2 * k + 1) for i in range(n_row)])  3.76 us
    ppermute x8, waiting for transfers between devices, to_col(): return lax.ppermute(array, ('row', 'col'), pairs_of)  3.62 us
    ppermute x3, waiting for transfers between devices, to_core(): return lax.ppermute(array, 'row', [(i, i ^ 1) for i in range(n_row)])  1.02 us
    ppermute x3, starting transfers between devices, to_core(): return lax.ppermute(array, 'row', [(i, i ^ 1) for i in range(n_row)])  0.72 us
  transfers between devices with their start and end apart: 17, of which 9 were waited for; matrix products, arithmetic and copies ran while one was open for 0% of the time, Pallas kernels for 12%

profile of v10, /device:TPU:0, one launch (start us, length us, event | category | flops | bytes accessed | tf_op | source)
XLA Modules:
  0.0 32.1 jit_solution(12646246934124049696)
XLA Ops:
  0.0 0.9 %shard_map.109 = (bf16[2,3,6,2,256]{4,3,2,1,0:T(2,128)(2,1)S(1)}, bf16[2,72,128]{2,1,0:T(8,128)(2,1)S(1)}) custom-call(bf16[3,6,2,256]{3,2,1,0:T(2,128)(2,1)} %bitcast.9, bf16[3,6,2,256]{3,2,1,0:T(2,128)(2,1)} %bitcast.10, bf16[2,64,72]{2,1,0:T(8,128)(2,1)} %bitcast.6, bf16[2,64,72]{2,1,0:T(8,128)(2,1)} %bitcast.7), custom_call_target="tpu_custom_call" | custom-call | tf_op jit(solution)/shard_map/pallas_call | solution.py:35
  0.9 3.5 %collective-permute-start.4 = (bf16[2,72,128]{2,1,0:T(8,128)(2,1)S(1)}, bf16[2,72,128]{2,1,0:T(8,128)(2,1)S(1)}, u32[]{:S(2)}, u32[]{:S(2)}) collective-permute-start(bf16[2,72,128]{2,1,0:T(8,128)(2,1)S(1)} %get-tuple-element.49.refs_4_), channel_id=1, source_target_pairs={{0,20},{4,16},{8,28},{12,24},{16,4},{20,0},{24,12},{28,8},{1,21},{... | collective-permute-start | bytes 110600 | tf_op jit(solution)/shard_map/ppermute | solution.py:443
  4.5 2.7 %collective-permute-start.3 = (bf16[2,3,6,2,256]{4,3,2,1,0:T(2,128)(2,1)S(1)}, bf16[2,3,6,2,256]{4,3,2,1,0:T(2,128)(2,1)S(1)}, u32[]{:S(2)}, u32[]{:S(2)}) collective-permute-start(bf16[2,3,6,2,256]{4,3,2,1,0:T(2,128)(2,1)S(1)} %get-tuple-element.48), channel_id=1, source_target_pairs={{0,7},{1,6},{2,5},{3,4},{4,3},{5,2},{6,1},{7,0},{8,15},{9,14},{10,... | collective-permute-start | bytes 110600 | tf_op jit(solution)/shard_map/ppermute | solution.py:440
  7.2 0.0 collective-permute-start.2
  7.2 0.8 %collective-permute-start.1 = (bf16[2,3,6,2,256]{4,3,2,1,0:T(2,128)(2,1)S(1)}, bf16[2,3,6,2,256]{4,3,2,1,0:T(2,128)(2,1)S(1)}, u32[]{:S(2)}, u32[]{:S(2)}) collective-permute-start(bf16[2,3,6,2,256]{4,3,2,1,0:T(2,128)(2,1)S(1)} %get-tuple-element.48), channel_id=1, source_target_pairs={{0,5},{1,4},{2,7},{3,6},{4,1},{5,0},{6,3},{7,2},{8,13},{9,12},{10,... | collective-permute-start | bytes 110600 | tf_op jit(solution)/shard_map/ppermute | solution.py:440
  7.9 0.0 collective-permute-start
  7.9 1.4 %shard_map.110 = (bf16[3,72,96]{2,1,0:T(8,128)(2,1)S(1)}, bf16[3,24,32]{2,1,0:T(8,128)(2,1)S(1)}, bf16[3,3,256,256]{3,2,1,0:T(8,128)(2,1)S(1)}, bf16[256,256]{1,0:T(8,128)(2,1)S(1)}, bf16[72,128]{1,0:T(8,128)(2,1)S(1)}) custom-call(bf16[2,64,72]{2,1,0:T(8,128)(2,1)} %bitcast.8, bf16[3,72,96]{2,1,0:T(8,128)(2,1)} %constant.6.clone.refs_0_, ...), custom_call_target="tpu_custom_call" | custom-call | tf_op jit(solution)/shard_map/pallas_call | solution.py:35
  9.3 0.0 collective-permute-done.4.refs_5_
  9.3 0.0 collective-permute-done.3.refs_3_
  9.4 1.6 %collective-permute-done.2.refs_2_ = bf16[2,3,6,2,256]{4,3,2,1,0:T(2,128)(2,1)S(1)} collective-permute-done((bf16[2,3,6,2,256]{4,3,2,1,0:T(2,128)(2,1)S(1)}, bf16[2,3,6,2,256]{4,3,2,1,0:T(2,128)(2,1)S(1)}, u32[]{:S(2)}, u32[]{:S(2)}) %collective-permute-start.2) | collective-permute-done | bytes 36896 | tf_op jit(solution)/shard_map/ppermute | solution.py:440
  10.9 0.0 collective-permute-done.1.refs_1_
  10.9 0.0 collective-permute-done.refs_0_
  10.9 0.2 shard_map.111
  11.1 1.5 %collective-permute-start.5 = (bf16[5,72,128]{2,1,0:T(8,128)(2,1)S(1)}, bf16[5,72,128]{2,1,0:T(8,128)(2,1)S(1)}, u32[]{:S(2)}, u32[]{:S(2)}) collective-permute-start(bf16[5,72,128]{2,1,0:T(8,128)(2,1)S(1)} %get-tuple-element.60.refs_0_), channel_id=1, source_target_pairs={{0,12},{4,8},{8,4},{12,0},{16,28},{20,24},{24,20},{28,16},{1,13},{... | collective-permute-start | bytes 276488 | tf_op jit(solution)/shard_map/ppermute | solution.py:443
  12.6 0.3 collective-permute-start.7
  12.9 0.2 collective-permute-start.6
  13.1 1.2 %shard_map.112 = (f32[72,256]{1,0:T(8,128)S(1)}, f32[72,256]{1,0:T(8,128)S(1)}) custom-call(bf16[2,3,6,2,256]{4,3,2,1,0:T(2,128)(2,1)S(1)} %collective-permute-done.refs_0_, bf16[2,3,6,2,256]{4,3,2,1,0:T(2,128)(2,1)S(1)} %collective-permute-done.1.refs_1_, bf16[2,3,6,2,256]{4,3,2,1,0:T(2,128)(2,1)S(1)} %collective-permute-done.2.refs_2_, ...), custom_call_target="tpu_custom_call" | custom-call | tf_op jit(solution)/shard_map/pallas_call | solution.py:35
  14.3 0.0 collective-permute-done.6.halo_odd
  14.3 0.0 collective-permute-done.7.halo_core.asker.refs_2_
  14.3 1.5 %collective-permute-done.5.refs_1_.halo_last = bf16[5,72,128]{2,1,0:T(8,128)(2,1)S(1)} collective-permute-done((bf16[5,72,128]{2,1,0:T(8,128)(2,1)S(1)}, bf16[5,72,128]{2,1,0:T(8,128)(2,1)S(1)}, u32[]{:S(2)}, u32[]{:S(2)}) %collective-permute-start.5) | collective-permute-done | bytes 92192 | tf_op jit(solution)/shard_map/ppermute | solution.py:443
  15.8 0.2 collective-permute-start.8
  16.0 0.0 copy-start
  16.0 0.6 %shard_map.114 = (bf16[72,256]{1,0:T(8,128)(2,1)S(1)}, bf16[72,128]{1,0:T(8,128)(2,1)S(1)}) custom-call(bf16[2,72,128]{2,1,0:T(8,128)(2,1)S(1)} %collective-permute-done.7.halo_core.asker.refs_2_, bf16[5,72,128]{2,1,0:T(8,128)(2,1)S(1)} %collective-permute-done.5.refs_1_.halo_last, bf16[72,128]{1,0:T(8,128)(2,1)S(1)} %collective-permute-done.6.halo_odd, ...), custom_call_target="tpu_custom_call" | custom-call | tf_op jit(solution)/shard_map/pallas_call | solution.py:35
  16.6 0.2 shard_map.115
  16.9 0.0 copy-start.1
  16.9 0.3 %collective-permute-done.8.kv_kept.refs_1_ = bf16[8,72,128]{2,1,0:T(8,128)(2,1)S(1)} collective-permute-done((bf16[8,72,128]{2,1,0:T(8,128)(2,1)S(1)}, bf16[8,72,128]{2,1,0:T(8,128)(2,1)S(1)}, u32[]{:S(2)}, u32[]{:S(2)}) %collective-permute-start.8) | collective-permute-done | bytes 147488 | tf_op jit(solution)/shard_map/ppermute | solution.py:446
  17.3 0.7 %shard_map.116 = (bf16[4,2,72,128]{3,2,1,0:T(8,128)(2,1)S(1)}, bf16[2,576,72]{2,1,0:T(8,128)(2,1)S(1)}, bf16[2,288,72]{2,1,0:T(8,128)(2,1)S(1)}) custom-call(bf16[8,72,128]{2,1,0:T(8,128)(2,1)S(1)} %collective-permute-done.8.kv_kept.refs_1_, bf16[2,72,128]{2,1,0:T(8,128)(2,1)S(1)} %collective-permute-done.7.halo_core.asker.refs_2_, ...), custom_call_target="tpu_custom_call" | custom-call | tf_op jit(solution)/shard_map/pallas_call | solution.py:35
  18.0 0.2 collective-permute-start.9
  18.2 0.0 copy-done
  18.2 0.5 %shard_map.117 = (bf16[4,2,72,128]{3,2,1,0:T(8,128)(2,1)S(1)}, f32[72,256]{1,0:T(8,128)S(1)}, bf16[256,256]{1,0:T(8,128)(2,1)S(1)}) custom-call(bf16[8,72,128]{2,1,0:T(8,128)(2,1)S(1)} %shard_map.113.kv.refs_0_, bf16[8,72,128]{2,1,0:T(8,128)(2,1)S(1)} %collective-permute-done.8.kv_kept.refs_1_, ...), custom_call_target="tpu_custom_call" | custom-call | tf_op jit(solution)/shard_map/pallas_call | solution.py:35
  18.8 0.7 %collective-permute-done.9.received = bf16[4,2,72,128]{3,2,1,0:T(8,128)(2,1)S(1)} collective-permute-done((bf16[4,2,72,128]{3,2,1,0:T(8,128)(2,1)S(1)}, bf16[4,2,72,128]{3,2,1,0:T(8,128)(2,1)S(1)}, u32[]{:S(2)}, u32[]{:S(2)}) %collective-permute-start.9) | collective-permute-done | bytes 147488 | tf_op jit(solution)/shard_map/ppermute | solution.py:446
  19.5 1.1 %collective-permute-start.10 = (bf16[2,72,128]{2,1,0:T(8,128)(2,1)S(1)}, bf16[2,72,128]{2,1,0:T(8,128)(2,1)S(1)}, u32[]{:S(2)}, u32[]{:S(2)}) collective-permute-start(bf16[2,72,128]{2,1,0:T(8,128)(2,1)S(1)} %get-tuple-element.81), channel_id=1, source_target_pairs={{0,28},{4,24},{8,20},{12,16},{16,12},{20,8},{24,4},{28,0},{1,29},{... | collective-permute-start | bytes 110600 | tf_op jit(solution)/shard_map/ppermute | solution.py:443
  20.5 0.4 %collective-permute-start.11 = (bf16[2,72,128]{2,1,0:T(8,128)(2,1)S(1)}, bf16[2,72,128]{2,1,0:T(8,128)(2,1)S(1)}, u32[]{:S(2)}, u32[]{:S(2)}) collective-permute-start(bf16[2,72,128]{2,1,0:T(8,128)(2,1)S(1)} %get-tuple-element.82), channel_id=1, source_target_pairs={{0,12},{4,8},{8,4},{12,0},{16,28},{20,24},{24,20},{28,16},{1,13},{... | collective-permute-start | bytes 110600 | tf_op jit(solution)/shard_map/ppermute | solution.py:443
  20.9 2.5 %collective-permute-start.12 = (bf16[2,72,128]{2,1,0:T(8,128)(2,1)S(1)}, bf16[2,72,128]{2,1,0:T(8,128)(2,1)S(1)}, u32[]{:S(2)}, u32[]{:S(2)}) collective-permute-start(bf16[2,72,128]{2,1,0:T(8,128)(2,1)S(1)} %get-tuple-element.83), channel_id=1, source_target_pairs={{0,20},{4,16},{8,28},{12,24},{16,4},{20,0},{24,12},{28,8},{1,21},{... | collective-permute-start | bytes 110600 | tf_op jit(solution)/shard_map/ppermute | solution.py:443
  23.4 1.4 %collective-permute-done.10.refs_0_ = bf16[2,72,128]{2,1,0:T(8,128)(2,1)S(1)} collective-permute-done((bf16[2,72,128]{2,1,0:T(8,128)(2,1)S(1)}, bf16[2,72,128]{2,1,0:T(8,128)(2,1)S(1)}, u32[]{:S(2)}, u32[]{:S(2)}) %collective-permute-start.10) | collective-permute-done | bytes 36896 | tf_op jit(solution)/shard_map/ppermute | solution.py:443
  24.8 0.0 collective-permute-done.11.refs_1_
  24.8 0.9 %collective-permute-done.12.refs_2_ = bf16[2,72,128]{2,1,0:T(8,128)(2,1)S(1)} collective-permute-done((bf16[2,72,128]{2,1,0:T(8,128)(2,1)S(1)}, bf16[2,72,128]{2,1,0:T(8,128)(2,1)S(1)}, u32[]{:S(2)}, u32[]{:S(2)}) %collective-permute-start.12) | collective-permute-done | bytes 36896 | tf_op jit(solution)/shard_map/ppermute | solution.py:443
  25.7 0.0 copy-done.1
  25.7 0.3 shard_map.119
  26.0 1.6 %collective-permute-start.13 = (bf16[24,256]{1,0:T(8,128)(2,1)S(1)}, bf16[24,256]{1,0:T(8,128)(2,1)S(1)}, u32[]{:S(2)}, u32[]{:S(2)}) collective-permute-start(bf16[24,256]{1,0:T(8,128)(2,1)S(1)} %get-tuple-element.87), channel_id=1, source_target_pairs={{0,7},{1,6},{2,5},{3,4},{4,3},{5,2},{6,1},{7,0},{8,15},{9,14},{10,... | collective-permute-start | bytes 36872 | tf_op jit(solution)/shard_map/ppermute | solution.py:440
  27.6 0.7 %collective-permute-start.14 = (bf16[24,256]{1,0:T(8,128)(2,1)S(1)}, bf16[24,256]{1,0:T(8,128)(2,1)S(1)}, u32[]{:S(2)}, u32[]{:S(2)}) collective-permute-start(bf16[24,256]{1,0:T(8,128)(2,1)S(1)} %get-tuple-element.88), channel_id=1, source_target_pairs={{0,6},{1,7},{2,4},{3,5},{4,2},{5,3},{6,0},{7,1},{8,14},{9,15},{10,... | collective-permute-start | bytes 36872 | tf_op jit(solution)/shard_map/ppermute | solution.py:440
  28.3 0.8 %collective-permute-start.15 = (bf16[24,256]{1,0:T(8,128)(2,1)S(1)}, bf16[24,256]{1,0:T(8,128)(2,1)S(1)}, u32[]{:S(2)}, u32[]{:S(2)}) collective-permute-start(bf16[24,256]{1,0:T(8,128)(2,1)S(1)} %get-tuple-element.89), channel_id=1, source_target_pairs={{0,5},{1,4},{2,7},{3,6},{4,1},{5,0},{6,3},{7,2},{8,13},{9,12},{10,... | collective-permute-start | bytes 36872 | tf_op jit(solution)/shard_map/ppermute | solution.py:440
  29.1 0.3 collective-permute-start.16
  29.4 0.7 %collective-permute-done.13.refs_0_ = bf16[24,256]{1,0:T(8,128)(2,1)S(1)} collective-permute-done((bf16[24,256]{1,0:T(8,128)(2,1)S(1)}, bf16[24,256]{1,0:T(8,128)(2,1)S(1)}, u32[]{:S(2)}, u32[]{:S(2)}) %collective-permute-start.13) | collective-permute-done | bytes 12320 | tf_op jit(solution)/shard_map/ppermute | solution.py:440
  30.1 0.6 %collective-permute-done.14.refs_1_ = bf16[24,256]{1,0:T(8,128)(2,1)S(1)} collective-permute-done((bf16[24,256]{1,0:T(8,128)(2,1)S(1)}, bf16[24,256]{1,0:T(8,128)(2,1)S(1)}, u32[]{:S(2)}, u32[]{:S(2)}) %collective-permute-start.14) | collective-permute-done | bytes 12320 | tf_op jit(solution)/shard_map/ppermute | solution.py:440
  30.7 0.7 %collective-permute-done.15.refs_2_ = bf16[24,256]{1,0:T(8,128)(2,1)S(1)} collective-permute-done((bf16[24,256]{1,0:T(8,128)(2,1)S(1)}, bf16[24,256]{1,0:T(8,128)(2,1)S(1)}, u32[]{:S(2)}, u32[]{:S(2)}) %collective-permute-start.15) | collective-permute-done | bytes 12320 | tf_op jit(solution)/shard_map/ppermute | solution.py:440
  31.4 0.0 collective-permute-done.16.refs_3_
  31.4 0.7 %shard_map.120 = bf16[3,6,2,256]{3,2,1,0:T(2,128)(2,1)} custom-call(bf16[24,256]{1,0:T(8,128)(2,1)S(1)} %collective-permute-done.13.refs_0_, bf16[24,256]{1,0:T(8,128)(2,1)S(1)} %collective-permute-done.14.refs_1_, bf16[24,256]{1,0:T(8,128)(2,1)S(1)} %collective-permute-done.15.refs_2_, bf16[24,256]{1,0:T(8,128)(2,1)S(1)} %collective-permute-done.16.refs_3_), custom_call_target="tpu_custom_call" | custom-call | tf_op jit(solution)/shard_map/pallas_call | solution.py:35
  (2 shorter events, 0.0 us)
Async XLA Ops:
  0.9 8.4 %collective-permute-start.4 = (bf16[2,72,128]{2,1,0:T(8,128)(2,1)S(1)}, bf16[2,72,128]{2,1,0:T(8,128)(2,1)S(1)}, u32[]{:S(2)}, u32[]{:S(2)}) collective-permute-start(bf16[2,72,128]{2,1,0:T(8,128)(2,1)S(1)} %get-tuple-element.49.refs_4_), channel_id=1, source_target_pairs={{0,20},{4,16},{8,28},{12,24},{16,4},{20,0},{24,12},{28,8},{1,21},{... | collective-permute-start | bytes 110600 | tf_op jit(solution)/shard_map/ppermute | solution.py:443
  4.5 4.9 %collective-permute-start.3 = (bf16[2,3,6,2,256]{4,3,2,1,0:T(2,128)(2,1)S(1)}, bf16[2,3,6,2,256]{4,3,2,1,0:T(2,128)(2,1)S(1)}, u32[]{:S(2)}, u32[]{:S(2)}) collective-permute-start(bf16[2,3,6,2,256]{4,3,2,1,0:T(2,128)(2,1)S(1)} %get-tuple-element.48), channel_id=1, source_target_pairs={{0,7},{1,6},{2,5},{3,4},{4,3},{5,2},{6,1},{7,0},{8,15},{9,14},{10,... | collective-permute-start | bytes 110600 | tf_op jit(solution)/shard_map/ppermute | solution.py:440
  7.2 3.8 %collective-permute-start.2 = (bf16[2,3,6,2,256]{4,3,2,1,0:T(2,128)(2,1)S(1)}, bf16[2,3,6,2,256]{4,3,2,1,0:T(2,128)(2,1)S(1)}, u32[]{:S(2)}, u32[]{:S(2)}) collective-permute-start(bf16[2,3,6,2,256]{4,3,2,1,0:T(2,128)(2,1)S(1)} %get-tuple-element.48), channel_id=1, source_target_pairs={{0,6},{1,7},{2,4},{3,5},{4,2},{5,3},{6,0},{7,1},{8,14},{9,15},{10,... | collective-permute-start | bytes 110600 | tf_op jit(solution)/shard_map/ppermute | solution.py:440
  7.2 3.8 %collective-permute-start.1 = (bf16[2,3,6,2,256]{4,3,2,1,0:T(2,128)(2,1)S(1)}, bf16[2,3,6,2,256]{4,3,2,1,0:T(2,128)(2,1)S(1)}, u32[]{:S(2)}, u32[]{:S(2)}) collective-permute-start(bf16[2,3,6,2,256]{4,3,2,1,0:T(2,128)(2,1)S(1)} %get-tuple-element.48), channel_id=1, source_target_pairs={{0,5},{1,4},{2,7},{3,6},{4,1},{5,0},{6,3},{7,2},{8,13},{9,12},{10,... | collective-permute-start | bytes 110600 | tf_op jit(solution)/shard_map/ppermute | solution.py:440
  7.9 3.0 %collective-permute-start = (bf16[2,3,6,2,256]{4,3,2,1,0:T(2,128)(2,1)S(1)}, bf16[2,3,6,2,256]{4,3,2,1,0:T(2,128)(2,1)S(1)}, u32[]{:S(2)}, u32[]{:S(2)}) collective-permute-start(bf16[2,3,6,2,256]{4,3,2,1,0:T(2,128)(2,1)S(1)} %get-tuple-element.48), channel_id=1, source_target_pairs={{0,4},{1,5},{2,6},{3,7},{4,0},{5,1},{6,2},{7,3},{8,12},{9,13},{10,... | collective-permute-start | bytes 110600 | tf_op jit(solution)/shard_map/ppermute | solution.py:440
  11.1 4.7 %collective-permute-start.5 = (bf16[5,72,128]{2,1,0:T(8,128)(2,1)S(1)}, bf16[5,72,128]{2,1,0:T(8,128)(2,1)S(1)}, u32[]{:S(2)}, u32[]{:S(2)}) collective-permute-start(bf16[5,72,128]{2,1,0:T(8,128)(2,1)S(1)} %get-tuple-element.60.refs_0_), channel_id=1, source_target_pairs={{0,12},{4,8},{8,4},{12,0},{16,28},{20,24},{24,20},{28,16},{1,13},{... | collective-permute-start | bytes 276488 | tf_op jit(solution)/shard_map/ppermute | solution.py:443
  12.6 1.7 %collective-permute-start.7 = (bf16[2,72,128]{2,1,0:T(8,128)(2,1)S(1)}, bf16[2,72,128]{2,1,0:T(8,128)(2,1)S(1)}, u32[]{:S(2)}, u32[]{:S(2)}) collective-permute-start(bf16[2,72,128]{2,1,0:T(8,128)(2,1)S(1)} %get-tuple-element.65), channel_id=1, source_target_pairs={{0,4},{4,0},{8,12},{12,8},{16,20},{20,16},{24,28},{28,24},{1,5},{5... | collective-permute-start | bytes 110600 | tf_op jit(solution)/shard_map/ppermute | solution.py:446
  12.9 1.4 %collective-permute-start.6 = (bf16[72,128]{1,0:T(8,128)(2,1)S(1)}, bf16[72,128]{1,0:T(8,128)(2,1)S(1)}, u32[]{:S(2)}, u32[]{:S(2)}) collective-permute-start(bf16[72,128]{1,0:T(8,128)(2,1)S(1)} %get-tuple-element.64), channel_id=1, source_target_pairs={{0,4},{24,28},{8,20},{12,16},{4,0},{28,24},{20,8},{16,12},{1,5},{2... | collective-permute-start | bytes 55304 | tf_op jit(solution)/shard_map/ppermute | solution.py:452
  15.8 1.4 %collective-permute-start.8 = (bf16[8,72,128]{2,1,0:T(8,128)(2,1)S(1)}, bf16[8,72,128]{2,1,0:T(8,128)(2,1)S(1)}, u32[]{:S(2)}, u32[]{:S(2)}) collective-permute-start(bf16[8,72,128]{2,1,0:T(8,128)(2,1)S(1)} %shard_map.113.kv.refs_0_), channel_id=1, source_target_pairs={{0,4},{4,0},{8,12},{12,8},{16,20},{20,16},{24,28},{28,24},{1,5},{5... | collective-permute-start | bytes 442376 | tf_op jit(solution)/shard_map/ppermute | solution.py:446
  16.0 2.2 %copy-start = (bf16[256,768]{1,0:T(8,128)(2,1)S(1)}, bf16[256,768]{1,0:T(8,128)(2,1)}, u32[]{:S(2)}) copy-start(bf16[256,768]{1,0:T(8,128)(2,1)} %refs_7_.1) | copy-start | bytes 1179652
  16.9 8.8 %copy-start.1 = (bf16[96,72]{1,0:T(8,128)(2,1)S(1)}, bf16[96,72]{1,0:T(8,128)(2,1)}, u32[]{:S(2)}) copy-start(bf16[96,72]{1,0:T(8,128)(2,1)} %constant.8.clone.refs_6_) | copy-start | bytes 41476
  18.0 1.4 %collective-permute-start.9 = (bf16[4,2,72,128]{3,2,1,0:T(8,128)(2,1)S(1)}, bf16[4,2,72,128]{3,2,1,0:T(8,128)(2,1)S(1)}, u32[]{:S(2)}, u32[]{:S(2)}) collective-permute-start(bf16[4,2,72,128]{3,2,1,0:T(8,128)(2,1)S(1)} %get-tuple-element.80), channel_id=1, source_target_pairs={{0,4},{4,0},{8,12},{12,8},{16,20},{20,16},{24,28},{28,24},{1,5},{5... | collective-permute-start | bytes 442376 | tf_op jit(solution)/shard_map/ppermute | solution.py:446
  19.5 5.3 %collective-permute-start.10 = (bf16[2,72,128]{2,1,0:T(8,128)(2,1)S(1)}, bf16[2,72,128]{2,1,0:T(8,128)(2,1)S(1)}, u32[]{:S(2)}, u32[]{:S(2)}) collective-permute-start(bf16[2,72,128]{2,1,0:T(8,128)(2,1)S(1)} %get-tuple-element.81), channel_id=1, source_target_pairs={{0,28},{4,24},{8,20},{12,16},{16,12},{20,8},{24,4},{28,0},{1,29},{... | collective-permute-start | bytes 110600 | tf_op jit(solution)/shard_map/ppermute | solution.py:443
  20.5 4.2 %collective-permute-start.11 = (bf16[2,72,128]{2,1,0:T(8,128)(2,1)S(1)}, bf16[2,72,128]{2,1,0:T(8,128)(2,1)S(1)}, u32[]{:S(2)}, u32[]{:S(2)}) collective-permute-start(bf16[2,72,128]{2,1,0:T(8,128)(2,1)S(1)} %get-tuple-element.82), channel_id=1, source_target_pairs={{0,12},{4,8},{8,4},{12,0},{16,28},{20,24},{24,20},{28,16},{1,13},{... | collective-permute-start | bytes 110600 | tf_op jit(solution)/shard_map/ppermute | solution.py:443
  20.9 4.7 %collective-permute-start.12 = (bf16[2,72,128]{2,1,0:T(8,128)(2,1)S(1)}, bf16[2,72,128]{2,1,0:T(8,128)(2,1)S(1)}, u32[]{:S(2)}, u32[]{:S(2)}) collective-permute-start(bf16[2,72,128]{2,1,0:T(8,128)(2,1)S(1)} %get-tuple-element.83), channel_id=1, source_target_pairs={{0,20},{4,16},{8,28},{12,24},{16,4},{20,0},{24,12},{28,8},{1,21},{... | collective-permute-start | bytes 110600 | tf_op jit(solution)/shard_map/ppermute | solution.py:443
  26.0 4.1 %collective-permute-start.13 = (bf16[24,256]{1,0:T(8,128)(2,1)S(1)}, bf16[24,256]{1,0:T(8,128)(2,1)S(1)}, u32[]{:S(2)}, u32[]{:S(2)}) collective-permute-start(bf16[24,256]{1,0:T(8,128)(2,1)S(1)} %get-tuple-element.87), channel_id=1, source_target_pairs={{0,7},{1,6},{2,5},{3,4},{4,3},{5,2},{6,1},{7,0},{8,15},{9,14},{10,... | collective-permute-start | bytes 36872 | tf_op jit(solution)/shard_map/ppermute | solution.py:440
  27.6 3.1 %collective-permute-start.14 = (bf16[24,256]{1,0:T(8,128)(2,1)S(1)}, bf16[24,256]{1,0:T(8,128)(2,1)S(1)}, u32[]{:S(2)}, u32[]{:S(2)}) collective-permute-start(bf16[24,256]{1,0:T(8,128)(2,1)S(1)} %get-tuple-element.88), channel_id=1, source_target_pairs={{0,6},{1,7},{2,4},{3,5},{4,2},{5,3},{6,0},{7,1},{8,14},{9,15},{10,... | collective-permute-start | bytes 36872 | tf_op jit(solution)/shard_map/ppermute | solution.py:440
  28.3 3.1 %collective-permute-start.15 = (bf16[24,256]{1,0:T(8,128)(2,1)S(1)}, bf16[24,256]{1,0:T(8,128)(2,1)S(1)}, u32[]{:S(2)}, u32[]{:S(2)}) collective-permute-start(bf16[24,256]{1,0:T(8,128)(2,1)S(1)} %get-tuple-element.89), channel_id=1, source_target_pairs={{0,5},{1,4},{2,7},{3,6},{4,1},{5,0},{6,3},{7,2},{8,13},{9,12},{10,... | collective-permute-start | bytes 36872 | tf_op jit(solution)/shard_map/ppermute | solution.py:440
  29.1 2.3 %collective-permute-start.16 = (bf16[24,256]{1,0:T(8,128)(2,1)S(1)}, bf16[24,256]{1,0:T(8,128)(2,1)S(1)}, u32[]{:S(2)}, u32[]{:S(2)}) collective-permute-start(bf16[24,256]{1,0:T(8,128)(2,1)S(1)} %get-tuple-element.90), channel_id=1, source_target_pairs={{0,4},{1,5},{2,6},{3,7},{4,0},{5,1},{6,2},{7,3},{8,12},{9,13},{10,... | collective-permute-start | bytes 36872 | tf_op jit(solution)/shard_map/ppermute | solution.py:440

commit v11 on v10

--- a/solution.py
+++ b/solution.py
@@ -235,21 +235,22 @@
     return sent, [(not e, j, offset) for e, j, offset in sent]
 
 
-def all_keys(kv, head):
+def all_keys(arrays, head):
     return jnp.concatenate(
-        [kv[2 * j + head].astype(F32) for j in range(kv.shape[0] // 2)], 0
+        [kv[2 * j + head].astype(F32) for kv in arrays for j in range(kv.shape[0] // 2)], 0
     ).astype(BF16)
 
 
-def score_kernel(kv, asker, grad_out, scores, probs_grads):
+def score_kernel(*refs):
+    *arrays, asker, grad_out, scores, probs_grads = refs
     asked, cotangent = by_head(asker[1], grad_out[...])
     for head in (0, 1):
-        keys = all_keys(kv, head)
+        keys = all_keys(arrays, head)
         scores[head] = dot(keys, asked[head], 1, 1)
         probs_grads[head] = dot(keys, cotangent[head], 1, 1)
 
 
-def softmax_kernel(offsets, kv_kept, asker, grad_out, scores, probs_grads, *outs):
+def softmax_kernel(offsets, late, asker, grad_out, scores, probs_grads, *outs):
     dkv_sent, grad_scores, kept_probs = outs
     strip = grad_out.shape[0]
     heads = (0, 1)
@@ -257,15 +258,11 @@
     sent, kept = chunks_of(offsets)
 
     def arranged(first, second):
-        return jnp.concatenate(
-            [
-                (second if late else first)[j * strip : (j + 1) * strip]
-                for late, j, _ in sent + kept
-            ],
-            0,
-        )
-
-    keys = [all_keys(kv_kept, h) for h in heads]
+        both = jnp.concatenate([first, second], 0)
+        places = [(len(offsets) if kept_here else 0) + j for kept_here, j, _ in sent + kept]
+        return jnp.concatenate([both[i * strip : (i + 1) * strip] for i in places], 0)
+
+    keys = [all_keys([late], h) for h in heads]
     late_scores = [dot(keys[h], asked[h], 1, 1) for h in heads]
     late_grads = [dot(keys[h], cotangent[h], 1, 1) for h in heads]
     both = [arranged(scores[h], late_scores[h]) for h in heads]
@@ -306,8 +303,8 @@
 
 
 def finish_kernel(offsets, *refs):
-    kv_sent, kv_kept, asker, grad_out, grad_scores, kept_probs, gz_ref, input_weight = refs[:8]
-    dkv_kept, base_ref, turned_ref = refs[8:]
+    arrays, (asker, grad_out, grad_scores, kept_probs, gz_ref, input_weight) = refs[:4], refs[4:10]
+    dkv_kept, base_ref, turned_ref = refs[10:]
     turned_ref[...] = turned_weight(gz_ref.shape[1], asker.shape[2], input_weight)
     strip, lanes = grad_out.shape
     asked, cotangent = by_head(asker[1], grad_out[...])
@@ -319,9 +316,9 @@
         dkv = dot(given, jnp.concatenate([asked[h], cotangent[h]], 0))
         for i, (_, _, offset) in enumerate(kept):
             dkv_kept[offset, h] = dkv[i * strip : (i + 1) * strip].astype(BF16)
-        keys = jnp.concatenate(
-            [(kv_kept if late else kv_sent)[2 * j + h].astype(F32) for late, j, _ in sent + kept], 0
-        )
+        keys = all_keys(arrays, h)
+        places = [(len(offsets) if kept_here else 0) + j for kept_here, j, _ in sent + kept]
+        keys = jnp.concatenate([keys.astype(F32)[i * strip : (i + 1) * strip] for i in places], 0)
         query.append(dot(grad_scores[h], keys.astype(BF16), 0, 0))
     low = lax.broadcasted_iota(jnp.int32, (strip, lanes), 1) < lanes // 2
     base_ref[...] = base(jnp.where(low, query[1], query[0]), gz_ref, input_weight)
@@ -509,7 +506,7 @@
         [pltpu.VMEM((2, n_col, padded, channels), F32)],
     )(*tiles, *parts, query)
     received = to_chip(sent, distances[-1])
-    halo_odd, halo_core = to_odd_chip(rim_chip), to_core(rim_core)
+    halo_odd, halo_core, early = to_odd_chip(rim_chip), to_core(rim_core), to_core(sent)
 
     whole = held((strip, channels), F32)
     conv, gate = call(
@@ -517,11 +514,10 @@
         (whole, whole),
         [pltpu.VMEM((n_col, rows, padded, channels), F32)] * 2,
     )(*tiles, shifts, conv_weight)
-    received, conv, halo_odd, halo_core = lax.optimization_barrier(
-        (received, conv, halo_odd, halo_core)
-    )
-    joined = doubled(sent, received, counts=(blocks, blocks))
-    other = to_core(joined)
+    received, conv, halo_odd, halo_core, early = lax.optimization_barrier(
+        (received, conv, halo_odd, halo_core, early)
+    )
+    late = to_core(received)
     grad_z, grad_out = call(
         rim_conv_kernel,
         (held((strip, channels), BF16), held((strip, lanes), BF16)),
@@ -530,8 +526,10 @@
     block = held((chips, pairs, strip, lanes), BF16)
     given = held((2 * lanes, channels), BF16)
     if 2 * chips <= UNROLLED_CHUNKS:
-        half = held((pairs, chips * strip, strip), F32)
-        scores, probs_grads = call(score_kernel, (half, half))(joined, halo_core, grad_out)
+        most = held((pairs, (2 * chips - blocks // 2) * strip, strip), F32)
+        scores, probs_grads = call(score_kernel, (most, most))(
+            sent, received, early, halo_core, grad_out
+        )
         dkv_sent, grad_scores, kept_probs = call(
             functools.partial(softmax_kernel, offsets),
             (
@@ -539,14 +537,25 @@
                 held((pairs, 2 * chips * strip, strip), BF16),
                 held((pairs, chips * strip, strip), BF16),
             ),
-        )(other, halo_core, grad_out, scores, probs_grads)
+        )(late, halo_core, grad_out, scores, probs_grads)
         from_core = to_core(dkv_sent)
         dkv_kept, complete, weight = call(
             functools.partial(finish_kernel, offsets), (block, whole, given)
         )(
-            joined, other, halo_core, grad_out, grad_scores, kept_probs, grad_z, input_weight
+            sent,
+            received,
+            early,
+            late,
+            halo_core,
+            grad_out,
+            grad_scores,
+            kept_probs,
+            grad_z,
+            input_weight,
         )
     else:
+        joined = doubled(sent, received, counts=(blocks, blocks))
+        other = doubled(early, late, counts=(blocks, blocks))
         dkv_sent, dkv_kept, complete, weight = call(
             functools.partial(long_kernel, offsets), (block, block, whole, given)
         )(joined, other, halo_core, grad_out, grad_z, input_weight)

time: 32.3 us -> 32.2 us (level)
  waiting for transfers between devices: 8.4 us -> 7.78 us
  starting transfers between devices: 16.8 us -> 17.2 us
    ppermute x3 -> x4, waiting for transfers between devices: 1.02 us -> 0.68 us  [to_core(): return lax.ppermute(array, 'row', [(i, i ^ 1) for i in range(n_row)])]
    ppermute x3 -> x4, starting transfers between devices: 0.72 us -> 1.05 us  [to_core(): return lax.ppermute(array, 'row', [(i, i ^ 1) for i in range(n_row)])]
    pallas_call x12 -> x11, Pallas kernels: 6.75 us -> 6.91 us  [run(): pl.pallas_call(kernel, out_shape=out_shape, in_specs=specs, out_specs=jax...]
  transfers between devices with their start and end apart: 17 -> 18, of which waited for: 9 -> 8; matrix products, arithmetic and copies ran while one was open for 0% -> 0% of each run, Pallas kernels for 12% -> 13%
where the time goes in v11:
time: 32.2 us; the launch traced here: 32 us
  starting transfers between devices  17.2 us (53%)
  waiting for transfers between devices  7.78 us (24%)
  Pallas kernels  6.91 us (21%)
    ppermute x5, starting transfers between devices, to_chip(): lax.ppermute(array, 'row', [(i, i ^ 2 * k + 1) for i in range(n_row)])  9.01 us
    pallas_call x11, Pallas kernels, run(): pl.pallas_call(kernel, out_shape=out_shape, in_specs=specs, out_specs=jax...  6.91 us
    ppermute x8, starting transfers between devices, to_col(): return lax.ppermute(array, ('row', 'col'), pairs_of)  6.88 us
    ppermute x5, waiting for transfers between devices, to_chip(): lax.ppermute(array, 'row', [(i, i ^ 2 * k + 1) for i in range(n_row)])  3.72 us
    ppermute x8, waiting for transfers between devices, to_col(): return lax.ppermute(array, ('row', 'col'), pairs_of)  3.38 us
    ppermute x4, starting transfers between devices, to_core(): return lax.ppermute(array, 'row', [(i, i ^ 1) for i in range(n_row)])  1.05 us
    ppermute x4, waiting for transfers between devices, to_core(): return lax.ppermute(array, 'row', [(i, i ^ 1) for i in range(n_row)])  0.68 us
  transfers between devices with their start and end apart: 18, of which 8 were waited for; matrix products, arithmetic and copies ran while one was open for 0% of the time, Pallas kernels for 13%

profile of v11, /device:TPU:0, one launch (start us, length us, event | category | flops | bytes accessed | tf_op | source)
XLA Modules:
  0.0 32.0 jit_solution(3588163683388129096)
XLA Ops:
  0.0 0.9 %shard_map.109 = (bf16[2,3,6,2,256]{4,3,2,1,0:T(2,128)(2,1)S(1)}, bf16[2,72,128]{2,1,0:T(8,128)(2,1)S(1)}) custom-call(bf16[3,6,2,256]{3,2,1,0:T(2,128)(2,1)} %bitcast.9, bf16[3,6,2,256]{3,2,1,0:T(2,128)(2,1)} %bitcast.10, bf16[2,64,72]{2,1,0:T(8,128)(2,1)} %bitcast.6, bf16[2,64,72]{2,1,0:T(8,128)(2,1)} %bitcast.7), custom_call_target="tpu_custom_call" | custom-call | tf_op jit(solution)/shard_map/pallas_call | solution.py:35
  0.9 3.5 %collective-permute-start.4 = (bf16[2,72,128]{2,1,0:T(8,128)(2,1)S(1)}, bf16[2,72,128]{2,1,0:T(8,128)(2,1)S(1)}, u32[]{:S(2)}, u32[]{:S(2)}) collective-permute-start(bf16[2,72,128]{2,1,0:T(8,128)(2,1)S(1)} %get-tuple-element.50.refs_4_), channel_id=1, source_target_pairs={{0,20},{4,16},{8,28},{12,24},{16,4},{20,0},{24,12},{28,8},{1,21},{... | collective-permute-start | bytes 110600 | tf_op jit(solution)/shard_map/ppermute | solution.py:440
  4.5 2.7 %collective-permute-start.3 = (bf16[2,3,6,2,256]{4,3,2,1,0:T(2,128)(2,1)S(1)}, bf16[2,3,6,2,256]{4,3,2,1,0:T(2,128)(2,1)S(1)}, u32[]{:S(2)}, u32[]{:S(2)}) collective-permute-start(bf16[2,3,6,2,256]{4,3,2,1,0:T(2,128)(2,1)S(1)} %get-tuple-element.49), channel_id=1, source_target_pairs={{0,7},{1,6},{2,5},{3,4},{4,3},{5,2},{6,1},{7,0},{8,15},{9,14},{10,... | collective-permute-start | bytes 110600 | tf_op jit(solution)/shard_map/ppermute | solution.py:437
  7.2 0.0 collective-permute-start.2
  7.2 0.8 %collective-permute-start.1 = (bf16[2,3,6,2,256]{4,3,2,1,0:T(2,128)(2,1)S(1)}, bf16[2,3,6,2,256]{4,3,2,1,0:T(2,128)(2,1)S(1)}, u32[]{:S(2)}, u32[]{:S(2)}) collective-permute-start(bf16[2,3,6,2,256]{4,3,2,1,0:T(2,128)(2,1)S(1)} %get-tuple-element.49), channel_id=1, source_target_pairs={{0,5},{1,4},{2,7},{3,6},{4,1},{5,0},{6,3},{7,2},{8,13},{9,12},{10,... | collective-permute-start | bytes 110600 | tf_op jit(solution)/shard_map/ppermute | solution.py:437
  7.9 0.0 collective-permute-start
  7.9 1.4 %shard_map.110 = (bf16[3,72,96]{2,1,0:T(8,128)(2,1)S(1)}, bf16[3,24,32]{2,1,0:T(8,128)(2,1)S(1)}, bf16[3,3,256,256]{3,2,1,0:T(8,128)(2,1)S(1)}, bf16[256,256]{1,0:T(8,128)(2,1)S(1)}, bf16[72,128]{1,0:T(8,128)(2,1)S(1)}) custom-call(bf16[2,64,72]{2,1,0:T(8,128)(2,1)} %bitcast.8, bf16[3,72,96]{2,1,0:T(8,128)(2,1)} %constant.6.clone.refs_0_, ...), custom_call_target="tpu_custom_call" | custom-call | tf_op jit(solution)/shard_map/pallas_call | solution.py:35
  9.3 0.0 collective-permute-done.4.refs_5_
  9.3 0.0 collective-permute-done.3.refs_3_
  9.4 1.6 %collective-permute-done.2.refs_2_ = bf16[2,3,6,2,256]{4,3,2,1,0:T(2,128)(2,1)S(1)} collective-permute-done((bf16[2,3,6,2,256]{4,3,2,1,0:T(2,128)(2,1)S(1)}, bf16[2,3,6,2,256]{4,3,2,1,0:T(2,128)(2,1)S(1)}, u32[]{:S(2)}, u32[]{:S(2)}) %collective-permute-start.2) | collective-permute-done | bytes 36896 | tf_op jit(solution)/shard_map/ppermute | solution.py:437
  10.9 0.0 collective-permute-done.1.refs_1_
  10.9 0.0 collective-permute-done.refs_0_
  10.9 0.2 shard_map.111
  11.1 0.3 collective-permute-start.8
  11.4 1.5 %collective-permute-start.5 = (bf16[5,72,128]{2,1,0:T(8,128)(2,1)S(1)}, bf16[5,72,128]{2,1,0:T(8,128)(2,1)S(1)}, u32[]{:S(2)}, u32[]{:S(2)}) collective-permute-start(bf16[5,72,128]{2,1,0:T(8,128)(2,1)S(1)} %get-tuple-element.61.refs_0_), channel_id=1, source_target_pairs={{0,12},{4,8},{8,4},{12,0},{16,28},{20,24},{24,20},{28,16},{1,13},{... | collective-permute-start | bytes 276488 | tf_op jit(solution)/shard_map/ppermute | solution.py:440
  12.9 0.2 collective-permute-start.7
  13.1 0.3 collective-permute-start.6
  13.4 1.2 %shard_map.112 = (f32[72,256]{1,0:T(8,128)S(1)}, f32[72,256]{1,0:T(8,128)S(1)}) custom-call(bf16[2,3,6,2,256]{4,3,2,1,0:T(2,128)(2,1)S(1)} %collective-permute-done.refs_0_, bf16[2,3,6,2,256]{4,3,2,1,0:T(2,128)(2,1)S(1)} %collective-permute-done.1.refs_1_, bf16[2,3,6,2,256]{4,3,2,1,0:T(2,128)(2,1)S(1)} %collective-permute-done.2.refs_2_, ...), custom_call_target="tpu_custom_call" | custom-call | tf_op jit(solution)/shard_map/pallas_call | solution.py:35
  14.6 0.0 collective-permute-done.6.halo_odd
  14.6 0.0 collective-permute-done.7.halo_core.refs_3_.asker.refs_4_
  14.6 0.0 collective-permute-done.8.refs_2_
  14.6 1.4 %collective-permute-done.5.halo_last.refs_1_ = bf16[5,72,128]{2,1,0:T(8,128)(2,1)S(1)} collective-permute-done((bf16[5,72,128]{2,1,0:T(8,128)(2,1)S(1)}, bf16[5,72,128]{2,1,0:T(8,128)(2,1)S(1)}, u32[]{:S(2)}, u32[]{:S(2)}) %collective-permute-start.5) | collective-permute-done | bytes 92192 | tf_op jit(solution)/shard_map/ppermute | solution.py:440
  16.0 0.2 collective-permute-start.9
  16.2 0.6 %shard_map.113 = (bf16[72,256]{1,0:T(8,128)(2,1)S(1)}, bf16[72,128]{1,0:T(8,128)(2,1)S(1)}) custom-call(bf16[2,72,128]{2,1,0:T(8,128)(2,1)S(1)} %collective-permute-done.7.halo_core.refs_3_.asker.refs_4_, bf16[5,72,128]{2,1,0:T(8,128)(2,1)S(1)} %collective-permute-done.5.halo_last.refs_1_, bf16[72,128]{1,0:T(8,128)(2,1)S(1)} %collective-permute-done.6.halo_odd, ...), custom_call_target="tpu_custom_call" | custom-call | tf_op jit(solution)/shard_map/pallas_call | solution.py:35
  16.8 0.4 %shard_map.114 = (f32[2,432,72]{2,1,0:T(8,128)S(1)}, f32[2,432,72]{2,1,0:T(8,128)S(1)}) custom-call(bf16[5,72,128]{2,1,0:T(8,128)(2,1)S(1)} %get-tuple-element.61.refs_0_, bf16[5,72,128]{2,1,0:T(8,128)(2,1)S(1)} %collective-permute-done.5.halo_last.refs_1_, bf16[5,72,128]{2,1,0:T(8,128)(2,1)S(1)} %collective-permute-done.8.refs_2_, ...), custom_call_target="tpu_custom_call" | custom-call | tf_op jit(solution)/shard_map/pallas_call | solution.py:35
  17.2 0.1 collective-permute-done.9.late.refs_3_
  17.3 0.7 %shard_map.115 = (bf16[4,2,72,128]{3,2,1,0:T(8,128)(2,1)S(1)}, bf16[2,576,72]{2,1,0:T(8,128)(2,1)S(1)}, bf16[2,288,72]{2,1,0:T(8,128)(2,1)S(1)}) custom-call(bf16[5,72,128]{2,1,0:T(8,128)(2,1)S(1)} %collective-permute-done.9.late.refs_3_, bf16[2,72,128]{2,1,0:T(8,128)(2,1)S(1)} %collective-permute-done.7.halo_core.refs_3_.asker.refs_4_, ...), custom_call_target="tpu_custom_call" | custom-call | tf_op jit(solution)/shard_map/pallas_call | solution.py:35
  18.0 0.3 collective-permute-start.10
  18.4 0.0 copy-done
  18.4 0.5 %shard_map.116 = (bf16[4,2,72,128]{3,2,1,0:T(8,128)(2,1)S(1)}, f32[72,256]{1,0:T(8,128)S(1)}, bf16[256,256]{1,0:T(8,128)(2,1)S(1)}) custom-call(bf16[5,72,128]{2,1,0:T(8,128)(2,1)S(1)} %get-tuple-element.61.refs_0_, bf16[5,72,128]{2,1,0:T(8,128)(2,1)S(1)} %collective-permute-done.5.halo_last.refs_1_, bf16[5,72,128]{2,1,0:T(8,128)(2,1)S(1)} %collective-permute-done.8.refs_2_, ...), custom_call_target="tpu_custom_call" | custom-call | tf_op jit(solution)/shard_map/pallas_call | solution.py:35
  18.9 0.6 %collective-permute-done.10.received = bf16[4,2,72,128]{3,2,1,0:T(8,128)(2,1)S(1)} collective-permute-done((bf16[4,2,72,128]{3,2,1,0:T(8,128)(2,1)S(1)}, bf16[4,2,72,128]{3,2,1,0:T(8,128)(2,1)S(1)}, u32[]{:S(2)}, u32[]{:S(2)}) %collective-permute-start.10) | collective-permute-done | bytes 147488 | tf_op jit(solution)/shard_map/ppermute | solution.py:443
  19.5 1.3 %collective-permute-start.11 = (bf16[2,72,128]{2,1,0:T(8,128)(2,1)S(1)}, bf16[2,72,128]{2,1,0:T(8,128)(2,1)S(1)}, u32[]{:S(2)}, u32[]{:S(2)}) collective-permute-start(bf16[2,72,128]{2,1,0:T(8,128)(2,1)S(1)} %get-tuple-element.83), channel_id=1, source_target_pairs={{0,28},{4,24},{8,20},{12,16},{16,12},{20,8},{24,4},{28,0},{1,29},{... | collective-permute-start | bytes 110600 | tf_op jit(solution)/shard_map/ppermute | solution.py:440
  20.8 0.3 collective-permute-start.12
  21.1 2.5 %collective-permute-start.13 = (bf16[2,72,128]{2,1,0:T(8,128)(2,1)S(1)}, bf16[2,72,128]{2,1,0:T(8,128)(2,1)S(1)}, u32[]{:S(2)}, u32[]{:S(2)}) collective-permute-start(bf16[2,72,128]{2,1,0:T(8,128)(2,1)S(1)} %get-tuple-element.85), channel_id=1, source_target_pairs={{0,20},{4,16},{8,28},{12,24},{16,4},{20,0},{24,12},{28,8},{1,21},{... | collective-permute-start | bytes 110600 | tf_op jit(solution)/shard_map/ppermute | solution.py:440
  23.5 1.3 %collective-permute-done.11.refs_0_ = bf16[2,72,128]{2,1,0:T(8,128)(2,1)S(1)} collective-permute-done((bf16[2,72,128]{2,1,0:T(8,128)(2,1)S(1)}, bf16[2,72,128]{2,1,0:T(8,128)(2,1)S(1)}, u32[]{:S(2)}, u32[]{:S(2)}) %collective-permute-start.11) | collective-permute-done | bytes 36896 | tf_op jit(solution)/shard_map/ppermute | solution.py:440
  24.9 0.0 collective-permute-done.12.refs_1_
  24.9 1.0 %collective-permute-done.13.refs_2_ = bf16[2,72,128]{2,1,0:T(8,128)(2,1)S(1)} collective-permute-done((bf16[2,72,128]{2,1,0:T(8,128)(2,1)S(1)}, bf16[2,72,128]{2,1,0:T(8,128)(2,1)S(1)}, u32[]{:S(2)}, u32[]{:S(2)}) %collective-permute-start.13) | collective-permute-done | bytes 36896 | tf_op jit(solution)/shard_map/ppermute | solution.py:440
  25.8 0.0 copy-done.1
  25.9 0.3 shard_map.118
  26.2 2.1 %collective-permute-start.14 = (bf16[24,256]{1,0:T(8,128)(2,1)S(1)}, bf16[24,256]{1,0:T(8,128)(2,1)S(1)}, u32[]{:S(2)}, u32[]{:S(2)}) collective-permute-start(bf16[24,256]{1,0:T(8,128)(2,1)S(1)} %get-tuple-element.89), channel_id=1, source_target_pairs={{0,7},{1,6},{2,5},{3,4},{4,3},{5,2},{6,1},{7,0},{8,15},{9,14},{10,... | collective-permute-start | bytes 36872 | tf_op jit(solution)/shard_map/ppermute | solution.py:437
  28.2 0.0 collective-permute-start.15
  28.2 1.0 %collective-permute-start.16 = (bf16[24,256]{1,0:T(8,128)(2,1)S(1)}, bf16[24,256]{1,0:T(8,128)(2,1)S(1)}, u32[]{:S(2)}, u32[]{:S(2)}) collective-permute-start(bf16[24,256]{1,0:T(8,128)(2,1)S(1)} %get-tuple-element.91), channel_id=1, source_target_pairs={{0,5},{1,4},{2,7},{3,6},{4,1},{5,0},{6,3},{7,2},{8,13},{9,12},{10,... | collective-permute-start | bytes 36872 | tf_op jit(solution)/shard_map/ppermute | solution.py:437
  29.3 0.3 collective-permute-start.17
  29.6 0.7 %collective-permute-done.14.refs_0_ = bf16[24,256]{1,0:T(8,128)(2,1)S(1)} collective-permute-done((bf16[24,256]{1,0:T(8,128)(2,1)S(1)}, bf16[24,256]{1,0:T(8,128)(2,1)S(1)}, u32[]{:S(2)}, u32[]{:S(2)}) %collective-permute-start.14) | collective-permute-done | bytes 12320 | tf_op jit(solution)/shard_map/ppermute | solution.py:437
  30.3 1.1 %collective-permute-done.15.refs_1_ = bf16[24,256]{1,0:T(8,128)(2,1)S(1)} collective-permute-done((bf16[24,256]{1,0:T(8,128)(2,1)S(1)}, bf16[24,256]{1,0:T(8,128)(2,1)S(1)}, u32[]{:S(2)}, u32[]{:S(2)}) %collective-permute-start.15) | collective-permute-done | bytes 12320 | tf_op jit(solution)/shard_map/ppermute | solution.py:437
  31.4 0.0 collective-permute-done.16.refs_2_
  31.4 0.0 collective-permute-done.17.refs_3_
  31.4 0.7 %shard_map.119 = bf16[3,6,2,256]{3,2,1,0:T(2,128)(2,1)} custom-call(bf16[24,256]{1,0:T(8,128)(2,1)S(1)} %collective-permute-done.14.refs_0_, bf16[24,256]{1,0:T(8,128)(2,1)S(1)} %collective-permute-done.15.refs_1_, bf16[24,256]{1,0:T(8,128)(2,1)S(1)} %collective-permute-done.16.refs_2_, bf16[24,256]{1,0:T(8,128)(2,1)S(1)} %collective-permute-done.17.refs_3_), custom_call_target="tpu_custom_call" | custom-call | tf_op jit(solution)/shard_map/pallas_call | solution.py:35
  (3 shorter events, 0.0 us)
Async XLA Ops:
  0.9 8.4 %collective-permute-start.4 = (bf16[2,72,128]{2,1,0:T(8,128)(2,1)S(1)}, bf16[2,72,128]{2,1,0:T(8,128)(2,1)S(1)}, u32[]{:S(2)}, u32[]{:S(2)}) collective-permute-start(bf16[2,72,128]{2,1,0:T(8,128)(2,1)S(1)} %get-tuple-element.50.refs_4_), channel_id=1, source_target_pairs={{0,20},{4,16},{8,28},{12,24},{16,4},{20,0},{24,12},{28,8},{1,21},{... | collective-permute-start | bytes 110600 | tf_op jit(solution)/shard_map/ppermute | solution.py:440
  4.5 4.9 %collective-permute-start.3 = (bf16[2,3,6,2,256]{4,3,2,1,0:T(2,128)(2,1)S(1)}, bf16[2,3,6,2,256]{4,3,2,1,0:T(2,128)(2,1)S(1)}, u32[]{:S(2)}, u32[]{:S(2)}) collective-permute-start(bf16[2,3,6,2,256]{4,3,2,1,0:T(2,128)(2,1)S(1)} %get-tuple-element.49), channel_id=1, source_target_pairs={{0,7},{1,6},{2,5},{3,4},{4,3},{5,2},{6,1},{7,0},{8,15},{9,14},{10,... | collective-permute-start | bytes 110600 | tf_op jit(solution)/shard_map/ppermute | solution.py:437
  7.2 3.8 %collective-permute-start.2 = (bf16[2,3,6,2,256]{4,3,2,1,0:T(2,128)(2,1)S(1)}, bf16[2,3,6,2,256]{4,3,2,1,0:T(2,128)(2,1)S(1)}, u32[]{:S(2)}, u32[]{:S(2)}) collective-permute-start(bf16[2,3,6,2,256]{4,3,2,1,0:T(2,128)(2,1)S(1)} %get-tuple-element.49), channel_id=1, source_target_pairs={{0,6},{1,7},{2,4},{3,5},{4,2},{5,3},{6,0},{7,1},{8,14},{9,15},{10,... | collective-permute-start | bytes 110600 | tf_op jit(solution)/shard_map/ppermute | solution.py:437
  7.2 3.8 %collective-permute-start.1 = (bf16[2,3,6,2,256]{4,3,2,1,0:T(2,128)(2,1)S(1)}, bf16[2,3,6,2,256]{4,3,2,1,0:T(2,128)(2,1)S(1)}, u32[]{:S(2)}, u32[]{:S(2)}) collective-permute-start(bf16[2,3,6,2,256]{4,3,2,1,0:T(2,128)(2,1)S(1)} %get-tuple-element.49), channel_id=1, source_target_pairs={{0,5},{1,4},{2,7},{3,6},{4,1},{5,0},{6,3},{7,2},{8,13},{9,12},{10,... | collective-permute-start | bytes 110600 | tf_op jit(solution)/shard_map/ppermute | solution.py:437
  7.9 3.0 %collective-permute-start = (bf16[2,3,6,2,256]{4,3,2,1,0:T(2,128)(2,1)S(1)}, bf16[2,3,6,2,256]{4,3,2,1,0:T(2,128)(2,1)S(1)}, u32[]{:S(2)}, u32[]{:S(2)}) collective-permute-start(bf16[2,3,6,2,256]{4,3,2,1,0:T(2,128)(2,1)S(1)} %get-tuple-element.49), channel_id=1, source_target_pairs={{0,4},{1,5},{2,6},{3,7},{4,0},{5,1},{6,2},{7,3},{8,12},{9,13},{10,... | collective-permute-start | bytes 110600 | tf_op jit(solution)/shard_map/ppermute | solution.py:437
  11.1 3.5 %collective-permute-start.8 = (bf16[5,72,128]{2,1,0:T(8,128)(2,1)S(1)}, bf16[5,72,128]{2,1,0:T(8,128)(2,1)S(1)}, u32[]{:S(2)}, u32[]{:S(2)}) collective-permute-start(bf16[5,72,128]{2,1,0:T(8,128)(2,1)S(1)} %get-tuple-element.61.refs_0_), channel_id=1, source_target_pairs={{0,4},{4,0},{8,12},{12,8},{16,20},{20,16},{24,28},{28,24},{1,5},{5... | collective-permute-start | bytes 276488 | tf_op jit(solution)/shard_map/ppermute | solution.py:443
  11.4 4.6 %collective-permute-start.5 = (bf16[5,72,128]{2,1,0:T(8,128)(2,1)S(1)}, bf16[5,72,128]{2,1,0:T(8,128)(2,1)S(1)}, u32[]{:S(2)}, u32[]{:S(2)}) collective-permute-start(bf16[5,72,128]{2,1,0:T(8,128)(2,1)S(1)} %get-tuple-element.61.refs_0_), channel_id=1, source_target_pairs={{0,12},{4,8},{8,4},{12,0},{16,28},{20,24},{24,20},{28,16},{1,13},{... | collective-permute-start | bytes 276488 | tf_op jit(solution)/shard_map/ppermute | solution.py:440
  12.9 1.7 %collective-permute-start.7 = (bf16[2,72,128]{2,1,0:T(8,128)(2,1)S(1)}, bf16[2,72,128]{2,1,0:T(8,128)(2,1)S(1)}, u32[]{:S(2)}, u32[]{:S(2)}) collective-permute-start(bf16[2,72,128]{2,1,0:T(8,128)(2,1)S(1)} %get-tuple-element.66), channel_id=1, source_target_pairs={{0,4},{4,0},{8,12},{12,8},{16,20},{20,16},{24,28},{28,24},{1,5},{5... | collective-permute-start | bytes 110600 | tf_op jit(solution)/shard_map/ppermute | solution.py:443
  13.1 1.5 %collective-permute-start.6 = (bf16[72,128]{1,0:T(8,128)(2,1)S(1)}, bf16[72,128]{1,0:T(8,128)(2,1)S(1)}, u32[]{:S(2)}, u32[]{:S(2)}) collective-permute-start(bf16[72,128]{1,0:T(8,128)(2,1)S(1)} %get-tuple-element.65), channel_id=1, source_target_pairs={{0,4},{24,28},{8,20},{12,16},{4,0},{28,24},{20,8},{16,12},{1,5},{2... | collective-permute-start | bytes 55304 | tf_op jit(solution)/shard_map/ppermute | solution.py:449
  16.0 1.3 %collective-permute-start.9 = (bf16[5,72,128]{2,1,0:T(8,128)(2,1)S(1)}, bf16[5,72,128]{2,1,0:T(8,128)(2,1)S(1)}, u32[]{:S(2)}, u32[]{:S(2)}) collective-permute-start(bf16[5,72,128]{2,1,0:T(8,128)(2,1)S(1)} %collective-permute-done.5.halo_last.refs_1_), channel_id=1, source_target_pairs={{0,4},{4,0},{8,12},{12,8},{16,20},{20,16},{24,28},{28,24},{1,5},{5... | collective-permute-start | bytes 276488 | tf_op jit(solution)/shard_map/ppermute | solution.py:443
  16.2 2.2 %copy-start = (bf16[256,768]{1,0:T(8,128)(2,1)S(1)}, bf16[256,768]{1,0:T(8,128)(2,1)}, u32[]{:S(2)}) copy-start(bf16[256,768]{1,0:T(8,128)(2,1)} %refs_9_.1) | copy-start | bytes 1179652
  17.3 8.6 %copy-start.1 = (bf16[96,72]{1,0:T(8,128)(2,1)S(1)}, bf16[96,72]{1,0:T(8,128)(2,1)}, u32[]{:S(2)}) copy-start(bf16[96,72]{1,0:T(8,128)(2,1)} %constant.8.clone.refs_6_) | copy-start | bytes 41476
  18.0 1.4 %collective-permute-start.10 = (bf16[4,2,72,128]{3,2,1,0:T(8,128)(2,1)S(1)}, bf16[4,2,72,128]{3,2,1,0:T(8,128)(2,1)S(1)}, u32[]{:S(2)}, u32[]{:S(2)}) collective-permute-start(bf16[4,2,72,128]{3,2,1,0:T(8,128)(2,1)S(1)} %get-tuple-element.82), channel_id=1, source_target_pairs={{0,4},{4,0},{8,12},{12,8},{16,20},{20,16},{24,28},{28,24},{1,5},{5... | collective-permute-start | bytes 442376 | tf_op jit(solution)/shard_map/ppermute | solution.py:443
  19.5 5.4 %collective-permute-start.11 = (bf16[2,72,128]{2,1,0:T(8,128)(2,1)S(1)}, bf16[2,72,128]{2,1,0:T(8,128)(2,1)S(1)}, u32[]{:S(2)}, u32[]{:S(2)}) collective-permute-start(bf16[2,72,128]{2,1,0:T(8,128)(2,1)S(1)} %get-tuple-element.83), channel_id=1, source_target_pairs={{0,28},{4,24},{8,20},{12,16},{16,12},{20,8},{24,4},{28,0},{1,29},{... | collective-permute-start | bytes 110600 | tf_op jit(solution)/shard_map/ppermute | solution.py:440
  20.8 4.1 %collective-permute-start.12 = (bf16[2,72,128]{2,1,0:T(8,128)(2,1)S(1)}, bf16[2,72,128]{2,1,0:T(8,128)(2,1)S(1)}, u32[]{:S(2)}, u32[]{:S(2)}) collective-permute-start(bf16[2,72,128]{2,1,0:T(8,128)(2,1)S(1)} %get-tuple-element.84), channel_id=1, source_target_pairs={{0,12},{4,8},{8,4},{12,0},{16,28},{20,24},{24,20},{28,16},{1,13},{... | collective-permute-start | bytes 110600 | tf_op jit(solution)/shard_map/ppermute | solution.py:440
  21.1 4.8 %collective-permute-start.13 = (bf16[2,72,128]{2,1,0:T(8,128)(2,1)S(1)}, bf16[2,72,128]{2,1,0:T(8,128)(2,1)S(1)}, u32[]{:S(2)}, u32[]{:S(2)}) collective-permute-start(bf16[2,72,128]{2,1,0:T(8,128)(2,1)S(1)} %get-tuple-element.85), channel_id=1, source_target_pairs={{0,20},{4,16},{8,28},{12,24},{16,4},{20,0},{24,12},{28,8},{1,21},{... | collective-permute-start | bytes 110600 | tf_op jit(solution)/shard_map/ppermute | solution.py:440
  26.2 4.1 %collective-permute-start.14 = (bf16[24,256]{1,0:T(8,128)(2,1)S(1)}, bf16[24,256]{1,0:T(8,128)(2,1)S(1)}, u32[]{:S(2)}, u32[]{:S(2)}) collective-permute-start(bf16[24,256]{1,0:T(8,128)(2,1)S(1)} %get-tuple-element.89), channel_id=1, source_target_pairs={{0,7},{1,6},{2,5},{3,4},{4,3},{5,2},{6,1},{7,0},{8,15},{9,14},{10,... | collective-permute-start | bytes 36872 | tf_op jit(solution)/shard_map/ppermute | solution.py:437
  28.2 3.1 %collective-permute-start.15 = (bf16[24,256]{1,0:T(8,128)(2,1)S(1)}, bf16[24,256]{1,0:T(8,128)(2,1)S(1)}, u32[]{:S(2)}, u32[]{:S(2)}) collective-permute-start(bf16[24,256]{1,0:T(8,128)(2,1)S(1)} %get-tuple-element.90), channel_id=1, source_target_pairs={{0,6},{1,7},{2,4},{3,5},{4,2},{5,3},{6,0},{7,1},{8,14},{9,15},{10,... | collective-permute-start | bytes 36872 | tf_op jit(solution)/shard_map/ppermute | solution.py:437
  28.2 3.1 %collective-permute-start.16 = (bf16[24,256]{1,0:T(8,128)(2,1)S(1)}, bf16[24,256]{1,0:T(8,128)(2,1)S(1)}, u32[]{:S(2)}, u32[]{:S(2)}) collective-permute-start(bf16[24,256]{1,0:T(8,128)(2,1)S(1)} %get-tuple-element.91), channel_id=1, source_target_pairs={{0,5},{1,4},{2,7},{3,6},{4,1},{5,0},{6,3},{7,2},{8,13},{9,12},{10,... | collective-permute-start | bytes 36872 | tf_op jit(solution)/shard_map/ppermute | solution.py:437
  29.3 2.1 %collective-permute-start.17 = (bf16[24,256]{1,0:T(8,128)(2,1)S(1)}, bf16[24,256]{1,0:T(8,128)(2,1)S(1)}, u32[]{:S(2)}, u32[]{:S(2)}) collective-permute-start(bf16[24,256]{1,0:T(8,128)(2,1)S(1)} %get-tuple-element.92), channel_id=1, source_target_pairs={{0,4},{1,5},{2,6},{3,7},{4,0},{5,1},{6,2},{7,3},{8,12},{9,13},{10,... | collective-permute-start | bytes 36872 | tf_op jit(solution)/shard_map/ppermute | solution.py:437

commit v12 on v11

--- a/solution.py
+++ b/solution.py
@@ -91,7 +91,7 @@
 
 
 def beside(left, right):
-    return jnp.concatenate([left.astype(F32), right.astype(F32)], 0).T.astype(BF16)
+    return jnp.concatenate([left, right], 0).T
 
 
 def pack_kernel(out_grad, pre_silu, keys, values, tile, kv, k_ref, v_ref, sems):
@@ -120,11 +120,11 @@
     used = rims.shape[1] * rims.shape[2]
     inner = jnp.where(lax.axis_index("row") % 2 == 1, rows - 1, 0)
     cols = tiles[0].shape[2]
-    rims[...] = jnp.zeros_like(rims)
+    rest = jnp.zeros((rims.shape[2] - cols, rims.shape[3]), F32)
     to_core[1] = query[...]
     for side, (row, out) in enumerate(((inner, to_core.at[0]), (rows - 1 - inner, to_chip))):
         for k, tile in enumerate(tiles):
-            rims[side, col ^ k, :cols] = pick(tile[0, row], col // per_sample)
+            rims[side, col ^ k] = jnp.concatenate([pick(tile[0, row], col // per_sample), rest], 0)
         flat = rims[side].reshape(used, -1).astype(BF16)
         out[...] = jnp.zeros_like(out)
         for part in range(flat.shape[1] // lanes):

time: 32.2 us -> 32.2 us (level)
  no operation moved by 1% of the time
where the time goes in v12:
time: 32.2 us; the launch traced here: 32 us
  starting transfers between devices  17.2 us (53%)
  waiting for transfers between devices  7.77 us (24%)
  Pallas kernels  6.88 us (21%)
    ppermute x5, starting transfers between devices, to_chip(): lax.ppermute(array, 'row', [(i, i ^ 2 * k + 1) for i in range(n_row)])  9.02 us
    ppermute x8, starting transfers between devices, to_col(): return lax.ppermute(array, ('row', 'col'), pairs_of)  6.88 us
    pallas_call x11, Pallas kernels, run(): pl.pallas_call(kernel, out_shape=out_shape, in_specs=specs, out_specs=jax...  6.88 us
    ppermute x5, waiting for transfers between devices, to_chip(): lax.ppermute(array, 'row', [(i, i ^ 2 * k + 1) for i in range(n_row)])  3.69 us
    ppermute x8, waiting for transfers between devices, to_col(): return lax.ppermute(array, ('row', 'col'), pairs_of)  3.4 us
    ppermute x4, starting transfers between devices, to_core(): return lax.ppermute(array, 'row', [(i, i ^ 1) for i in range(n_row)])  1.04 us
    ppermute x4, waiting for transfers between devices, to_core(): return lax.ppermute(array, 'row', [(i, i ^ 1) for i in range(n_row)])  0.67 us
  transfers between devices with their start and end apart: 18, of which 8 were waited for; matrix products, arithmetic and copies ran while one was open for 0% of the time, Pallas kernels for 13%

profile of v12, /device:TPU:0, one launch (start us, length us, event | category | flops | bytes accessed | tf_op | source)
XLA Modules:
  0.0 32.0 jit_solution(12503806292401998358)
XLA Ops:
  0.0 0.9 %shard_map.109 = (bf16[2,3,6,2,256]{4,3,2,1,0:T(2,128)(2,1)S(1)}, bf16[2,72,128]{2,1,0:T(8,128)(2,1)S(1)}) custom-call(bf16[3,6,2,256]{3,2,1,0:T(2,128)(2,1)} %bitcast.9, bf16[3,6,2,256]{3,2,1,0:T(2,128)(2,1)} %bitcast.10, bf16[2,64,72]{2,1,0:T(8,128)(2,1)} %bitcast.6, bf16[2,64,72]{2,1,0:T(8,128)(2,1)} %bitcast.7), custom_call_target="tpu_custom_call" | custom-call | tf_op jit(solution)/shard_map/pallas_call | solution.py:35
  0.9 3.5 %collective-permute-start.4 = (bf16[2,72,128]{2,1,0:T(8,128)(2,1)S(1)}, bf16[2,72,128]{2,1,0:T(8,128)(2,1)S(1)}, u32[]{:S(2)}, u32[]{:S(2)}) collective-permute-start(bf16[2,72,128]{2,1,0:T(8,128)(2,1)S(1)} %get-tuple-element.50.refs_4_), channel_id=1, source_target_pairs={{0,20},{4,16},{8,28},{12,24},{16,4},{20,0},{24,12},{28,8},{1,21},{... | collective-permute-start | bytes 110600 | tf_op jit(solution)/shard_map/ppermute | solution.py:440
  4.4 2.7 %collective-permute-start.3 = (bf16[2,3,6,2,256]{4,3,2,1,0:T(2,128)(2,1)S(1)}, bf16[2,3,6,2,256]{4,3,2,1,0:T(2,128)(2,1)S(1)}, u32[]{:S(2)}, u32[]{:S(2)}) collective-permute-start(bf16[2,3,6,2,256]{4,3,2,1,0:T(2,128)(2,1)S(1)} %get-tuple-element.49), channel_id=1, source_target_pairs={{0,7},{1,6},{2,5},{3,4},{4,3},{5,2},{6,1},{7,0},{8,15},{9,14},{10,... | collective-permute-start | bytes 110600 | tf_op jit(solution)/shard_map/ppermute | solution.py:437
  7.2 0.0 collective-permute-start.2
  7.2 0.8 %collective-permute-start.1 = (bf16[2,3,6,2,256]{4,3,2,1,0:T(2,128)(2,1)S(1)}, bf16[2,3,6,2,256]{4,3,2,1,0:T(2,128)(2,1)S(1)}, u32[]{:S(2)}, u32[]{:S(2)}) collective-permute-start(bf16[2,3,6,2,256]{4,3,2,1,0:T(2,128)(2,1)S(1)} %get-tuple-element.49), channel_id=1, source_target_pairs={{0,5},{1,4},{2,7},{3,6},{4,1},{5,0},{6,3},{7,2},{8,13},{9,12},{10,... | collective-permute-start | bytes 110600 | tf_op jit(solution)/shard_map/ppermute | solution.py:437
  7.9 0.0 collective-permute-start
  7.9 1.4 %shard_map.110 = (bf16[3,72,96]{2,1,0:T(8,128)(2,1)S(1)}, bf16[3,24,32]{2,1,0:T(8,128)(2,1)S(1)}, bf16[3,3,256,256]{3,2,1,0:T(8,128)(2,1)S(1)}, bf16[256,256]{1,0:T(8,128)(2,1)S(1)}, bf16[72,128]{1,0:T(8,128)(2,1)S(1)}) custom-call(bf16[2,64,72]{2,1,0:T(8,128)(2,1)} %bitcast.8, bf16[3,72,96]{2,1,0:T(8,128)(2,1)} %constant.6.clone.refs_0_, ...), custom_call_target="tpu_custom_call" | custom-call | tf_op jit(solution)/shard_map/pallas_call | solution.py:35
  9.3 0.0 collective-permute-done.4.refs_5_
  9.3 0.0 collective-permute-done.3.refs_3_
  9.3 1.6 %collective-permute-done.2.refs_2_ = bf16[2,3,6,2,256]{4,3,2,1,0:T(2,128)(2,1)S(1)} collective-permute-done((bf16[2,3,6,2,256]{4,3,2,1,0:T(2,128)(2,1)S(1)}, bf16[2,3,6,2,256]{4,3,2,1,0:T(2,128)(2,1)S(1)}, u32[]{:S(2)}, u32[]{:S(2)}) %collective-permute-start.2) | collective-permute-done | bytes 36896 | tf_op jit(solution)/shard_map/ppermute | solution.py:437
  10.9 0.0 collective-permute-done.1.refs_1_
  10.9 0.0 collective-permute-done.refs_0_
  10.9 0.2 shard_map.111
  11.1 0.3 collective-permute-start.8
  11.4 1.5 %collective-permute-start.5 = (bf16[5,72,128]{2,1,0:T(8,128)(2,1)S(1)}, bf16[5,72,128]{2,1,0:T(8,128)(2,1)S(1)}, u32[]{:S(2)}, u32[]{:S(2)}) collective-permute-start(bf16[5,72,128]{2,1,0:T(8,128)(2,1)S(1)} %get-tuple-element.61.refs_0_), channel_id=1, source_target_pairs={{0,12},{4,8},{8,4},{12,0},{16,28},{20,24},{24,20},{28,16},{1,13},{... | collective-permute-start | bytes 276488 | tf_op jit(solution)/shard_map/ppermute | solution.py:440
  12.8 0.2 collective-permute-start.7
  13.1 0.3 collective-permute-start.6
  13.4 1.2 %shard_map.112 = (f32[72,256]{1,0:T(8,128)S(1)}, f32[72,256]{1,0:T(8,128)S(1)}) custom-call(bf16[2,3,6,2,256]{4,3,2,1,0:T(2,128)(2,1)S(1)} %collective-permute-done.refs_0_, bf16[2,3,6,2,256]{4,3,2,1,0:T(2,128)(2,1)S(1)} %collective-permute-done.1.refs_1_, bf16[2,3,6,2,256]{4,3,2,1,0:T(2,128)(2,1)S(1)} %collective-permute-done.2.refs_2_, ...), custom_call_target="tpu_custom_call" | custom-call | tf_op jit(solution)/shard_map/pallas_call | solution.py:35
  14.5 0.0 collective-permute-done.6.halo_odd
  14.5 0.0 collective-permute-done.7.halo_core.refs_3_.asker.refs_4_
  14.6 0.0 collective-permute-done.8.refs_2_
  14.6 1.4 %collective-permute-done.5.halo_last.refs_1_ = bf16[5,72,128]{2,1,0:T(8,128)(2,1)S(1)} collective-permute-done((bf16[5,72,128]{2,1,0:T(8,128)(2,1)S(1)}, bf16[5,72,128]{2,1,0:T(8,128)(2,1)S(1)}, u32[]{:S(2)}, u32[]{:S(2)}) %collective-permute-start.5) | collective-permute-done | bytes 92192 | tf_op jit(solution)/shard_map/ppermute | solution.py:440
  16.0 0.2 collective-permute-start.9
  16.2 0.6 %shard_map.113 = (bf16[72,256]{1,0:T(8,128)(2,1)S(1)}, bf16[72,128]{1,0:T(8,128)(2,1)S(1)}) custom-call(bf16[2,72,128]{2,1,0:T(8,128)(2,1)S(1)} %collective-permute-done.7.halo_core.refs_3_.asker.refs_4_, bf16[5,72,128]{2,1,0:T(8,128)(2,1)S(1)} %collective-permute-done.5.halo_last.refs_1_, bf16[72,128]{1,0:T(8,128)(2,1)S(1)} %collective-permute-done.6.halo_odd, ...), custom_call_target="tpu_custom_call" | custom-call | tf_op jit(solution)/shard_map/pallas_call | solution.py:35
  16.8 0.4 %shard_map.114 = (f32[2,432,72]{2,1,0:T(8,128)S(1)}, f32[2,432,72]{2,1,0:T(8,128)S(1)}) custom-call(bf16[5,72,128]{2,1,0:T(8,128)(2,1)S(1)} %get-tuple-element.61.refs_0_, bf16[5,72,128]{2,1,0:T(8,128)(2,1)S(1)} %collective-permute-done.5.halo_last.refs_1_, bf16[5,72,128]{2,1,0:T(8,128)(2,1)S(1)} %collective-permute-done.8.refs_2_, ...), custom_call_target="tpu_custom_call" | custom-call | tf_op jit(solution)/shard_map/pallas_call | solution.py:35
  17.2 0.1 collective-permute-done.9.late.refs_3_
  17.3 0.7 %shard_map.115 = (bf16[4,2,72,128]{3,2,1,0:T(8,128)(2,1)S(1)}, bf16[2,576,72]{2,1,0:T(8,128)(2,1)S(1)}, bf16[2,288,72]{2,1,0:T(8,128)(2,1)S(1)}) custom-call(bf16[5,72,128]{2,1,0:T(8,128)(2,1)S(1)} %collective-permute-done.9.late.refs_3_, bf16[2,72,128]{2,1,0:T(8,128)(2,1)S(1)} %collective-permute-done.7.halo_core.refs_3_.asker.refs_4_, ...), custom_call_target="tpu_custom_call" | custom-call | tf_op jit(solution)/shard_map/pallas_call | solution.py:35
  18.0 0.3 collective-permute-start.10
  18.3 0.0 copy-done
  18.3 0.5 %shard_map.116 = (bf16[4,2,72,128]{3,2,1,0:T(8,128)(2,1)S(1)}, f32[72,256]{1,0:T(8,128)S(1)}, bf16[256,256]{1,0:T(8,128)(2,1)S(1)}) custom-call(bf16[5,72,128]{2,1,0:T(8,128)(2,1)S(1)} %get-tuple-element.61.refs_0_, bf16[5,72,128]{2,1,0:T(8,128)(2,1)S(1)} %collective-permute-done.5.halo_last.refs_1_, bf16[5,72,128]{2,1,0:T(8,128)(2,1)S(1)} %collective-permute-done.8.refs_2_, ...), custom_call_target="tpu_custom_call" | custom-call | tf_op jit(solution)/shard_map/pallas_call | solution.py:35
  18.9 0.6 %collective-permute-done.10.received = bf16[4,2,72,128]{3,2,1,0:T(8,128)(2,1)S(1)} collective-permute-done((bf16[4,2,72,128]{3,2,1,0:T(8,128)(2,1)S(1)}, bf16[4,2,72,128]{3,2,1,0:T(8,128)(2,1)S(1)}, u32[]{:S(2)}, u32[]{:S(2)}) %collective-permute-start.10) | collective-permute-done | bytes 147488 | tf_op jit(solution)/shard_map/ppermute | solution.py:443
  19.5 1.3 %collective-permute-start.11 = (bf16[2,72,128]{2,1,0:T(8,128)(2,1)S(1)}, bf16[2,72,128]{2,1,0:T(8,128)(2,1)S(1)}, u32[]{:S(2)}, u32[]{:S(2)}) collective-permute-start(bf16[2,72,128]{2,1,0:T(8,128)(2,1)S(1)} %get-tuple-element.83), channel_id=1, source_target_pairs={{0,28},{4,24},{8,20},{12,16},{16,12},{20,8},{24,4},{28,0},{1,29},{... | collective-permute-start | bytes 110600 | tf_op jit(solution)/shard_map/ppermute | solution.py:440
  20.8 0.3 collective-permute-start.12
  21.0 2.5 %collective-permute-start.13 = (bf16[2,72,128]{2,1,0:T(8,128)(2,1)S(1)}, bf16[2,72,128]{2,1,0:T(8,128)(2,1)S(1)}, u32[]{:S(2)}, u32[]{:S(2)}) collective-permute-start(bf16[2,72,128]{2,1,0:T(8,128)(2,1)S(1)} %get-tuple-element.85), channel_id=1, source_target_pairs={{0,20},{4,16},{8,28},{12,24},{16,4},{20,0},{24,12},{28,8},{1,21},{... | collective-permute-start | bytes 110600 | tf_op jit(solution)/shard_map/ppermute | solution.py:440
  23.5 1.3 %collective-permute-done.11.refs_0_ = bf16[2,72,128]{2,1,0:T(8,128)(2,1)S(1)} collective-permute-done((bf16[2,72,128]{2,1,0:T(8,128)(2,1)S(1)}, bf16[2,72,128]{2,1,0:T(8,128)(2,1)S(1)}, u32[]{:S(2)}, u32[]{:S(2)}) %collective-permute-start.11) | collective-permute-done | bytes 36896 | tf_op jit(solution)/shard_map/ppermute | solution.py:440
  24.8 0.0 collective-permute-done.12.refs_1_
  24.8 1.0 %collective-permute-done.13.refs_2_ = bf16[2,72,128]{2,1,0:T(8,128)(2,1)S(1)} collective-permute-done((bf16[2,72,128]{2,1,0:T(8,128)(2,1)S(1)}, bf16[2,72,128]{2,1,0:T(8,128)(2,1)S(1)}, u32[]{:S(2)}, u32[]{:S(2)}) %collective-permute-start.13) | collective-permute-done | bytes 36896 | tf_op jit(solution)/shard_map/ppermute | solution.py:440
  25.8 0.0 copy-done.1
  25.8 0.3 shard_map.118
  26.1 2.1 %collective-permute-start.14 = (bf16[24,256]{1,0:T(8,128)(2,1)S(1)}, bf16[24,256]{1,0:T(8,128)(2,1)S(1)}, u32[]{:S(2)}, u32[]{:S(2)}) collective-permute-start(bf16[24,256]{1,0:T(8,128)(2,1)S(1)} %get-tuple-element.89), channel_id=1, source_target_pairs={{0,7},{1,6},{2,5},{3,4},{4,3},{5,2},{6,1},{7,0},{8,15},{9,14},{10,... | collective-permute-start | bytes 36872 | tf_op jit(solution)/shard_map/ppermute | solution.py:437
  28.2 0.0 collective-permute-start.15
  28.2 1.0 %collective-permute-start.16 = (bf16[24,256]{1,0:T(8,128)(2,1)S(1)}, bf16[24,256]{1,0:T(8,128)(2,1)S(1)}, u32[]{:S(2)}, u32[]{:S(2)}) collective-permute-start(bf16[24,256]{1,0:T(8,128)(2,1)S(1)} %get-tuple-element.91), channel_id=1, source_target_pairs={{0,5},{1,4},{2,7},{3,6},{4,1},{5,0},{6,3},{7,2},{8,13},{9,12},{10,... | collective-permute-start | bytes 36872 | tf_op jit(solution)/shard_map/ppermute | solution.py:437
  29.2 0.3 collective-permute-start.17
  29.5 0.7 %collective-permute-done.14.refs_0_ = bf16[24,256]{1,0:T(8,128)(2,1)S(1)} collective-permute-done((bf16[24,256]{1,0:T(8,128)(2,1)S(1)}, bf16[24,256]{1,0:T(8,128)(2,1)S(1)}, u32[]{:S(2)}, u32[]{:S(2)}) %collective-permute-start.14) | collective-permute-done | bytes 12320 | tf_op jit(solution)/shard_map/ppermute | solution.py:437
  30.2 1.1 %collective-permute-done.15.refs_1_ = bf16[24,256]{1,0:T(8,128)(2,1)S(1)} collective-permute-done((bf16[24,256]{1,0:T(8,128)(2,1)S(1)}, bf16[24,256]{1,0:T(8,128)(2,1)S(1)}, u32[]{:S(2)}, u32[]{:S(2)}) %collective-permute-start.15) | collective-permute-done | bytes 12320 | tf_op jit(solution)/shard_map/ppermute | solution.py:437
  31.3 0.0 collective-permute-done.16.refs_2_
  31.3 0.0 collective-permute-done.17.refs_3_
  31.3 0.7 %shard_map.119 = bf16[3,6,2,256]{3,2,1,0:T(2,128)(2,1)} custom-call(bf16[24,256]{1,0:T(8,128)(2,1)S(1)} %collective-permute-done.14.refs_0_, bf16[24,256]{1,0:T(8,128)(2,1)S(1)} %collective-permute-done.15.refs_1_, bf16[24,256]{1,0:T(8,128)(2,1)S(1)} %collective-permute-done.16.refs_2_, bf16[24,256]{1,0:T(8,128)(2,1)S(1)} %collective-permute-done.17.refs_3_), custom_call_target="tpu_custom_call" | custom-call | tf_op jit(solution)/shard_map/pallas_call | solution.py:35
  (3 shorter events, 0.0 us)
Async XLA Ops:
  0.9 8.4 %collective-permute-start.4 = (bf16[2,72,128]{2,1,0:T(8,128)(2,1)S(1)}, bf16[2,72,128]{2,1,0:T(8,128)(2,1)S(1)}, u32[]{:S(2)}, u32[]{:S(2)}) collective-permute-start(bf16[2,72,128]{2,1,0:T(8,128)(2,1)S(1)} %get-tuple-element.50.refs_4_), channel_id=1, source_target_pairs={{0,20},{4,16},{8,28},{12,24},{16,4},{20,0},{24,12},{28,8},{1,21},{... | collective-permute-start | bytes 110600 | tf_op jit(solution)/shard_map/ppermute | solution.py:440
  4.4 4.9 %collective-permute-start.3 = (bf16[2,3,6,2,256]{4,3,2,1,0:T(2,128)(2,1)S(1)}, bf16[2,3,6,2,256]{4,3,2,1,0:T(2,128)(2,1)S(1)}, u32[]{:S(2)}, u32[]{:S(2)}) collective-permute-start(bf16[2,3,6,2,256]{4,3,2,1,0:T(2,128)(2,1)S(1)} %get-tuple-element.49), channel_id=1, source_target_pairs={{0,7},{1,6},{2,5},{3,4},{4,3},{5,2},{6,1},{7,0},{8,15},{9,14},{10,... | collective-permute-start | bytes 110600 | tf_op jit(solution)/shard_map/ppermute | solution.py:437
  7.2 3.8 %collective-permute-start.2 = (bf16[2,3,6,2,256]{4,3,2,1,0:T(2,128)(2,1)S(1)}, bf16[2,3,6,2,256]{4,3,2,1,0:T(2,128)(2,1)S(1)}, u32[]{:S(2)}, u32[]{:S(2)}) collective-permute-start(bf16[2,3,6,2,256]{4,3,2,1,0:T(2,128)(2,1)S(1)} %get-tuple-element.49), channel_id=1, source_target_pairs={{0,6},{1,7},{2,4},{3,5},{4,2},{5,3},{6,0},{7,1},{8,14},{9,15},{10,... | collective-permute-start | bytes 110600 | tf_op jit(solution)/shard_map/ppermute | solution.py:437
  7.2 3.8 %collective-permute-start.1 = (bf16[2,3,6,2,256]{4,3,2,1,0:T(2,128)(2,1)S(1)}, bf16[2,3,6,2,256]{4,3,2,1,0:T(2,128)(2,1)S(1)}, u32[]{:S(2)}, u32[]{:S(2)}) collective-permute-start(bf16[2,3,6,2,256]{4,3,2,1,0:T(2,128)(2,1)S(1)} %get-tuple-element.49), channel_id=1, source_target_pairs={{0,5},{1,4},{2,7},{3,6},{4,1},{5,0},{6,3},{7,2},{8,13},{9,12},{10,... | collective-permute-start | bytes 110600 | tf_op jit(solution)/shard_map/ppermute | solution.py:437
  7.9 3.0 %collective-permute-start = (bf16[2,3,6,2,256]{4,3,2,1,0:T(2,128)(2,1)S(1)}, bf16[2,3,6,2,256]{4,3,2,1,0:T(2,128)(2,1)S(1)}, u32[]{:S(2)}, u32[]{:S(2)}) collective-permute-start(bf16[2,3,6,2,256]{4,3,2,1,0:T(2,128)(2,1)S(1)} %get-tuple-element.49), channel_id=1, source_target_pairs={{0,4},{1,5},{2,6},{3,7},{4,0},{5,1},{6,2},{7,3},{8,12},{9,13},{10,... | collective-permute-start | bytes 110600 | tf_op jit(solution)/shard_map/ppermute | solution.py:437
  11.1 3.5 %collective-permute-start.8 = (bf16[5,72,128]{2,1,0:T(8,128)(2,1)S(1)}, bf16[5,72,128]{2,1,0:T(8,128)(2,1)S(1)}, u32[]{:S(2)}, u32[]{:S(2)}) collective-permute-start(bf16[5,72,128]{2,1,0:T(8,128)(2,1)S(1)} %get-tuple-element.61.refs_0_), channel_id=1, source_target_pairs={{0,4},{4,0},{8,12},{12,8},{16,20},{20,16},{24,28},{28,24},{1,5},{5... | collective-permute-start | bytes 276488 | tf_op jit(solution)/shard_map/ppermute | solution.py:443
  11.4 4.6 %collective-permute-start.5 = (bf16[5,72,128]{2,1,0:T(8,128)(2,1)S(1)}, bf16[5,72,128]{2,1,0:T(8,128)(2,1)S(1)}, u32[]{:S(2)}, u32[]{:S(2)}) collective-permute-start(bf16[5,72,128]{2,1,0:T(8,128)(2,1)S(1)} %get-tuple-element.61.refs_0_), channel_id=1, source_target_pairs={{0,12},{4,8},{8,4},{12,0},{16,28},{20,24},{24,20},{28,16},{1,13},{... | collective-permute-start | bytes 276488 | tf_op jit(solution)/shard_map/ppermute | solution.py:440
  12.8 1.7 %collective-permute-start.7 = (bf16[2,72,128]{2,1,0:T(8,128)(2,1)S(1)}, bf16[2,72,128]{2,1,0:T(8,128)(2,1)S(1)}, u32[]{:S(2)}, u32[]{:S(2)}) collective-permute-start(bf16[2,72,128]{2,1,0:T(8,128)(2,1)S(1)} %get-tuple-element.66), channel_id=1, source_target_pairs={{0,4},{4,0},{8,12},{12,8},{16,20},{20,16},{24,28},{28,24},{1,5},{5... | collective-permute-start | bytes 110600 | tf_op jit(solution)/shard_map/ppermute | solution.py:443
  13.1 1.5 %collective-permute-start.6 = (bf16[72,128]{1,0:T(8,128)(2,1)S(1)}, bf16[72,128]{1,0:T(8,128)(2,1)S(1)}, u32[]{:S(2)}, u32[]{:S(2)}) collective-permute-start(bf16[72,128]{1,0:T(8,128)(2,1)S(1)} %get-tuple-element.65), channel_id=1, source_target_pairs={{0,4},{24,28},{8,20},{12,16},{4,0},{28,24},{20,8},{16,12},{1,5},{2... | collective-permute-start | bytes 55304 | tf_op jit(solution)/shard_map/ppermute | solution.py:449
  16.0 1.3 %collective-permute-start.9 = (bf16[5,72,128]{2,1,0:T(8,128)(2,1)S(1)}, bf16[5,72,128]{2,1,0:T(8,128)(2,1)S(1)}, u32[]{:S(2)}, u32[]{:S(2)}) collective-permute-start(bf16[5,72,128]{2,1,0:T(8,128)(2,1)S(1)} %collective-permute-done.5.halo_last.refs_1_), channel_id=1, source_target_pairs={{0,4},{4,0},{8,12},{12,8},{16,20},{20,16},{24,28},{28,24},{1,5},{5... | collective-permute-start | bytes 276488 | tf_op jit(solution)/shard_map/ppermute | solution.py:443
  16.2 2.1 %copy-start = (bf16[256,768]{1,0:T(8,128)(2,1)S(1)}, bf16[256,768]{1,0:T(8,128)(2,1)}, u32[]{:S(2)}) copy-start(bf16[256,768]{1,0:T(8,128)(2,1)} %refs_9_.1) | copy-start | bytes 1179652
  17.2 8.5 %copy-start.1 = (bf16[96,72]{1,0:T(8,128)(2,1)S(1)}, bf16[96,72]{1,0:T(8,128)(2,1)}, u32[]{:S(2)}) copy-start(bf16[96,72]{1,0:T(8,128)(2,1)} %constant.8.clone.refs_6_) | copy-start | bytes 41476
  18.0 1.4 %collective-permute-start.10 = (bf16[4,2,72,128]{3,2,1,0:T(8,128)(2,1)S(1)}, bf16[4,2,72,128]{3,2,1,0:T(8,128)(2,1)S(1)}, u32[]{:S(2)}, u32[]{:S(2)}) collective-permute-start(bf16[4,2,72,128]{3,2,1,0:T(8,128)(2,1)S(1)} %get-tuple-element.82), channel_id=1, source_target_pairs={{0,4},{4,0},{8,12},{12,8},{16,20},{20,16},{24,28},{28,24},{1,5},{5... | collective-permute-start | bytes 442376 | tf_op jit(solution)/shard_map/ppermute | solution.py:443
  19.5 5.4 %collective-permute-start.11 = (bf16[2,72,128]{2,1,0:T(8,128)(2,1)S(1)}, bf16[2,72,128]{2,1,0:T(8,128)(2,1)S(1)}, u32[]{:S(2)}, u32[]{:S(2)}) collective-permute-start(bf16[2,72,128]{2,1,0:T(8,128)(2,1)S(1)} %get-tuple-element.83), channel_id=1, source_target_pairs={{0,28},{4,24},{8,20},{12,16},{16,12},{20,8},{24,4},{28,0},{1,29},{... | collective-permute-start | bytes 110600 | tf_op jit(solution)/shard_map/ppermute | solution.py:440
  20.8 4.0 %collective-permute-start.12 = (bf16[2,72,128]{2,1,0:T(8,128)(2,1)S(1)}, bf16[2,72,128]{2,1,0:T(8,128)(2,1)S(1)}, u32[]{:S(2)}, u32[]{:S(2)}) collective-permute-start(bf16[2,72,128]{2,1,0:T(8,128)(2,1)S(1)} %get-tuple-element.84), channel_id=1, source_target_pairs={{0,12},{4,8},{8,4},{12,0},{16,28},{20,24},{24,20},{28,16},{1,13},{... | collective-permute-start | bytes 110600 | tf_op jit(solution)/shard_map/ppermute | solution.py:440
  21.0 4.8 %collective-permute-start.13 = (bf16[2,72,128]{2,1,0:T(8,128)(2,1)S(1)}, bf16[2,72,128]{2,1,0:T(8,128)(2,1)S(1)}, u32[]{:S(2)}, u32[]{:S(2)}) collective-permute-start(bf16[2,72,128]{2,1,0:T(8,128)(2,1)S(1)} %get-tuple-element.85), channel_id=1, source_target_pairs={{0,20},{4,16},{8,28},{12,24},{16,4},{20,0},{24,12},{28,8},{1,21},{... | collective-permute-start | bytes 110600 | tf_op jit(solution)/shard_map/ppermute | solution.py:440
  26.1 4.1 %collective-permute-start.14 = (bf16[24,256]{1,0:T(8,128)(2,1)S(1)}, bf16[24,256]{1,0:T(8,128)(2,1)S(1)}, u32[]{:S(2)}, u32[]{:S(2)}) collective-permute-start(bf16[24,256]{1,0:T(8,128)(2,1)S(1)} %get-tuple-element.89), channel_id=1, source_target_pairs={{0,7},{1,6},{2,5},{3,4},{4,3},{5,2},{6,1},{7,0},{8,15},{9,14},{10,... | collective-permute-start | bytes 36872 | tf_op jit(solution)/shard_map/ppermute | solution.py:437
  28.2 3.1 %collective-permute-start.15 = (bf16[24,256]{1,0:T(8,128)(2,1)S(1)}, bf16[24,256]{1,0:T(8,128)(2,1)S(1)}, u32[]{:S(2)}, u32[]{:S(2)}) collective-permute-start(bf16[24,256]{1,0:T(8,128)(2,1)S(1)} %get-tuple-element.90), channel_id=1, source_target_pairs={{0,6},{1,7},{2,4},{3,5},{4,2},{5,3},{6,0},{7,1},{8,14},{9,15},{10,... | collective-permute-start | bytes 36872 | tf_op jit(solution)/shard_map/ppermute | solution.py:437
  28.2 3.1 %collective-permute-start.16 = (bf16[24,256]{1,0:T(8,128)(2,1)S(1)}, bf16[24,256]{1,0:T(8,128)(2,1)S(1)}, u32[]{:S(2)}, u32[]{:S(2)}) collective-permute-start(bf16[24,256]{1,0:T(8,128)(2,1)S(1)} %get-tuple-element.91), channel_id=1, source_target_pairs={{0,5},{1,4},{2,7},{3,6},{4,1},{5,0},{6,3},{7,2},{8,13},{9,12},{10,... | collective-permute-start | bytes 36872 | tf_op jit(solution)/shard_map/ppermute | solution.py:437
  29.2 2.1 %collective-permute-start.17 = (bf16[24,256]{1,0:T(8,128)(2,1)S(1)}, bf16[24,256]{1,0:T(8,128)(2,1)S(1)}, u32[]{:S(2)}, u32[]{:S(2)}) collective-permute-start(bf16[24,256]{1,0:T(8,128)(2,1)S(1)} %get-tuple-element.92), channel_id=1, source_target_pairs={{0,4},{1,5},{2,6},{3,7},{4,0},{5,1},{6,2},{7,3},{8,12},{9,13},{10,... | collective-permute-start | bytes 36872 | tf_op jit(solution)/shard_map/ppermute | solution.py:437

commit v13 on v12

--- a/solution.py
+++ b/solution.py
@@ -113,7 +113,7 @@
 
 
 def rim_kernel(n_col, per_sample, *refs):
-    tiles, (*parts, query, to_core, to_chip, joined, rims) = refs[:n_col], refs[n_col:]
+    tiles, (*parts, query, to_core, to_chip, joined, ours, rims) = refs[:n_col], refs[n_col:]
     col = lax.axis_index("col")
     rows = tiles[0].shape[1]
     lanes = to_chip.shape[1]
@@ -130,6 +130,7 @@
         for part in range(flat.shape[1] // lanes):
             out[part * used : (part + 1) * used] = flat[:, part * lanes : (part + 1) * lanes]
     join_kernel([part.shape[0] for part in parts], *parts, joined)
+    join_kernel([part.shape[0] for part in parts], *parts, ours)
     joined[joined.shape[0] - 1] = to_chip[...]
 
 
@@ -500,13 +501,13 @@
 
     rim = held((strip, lanes), BF16)
     blocks = sum(part.shape[0] for part in parts)
-    rim_core, rim_chip, sent = call(
+    rim_core, rim_chip, sent, ours = call(
         functools.partial(rim_kernel, n_col, per_sample),
-        (held((2, strip, lanes), BF16), rim, held((blocks + 1, strip, lanes), BF16)),
+        (held((2, strip, lanes), BF16), rim, held((blocks + 1, strip, lanes), BF16), held((blocks, strip, lanes), BF16)),
         [pltpu.VMEM((2, n_col, padded, channels), F32)],
     )(*tiles, *parts, query)
     received = to_chip(sent, distances[-1])
-    halo_odd, halo_core, early = to_odd_chip(rim_chip), to_core(rim_core), to_core(sent)
+    halo_odd, halo_core, early = to_odd_chip(rim_chip), to_core(rim_core), to_core(ours)
 
     whole = held((strip, channels), F32)
     conv, gate = call(

time: 32.2 us -> 32.2 us (level)
  transfers between devices with their start and end apart: 18 -> 18, of which waited for: 8 -> 9; matrix products, arithmetic and copies ran while one was open for 0% -> 0% of each run, Pallas kernels for 13% -> 13%
where the time goes in v13:
time: 32.2 us; the launch traced here: 32 us
  starting transfers between devices  17.5 us (54%)
  waiting for transfers between devices  7.5 us (23%)
  Pallas kernels  6.88 us (21%)
    ppermute x5, starting transfers between devices, to_chip(): lax.ppermute(array, 'row', [(i, i ^ 2 * k + 1) for i in range(n_row)])  9.03 us
    ppermute x8, starting transfers between devices, to_col(): return lax.ppermute(array, ('row', 'col'), pairs_of)  7.18 us
    pallas_call x11, Pallas kernels, run(): pl.pallas_call(kernel, out_shape=out_shape, in_specs=specs, out_specs=jax...  6.88 us
    ppermute x5, waiting for transfers between devices, to_chip(): lax.ppermute(array, 'row', [(i, i ^ 2 * k + 1) for i in range(n_row)])  3.51 us
    ppermute x8, waiting for transfers between devices, to_col(): return lax.ppermute(array, ('row', 'col'), pairs_of)  3.26 us
    ppermute x4, starting transfers between devices, to_core(): return lax.ppermute(array, 'row', [(i, i ^ 1) for i in range(n_row)])  0.96 us
    ppermute x4, waiting for transfers between devices, to_core(): return lax.ppermute(array, 'row', [(i, i ^ 1) for i in range(n_row)])  0.73 us
  transfers between devices with their start and end apart: 18, of which 9 were waited for; matrix products, arithmetic and copies ran while one was open for 0% of the time, Pallas kernels for 13%

profile of v13, /device:TPU:0, one launch (start us, length us, event | category | flops | bytes accessed | tf_op | source)
XLA Modules:
  0.0 32.0 jit_solution(5918438436145133831)
XLA Ops:
  0.0 0.9 %shard_map.109 = (bf16[2,3,6,2,256]{4,3,2,1,0:T(2,128)(2,1)S(1)}, bf16[2,72,128]{2,1,0:T(8,128)(2,1)S(1)}) custom-call(bf16[3,6,2,256]{3,2,1,0:T(2,128)(2,1)} %bitcast.9, bf16[3,6,2,256]{3,2,1,0:T(2,128)(2,1)} %bitcast.10, bf16[2,64,72]{2,1,0:T(8,128)(2,1)} %bitcast.6, bf16[2,64,72]{2,1,0:T(8,128)(2,1)} %bitcast.7), custom_call_target="tpu_custom_call" | custom-call | tf_op jit(solution)/shard_map/pallas_call | solution.py:35
  0.9 3.5 %collective-permute-start.4 = (bf16[2,72,128]{2,1,0:T(8,128)(2,1)S(1)}, bf16[2,72,128]{2,1,0:T(8,128)(2,1)S(1)}, u32[]{:S(2)}, u32[]{:S(2)}) collective-permute-start(bf16[2,72,128]{2,1,0:T(8,128)(2,1)S(1)} %get-tuple-element.51.refs_4_), channel_id=1, source_target_pairs={{0,20},{4,16},{8,28},{12,24},{16,4},{20,0},{24,12},{28,8},{1,21},{... | collective-permute-start | bytes 110600 | tf_op jit(solution)/shard_map/ppermute | solution.py:441
  4.4 2.7 %collective-permute-start.3 = (bf16[2,3,6,2,256]{4,3,2,1,0:T(2,128)(2,1)S(1)}, bf16[2,3,6,2,256]{4,3,2,1,0:T(2,128)(2,1)S(1)}, u32[]{:S(2)}, u32[]{:S(2)}) collective-permute-start(bf16[2,3,6,2,256]{4,3,2,1,0:T(2,128)(2,1)S(1)} %get-tuple-element.50), channel_id=1, source_target_pairs={{0,7},{1,6},{2,5},{3,4},{4,3},{5,2},{6,1},{7,0},{8,15},{9,14},{10,... | collective-permute-start | bytes 110600 | tf_op jit(solution)/shard_map/ppermute | solution.py:438
  7.2 0.0 collective-permute-start.2
  7.2 0.8 %collective-permute-start.1 = (bf16[2,3,6,2,256]{4,3,2,1,0:T(2,128)(2,1)S(1)}, bf16[2,3,6,2,256]{4,3,2,1,0:T(2,128)(2,1)S(1)}, u32[]{:S(2)}, u32[]{:S(2)}) collective-permute-start(bf16[2,3,6,2,256]{4,3,2,1,0:T(2,128)(2,1)S(1)} %get-tuple-element.50), channel_id=1, source_target_pairs={{0,5},{1,4},{2,7},{3,6},{4,1},{5,0},{6,3},{7,2},{8,13},{9,12},{10,... | collective-permute-start | bytes 110600 | tf_op jit(solution)/shard_map/ppermute | solution.py:438
  7.9 0.0 collective-permute-start
  7.9 1.4 %shard_map.110 = (bf16[3,72,96]{2,1,0:T(8,128)(2,1)S(1)}, bf16[3,24,32]{2,1,0:T(8,128)(2,1)S(1)}, bf16[3,3,256,256]{3,2,1,0:T(8,128)(2,1)S(1)}, bf16[256,256]{1,0:T(8,128)(2,1)S(1)}, bf16[72,128]{1,0:T(8,128)(2,1)S(1)}) custom-call(bf16[2,64,72]{2,1,0:T(8,128)(2,1)} %bitcast.8, bf16[3,72,96]{2,1,0:T(8,128)(2,1)} %constant.6.clone.refs_0_, ...), custom_call_target="tpu_custom_call" | custom-call | tf_op jit(solution)/shard_map/pallas_call | solution.py:35
  9.3 0.0 collective-permute-done.4.refs_5_
  9.3 0.0 collective-permute-done.3.refs_3_
  9.3 1.6 %collective-permute-done.2.refs_2_ = bf16[2,3,6,2,256]{4,3,2,1,0:T(2,128)(2,1)S(1)} collective-permute-done((bf16[2,3,6,2,256]{4,3,2,1,0:T(2,128)(2,1)S(1)}, bf16[2,3,6,2,256]{4,3,2,1,0:T(2,128)(2,1)S(1)}, u32[]{:S(2)}, u32[]{:S(2)}) %collective-permute-start.2) | collective-permute-done | bytes 36896 | tf_op jit(solution)/shard_map/ppermute | solution.py:438
  10.9 0.0 collective-permute-done.1.refs_1_
  10.9 0.0 collective-permute-done.refs_0_
  10.9 0.2 shard_map.111
  11.1 1.5 %collective-permute-start.5 = (bf16[5,72,128]{2,1,0:T(8,128)(2,1)S(1)}, bf16[5,72,128]{2,1,0:T(8,128)(2,1)S(1)}, u32[]{:S(2)}, u32[]{:S(2)}) collective-permute-start(bf16[5,72,128]{2,1,0:T(8,128)(2,1)S(1)} %get-tuple-element.62.refs_0_), channel_id=1, source_target_pairs={{0,12},{4,8},{8,4},{12,0},{16,28},{20,24},{24,20},{28,16},{1,13},{... | collective-permute-start | bytes 276488 | tf_op jit(solution)/shard_map/ppermute | solution.py:441
  12.6 0.3 collective-permute-start.8
  12.9 0.2 collective-permute-start.7
  13.1 0.3 collective-permute-start.6
  13.4 1.2 %shard_map.112 = (f32[72,256]{1,0:T(8,128)S(1)}, f32[72,256]{1,0:T(8,128)S(1)}) custom-call(bf16[2,3,6,2,256]{4,3,2,1,0:T(2,128)(2,1)S(1)} %collective-permute-done.refs_0_, bf16[2,3,6,2,256]{4,3,2,1,0:T(2,128)(2,1)S(1)} %collective-permute-done.1.refs_1_, bf16[2,3,6,2,256]{4,3,2,1,0:T(2,128)(2,1)S(1)} %collective-permute-done.2.refs_2_, ...), custom_call_target="tpu_custom_call" | custom-call | tf_op jit(solution)/shard_map/pallas_call | solution.py:35
  14.5 0.0 collective-permute-done.6.halo_odd
  14.6 0.0 collective-permute-done.7.halo_core.refs_3_.asker.refs_4_
  14.6 0.0 collective-permute-done.8.refs_2_
  14.6 1.2 %collective-permute-done.5.halo_last.refs_1_ = bf16[5,72,128]{2,1,0:T(8,128)(2,1)S(1)} collective-permute-done((bf16[5,72,128]{2,1,0:T(8,128)(2,1)S(1)}, bf16[5,72,128]{2,1,0:T(8,128)(2,1)S(1)}, u32[]{:S(2)}, u32[]{:S(2)}) %collective-permute-start.5) | collective-permute-done | bytes 92192 | tf_op jit(solution)/shard_map/ppermute | solution.py:441
  15.8 0.1 collective-permute-start.9
  16.0 0.6 %shard_map.113 = (bf16[72,256]{1,0:T(8,128)(2,1)S(1)}, bf16[72,128]{1,0:T(8,128)(2,1)S(1)}) custom-call(bf16[2,72,128]{2,1,0:T(8,128)(2,1)S(1)} %collective-permute-done.7.halo_core.refs_3_.asker.refs_4_, bf16[5,72,128]{2,1,0:T(8,128)(2,1)S(1)} %collective-permute-done.5.halo_last.refs_1_, bf16[72,128]{1,0:T(8,128)(2,1)S(1)} %collective-permute-done.6.halo_odd, ...), custom_call_target="tpu_custom_call" | custom-call | tf_op jit(solution)/shard_map/pallas_call | solution.py:35
  16.6 0.4 %shard_map.114 = (f32[2,432,72]{2,1,0:T(8,128)S(1)}, f32[2,432,72]{2,1,0:T(8,128)S(1)}) custom-call(bf16[5,72,128]{2,1,0:T(8,128)(2,1)S(1)} %get-tuple-element.62.refs_0_, bf16[5,72,128]{2,1,0:T(8,128)(2,1)S(1)} %collective-permute-done.5.halo_last.refs_1_, bf16[4,72,128]{2,1,0:T(8,128)(2,1)S(1)} %collective-permute-done.8.refs_2_, ...), custom_call_target="tpu_custom_call" | custom-call | tf_op jit(solution)/shard_map/pallas_call | solution.py:35
  16.9 0.1 collective-permute-done.9.late.refs_3_
  17.1 0.7 %shard_map.115 = (bf16[4,2,72,128]{3,2,1,0:T(8,128)(2,1)S(1)}, bf16[2,576,72]{2,1,0:T(8,128)(2,1)S(1)}, bf16[2,288,72]{2,1,0:T(8,128)(2,1)S(1)}) custom-call(bf16[5,72,128]{2,1,0:T(8,128)(2,1)S(1)} %collective-permute-done.9.late.refs_3_, bf16[2,72,128]{2,1,0:T(8,128)(2,1)S(1)} %collective-permute-done.7.halo_core.refs_3_.asker.refs_4_, ...), custom_call_target="tpu_custom_call" | custom-call | tf_op jit(solution)/shard_map/pallas_call | solution.py:35
  17.8 0.3 collective-permute-start.10
  18.1 0.0 copy-done
  18.1 0.5 %shard_map.116 = (bf16[4,2,72,128]{3,2,1,0:T(8,128)(2,1)S(1)}, f32[72,256]{1,0:T(8,128)S(1)}, bf16[256,256]{1,0:T(8,128)(2,1)S(1)}) custom-call(bf16[5,72,128]{2,1,0:T(8,128)(2,1)S(1)} %get-tuple-element.62.refs_0_, bf16[5,72,128]{2,1,0:T(8,128)(2,1)S(1)} %collective-permute-done.5.halo_last.refs_1_, bf16[4,72,128]{2,1,0:T(8,128)(2,1)S(1)} %collective-permute-done.8.refs_2_, ...), custom_call_target="tpu_custom_call" | custom-call | tf_op jit(solution)/shard_map/pallas_call | solution.py:35
  18.7 0.6 %collective-permute-done.10.received = bf16[4,2,72,128]{3,2,1,0:T(8,128)(2,1)S(1)} collective-permute-done((bf16[4,2,72,128]{3,2,1,0:T(8,128)(2,1)S(1)}, bf16[4,2,72,128]{3,2,1,0:T(8,128)(2,1)S(1)}, u32[]{:S(2)}, u32[]{:S(2)}) %collective-permute-start.10) | collective-permute-done | bytes 147488 | tf_op jit(solution)/shard_map/ppermute | solution.py:444
  19.3 1.0 %collective-permute-start.11 = (bf16[2,72,128]{2,1,0:T(8,128)(2,1)S(1)}, bf16[2,72,128]{2,1,0:T(8,128)(2,1)S(1)}, u32[]{:S(2)}, u32[]{:S(2)}) collective-permute-start(bf16[2,72,128]{2,1,0:T(8,128)(2,1)S(1)} %get-tuple-element.85), channel_id=1, source_target_pairs={{0,28},{4,24},{8,20},{12,16},{16,12},{20,8},{24,4},{28,0},{1,29},{... | collective-permute-start | bytes 110600 | tf_op jit(solution)/shard_map/ppermute | solution.py:441
  20.4 0.5 %collective-permute-start.12 = (bf16[2,72,128]{2,1,0:T(8,128)(2,1)S(1)}, bf16[2,72,128]{2,1,0:T(8,128)(2,1)S(1)}, u32[]{:S(2)}, u32[]{:S(2)}) collective-permute-start(bf16[2,72,128]{2,1,0:T(8,128)(2,1)S(1)} %get-tuple-element.86), channel_id=1, source_target_pairs={{0,12},{4,8},{8,4},{12,0},{16,28},{20,24},{24,20},{28,16},{1,13},{... | collective-permute-start | bytes 110600 | tf_op jit(solution)/shard_map/ppermute | solution.py:441
  20.9 2.5 %collective-permute-start.13 = (bf16[2,72,128]{2,1,0:T(8,128)(2,1)S(1)}, bf16[2,72,128]{2,1,0:T(8,128)(2,1)S(1)}, u32[]{:S(2)}, u32[]{:S(2)}) collective-permute-start(bf16[2,72,128]{2,1,0:T(8,128)(2,1)S(1)} %get-tuple-element.87), channel_id=1, source_target_pairs={{0,20},{4,16},{8,28},{12,24},{16,4},{20,0},{24,12},{28,8},{1,21},{... | collective-permute-start | bytes 110600 | tf_op jit(solution)/shard_map/ppermute | solution.py:441
  23.3 1.3 %collective-permute-done.11.refs_0_ = bf16[2,72,128]{2,1,0:T(8,128)(2,1)S(1)} collective-permute-done((bf16[2,72,128]{2,1,0:T(8,128)(2,1)S(1)}, bf16[2,72,128]{2,1,0:T(8,128)(2,1)S(1)}, u32[]{:S(2)}, u32[]{:S(2)}) %collective-permute-start.11) | collective-permute-done | bytes 36896 | tf_op jit(solution)/shard_map/ppermute | solution.py:441
  24.6 0.0 collective-permute-done.12.refs_1_
  24.6 1.0 %collective-permute-done.13.refs_2_ = bf16[2,72,128]{2,1,0:T(8,128)(2,1)S(1)} collective-permute-done((bf16[2,72,128]{2,1,0:T(8,128)(2,1)S(1)}, bf16[2,72,128]{2,1,0:T(8,128)(2,1)S(1)}, u32[]{:S(2)}, u32[]{:S(2)}) %collective-permute-start.13) | collective-permute-done | bytes 36896 | tf_op jit(solution)/shard_map/ppermute | solution.py:441
  25.6 0.0 copy-done.1
  25.6 0.3 shard_map.118
  25.9 1.4 %collective-permute-start.14 = (bf16[24,256]{1,0:T(8,128)(2,1)S(1)}, bf16[24,256]{1,0:T(8,128)(2,1)S(1)}, u32[]{:S(2)}, u32[]{:S(2)}) collective-permute-start(bf16[24,256]{1,0:T(8,128)(2,1)S(1)} %get-tuple-element.91), channel_id=1, source_target_pairs={{0,7},{1,6},{2,5},{3,4},{4,3},{5,2},{6,1},{7,0},{8,15},{9,14},{10,... | collective-permute-start | bytes 36872 | tf_op jit(solution)/shard_map/ppermute | solution.py:438
  27.4 0.8 %collective-permute-start.15 = (bf16[24,256]{1,0:T(8,128)(2,1)S(1)}, bf16[24,256]{1,0:T(8,128)(2,1)S(1)}, u32[]{:S(2)}, u32[]{:S(2)}) collective-permute-start(bf16[24,256]{1,0:T(8,128)(2,1)S(1)} %get-tuple-element.92), channel_id=1, source_target_pairs={{0,6},{1,7},{2,4},{3,5},{4,2},{5,3},{6,0},{7,1},{8,14},{9,15},{10,... | collective-permute-start | bytes 36872 | tf_op jit(solution)/shard_map/ppermute | solution.py:438
  28.2 1.5 %collective-permute-start.16 = (bf16[24,256]{1,0:T(8,128)(2,1)S(1)}, bf16[24,256]{1,0:T(8,128)(2,1)S(1)}, u32[]{:S(2)}, u32[]{:S(2)}) collective-permute-start(bf16[24,256]{1,0:T(8,128)(2,1)S(1)} %get-tuple-element.93), channel_id=1, source_target_pairs={{0,5},{1,4},{2,7},{3,6},{4,1},{5,0},{6,3},{7,2},{8,13},{9,12},{10,... | collective-permute-start | bytes 36872 | tf_op jit(solution)/shard_map/ppermute | solution.py:438
  29.6 0.0 collective-permute-start.17
  29.6 0.4 %collective-permute-done.14.refs_0_ = bf16[24,256]{1,0:T(8,128)(2,1)S(1)} collective-permute-done((bf16[24,256]{1,0:T(8,128)(2,1)S(1)}, bf16[24,256]{1,0:T(8,128)(2,1)S(1)}, u32[]{:S(2)}, u32[]{:S(2)}) %collective-permute-start.14) | collective-permute-done | bytes 12320 | tf_op jit(solution)/shard_map/ppermute | solution.py:438
  30.0 0.5 %collective-permute-done.15.refs_1_ = bf16[24,256]{1,0:T(8,128)(2,1)S(1)} collective-permute-done((bf16[24,256]{1,0:T(8,128)(2,1)S(1)}, bf16[24,256]{1,0:T(8,128)(2,1)S(1)}, u32[]{:S(2)}, u32[]{:S(2)}) %collective-permute-start.15) | collective-permute-done | bytes 12320 | tf_op jit(solution)/shard_map/ppermute | solution.py:438
  30.5 0.8 %collective-permute-done.16.refs_2_ = bf16[24,256]{1,0:T(8,128)(2,1)S(1)} collective-permute-done((bf16[24,256]{1,0:T(8,128)(2,1)S(1)}, bf16[24,256]{1,0:T(8,128)(2,1)S(1)}, u32[]{:S(2)}, u32[]{:S(2)}) %collective-permute-start.16) | collective-permute-done | bytes 12320 | tf_op jit(solution)/shard_map/ppermute | solution.py:438
  31.3 0.0 collective-permute-done.17.refs_3_
  31.3 0.7 %shard_map.119 = bf16[3,6,2,256]{3,2,1,0:T(2,128)(2,1)} custom-call(bf16[24,256]{1,0:T(8,128)(2,1)S(1)} %collective-permute-done.14.refs_0_, bf16[24,256]{1,0:T(8,128)(2,1)S(1)} %collective-permute-done.15.refs_1_, bf16[24,256]{1,0:T(8,128)(2,1)S(1)} %collective-permute-done.16.refs_2_, bf16[24,256]{1,0:T(8,128)(2,1)S(1)} %collective-permute-done.17.refs_3_), custom_call_target="tpu_custom_call" | custom-call | tf_op jit(solution)/shard_map/pallas_call | solution.py:35
  (3 shorter events, 0.0 us)
Async XLA Ops:
  0.9 8.4 %collective-permute-start.4 = (bf16[2,72,128]{2,1,0:T(8,128)(2,1)S(1)}, bf16[2,72,128]{2,1,0:T(8,128)(2,1)S(1)}, u32[]{:S(2)}, u32[]{:S(2)}) collective-permute-start(bf16[2,72,128]{2,1,0:T(8,128)(2,1)S(1)} %get-tuple-element.51.refs_4_), channel_id=1, source_target_pairs={{0,20},{4,16},{8,28},{12,24},{16,4},{20,0},{24,12},{28,8},{1,21},{... | collective-permute-start | bytes 110600 | tf_op jit(solution)/shard_map/ppermute | solution.py:441
  4.4 4.9 %collective-permute-start.3 = (bf16[2,3,6,2,256]{4,3,2,1,0:T(2,128)(2,1)S(1)}, bf16[2,3,6,2,256]{4,3,2,1,0:T(2,128)(2,1)S(1)}, u32[]{:S(2)}, u32[]{:S(2)}) collective-permute-start(bf16[2,3,6,2,256]{4,3,2,1,0:T(2,128)(2,1)S(1)} %get-tuple-element.50), channel_id=1, source_target_pairs={{0,7},{1,6},{2,5},{3,4},{4,3},{5,2},{6,1},{7,0},{8,15},{9,14},{10,... | collective-permute-start | bytes 110600 | tf_op jit(solution)/shard_map/ppermute | solution.py:438
  7.2 3.8 %collective-permute-start.2 = (bf16[2,3,6,2,256]{4,3,2,1,0:T(2,128)(2,1)S(1)}, bf16[2,3,6,2,256]{4,3,2,1,0:T(2,128)(2,1)S(1)}, u32[]{:S(2)}, u32[]{:S(2)}) collective-permute-start(bf16[2,3,6,2,256]{4,3,2,1,0:T(2,128)(2,1)S(1)} %get-tuple-element.50), channel_id=1, source_target_pairs={{0,6},{1,7},{2,4},{3,5},{4,2},{5,3},{6,0},{7,1},{8,14},{9,15},{10,... | collective-permute-start | bytes 110600 | tf_op jit(solution)/shard_map/ppermute | solution.py:438
  7.2 3.8 %collective-permute-start.1 = (bf16[2,3,6,2,256]{4,3,2,1,0:T(2,128)(2,1)S(1)}, bf16[2,3,6,2,256]{4,3,2,1,0:T(2,128)(2,1)S(1)}, u32[]{:S(2)}, u32[]{:S(2)}) collective-permute-start(bf16[2,3,6,2,256]{4,3,2,1,0:T(2,128)(2,1)S(1)} %get-tuple-element.50), channel_id=1, source_target_pairs={{0,5},{1,4},{2,7},{3,6},{4,1},{5,0},{6,3},{7,2},{8,13},{9,12},{10,... | collective-permute-start | bytes 110600 | tf_op jit(solution)/shard_map/ppermute | solution.py:438
  7.9 3.0 %collective-permute-start = (bf16[2,3,6,2,256]{4,3,2,1,0:T(2,128)(2,1)S(1)}, bf16[2,3,6,2,256]{4,3,2,1,0:T(2,128)(2,1)S(1)}, u32[]{:S(2)}, u32[]{:S(2)}) collective-permute-start(bf16[2,3,6,2,256]{4,3,2,1,0:T(2,128)(2,1)S(1)} %get-tuple-element.50), channel_id=1, source_target_pairs={{0,4},{1,5},{2,6},{3,7},{4,0},{5,1},{6,2},{7,3},{8,12},{9,13},{10,... | collective-permute-start | bytes 110600 | tf_op jit(solution)/shard_map/ppermute | solution.py:438
  11.1 4.7 %collective-permute-start.5 = (bf16[5,72,128]{2,1,0:T(8,128)(2,1)S(1)}, bf16[5,72,128]{2,1,0:T(8,128)(2,1)S(1)}, u32[]{:S(2)}, u32[]{:S(2)}) collective-permute-start(bf16[5,72,128]{2,1,0:T(8,128)(2,1)S(1)} %get-tuple-element.62.refs_0_), channel_id=1, source_target_pairs={{0,12},{4,8},{8,4},{12,0},{16,28},{20,24},{24,20},{28,16},{1,13},{... | collective-permute-start | bytes 276488 | tf_op jit(solution)/shard_map/ppermute | solution.py:441
  12.6 2.0 %collective-permute-start.8 = (bf16[4,72,128]{2,1,0:T(8,128)(2,1)S(1)}, bf16[4,72,128]{2,1,0:T(8,128)(2,1)S(1)}, u32[]{:S(2)}, u32[]{:S(2)}) collective-permute-start(bf16[4,72,128]{2,1,0:T(8,128)(2,1)S(1)} %get-tuple-element.68), channel_id=1, source_target_pairs={{0,4},{4,0},{8,12},{12,8},{16,20},{20,16},{24,28},{28,24},{1,5},{5... | collective-permute-start | bytes 221192 | tf_op jit(solution)/shard_map/ppermute | solution.py:444
  12.9 1.7 %collective-permute-start.7 = (bf16[2,72,128]{2,1,0:T(8,128)(2,1)S(1)}, bf16[2,72,128]{2,1,0:T(8,128)(2,1)S(1)}, u32[]{:S(2)}, u32[]{:S(2)}) collective-permute-start(bf16[2,72,128]{2,1,0:T(8,128)(2,1)S(1)} %get-tuple-element.67), channel_id=1, source_target_pairs={{0,4},{4,0},{8,12},{12,8},{16,20},{20,16},{24,28},{28,24},{1,5},{5... | collective-permute-start | bytes 110600 | tf_op jit(solution)/shard_map/ppermute | solution.py:444
  13.1 1.5 %collective-permute-start.6 = (bf16[72,128]{1,0:T(8,128)(2,1)S(1)}, bf16[72,128]{1,0:T(8,128)(2,1)S(1)}, u32[]{:S(2)}, u32[]{:S(2)}) collective-permute-start(bf16[72,128]{1,0:T(8,128)(2,1)S(1)} %get-tuple-element.66), channel_id=1, source_target_pairs={{0,4},{24,28},{8,20},{12,16},{4,0},{28,24},{20,8},{16,12},{1,5},{2... | collective-permute-start | bytes 55304 | tf_op jit(solution)/shard_map/ppermute | solution.py:450
  15.8 1.3 %collective-permute-start.9 = (bf16[5,72,128]{2,1,0:T(8,128)(2,1)S(1)}, bf16[5,72,128]{2,1,0:T(8,128)(2,1)S(1)}, u32[]{:S(2)}, u32[]{:S(2)}) collective-permute-start(bf16[5,72,128]{2,1,0:T(8,128)(2,1)S(1)} %collective-permute-done.5.halo_last.refs_1_), channel_id=1, source_target_pairs={{0,4},{4,0},{8,12},{12,8},{16,20},{20,16},{24,28},{28,24},{1,5},{5... | collective-permute-start | bytes 276488 | tf_op jit(solution)/shard_map/ppermute | solution.py:444
  15.9 2.2 %copy-start = (bf16[256,768]{1,0:T(8,128)(2,1)S(1)}, bf16[256,768]{1,0:T(8,128)(2,1)}, u32[]{:S(2)}) copy-start(bf16[256,768]{1,0:T(8,128)(2,1)} %refs_9_.1) | copy-start | bytes 1179652
  17.1 8.5 %copy-start.1 = (bf16[96,72]{1,0:T(8,128)(2,1)S(1)}, bf16[96,72]{1,0:T(8,128)(2,1)}, u32[]{:S(2)}) copy-start(bf16[96,72]{1,0:T(8,128)(2,1)} %constant.8.clone.refs_6_) | copy-start | bytes 41476
  17.8 1.4 %collective-permute-start.10 = (bf16[4,2,72,128]{3,2,1,0:T(8,128)(2,1)S(1)}, bf16[4,2,72,128]{3,2,1,0:T(8,128)(2,1)S(1)}, u32[]{:S(2)}, u32[]{:S(2)}) collective-permute-start(bf16[4,2,72,128]{3,2,1,0:T(8,128)(2,1)S(1)} %get-tuple-element.84), channel_id=1, source_target_pairs={{0,4},{4,0},{8,12},{12,8},{16,20},{20,16},{24,28},{28,24},{1,5},{5... | collective-permute-start | bytes 442376 | tf_op jit(solution)/shard_map/ppermute | solution.py:444
  19.3 5.3 %collective-permute-start.11 = (bf16[2,72,128]{2,1,0:T(8,128)(2,1)S(1)}, bf16[2,72,128]{2,1,0:T(8,128)(2,1)S(1)}, u32[]{:S(2)}, u32[]{:S(2)}) collective-permute-start(bf16[2,72,128]{2,1,0:T(8,128)(2,1)S(1)} %get-tuple-element.85), channel_id=1, source_target_pairs={{0,28},{4,24},{8,20},{12,16},{16,12},{20,8},{24,4},{28,0},{1,29},{... | collective-permute-start | bytes 110600 | tf_op jit(solution)/shard_map/ppermute | solution.py:441
  20.4 4.2 %collective-permute-start.12 = (bf16[2,72,128]{2,1,0:T(8,128)(2,1)S(1)}, bf16[2,72,128]{2,1,0:T(8,128)(2,1)S(1)}, u32[]{:S(2)}, u32[]{:S(2)}) collective-permute-start(bf16[2,72,128]{2,1,0:T(8,128)(2,1)S(1)} %get-tuple-element.86), channel_id=1, source_target_pairs={{0,12},{4,8},{8,4},{12,0},{16,28},{20,24},{24,20},{28,16},{1,13},{... | collective-permute-start | bytes 110600 | tf_op jit(solution)/shard_map/ppermute | solution.py:441
  20.9 4.7 %collective-permute-start.13 = (bf16[2,72,128]{2,1,0:T(8,128)(2,1)S(1)}, bf16[2,72,128]{2,1,0:T(8,128)(2,1)S(1)}, u32[]{:S(2)}, u32[]{:S(2)}) collective-permute-start(bf16[2,72,128]{2,1,0:T(8,128)(2,1)S(1)} %get-tuple-element.87), channel_id=1, source_target_pairs={{0,20},{4,16},{8,28},{12,24},{16,4},{20,0},{24,12},{28,8},{1,21},{... | collective-permute-start | bytes 110600 | tf_op jit(solution)/shard_map/ppermute | solution.py:441
  25.9 4.1 %collective-permute-start.14 = (bf16[24,256]{1,0:T(8,128)(2,1)S(1)}, bf16[24,256]{1,0:T(8,128)(2,1)S(1)}, u32[]{:S(2)}, u32[]{:S(2)}) collective-permute-start(bf16[24,256]{1,0:T(8,128)(2,1)S(1)} %get-tuple-element.91), channel_id=1, source_target_pairs={{0,7},{1,6},{2,5},{3,4},{4,3},{5,2},{6,1},{7,0},{8,15},{9,14},{10,... | collective-permute-start | bytes 36872 | tf_op jit(solution)/shard_map/ppermute | solution.py:438
  27.4 3.1 %collective-permute-start.15 = (bf16[24,256]{1,0:T(8,128)(2,1)S(1)}, bf16[24,256]{1,0:T(8,128)(2,1)S(1)}, u32[]{:S(2)}, u32[]{:S(2)}) collective-permute-start(bf16[24,256]{1,0:T(8,128)(2,1)S(1)} %get-tuple-element.92), channel_id=1, source_target_pairs={{0,6},{1,7},{2,4},{3,5},{4,2},{5,3},{6,0},{7,1},{8,14},{9,15},{10,... | collective-permute-start | bytes 36872 | tf_op jit(solution)/shard_map/ppermute | solution.py:438
  28.2 3.1 %collective-permute-start.16 = (bf16[24,256]{1,0:T(8,128)(2,1)S(1)}, bf16[24,256]{1,0:T(8,128)(2,1)S(1)}, u32[]{:S(2)}, u32[]{:S(2)}) collective-permute-start(bf16[24,256]{1,0:T(8,128)(2,1)S(1)} %get-tuple-element.93), channel_id=1, source_target_pairs={{0,5},{1,4},{2,7},{3,6},{4,1},{5,0},{6,3},{7,2},{8,13},{9,12},{10,... | collective-permute-start | bytes 36872 | tf_op jit(solution)/shard_map/ppermute | solution.py:438
  29.6 1.7 %collective-permute-start.17 = (bf16[24,256]{1,0:T(8,128)(2,1)S(1)}, bf16[24,256]{1,0:T(8,128)(2,1)S(1)}, u32[]{:S(2)}, u32[]{:S(2)}) collective-permute-start(bf16[24,256]{1,0:T(8,128)(2,1)S(1)} %get-tuple-element.94), channel_id=1, source_target_pairs={{0,4},{1,5},{2,6},{3,7},{4,0},{5,1},{6,2},{7,3},{8,12},{9,13},{10,... | collective-permute-start | bytes 36872 | tf_op jit(solution)/shard_map/ppermute | solution.py:438
